TPU v7x, 32 devices: a whole 2x2x4 slice. The times are simulated.
32 devices in a mesh: hi: 8 (over z, y), lo: 4 (over x, core).
Axes of the slice: x: 2, y: 2, z: 4, core: 2. Of those that a mesh axis runs over, the one named last changes fastest.
Arguments:
- state: bfloat16 [2, 8388608], P(None, ('hi', 'lo')), may hold values from -6 to 6
- gates: bfloat16 [4, 3, 2, 64, 64], replicated, may hold values from -0.5 to 0.5
- regroup: int32 [4], replicated, may hold values from 0 to 3, each once
Outputs:
- final_state: bfloat16 [2, 8388608], P(None, ('hi', 'lo'))
Inputs may be any that keep to these rules, and one draw needn't show every extreme that they name: `regroup`: each value of 0 to 3 appears once.
All inputs are finite; a program needn't handle non-finite values.
Results may differ from a plain program's by a relative error of at most 0.02.
Values may be sent and summed in bfloat16 or wider, within the bound.
No kernel may reach another device: no remote copies, remote signals or barrier semaphores. Data moves between devices by JAX's collectives and lax.ppermute only.
A program may use at most 64 MiB of HBM per device.

v0:
```python
import functools

import jax
import jax.numpy as jnp
from jax import lax
from jax.experimental import pallas as pl
from jax.experimental.pallas import tpu as pltpu
from jax.sharding import PartitionSpec as P

GQ = 6
G = 2**GQ
HALF = G // 2
BF = jnp.bfloat16
F32 = jnp.float32


def product(later, earlier):
    dot = functools.partial(jnp.einsum, "ij,jk->ik", precision=lax.Precision.HIGHEST, preferred_element_type=F32)
    real = dot(later[0], earlier[0]) - dot(later[1], earlier[1])
    imag = dot(later[0], earlier[1]) + dot(later[1], earlier[0])
    return jnp.stack([real, imag])


def as_real(gate):
    upper = jnp.stack([gate[0], -gate[1]], axis=1)
    lower = jnp.stack([gate[1], gate[0]], axis=1)
    return jnp.stack([upper, lower], axis=0)


def times_i(w, axis):
    first, second = jnp.split(w, 2, axis=axis)
    return jnp.concatenate([-second, first], axis=axis)


def flip(w, axis, bit):
    return jnp.where(bit == 0, w, jnp.flip(w, axis))


def first_weights(gate):
    m = as_real(gate).reshape(2, 2, HALF, 2, 2, HALF)
    w = jnp.einsum("pqrsuv,xy->qpxrsyuv", m, jnp.eye(2, dtype=m.dtype))
    return w.reshape(4 * G, 4 * G).astype(BF)


def right_weights(gate, in_low, in_bit, out_bit):
    m = as_real(gate)
    m = m.reshape(2, 2, HALF, 2, G)
    if in_low:
        m = m.reshape(2, 2, HALF, 2, HALF, 2)
        w = jnp.einsum("pirsht,xy->xsthiypr", m, jnp.eye(2, dtype=m.dtype))
    else:
        m = flip(m.reshape(2, 2, HALF, 2, 2, HALF), 4, in_bit)
        w = jnp.einsum("pirsjh,xy->jxshiypr", m, jnp.eye(2, dtype=m.dtype))
    w = flip(w, 4, out_bit)
    both = jnp.stack([w, times_i(w, 6)], axis=4)
    return both.reshape(4 * G, 8 * G).astype(BF)


def left_weights(gate, order, out_bit):
    g = jnp.concatenate([gate[0][:, order], gate[1][:, order]], axis=1)
    return flip(g.reshape(2, HALF, 2 * G), 0, out_bit).reshape(G, 2 * G).astype(BF)


def last_weights(gate, in_bit):
    m = as_real(gate).reshape(2, HALF, 2, 2, 2, HALF)
    m = flip(m, 4, in_bit)
    w = jnp.einsum("phtsjr,xy->ptxhjysr", m, jnp.eye(2, dtype=m.dtype))
    return w.reshape(4 * G, 4 * G).astype(BF)


def turn(parts):
    lane = lax.broadcasted_iota(jnp.int32, (parts[0].shape[0], 128), 1)
    wide = lane < 64
    narrow = (lane & 32) == 0
    out = [[None, None] for _ in range(8)]
    for n in range(2):
        for m in range(2):
            a = [parts[n * 4 + r][:, m * 128 : (m + 1) * 128] for r in range(4)]
            s = [None] * 4
            for r in range(2):
                s[r] = jnp.where(wide, a[r], pltpu.roll(a[r + 2], 64, 1))
                s[r + 2] = jnp.where(wide, pltpu.roll(a[r], 64, 1), a[r + 2])
            for r in (0, 2):
                out[m * 4 + r][n] = jnp.where(narrow, s[r], pltpu.roll(s[r + 1], 32, 1))
                out[m * 4 + r + 1][n] = jnp.where(narrow, pltpu.roll(s[r], 96, 1), s[r + 1])
    return out


NT = (((1,), (1,)), ((), ()))


def both_gates(x, w, g):
    n = x.shape[0]
    z = jnp.dot(x.reshape(n * G, 4 * G), w, preferred_element_type=F32).astype(BF)
    outs = []
    for k in range(n):
        rows = z[k * G : (k + 1) * G]
        s = jnp.concatenate([rows[:, : 4 * G], rows[:, 4 * G :]], axis=0)
        outs.append(jnp.dot(g, s, preferred_element_type=F32).astype(BF))
    return outs


def store_blocks(outs, at, blocks):
    for k, out in enumerate(outs):
        for i in range(2):
            for j in range(2):
                blocks[2 * i + j][at + k] = out[j * HALF : (j + 1) * HALF, i * 128 : (i + 1) * 128]


STEP = 8


def first_kernel(x_ref, w0_ref, w1_ref, g_ref, o00, o01, o10, o11, turned):
    def relayout(k, carry):
        rows = pl.ds(k * 256, 256)
        x = jnp.concatenate([x_ref[0, rows, :], x_ref[1, rows, :]], axis=1)
        r = lax.dot_general(w0_ref[...], x, NT, preferred_element_type=F32)
        tiles = turn([r[g * HALF : (g + 1) * HALF] for g in range(8)])
        for q in range(8):
            for n in range(2):
                turned[n, pl.ds(k * 8 + q, HALF, stride=G), :] = tiles[q][n]
        return carry

    lax.fori_loop(0, G // 8, relayout, 0)

    def gates(k, carry):
        rows = pl.ds(k * STEP * G, STEP * G)
        x = jnp.concatenate([turned[0, rows, :], turned[1, rows, :]], axis=1).astype(BF).reshape(STEP, G, 4 * G)
        store_blocks(both_gates(x, w1_ref[...], g_ref[...]), k * STEP, (o00, o01, o10, o11))
        return carry

    lax.fori_loop(0, HALF // STEP, gates, 0)


def middle_kernel(*refs):
    *ins, w1_ref, g_ref, o00, o01, o10, o11 = refs

    def gates(k, carry):
        at = pl.ds(k * STEP, STEP)
        halves = [jnp.concatenate([x[i, at] for x in ins], axis=1) for i in range(2)]
        x = jnp.concatenate(halves, axis=2)
        store_blocks(both_gates(x, w1_ref[...], g_ref[...]), k * STEP, (o00, o01, o10, o11))
        return carry

    lax.fori_loop(0, HALF // STEP, gates, 0)


def last_kernel(bit_ref, b00, b01, b10, b11, w_ref, o_ref, wide):
    bit = bit_ref[0]
    blocks = ((b00, b01), (b10, b11))

    def widen(k, carry):
        for i in range(2):
            for j in range(2):
                start = pl.multiple_of(k * G + (bit ^ j) * HALF, HALF)
                wide[i, pl.ds(start, HALF), :] = blocks[i][j][k].astype(F32)
        return carry

    lax.fori_loop(0, HALF, widen, 0)

    def relayout(k, carry):
        halves = [
            jnp.concatenate([wide[i, pl.ds(k * 8 + q, HALF, stride=G), :] for q in range(8)], axis=0) for i in range(2)
        ]
        x = jnp.concatenate(halves, axis=1).astype(BF)
        r = lax.dot_general(w_ref[...], x, NT, preferred_element_type=F32)
        tiles = turn([r[g * HALF : (g + 1) * HALF] for g in range(8)])
        for q in range(8):
            for n in range(2):
                o_ref[n, pl.ds(k * 256 + q * HALF, HALF), :] = tiles[q][n].astype(BF)
        return carry

    lax.fori_loop(0, G // 8, relayout, 0)


def pick_kernel(s_ref, b00, b01, b10, b11, *outs):
    blocks = ((b00, b01), (b10, b11))
    rows = outs[0].shape[2]
    for o, out in enumerate(outs):
        j = s_ref[o, 0]
        at = pl.ds(pl.multiple_of(s_ref[o, 1] * rows, rows), rows)
        for i in range(2):
            out[i] = jnp.where(j == 0, blocks[i][0][:, at, :], blocks[i][1][:, at, :])


VMEM = pl.BlockSpec(memory_space=pltpu.VMEM)
SMEM = pl.BlockSpec(memory_space=pltpu.SMEM)


def call(kernel, outs, args, specs=None, scratch=()):
    return pl.pallas_call(
        kernel,
        out_shape=outs,
        in_specs=specs or [VMEM] * len(args),
        out_specs=jax.tree.map(lambda _: VMEM, outs),
        scratch_shapes=scratch,
        compiler_params=pltpu.CompilerParams(vmem_limit_bytes=40 * 2**20),
    )(*args)


def exchange(blocks, b_bit, a_bit):
    size = lax.axis_size("hi")
    out = []
    for at, block in enumerate(blocks):
        apart = (at >> 1 << b_bit) | ((at & 1) << a_bit)
        out.append(lax.ppermute(block, "hi", [(d, d ^ apart) for d in range(size)]) if apart else block)
    return out


def on_device(state, gates, regroup):
    hi_bits = lax.axis_size("hi").bit_length() - 1
    groups = lax.axis_size("lo")
    hi = lax.axis_index("hi")
    lo = lax.axis_index("lo")
    bits = [k % hi_bits for k in range(4)]
    own = [hi >> bit & 1 for bit in bits]
    top = G // groups

    g = gates.astype(F32)
    w0 = first_weights(product(product(g[3, 0], g[2, 0]), product(g[1, 0], g[0, 0])))
    w1a = right_weights(g[0, 1], True, None, own[0])
    w1b = right_weights(product(g[2, 1], g[1, 1]), False, own[0], own[2])
    w1c = last_weights(g[3, 1], own[2])
    ga = left_weights(product(g[1, 2], g[0, 2]), jnp.arange(G), own[1])

    block = jax.ShapeDtypeStruct((HALF, HALF, 128), BF)
    x = state.reshape(2, -1, 128)
    blocks = call(
        first_kernel,
        [block] * 4,
        (x, w0, w1a, ga),
        scratch=[pltpu.VMEM((2, HALF * G, 128), F32)],
    )
    blocks = exchange(blocks, bits[0], bits[1])

    if groups == 4:
        order = (jnp.arange(G) // top ^ lo) * top + jnp.arange(G) % top
        sent = regroup[jnp.arange(groups) ^ lo]
        table = jnp.stack([sent // 2 ^ own[1], sent % 2], axis=1)
        part = jax.ShapeDtypeStruct((2, HALF, top, 128), BF)
        parts = call(pick_kernel, [part] * groups, (table, *blocks), specs=[SMEM] + [VMEM] * 4)
        parts = [parts[0]] + [
            lax.ppermute(parts[o], "lo", [(d, d ^ o) for d in range(groups)]) for o in range(1, groups)
        ]
    else:
        order = jnp.arange(G)
        whole = jnp.stack([flip(jnp.stack(blocks[2 * i : 2 * i + 2], 1), 1, own[1]) for i in range(2)])
        whole = whole.reshape(2, HALF, groups, top, 128)
        whole = lax.all_to_all(jnp.take(whole, regroup, axis=2), "lo", split_axis=2, concat_axis=2, tiled=True)
        parts = [whole.reshape(2, HALF, G, 128)]
    gb = left_weights(product(g[3, 2], g[2, 2]), order, own[3])
    blocks = call(middle_kernel, [block] * 4, (*parts, w1b, gb))
    blocks = exchange(blocks, bits[2], bits[3])

    out = call(
        last_kernel,
        jax.ShapeDtypeStruct(x.shape, BF),
        (own[3].reshape(1), *blocks, w1c),
        specs=[SMEM] + [VMEM] * 5,
        scratch=[pltpu.VMEM((2, HALF * G, 128), F32)],
    )
    return out.reshape(state.shape)


def solution(mesh):
    placed = (P(None, ("hi", "lo")), P(), P())
    return jax.shard_map(
        on_device, mesh=mesh, in_specs=placed, out_specs=P(None, ("hi", "lo")), check_vma=False
    )
```

profile of v0, /device:TPU:0, one launch (start us, length us, event | category | flops | bytes accessed | tf_op | source)
XLA Modules:
  0.0 102.6 jit_solution(11542400834274812358)
XLA Ops:
  0.0 0.9 fusion.22
  0.9 0.9 fusion.16
  1.8 0.9 fusion.32
  2.6 0.9 fusion.26
  3.5 0.9 fusion.42
  4.4 0.9 fusion.36
  5.5 0.6 fusion.105
  6.8 0.6 gather_fusion.1
  7.5 0.6 gather_fusion.2
  8.1 0.7 copy.35
  11.9 0.6 rev.24
  13.2 0.7 fusion.104
  14.0 0.7 fusion.3
  14.7 1.4 %maximum_bitcast_fusion = bf16[2,2,2,32,1,2,2,2,32]{8,7,6,5,4,3,2,1,0:T(2,128)(2,1)S(1)} fusion(bf16[2,2,2,32,2,2,1,32]{7,6,5,4,3,2,1,0:T(2,128)(2,1)S(1)} %bitcast.170, bf16[2,2,2,32,2,2,1,32]{7,6,5,4,3,2,1,0:T(2,128)(2,1)S(1)} %fusion.3), kind=kLoop, calls=%fused_computation.33 | loop fusion | flops 262144 | bytes 262144 | tf_op jit(solution)/shard_map/stack | solution.py:55
  16.0 1.6 %pad_maximum_fusion = bf16[2,2,2,32,2,2,2,2,32]{8,7,6,5,4,3,2,1,0:T(2,128)(2,1)S(1)} fusion(bf16[2,2,2,32,1,2,2,2,32]{8,7,6,5,4,3,2,1,0:T(2,128)(2,1)S(1)} %maximum_bitcast_fusion, bf16[2,2,2,32,1,2,2,2,32]{8,7,6,5,4,3,2,1,0:T(2,128)(2,1)S(1)} %bitcast.171), kind=kLoop, calls=%fused_computation.21 | loop fusion | flops 131072 | bytes 524288 | tf_op jit(solution)/shard_map/stack | solution.py:55
  17.7 1.1 %convert_element_type.41.w1_ref = bf16[256,512]{1,0:T(8,128)(2,1)S(1)} reshape(bf16[2,2,2,32,2,2,2,2,32]{8,7,6,5,4,3,2,1,0:T(2,128)(2,1)S(1)} %pad_maximum_fusion) | data formatting | bytes 524288 | tf_op jit(solution)/shard_map/convert_element_type | solution.py:56
  18.7 0.6 multiply_bitcast_fusion
  19.4 0.8 copy.28
  20.6 1.4 %copy.47 = bf16[1,2,2048,128]{3,2,1,0:T(8,128)(2,1)S(1)} copy(bf16[1,2,2048,128]{3,1,2,0:T(2,128)(2,1)} %bitcast.172) | data formatting | bytes 2097152
  22.0 6.3 %shard_map.37 = (bf16[32,32,128]{2,1,0:T(8,128)(2,1)S(1)}, bf16[32,32,128]{2,1,0:T(8,128)(2,1)S(1)}, bf16[32,32,128]{2,1,0:T(8,128)(2,1)S(1)}, bf16[32,32,128]{2,1,0:T(8,128)(2,1)S(1)}) custom-call(bf16[2,2048,128]{2,1,0:T(8,128)(2,1)S(1)} %bitcast.165, bf16[256,256]{1,0:T(8,128)(2,1)S(1)} %convert_element_type.39.w0_ref, ...), custom_call_target="tpu_custom_call" | custom-call | tf_op jit(solution)/shard_map/pallas_call | solution.py:191
  28.3 3.1 %collective-permute-start = (bf16[32,32,128]{2,1,0:T(8,128)(2,1)S(1)}, bf16[32,32,128]{2,1,0:T(8,128)(2,1)S(1)}, u32[]{:S(2)}, u32[]{:S(2)}) collective-permute-start(bf16[32,32,128]{2,1,0:T(8,128)(2,1)S(1)} %get-tuple-element.18), channel_id=1, source_target_pairs={{0,8},{4,12},{8,0},{12,4},{16,24},{20,28},{24,16},{28,20},{1,9},{5... | collective-permute-start | bytes 786440 | tf_op jit(solution)/shard_map/ppermute | solution.py:206
  31.4 1.5 %collective-permute-start.1 = (bf16[32,32,128]{2,1,0:T(8,128)(2,1)S(1)}, bf16[32,32,128]{2,1,0:T(8,128)(2,1)S(1)}, u32[]{:S(2)}, u32[]{:S(2)}) collective-permute-start(bf16[32,32,128]{2,1,0:T(8,128)(2,1)S(1)} %get-tuple-element.19), channel_id=1, source_target_pairs={{0,4},{4,0},{8,12},{12,8},{16,20},{20,16},{24,28},{28,24},{1,5},{5... | collective-permute-start | bytes 786440 | tf_op jit(solution)/shard_map/ppermute | solution.py:206
  33.4 0.6 gather_fusion
  34.6 0.6 gather_fusion.3
  35.2 0.6 gather_fusion.4
  36.1 0.7 copy-done.9
  37.0 0.7 fusion.103
  37.7 0.7 fusion.2
  38.4 0.8 maximum_maximum_fusion.3
  39.2 1.4 %maximum_bitcast_fusion.1 = bf16[2,2,2,32,1,2,2,2,32]{8,7,6,5,4,3,2,1,0:T(2,128)(2,1)S(1)} fusion(bf16[2,2,2,32,2,2,1,32]{7,6,5,4,3,2,1,0:T(2,128)(2,1)S(1)} %bitcast.168, bf16[2,2,2,32,2,2,1,32]{7,6,5,4,3,2,1,0:T(2,128)(2,1)S(1)} %fusion.2), kind=kLoop, calls=%fused_computation.34 | loop fusion | flops 262144 | bytes 262144 | tf_op jit(solution)/shard_map/stack | solution.py:55
  40.7 1.6 %pad_maximum_fusion.1 = bf16[2,2,2,32,2,2,2,2,32]{8,7,6,5,4,3,2,1,0:T(2,128)(2,1)S(1)} fusion(bf16[2,2,2,32,1,2,2,2,32]{8,7,6,5,4,3,2,1,0:T(2,128)(2,1)S(1)} %maximum_bitcast_fusion.1, bf16[2,2,2,32,1,2,2,2,32]{8,7,6,5,4,3,2,1,0:T(2,128)(2,1)S(1)} %bitcast.169), kind=kLoop, calls=%fused_computation.22 | loop fusion | flops 131072 | bytes 524288 | tf_op jit(solution)/shard_map/stack | solution.py:55
  42.3 2.5 %collective-permute-done.1.b10 = bf16[32,32,128]{2,1,0:T(8,128)(2,1)S(1)} collective-permute-done((bf16[32,32,128]{2,1,0:T(8,128)(2,1)S(1)}, bf16[32,32,128]{2,1,0:T(8,128)(2,1)S(1)}, u32[]{:S(2)}, u32[]{:S(2)}) %collective-permute-start.1) | collective-permute-done | bytes 262176 | tf_op jit(solution)/shard_map/ppermute | solution.py:206
  44.8 0.8 shard_map.38
  45.7 1.6 %collective-permute-start.4 = (bf16[2,32,16,128]{3,2,1,0:T(8,128)(2,1)S(1)}, bf16[2,32,16,128]{3,2,1,0:T(8,128)(2,1)S(1)}, u32[]{:S(2)}, u32[]{:S(2)}) collective-permute-start(bf16[2,32,16,128]{3,2,1,0:T(8,128)(2,1)S(1)} %get-tuple-element.23), channel_id=1, source_target_pairs={{0,2},{1,3},{2,0},{3,1},{4,6},{5,7},{6,4},{7,5},{8,10},{9,11},{10,... | collective-permute-start | bytes 786440 | tf_op jit(solution)/shard_map/ppermute | solution.py:243
  47.7 2.1 %rev.27 = f32[2,32,2,2,2,32]{5,4,2,1,3,0:T(2,128)} reverse(f32[2,32,2,2,2,32]{5,4,2,1,3,0:T(2,128)} %maximum_maximum_fusion.3), dimensions={4} | reverse | bytes 131072 | tf_op jit(solution)/shard_map/jit(_flip)/rev | solution.py:36
  49.8 1.1 %convert_element_type.44.refs_4_ = bf16[256,512]{1,0:T(8,128)(2,1)S(1)} reshape(bf16[2,2,2,32,2,2,2,2,32]{8,7,6,5,4,3,2,1,0:T(2,128)(2,1)S(1)} %pad_maximum_fusion.1) | data formatting | bytes 524288 | tf_op jit(solution)/shard_map/convert_element_type | solution.py:56
  50.9 4.0 %collective-permute-done.4.refs_2_ = bf16[2,32,16,128]{3,2,1,0:T(8,128)(2,1)S(1)} collective-permute-done((bf16[2,32,16,128]{3,2,1,0:T(8,128)(2,1)S(1)}, bf16[2,32,16,128]{3,2,1,0:T(8,128)(2,1)S(1)}, u32[]{:S(2)}, u32[]{:S(2)}) %collective-permute-start.4) | collective-permute-done | bytes 262176 | tf_op jit(solution)/shard_map/ppermute | solution.py:243
  54.9 4.7 %collective-permute-done.5.refs_3_ = bf16[2,32,16,128]{3,2,1,0:T(8,128)(2,1)S(1)} collective-permute-done((bf16[2,32,16,128]{3,2,1,0:T(8,128)(2,1)S(1)}, bf16[2,32,16,128]{3,2,1,0:T(8,128)(2,1)S(1)}, u32[]{:S(2)}, u32[]{:S(2)}) %collective-permute-start.5) | collective-permute-done | bytes 262176 | tf_op jit(solution)/shard_map/ppermute | solution.py:243
  59.6 1.7 %shard_map.39 = (bf16[32,32,128]{2,1,0:T(8,128)(2,1)S(1)}, bf16[32,32,128]{2,1,0:T(8,128)(2,1)S(1)}, bf16[32,32,128]{2,1,0:T(8,128)(2,1)S(1)}, bf16[32,32,128]{2,1,0:T(8,128)(2,1)S(1)}) custom-call(bf16[2,32,16,128]{3,2,1,0:T(8,128)(2,1)S(1)} %get-tuple-element.21.refs_0_, bf16[2,32,16,128]{3,2,1,0:T(8,128)(2,1)S(1)} %collective-permute-done.3.refs_1_, ...), custom_call_target="tpu_custom_call" | custom-call | tf_op jit(solution)/shard_map/pallas_call | solution.py:191
  61.4 1.6 %collective-permute-start.6 = (bf16[32,32,128]{2,1,0:T(8,128)(2,1)S(1)}, bf16[32,32,128]{2,1,0:T(8,128)(2,1)S(1)}, u32[]{:S(2)}, u32[]{:S(2)}) collective-permute-start(bf16[32,32,128]{2,1,0:T(8,128)(2,1)S(1)} %get-tuple-element.26), channel_id=1, source_target_pairs={{0,4},{4,0},{8,12},{12,8},{16,20},{20,16},{24,28},{28,24},{1,5},{5... | collective-permute-start | bytes 786440 | tf_op jit(solution)/shard_map/ppermute | solution.py:206
  63.0 2.6 %collective-permute-start.7 = (bf16[32,32,128]{2,1,0:T(8,128)(2,1)S(1)}, bf16[32,32,128]{2,1,0:T(8,128)(2,1)S(1)}, u32[]{:S(2)}, u32[]{:S(2)}) collective-permute-start(bf16[32,32,128]{2,1,0:T(8,128)(2,1)S(1)} %get-tuple-element.27), channel_id=1, source_target_pairs={{0,16},{4,20},{8,24},{12,28},{16,0},{20,4},{24,8},{28,12},{1,17},{... | collective-permute-start | bytes 786440 | tf_op jit(solution)/shard_map/ppermute | solution.py:206
  66.2 0.4 fusion.1
  66.6 0.4 convert_element_type.49.w_ref
  67.0 2.9 %collective-permute-done.6.b01 = bf16[32,32,128]{2,1,0:T(8,128)(2,1)S(1)} collective-permute-done((bf16[32,32,128]{2,1,0:T(8,128)(2,1)S(1)}, bf16[32,32,128]{2,1,0:T(8,128)(2,1)S(1)}, u32[]{:S(2)}, u32[]{:S(2)}) %collective-permute-start.6) | collective-permute-done | bytes 262176 | tf_op jit(solution)/shard_map/ppermute | solution.py:206
  69.9 13.4 %collective-permute-done.7.b10 = bf16[32,32,128]{2,1,0:T(8,128)(2,1)S(1)} collective-permute-done((bf16[32,32,128]{2,1,0:T(8,128)(2,1)S(1)}, bf16[32,32,128]{2,1,0:T(8,128)(2,1)S(1)}, u32[]{:S(2)}, u32[]{:S(2)}) %collective-permute-start.7) | collective-permute-done | bytes 262176 | tf_op jit(solution)/shard_map/ppermute | solution.py:206
  83.3 5.6 %collective-permute-done.8.b11 = bf16[32,32,128]{2,1,0:T(8,128)(2,1)S(1)} collective-permute-done((bf16[32,32,128]{2,1,0:T(8,128)(2,1)S(1)}, bf16[32,32,128]{2,1,0:T(8,128)(2,1)S(1)}, u32[]{:S(2)}, u32[]{:S(2)}) %collective-permute-start.8) | collective-permute-done | bytes 262176 | tf_op jit(solution)/shard_map/ppermute | solution.py:206
  88.9 4.0 %shard_map.40 = bf16[2,2048,128]{2,1,0:T(8,128)(2,1)S(1)} custom-call(s32[1]{0:T(128)} %bitcast.bit_ref, bf16[32,32,128]{2,1,0:T(8,128)(2,1)S(1)} %get-tuple-element.25.b00, bf16[32,32,128]{2,1,0:T(8,128)(2,1)S(1)} %collective-permute-done.6.b01, bf16[32,32,128]{2,1,0:T(8,128)(2,1)S(1)} %collective-permute-done.7.b10, ...), custom_call_target="tpu_custom_call" | custom-call | tf_op jit(solution)/shard_map/pallas_call | solution.py:191
  92.9 9.7 %copy.46 = bf16[1,2,2048,128]{3,1,2,0:T(2,128)(2,1)} copy(bf16[1,2,2048,128]{3,2,1,0:T(8,128)(2,1)S(1)} %bitcast.164) | data formatting | bytes 2097152
  (92 shorter events, 7.5 us)
Async XLA Ops:
  0.0 33.3 %copy-start = (s32[4]{0:T(128)S(1)}, s32[4]{0:T(128)}, u32[]{:S(2)}) copy-start(s32[4]{0:T(128)} %param.5) | copy-start | bytes 52
  0.0 5.2 %copy-start.1 = (bf16[4,3,2,64,64]{4,3,2,1,0:T(8,128)(2,1)S(1)}, bf16[4,3,2,64,64]{4,3,2,1,0:T(8,128)(2,1)}, u32[]{:S(2)}) copy-start(bf16[4,3,2,64,64]{4,3,2,1,0:T(8,128)(2,1)} %param.4) | copy-start | bytes 589828
  20.6 1.4 %copy-start.11 = (bf16[64,128]{1,0:T(8,128)(2,1)S(1)}, bf16[64,128]{1,0:T(8,128)(2,1)}, u32[]{:S(2)}) copy-start(bf16[64,128]{1,0:T(8,128)(2,1)} %copy.35) | copy-start | bytes 49156
  28.3 14.0 %collective-permute-start = (bf16[32,32,128]{2,1,0:T(8,128)(2,1)S(1)}, bf16[32,32,128]{2,1,0:T(8,128)(2,1)S(1)}, u32[]{:S(2)}, u32[]{:S(2)}) collective-permute-start(bf16[32,32,128]{2,1,0:T(8,128)(2,1)S(1)} %get-tuple-element.18), channel_id=1, source_target_pairs={{0,8},{4,12},{8,0},{12,4},{16,24},{20,28},{24,16},{28,20},{1,9},{5... | collective-permute-start | bytes 786440 | tf_op jit(solution)/shard_map/ppermute | solution.py:206
  31.4 13.4 %collective-permute-start.1 = (bf16[32,32,128]{2,1,0:T(8,128)(2,1)S(1)}, bf16[32,32,128]{2,1,0:T(8,128)(2,1)S(1)}, u32[]{:S(2)}, u32[]{:S(2)}) collective-permute-start(bf16[32,32,128]{2,1,0:T(8,128)(2,1)S(1)} %get-tuple-element.19), channel_id=1, source_target_pairs={{0,4},{4,0},{8,12},{12,8},{16,20},{20,16},{24,28},{28,24},{1,5},{5... | collective-permute-start | bytes 786440 | tf_op jit(solution)/shard_map/ppermute | solution.py:206
  32.9 11.9 %collective-permute-start.2 = (bf16[32,32,128]{2,1,0:T(8,128)(2,1)S(1)}, bf16[32,32,128]{2,1,0:T(8,128)(2,1)S(1)}, u32[]{:S(2)}, u32[]{:S(2)}) collective-permute-start(bf16[32,32,128]{2,1,0:T(8,128)(2,1)S(1)} %get-tuple-element.20), channel_id=1, source_target_pairs={{0,12},{4,8},{8,4},{12,0},{16,28},{20,24},{24,20},{28,16},{1,13},{... | collective-permute-start | bytes 786440 | tf_op jit(solution)/shard_map/ppermute | solution.py:206
  35.2 0.8 copy-start.10
  36.1 2.3 %copy-start.2 = (f32[1,32,2,1,2,32]{5,4,2,1,3,0:T(2,128)}, f32[1,32,2,1,2,32]{5,4,2,1,3,0:T(2,128)S(1)}, u32[]{:S(2)}) copy-start(f32[1,32,2,1,2,32]{5,4,2,1,3,0:T(2,128)S(1)} %squeeze.119) | copy-start | bytes 49156
  36.1 0.8 copy-start.9
  36.1 2.3 %copy-start.5 = (f32[1,32,2,1,2,32]{5,4,2,1,3,0:T(2,128)}, f32[1,32,2,1,2,32]{5,4,2,1,3,0:T(2,128)S(1)}, u32[]{:S(2)}) copy-start(f32[1,32,2,1,2,32]{5,4,2,1,3,0:T(2,128)S(1)} %neg.39) | copy-start | bytes 49156
  37.0 1.4 %copy-start.7 = (f32[1,32,2,1,2,32]{5,4,2,1,3,0:T(2,128)}, f32[1,32,2,1,2,32]{5,4,2,1,3,0:T(2,128)S(1)}, u32[]{:S(2)}) copy-start(f32[1,32,2,1,2,32]{5,4,2,1,3,0:T(2,128)S(1)} %stack.116) | copy-start | bytes 49156
  45.6 5.2 %collective-permute-start.3 = (bf16[2,32,16,128]{3,2,1,0:T(8,128)(2,1)S(1)}, bf16[2,32,16,128]{3,2,1,0:T(8,128)(2,1)S(1)}, u32[]{:S(2)}, u32[]{:S(2)}) collective-permute-start(bf16[2,32,16,128]{3,2,1,0:T(8,128)(2,1)S(1)} %get-tuple-element.22), channel_id=1, source_target_pairs={{0,1},{1,0},{2,3},{3,2},{4,5},{5,4},{6,7},{7,6},{8,9},{9,8},{10,11... | collective-permute-start | bytes 786440 | tf_op jit(solution)/shard_map/ppermute | solution.py:243
  45.7 9.2 %collective-permute-start.4 = (bf16[2,32,16,128]{3,2,1,0:T(8,128)(2,1)S(1)}, bf16[2,32,16,128]{3,2,1,0:T(8,128)(2,1)S(1)}, u32[]{:S(2)}, u32[]{:S(2)}) collective-permute-start(bf16[2,32,16,128]{3,2,1,0:T(8,128)(2,1)S(1)} %get-tuple-element.23), channel_id=1, source_target_pairs={{0,2},{1,3},{2,0},{3,1},{4,6},{5,7},{6,4},{7,5},{8,10},{9,11},{10,... | collective-permute-start | bytes 786440 | tf_op jit(solution)/shard_map/ppermute | solution.py:243
  47.3 12.3 %collective-permute-start.5 = (bf16[2,32,16,128]{3,2,1,0:T(8,128)(2,1)S(1)}, bf16[2,32,16,128]{3,2,1,0:T(8,128)(2,1)S(1)}, u32[]{:S(2)}, u32[]{:S(2)}) collective-permute-start(bf16[2,32,16,128]{3,2,1,0:T(8,128)(2,1)S(1)} %get-tuple-element.24), channel_id=1, source_target_pairs={{0,3},{1,2},{2,1},{3,0},{4,7},{5,6},{6,5},{7,4},{8,11},{9,10},{10,... | collective-permute-start | bytes 786440 | tf_op jit(solution)/shard_map/ppermute | solution.py:243
  59.6 6.2 %copy-start.3 = (f32[1,32,2,1,2,32]{5,4,2,1,3,0:T(2,128)S(1)}, f32[1,32,2,1,2,32]{5,4,2,1,3,0:T(2,128)}, u32[]{:S(2)}) copy-start(f32[1,32,2,1,2,32]{5,4,2,1,3,0:T(2,128)} %copy-done.2) | copy-start | bytes 49156
  59.6 6.2 %copy-start.4 = (f32[2,32,2,2,2,32]{5,4,2,1,3,0:T(2,128)S(1)}, f32[2,32,2,2,2,32]{5,4,2,1,3,0:T(2,128)}, u32[]{:S(2)}) copy-start(f32[2,32,2,2,2,32]{5,4,2,1,3,0:T(2,128)} %rev.27) | copy-start | bytes 196612
  59.6 6.2 %copy-start.6 = (f32[1,32,2,1,2,32]{5,4,2,1,3,0:T(2,128)S(1)}, f32[1,32,2,1,2,32]{5,4,2,1,3,0:T(2,128)}, u32[]{:S(2)}) copy-start(f32[1,32,2,1,2,32]{5,4,2,1,3,0:T(2,128)} %copy-done.5) | copy-start | bytes 49156
  59.6 6.2 %copy-start.8 = (f32[1,32,2,1,2,32]{5,4,2,1,3,0:T(2,128)S(1)}, f32[1,32,2,1,2,32]{5,4,2,1,3,0:T(2,128)}, u32[]{:S(2)}) copy-start(f32[1,32,2,1,2,32]{5,4,2,1,3,0:T(2,128)} %copy-done.7) | copy-start | bytes 49156
  61.4 8.6 %collective-permute-start.6 = (bf16[32,32,128]{2,1,0:T(8,128)(2,1)S(1)}, bf16[32,32,128]{2,1,0:T(8,128)(2,1)S(1)}, u32[]{:S(2)}, u32[]{:S(2)}) collective-permute-start(bf16[32,32,128]{2,1,0:T(8,128)(2,1)S(1)} %get-tuple-element.26), channel_id=1, source_target_pairs={{0,4},{4,0},{8,12},{12,8},{16,20},{20,16},{24,28},{28,24},{1,5},{5... | collective-permute-start | bytes 786440 | tf_op jit(solution)/shard_map/ppermute | solution.py:206
  63.0 20.3 %collective-permute-start.7 = (bf16[32,32,128]{2,1,0:T(8,128)(2,1)S(1)}, bf16[32,32,128]{2,1,0:T(8,128)(2,1)S(1)}, u32[]{:S(2)}, u32[]{:S(2)}) collective-permute-start(bf16[32,32,128]{2,1,0:T(8,128)(2,1)S(1)} %get-tuple-element.27), channel_id=1, source_target_pairs={{0,16},{4,20},{8,24},{12,28},{16,0},{20,4},{24,8},{28,12},{1,17},{... | collective-permute-start | bytes 786440 | tf_op jit(solution)/shard_map/ppermute | solution.py:206
  65.5 23.3 %collective-permute-start.8 = (bf16[32,32,128]{2,1,0:T(8,128)(2,1)S(1)}, bf16[32,32,128]{2,1,0:T(8,128)(2,1)S(1)}, u32[]{:S(2)}, u32[]{:S(2)}) collective-permute-start(bf16[32,32,128]{2,1,0:T(8,128)(2,1)S(1)} %get-tuple-element.28), channel_id=1, source_target_pairs={{0,20},{4,16},{8,28},{12,24},{16,4},{20,0},{24,12},{28,8},{1,21},{... | collective-permute-start | bytes 786440 | tf_op jit(solution)/shard_map/ppermute | solution.py:206
where the time goes:
time: 104 us; the launch traced here: 103 us
  waiting for transfers between devices  33.1 us (32%)
  local copies, waits for them, and re-layouts  25.4 us (24%)
  Pallas kernels  13 us (12%)
  other arithmetic  12 us (12%)
  starting transfers between devices  11 us (11%)
  matrix products  7.6 us (7%)
    ppermute x6, waiting for transfers between devices, exchange(): lax.ppermute(block, 'hi', [(d, d ^ apart) for d in range(size)])  24.3 us
    pallas_call x4, Pallas kernels, call(): pl.pallas_call(kernel, out_shape=outs, in_specs=specs or [VMEM] * len(arg...  13 us
    unnamed x26, local copies, waits for them, and re-layouts  11.9 us
    ppermute x6, starting transfers between devices, exchange(): lax.ppermute(block, 'hi', [(d, d ^ apart) for d in range(size)])  9.08 us
    ppermute x3, waiting for transfers between devices, on_device(): lax.ppermute(parts[o], 'lo', [(d, d ^ o) for d in range(groups)])  8.75 us
    another operation x4, other arithmetic, right_weights(): both = jnp.stack([w, times_i(w, 6)], axis=4)  6 us
    dot_general x12, matrix products, product(): real = dot(later[0], earlier[0]) - dot(later[1], earlier[1])  3.82 us
    dot_general x12, matrix products, product(): imag = dot(later[0], earlier[1]) + dot(later[1], earlier[0])  3.78 us
  transfers between devices with their start and end apart: 9, of which 6 were waited for; matrix products, arithmetic and copies ran while one was open for 12% of the time, Pallas kernels for 0%

commit v1 on v0

v1 whole, which is shorter than its diff:
```python
import functools

import jax
import jax.numpy as jnp
from jax import lax
from jax.experimental import pallas as pl
from jax.experimental.pallas import tpu as pltpu
from jax.sharding import PartitionSpec as P

GQ = 6
G = 2**GQ
HALF = G // 2
BF = jnp.bfloat16
F32 = jnp.float32


def iotas(rows, columns):
    shape = (rows, columns)
    return lax.broadcasted_iota(jnp.int32, shape, 0), lax.broadcasted_iota(jnp.int32, shape, 1)


def dot(x, y):
    return jnp.dot(x, y, preferred_element_type=F32)


def turned_dot(x, y):
    return lax.dot_general(x, y, (((1,), (1,)), ((), ())), preferred_element_type=F32)


def ones(where):
    return where.astype(F32).astype(BF)


def gate_of(ref, layer, block):
    return jnp.concatenate([ref[layer, block, 0], ref[layer, block, 1]], axis=1)


def squared(gate):
    return jnp.concatenate([gate, jnp.concatenate([-gate[:, G:], gate[:, :G]], axis=1)], axis=0)


def product(later, earlier):
    return dot(later, squared(earlier))


def wide_product(later, earlier):
    parts = []
    for x in (later, squared(earlier)):
        high = x.astype(BF)
        parts.append((high, (x - high.astype(F32)).astype(BF)))
    (lh, ll), (eh, el) = parts
    return dot(jnp.concatenate([lh, lh, ll], axis=1), jnp.concatenate([eh, el, eh], axis=0))


def first_weights(gate):
    real = jnp.concatenate([gate[:, :G], gate[:, :G]], axis=1)
    imag = jnp.concatenate([gate[:, G:], gate[:, G:]], axis=1)
    low = iotas(HALF, 2 * G)[1] < G
    rows = []
    for ch in range(2):
        r, i = (x[ch * HALF : (ch + 1) * HALF] for x in (real, imag))
        for pair in ((r, -i), (i, r)):
            for mask in (low, ~low):
                rows.append(jnp.concatenate([jnp.where(mask, x, 0.0) for x in pair], axis=1))
    return jnp.concatenate(rows, axis=0).astype(BF)


def right_weights(gate, low, in_bit, out_bit):
    k, b = iotas(G, G)
    order = ((k & (HALF - 1)) << 1 | k >> GQ - 1) if low else k ^ in_bit * HALF
    gate = gate.astype(BF)
    t = turned_dot(ones(b == order), jnp.concatenate([gate[:, :G], gate[:, G:]], axis=0)).astype(BF)
    at, n = iotas(2 * G, 8 * G)
    bit = lambda i: n >> i & 1
    to = ((bit(7) ^ out_bit) << GQ - 1) | n & (HALF - 1)
    turn_i = bit(8)
    part = bit(5) ^ turn_i
    sign_i = turn_i & (1 - bit(5))
    ch = iotas(G, 8 * G)[1] >> 6 & 1
    made = []
    for p in range(2):
        minus = sign_i ^ ((1 - part) & p)
        place = jnp.where(at == to + (part ^ p) * G, (1 - 2 * minus).astype(F32), 0.0).astype(BF)
        y = dot(t, place)
        made.append([jnp.where(ch == c, y, 0.0).astype(BF) for c in range(2)])
    if low:
        rows = [made[p][c] for c in range(2) for p in range(2)]
    else:
        rows = [made[p][c][i * HALF : (i + 1) * HALF] for i in range(2) for c in range(2) for p in range(2)]
    return jnp.concatenate(rows, axis=0)


def left_weights(gate, step, out_bit):
    k, a = iotas(G, G)
    rows = dot(ones(a == k ^ out_bit * HALF), gate.astype(BF)).astype(BF)
    k, a = iotas(2 * G, 2 * G)
    return dot(rows, ones(a == k ^ step)).astype(BF)


def last_weights(gate, in_bit):
    k, b = iotas(G, G)
    t = dot(ones(b == ((k & (HALF - 1)) << 1 | k >> GQ - 1)), gate).astype(BF)
    at, n = iotas(2 * G, 4 * G)
    p_in = n >> 5 & 1
    b_in = ((n >> 7 ^ in_bit) << GQ - 1) | n & (HALF - 1)
    ch = iotas(HALF, 4 * G)[1] >> 6 & 1
    rows = []
    for p in range(2):
        minus = (1 - p) * p_in
        place = jnp.where(at == b_in + (p_in ^ p) * G, (1 - 2 * minus).astype(F32), 0.0).astype(BF)
        y = dot(t, place)
        for b0 in range(2):
            for c in range(2):
                rows.append(jnp.where(ch == c, y[b0 * HALF : (b0 + 1) * HALF], 0.0).astype(BF))
    return jnp.concatenate(rows, axis=0)


def turn(parts):
    lane = lax.broadcasted_iota(jnp.int32, (parts[0].shape[0], 128), 1)
    wide = lane < 64
    narrow = (lane & 32) == 0
    out = [[None, None] for _ in range(8)]
    for n in range(2):
        for m in range(2):
            a = [parts[n * 4 + r][:, m * 128 : (m + 1) * 128] for r in range(4)]
            s = [None] * 4
            for r in range(2):
                s[r] = jnp.where(wide, a[r], pltpu.roll(a[r + 2], 64, 1))
                s[r + 2] = jnp.where(wide, pltpu.roll(a[r], 64, 1), a[r + 2])
            for r in (0, 2):
                out[m * 4 + r][n] = jnp.where(narrow, s[r], pltpu.roll(s[r + 1], 32, 1))
                out[m * 4 + r + 1][n] = jnp.where(narrow, pltpu.roll(s[r], 96, 1), s[r + 1])
    return out


def both_gates(x, w, g):
    n = x.shape[0]
    z = jnp.dot(x.reshape(n * G, 4 * G), w, preferred_element_type=F32).astype(BF)
    outs = []
    for k in range(n):
        rows = z[k * G : (k + 1) * G]
        s = jnp.concatenate([rows[:, : 4 * G], rows[:, 4 * G :]], axis=0)
        outs.append(jnp.dot(g, s, preferred_element_type=F32).astype(BF))
    return outs


def store_blocks(outs, at, blocks):
    for k, out in enumerate(outs):
        for i in range(2):
            for j in range(2):
                blocks[2 * i + j][at + k] = out[j * HALF : (j + 1) * HALF, i * 128 : (i + 1) * 128]


STEP = 8


def own_bits():
    hi_bits = lax.axis_size("hi").bit_length() - 1
    hi = lax.axis_index("hi")
    return [hi >> k % hi_bits & 1 for k in range(4)]


def first_kernel(x_ref, gates, o00, o01, o10, o11, spread, turned, w1_ref):
    own = own_bits()
    late = product(gate_of(gates, 3, 0), gate_of(gates, 2, 0))
    early = product(gate_of(gates, 1, 0), gate_of(gates, 0, 0))
    w0 = first_weights(wide_product(late, early))
    w1_ref[...] = right_weights(gate_of(gates, 0, 1), True, 0, own[0])
    g = left_weights(product(gate_of(gates, 1, 2), gate_of(gates, 0, 2)), 0, own[1])

    for k in range(G // 8):
        spread[k * 512 : (k + 1) * 512, :] = x_ref[k * 512 : (k + 1) * 512, :].astype(F32)
        x = jnp.concatenate([spread[pl.ds(k * 512 + p, 256, stride=2), :] for p in range(2)], axis=1).astype(BF)
        r = turned_dot(w0, x)
        tiles = turn([r[g * HALF : (g + 1) * HALF] for g in range(8)])
        for q in range(8):
            for n in range(2):
                turned[n, pl.ds(k * 8 + q, HALF, stride=G), :] = tiles[q][n]

    for k in range(0, HALF, STEP):
        rows = slice(k * G, (k + STEP) * G)
        x = jnp.concatenate([turned[0, rows, :], turned[1, rows, :]], axis=1).astype(BF).reshape(STEP, G, 4 * G)
        store_blocks(both_gates(x, w1_ref[...], g), k, (o00, o01, o10, o11))


def weights_kernel(top, gates, w1_ref, g_ref, w_ref):
    own = own_bits()
    w1_ref[...] = right_weights(product(gate_of(gates, 2, 1), gate_of(gates, 1, 1)), False, own[0], own[2])
    step = top * lax.axis_index("lo") if top else 0
    g_ref[...] = left_weights(product(gate_of(gates, 3, 2), gate_of(gates, 2, 2)), step, own[3])
    w_ref[...] = last_weights(gate_of(gates, 3, 1), own[2])


def middle_kernel(*refs):
    *ins, w1_ref, g_ref, o00, o01, o10, o11 = refs
    for k in range(0, HALF, STEP):
        halves = [jnp.concatenate([x[i, k : k + STEP] for x in ins], axis=1) for i in range(2)]
        x = jnp.concatenate(halves, axis=2)
        store_blocks(both_gates(x, w1_ref[...], g_ref[...]), k, (o00, o01, o10, o11))


def last_kernel(b00, b01, b10, b11, w_ref, o_ref, wide, spread):
    bit = own_bits()[3]
    blocks = ((b00, b01), (b10, b11))
    for k in range(HALF):
        for j in range(2):
            rows = pl.ds(pl.multiple_of(k * G + (bit ^ j) * HALF, HALF), HALF)
            for i in range(2):
                wide[i, rows, :] = blocks[i][j][k].astype(F32)
    for k in range(G // 8):
        halves = [
            jnp.concatenate([wide[i, pl.ds(k * 8 + q, HALF, stride=G), :] for q in range(8)], axis=0) for i in range(2)
        ]
        x = jnp.concatenate(halves, axis=1).astype(BF)
        r = turned_dot(w_ref[...], x)
        tiles = turn([r[g * HALF : (g + 1) * HALF] for g in range(8)])
        for q in range(8):
            for n in range(2):
                spread[pl.ds((k * 8 + q) * G + n, HALF, stride=2), :] = tiles[q][n]
        o_ref[k * 512 : (k + 1) * 512, :] = spread[k * 512 : (k + 1) * 512, :].astype(BF)


def pick_kernel(regroup, b00, b01, b10, b11, *outs):
    blocks = ((b00, b01), (b10, b11))
    own = own_bits()[1]
    lo = lax.axis_index("lo")
    rows = outs[0].shape[2]
    for o, out in enumerate(outs):
        t = regroup[lo ^ o]
        j = t >> 1 ^ own
        at = pl.ds(pl.multiple_of((t & 1) * rows, rows), rows)
        for i in range(2):
            out[i] = jnp.where(j == 0, blocks[i][0][:, at, :], blocks[i][1][:, at, :])


VMEM = pl.BlockSpec(memory_space=pltpu.VMEM)
SMEM = pl.BlockSpec(memory_space=pltpu.SMEM)


def call(kernel, outs, args, specs=None, scratch=()):
    return pl.pallas_call(
        kernel,
        out_shape=outs,
        in_specs=specs or [VMEM] * len(args),
        out_specs=jax.tree.map(lambda _: VMEM, outs),
        scratch_shapes=scratch,
        compiler_params=pltpu.CompilerParams(vmem_limit_bytes=40 * 2**20),
    )(*args)


def exchange(blocks, b_bit, a_bit):
    size = lax.axis_size("hi")
    out = []
    for at, block in enumerate(blocks):
        apart = (at >> 1 << b_bit) | ((at & 1) << a_bit)
        out.append(lax.ppermute(block, "hi", [(d, d ^ apart) for d in range(size)]) if apart else block)
    return out


def on_device(state, gates, regroup):
    hi_bits = lax.axis_size("hi").bit_length() - 1
    groups = lax.axis_size("lo")
    bits = [k % hi_bits for k in range(4)]
    top = G // groups
    whole = 2 * state.shape[1] // 128

    block = jax.ShapeDtypeStruct((HALF, HALF, 128), BF)
    turned = pltpu.VMEM((2, HALF * G, 128), F32)
    spread = pltpu.VMEM((whole, 128), F32)
    x = state.reshape(2, -1, 128).transpose(1, 0, 2).reshape(whole, 128)
    blocks = call(first_kernel, [block] * 4, (x, gates), scratch=[spread, turned, pltpu.VMEM((4 * G, 8 * G), BF)])
    blocks = exchange(blocks, bits[0], bits[1])
    shapes = [jax.ShapeDtypeStruct(shape, BF) for shape in ((4 * G, 8 * G), (G, 2 * G), (4 * G, 4 * G))]
    w1, g, w = call(functools.partial(weights_kernel, top if groups == 4 else 0), shapes, (gates,))

    if groups == 4:
        part = jax.ShapeDtypeStruct((2, HALF, top, 128), BF)
        parts = call(pick_kernel, [part] * groups, (regroup, *blocks), specs=[SMEM] + [VMEM] * 4)
        parts = [parts[0]] + [
            lax.ppermute(parts[o], "lo", [(d, d ^ o) for d in range(groups)]) for o in range(1, groups)
        ]
    else:
        own = lax.axis_index("hi") >> bits[1] & 1
        halves = [jnp.stack(blocks[2 * i : 2 * i + 2], 1) for i in range(2)]
        both = jnp.stack([jnp.where(own == 0, half, jnp.flip(half, 1)) for half in halves])
        both = jnp.take(both.reshape(2, HALF, groups, top, 128), regroup, axis=2)
        both = lax.all_to_all(both, "lo", split_axis=2, concat_axis=2, tiled=True)
        parts = [both.reshape(2, HALF, G, 128)]
    blocks = call(middle_kernel, [block] * 4, (*parts, w1, g))
    blocks = exchange(blocks, bits[2], bits[3])

    out = call(last_kernel, jax.ShapeDtypeStruct((whole, 128), BF), (*blocks, w), scratch=[turned, spread])
    return out.reshape(-1, 2, 128).transpose(1, 0, 2).reshape(state.shape)


def solution(mesh):
    placed = (P(None, ("hi", "lo")), P(), P())
    return jax.shard_map(
        on_device, mesh=mesh, in_specs=placed, out_specs=P(None, ("hi", "lo")), check_vma=False
    )
```

time: 104 us -> 70.3 us (0.68); the launches traced: 103 us -> 70.1 us
  local copies, waits for them, and re-layouts: 25.4 us -> 2.23 us
  waiting for transfers between devices: 33.1 us -> 46 us
  other arithmetic: 12 us -> 0 us
  matrix products: 7.6 us -> 0 us
  Pallas kernels: 13 us -> 10.8 us
    ppermute x6, waiting for transfers between devices: 24.3 us -> 34.9 us  [exchange(): lax.ppermute(block, 'hi', [(d, d ^ apart) for d in range(size)])]
    another operation x14 -> x0, other arithmetic: 10 us -> none  [the longest x4 6 us: right_weights(): both = jnp.stack([w, times_i(w, 6)], axis=4)]
    unnamed x26 -> x8, local copies, waits for them, and re-layouts: 11.9 us -> 2.23 us
    dot_general x24 -> x0, matrix products: 7.6 us -> none  [the longest x12 3.82 us: product(): real = dot(later[0], earlier[0]) - dot(later[1], earlier[1])]
    convert_element_type x5 -> x0, local copies, waits for them, and re-layouts: 3.65 us -> none  [the longest x2 2.13 us: right_weights(): return both.reshape(4 * G, 8 * G).astype(BF)]
    gather x6 -> x0, local copies, waits for them, and re-layouts: 3.3 us -> none  [the longest x4 2.57 us: left_weights(): g = jnp.concatenate([gate[0][:, order], gate[1][:, order]], axis=1)]
    rev x2 -> x0, local copies, waits for them, and re-layouts: 2.71 us -> none  [flip(): return jnp.where(bit == 0, w, jnp.flip(w, axis))]
    ppermute x3, waiting for transfers between devices: 8.75 us -> 11.1 us  [on_device(): lax.ppermute(parts[o], 'lo', [(d, d ^ o) for d in range(groups)])]
  transfers between devices with their start and end apart: 9 -> 9, of which waited for: 6 -> 7; matrix products, arithmetic and copies ran while one was open for 12% -> 0% of each run, Pallas kernels for 0% -> 1%
where the time goes in v1:
time: 70.3 us; the launch traced here: 70.1 us
  waiting for transfers between devices  46 us (65%)
  starting transfers between devices  11 us (16%)
  Pallas kernels  10.8 us (15%)
  local copies, waits for them, and re-layouts  2.23 us (3%)
    ppermute x6, waiting for transfers between devices, exchange(): lax.ppermute(block, 'hi', [(d, d ^ apart) for d in range(size)])  34.9 us
    ppermute x3, waiting for transfers between devices, on_device(): lax.ppermute(parts[o], 'lo', [(d, d ^ o) for d in range(groups)])  11.1 us
    pallas_call x5, Pallas kernels, call(): pl.pallas_call(kernel, out_shape=outs, in_specs=specs or [VMEM] * len(arg...  10.8 us
    ppermute x6, starting transfers between devices, exchange(): lax.ppermute(block, 'hi', [(d, d ^ apart) for d in range(size)])  9.09 us
    unnamed x8, local copies, waits for them, and re-layouts  2.23 us
    ppermute x3, starting transfers between devices, on_device(): lax.ppermute(parts[o], 'lo', [(d, d ^ o) for d in range(groups)])  1.93 us
  transfers between devices with their start and end apart: 9, of which 7 were waited for; matrix products, arithmetic and copies ran while one was open for 0% of the time, Pallas kernels for 1%

profile of v1, /device:TPU:0, one launch (start us, length us, event | category | flops | bytes accessed | tf_op | source)
XLA Modules:
  0.0 70.1 jit_solution(14501148007167396315)
XLA Ops:
  0.0 0.0 copy-start
  0.0 1.0 %copy-done = bf16[4,3,2,64,64]{4,3,2,1,0:T(8,128)(2,1)S(1)} copy-done((bf16[4,3,2,64,64]{4,3,2,1,0:T(8,128)(2,1)S(1)}, bf16[4,3,2,64,64]{4,3,2,1,0:T(8,128)(2,1)}, u32[]{:S(2)}) %copy-start) | copy-done | bytes 196632
  1.0 0.0 copy-start.2
  1.0 1.2 %copy-done.2 = bf16[2,262144]{1,0:T(2,128)(2,1)S(1)} copy-done((bf16[2,262144]{1,0:T(2,128)(2,1)S(1)}, bf16[2,262144]{1,0:T(2,128)(2,1)}, u32[]{:S(2)}) %copy-start.2) | copy-done | bytes 1048600
  2.2 3.5 %shard_map.37 = (bf16[32,32,128]{2,1,0:T(8,128)(2,1)S(1)}, bf16[32,32,128]{2,1,0:T(8,128)(2,1)S(1)}, bf16[32,32,128]{2,1,0:T(8,128)(2,1)S(1)}, bf16[32,32,128]{2,1,0:T(8,128)(2,1)S(1)}) custom-call(bf16[4096,128]{1,0:T(8,128)(2,1)S(1)} %bitcast.10, bf16[4,3,2,64,64]{4,3,2,1,0:T(8,128)(2,1)S(1)} %copy-done), custom_call_target="tpu_custom_call" | custom-call | tf_op jit(solution)/shard_map/pallas_call | solution.py:241
  5.7 3.1 %collective-permute-start = (bf16[32,32,128]{2,1,0:T(8,128)(2,1)S(1)}, bf16[32,32,128]{2,1,0:T(8,128)(2,1)S(1)}, u32[]{:S(2)}, u32[]{:S(2)}) collective-permute-start(bf16[32,32,128]{2,1,0:T(8,128)(2,1)S(1)} %get-tuple-element.21), channel_id=1, source_target_pairs={{0,8},{4,12},{8,0},{12,4},{16,24},{20,28},{24,16},{28,20},{1,9},{5... | collective-permute-start | bytes 786440 | tf_op jit(solution)/shard_map/ppermute | solution.py:256
  8.8 1.5 %collective-permute-start.1 = (bf16[32,32,128]{2,1,0:T(8,128)(2,1)S(1)}, bf16[32,32,128]{2,1,0:T(8,128)(2,1)S(1)}, u32[]{:S(2)}, u32[]{:S(2)}) collective-permute-start(bf16[32,32,128]{2,1,0:T(8,128)(2,1)S(1)} %get-tuple-element.22), channel_id=1, source_target_pairs={{0,4},{4,0},{8,12},{12,8},{16,20},{20,16},{24,28},{28,24},{1,5},{5... | collective-permute-start | bytes 786440 | tf_op jit(solution)/shard_map/ppermute | solution.py:256
  10.3 0.0 copy-start.3
  10.3 0.0 collective-permute-start.2
  10.4 5.6 %collective-permute-done.b01 = bf16[32,32,128]{2,1,0:T(8,128)(2,1)S(1)} collective-permute-done((bf16[32,32,128]{2,1,0:T(8,128)(2,1)S(1)}, bf16[32,32,128]{2,1,0:T(8,128)(2,1)S(1)}, u32[]{:S(2)}, u32[]{:S(2)}) %collective-permute-start) | collective-permute-done | bytes 262176 | tf_op jit(solution)/shard_map/ppermute | solution.py:256
  16.0 6.2 %collective-permute-done.1.b10 = bf16[32,32,128]{2,1,0:T(8,128)(2,1)S(1)} collective-permute-done((bf16[32,32,128]{2,1,0:T(8,128)(2,1)S(1)}, bf16[32,32,128]{2,1,0:T(8,128)(2,1)S(1)}, u32[]{:S(2)}, u32[]{:S(2)}) %collective-permute-start.1) | collective-permute-done | bytes 262176 | tf_op jit(solution)/shard_map/ppermute | solution.py:256
  22.2 0.0 collective-permute-done.2.b11
  22.2 0.0 copy-done.3
  22.2 0.0 copy-start.1
  22.2 0.8 %shard_map.38 = (bf16[2,32,16,128]{3,2,1,0:T(8,128)(2,1)S(1)}, bf16[2,32,16,128]{3,2,1,0:T(8,128)(2,1)S(1)}, bf16[2,32,16,128]{3,2,1,0:T(8,128)(2,1)S(1)}, bf16[2,32,16,128]{3,2,1,0:T(8,128)(2,1)S(1)}) custom-call(s32[4]{0:T(128)S(1)} %copy-done.3, bf16[32,32,128]{2,1,0:T(8,128)(2,1)S(1)} %get-tuple-element.20.b00, ...), custom_call_target="tpu_custom_call" | custom-call | tf_op jit(solution)/shard_map/pallas_call | solution.py:241
  23.1 0.1 collective-permute-start.3
  23.1 1.6 %collective-permute-start.4 = (bf16[2,32,16,128]{3,2,1,0:T(8,128)(2,1)S(1)}, bf16[2,32,16,128]{3,2,1,0:T(8,128)(2,1)S(1)}, u32[]{:S(2)}, u32[]{:S(2)}) collective-permute-start(bf16[2,32,16,128]{3,2,1,0:T(8,128)(2,1)S(1)} %get-tuple-element.26), channel_id=1, source_target_pairs={{0,2},{1,3},{2,0},{3,1},{4,6},{5,7},{6,4},{7,5},{8,10},{9,11},{10,... | collective-permute-start | bytes 786440 | tf_op jit(solution)/shard_map/ppermute | solution.py:280
  24.7 0.3 collective-permute-start.5
  25.0 0.0 copy-done.1
  25.0 0.9 %shard_map.39 = (bf16[256,512]{1,0:T(8,128)(2,1)S(1)}, bf16[64,128]{1,0:T(8,128)(2,1)S(1)}, bf16[256,256]{1,0:T(8,128)(2,1)S(1)}) custom-call(bf16[4,3,2,64,64]{4,3,2,1,0:T(8,128)(2,1)S(1)} %copy-done.1), custom_call_target="tpu_custom_call" | custom-call | tf_op jit(solution)/shard_map/pallas_call | solution.py:241
  25.9 0.0 collective-permute-done.3.refs_1_
  25.9 6.4 %collective-permute-done.4.refs_2_ = bf16[2,32,16,128]{3,2,1,0:T(8,128)(2,1)S(1)} collective-permute-done((bf16[2,32,16,128]{3,2,1,0:T(8,128)(2,1)S(1)}, bf16[2,32,16,128]{3,2,1,0:T(8,128)(2,1)S(1)}, u32[]{:S(2)}, u32[]{:S(2)}) %collective-permute-start.4) | collective-permute-done | bytes 262176 | tf_op jit(solution)/shard_map/ppermute | solution.py:280
  32.3 4.7 %collective-permute-done.5.refs_3_ = bf16[2,32,16,128]{3,2,1,0:T(8,128)(2,1)S(1)} collective-permute-done((bf16[2,32,16,128]{3,2,1,0:T(8,128)(2,1)S(1)}, bf16[2,32,16,128]{3,2,1,0:T(8,128)(2,1)S(1)}, u32[]{:S(2)}, u32[]{:S(2)}) %collective-permute-start.5) | collective-permute-done | bytes 262176 | tf_op jit(solution)/shard_map/ppermute | solution.py:280
  37.0 1.3 %shard_map.40 = (bf16[32,32,128]{2,1,0:T(8,128)(2,1)S(1)}, bf16[32,32,128]{2,1,0:T(8,128)(2,1)S(1)}, bf16[32,32,128]{2,1,0:T(8,128)(2,1)S(1)}, bf16[32,32,128]{2,1,0:T(8,128)(2,1)S(1)}) custom-call(bf16[2,32,16,128]{3,2,1,0:T(8,128)(2,1)S(1)} %get-tuple-element.24.refs_0_, bf16[2,32,16,128]{3,2,1,0:T(8,128)(2,1)S(1)} %collective-permute-done.3.refs_1_, ...), custom_call_target="tpu_custom_call" | custom-call | tf_op jit(solution)/shard_map/pallas_call | solution.py:241
  38.3 1.6 %collective-permute-start.6 = (bf16[32,32,128]{2,1,0:T(8,128)(2,1)S(1)}, bf16[32,32,128]{2,1,0:T(8,128)(2,1)S(1)}, u32[]{:S(2)}, u32[]{:S(2)}) collective-permute-start(bf16[32,32,128]{2,1,0:T(8,128)(2,1)S(1)} %get-tuple-element.31), channel_id=1, source_target_pairs={{0,4},{4,0},{8,12},{12,8},{16,20},{20,16},{24,28},{28,24},{1,5},{5... | collective-permute-start | bytes 786440 | tf_op jit(solution)/shard_map/ppermute | solution.py:256
  39.9 2.6 %collective-permute-start.7 = (bf16[32,32,128]{2,1,0:T(8,128)(2,1)S(1)}, bf16[32,32,128]{2,1,0:T(8,128)(2,1)S(1)}, u32[]{:S(2)}, u32[]{:S(2)}) collective-permute-start(bf16[32,32,128]{2,1,0:T(8,128)(2,1)S(1)} %get-tuple-element.32), channel_id=1, source_target_pairs={{0,16},{4,20},{8,24},{12,28},{16,0},{20,4},{24,8},{28,12},{1,17},{... | collective-permute-start | bytes 786440 | tf_op jit(solution)/shard_map/ppermute | solution.py:256
  42.5 0.3 collective-permute-start.8
  42.8 4.1 %collective-permute-done.6.b01 = bf16[32,32,128]{2,1,0:T(8,128)(2,1)S(1)} collective-permute-done((bf16[32,32,128]{2,1,0:T(8,128)(2,1)S(1)}, bf16[32,32,128]{2,1,0:T(8,128)(2,1)S(1)}, u32[]{:S(2)}, u32[]{:S(2)}) %collective-permute-start.6) | collective-permute-done | bytes 262176 | tf_op jit(solution)/shard_map/ppermute | solution.py:256
  46.9 13.3 %collective-permute-done.7.b10 = bf16[32,32,128]{2,1,0:T(8,128)(2,1)S(1)} collective-permute-done((bf16[32,32,128]{2,1,0:T(8,128)(2,1)S(1)}, bf16[32,32,128]{2,1,0:T(8,128)(2,1)S(1)}, u32[]{:S(2)}, u32[]{:S(2)}) %collective-permute-start.7) | collective-permute-done | bytes 262176 | tf_op jit(solution)/shard_map/ppermute | solution.py:256
  60.2 5.6 %collective-permute-done.8.b11 = bf16[32,32,128]{2,1,0:T(8,128)(2,1)S(1)} collective-permute-done((bf16[32,32,128]{2,1,0:T(8,128)(2,1)S(1)}, bf16[32,32,128]{2,1,0:T(8,128)(2,1)S(1)}, u32[]{:S(2)}, u32[]{:S(2)}) %collective-permute-start.8) | collective-permute-done | bytes 262176 | tf_op jit(solution)/shard_map/ppermute | solution.py:256
  65.8 4.3 %shard_map.41 = bf16[4096,128]{1,0:T(8,128)(2,1)} custom-call(bf16[32,32,128]{2,1,0:T(8,128)(2,1)S(1)} %get-tuple-element.30.b00, bf16[32,32,128]{2,1,0:T(8,128)(2,1)S(1)} %collective-permute-done.6.b01, bf16[32,32,128]{2,1,0:T(8,128)(2,1)S(1)} %collective-permute-done.7.b10, bf16[32,32,128]{2,1,0:T(8,128)(2,1)S(1)} %collective-permute-done.8.b11, ...), custom_call_target="tpu_custom_call" | custom-call | tf_op jit(solution)/shard_map/pallas_call | solution.py:241
Async XLA Ops:
  0.0 1.0 %copy-start = (bf16[4,3,2,64,64]{4,3,2,1,0:T(8,128)(2,1)S(1)}, bf16[4,3,2,64,64]{4,3,2,1,0:T(8,128)(2,1)}, u32[]{:S(2)}) copy-start(bf16[4,3,2,64,64]{4,3,2,1,0:T(8,128)(2,1)} %gates.3) | copy-start | bytes 589828
  1.0 1.2 %copy-start.2 = (bf16[2,262144]{1,0:T(2,128)(2,1)S(1)}, bf16[2,262144]{1,0:T(2,128)(2,1)}, u32[]{:S(2)}) copy-start(bf16[2,262144]{1,0:T(2,128)(2,1)} %param.3) | copy-start | bytes 3145732
  5.7 10.2 %collective-permute-start = (bf16[32,32,128]{2,1,0:T(8,128)(2,1)S(1)}, bf16[32,32,128]{2,1,0:T(8,128)(2,1)S(1)}, u32[]{:S(2)}, u32[]{:S(2)}) collective-permute-start(bf16[32,32,128]{2,1,0:T(8,128)(2,1)S(1)} %get-tuple-element.21), channel_id=1, source_target_pairs={{0,8},{4,12},{8,0},{12,4},{16,24},{20,28},{24,16},{28,20},{1,9},{5... | collective-permute-start | bytes 786440 | tf_op jit(solution)/shard_map/ppermute | solution.py:256
  8.8 13.4 %collective-permute-start.1 = (bf16[32,32,128]{2,1,0:T(8,128)(2,1)S(1)}, bf16[32,32,128]{2,1,0:T(8,128)(2,1)S(1)}, u32[]{:S(2)}, u32[]{:S(2)}) collective-permute-start(bf16[32,32,128]{2,1,0:T(8,128)(2,1)S(1)} %get-tuple-element.22), channel_id=1, source_target_pairs={{0,4},{4,0},{8,12},{12,8},{16,20},{20,16},{24,28},{28,24},{1,5},{5... | collective-permute-start | bytes 786440 | tf_op jit(solution)/shard_map/ppermute | solution.py:256
  10.3 11.9 %copy-start.3 = (s32[4]{0:T(128)S(1)}, s32[4]{0:T(128)}, u32[]{:S(2)}) copy-start(s32[4]{0:T(128)} %regroup.1) | copy-start | bytes 52
  10.3 11.9 %collective-permute-start.2 = (bf16[32,32,128]{2,1,0:T(8,128)(2,1)S(1)}, bf16[32,32,128]{2,1,0:T(8,128)(2,1)S(1)}, u32[]{:S(2)}, u32[]{:S(2)}) collective-permute-start(bf16[32,32,128]{2,1,0:T(8,128)(2,1)S(1)} %get-tuple-element.23), channel_id=1, source_target_pairs={{0,12},{4,8},{8,4},{12,0},{16,28},{20,24},{24,20},{28,16},{1,13},{... | collective-permute-start | bytes 786440 | tf_op jit(solution)/shard_map/ppermute | solution.py:256
  22.2 2.8 %copy-start.1 = (bf16[4,3,2,64,64]{4,3,2,1,0:T(8,128)(2,1)S(1)}, bf16[4,3,2,64,64]{4,3,2,1,0:T(8,128)(2,1)}, u32[]{:S(2)}) copy-start(bf16[4,3,2,64,64]{4,3,2,1,0:T(8,128)(2,1)} %gates.3) | copy-start | bytes 589828
  23.1 2.8 %collective-permute-start.3 = (bf16[2,32,16,128]{3,2,1,0:T(8,128)(2,1)S(1)}, bf16[2,32,16,128]{3,2,1,0:T(8,128)(2,1)S(1)}, u32[]{:S(2)}, u32[]{:S(2)}) collective-permute-start(bf16[2,32,16,128]{3,2,1,0:T(8,128)(2,1)S(1)} %get-tuple-element.25), channel_id=1, source_target_pairs={{0,1},{1,0},{2,3},{3,2},{4,5},{5,4},{6,7},{7,6},{8,9},{9,8},{10,11... | collective-permute-start | bytes 786440 | tf_op jit(solution)/shard_map/ppermute | solution.py:280
  23.1 9.2 %collective-permute-start.4 = (bf16[2,32,16,128]{3,2,1,0:T(8,128)(2,1)S(1)}, bf16[2,32,16,128]{3,2,1,0:T(8,128)(2,1)S(1)}, u32[]{:S(2)}, u32[]{:S(2)}) collective-permute-start(bf16[2,32,16,128]{3,2,1,0:T(8,128)(2,1)S(1)} %get-tuple-element.26), channel_id=1, source_target_pairs={{0,2},{1,3},{2,0},{3,1},{4,6},{5,7},{6,4},{7,5},{8,10},{9,11},{10,... | collective-permute-start | bytes 786440 | tf_op jit(solution)/shard_map/ppermute | solution.py:280
  24.7 12.3 %collective-permute-start.5 = (bf16[2,32,16,128]{3,2,1,0:T(8,128)(2,1)S(1)}, bf16[2,32,16,128]{3,2,1,0:T(8,128)(2,1)S(1)}, u32[]{:S(2)}, u32[]{:S(2)}) collective-permute-start(bf16[2,32,16,128]{3,2,1,0:T(8,128)(2,1)S(1)} %get-tuple-element.27), channel_id=1, source_target_pairs={{0,3},{1,2},{2,1},{3,0},{4,7},{5,6},{6,5},{7,4},{8,11},{9,10},{10,... | collective-permute-start | bytes 786440 | tf_op jit(solution)/shard_map/ppermute | solution.py:280
  38.3 8.6 %collective-permute-start.6 = (bf16[32,32,128]{2,1,0:T(8,128)(2,1)S(1)}, bf16[32,32,128]{2,1,0:T(8,128)(2,1)S(1)}, u32[]{:S(2)}, u32[]{:S(2)}) collective-permute-start(bf16[32,32,128]{2,1,0:T(8,128)(2,1)S(1)} %get-tuple-element.31), channel_id=1, source_target_pairs={{0,4},{4,0},{8,12},{12,8},{16,20},{20,16},{24,28},{28,24},{1,5},{5... | collective-permute-start | bytes 786440 | tf_op jit(solution)/shard_map/ppermute | solution.py:256
  39.9 20.3 %collective-permute-start.7 = (bf16[32,32,128]{2,1,0:T(8,128)(2,1)S(1)}, bf16[32,32,128]{2,1,0:T(8,128)(2,1)S(1)}, u32[]{:S(2)}, u32[]{:S(2)}) collective-permute-start(bf16[32,32,128]{2,1,0:T(8,128)(2,1)S(1)} %get-tuple-element.32), channel_id=1, source_target_pairs={{0,16},{4,20},{8,24},{12,28},{16,0},{20,4},{24,8},{28,12},{1,17},{... | collective-permute-start | bytes 786440 | tf_op jit(solution)/shard_map/ppermute | solution.py:256
  42.5 23.3 %collective-permute-start.8 = (bf16[32,32,128]{2,1,0:T(8,128)(2,1)S(1)}, bf16[32,32,128]{2,1,0:T(8,128)(2,1)S(1)}, u32[]{:S(2)}, u32[]{:S(2)}) collective-permute-start(bf16[32,32,128]{2,1,0:T(8,128)(2,1)S(1)} %get-tuple-element.33), channel_id=1, source_target_pairs={{0,20},{4,16},{8,28},{12,24},{16,4},{20,0},{24,12},{28,8},{1,21},{... | collective-permute-start | bytes 786440 | tf_op jit(solution)/shard_map/ppermute | solution.py:256

commit v2 on v1

--- a/solution.py
+++ b/solution.py
@@ -144,14 +144,24 @@
     return outs
 
 
+PLACES = ((1, 0), (1, 1), (0, 1), (0, 0))
+APART = (2, 3, 1, 0)
+
+
+def by_place(blocks):
+    return dict(zip(PLACES, blocks))
+
+
 def store_blocks(outs, at, blocks):
+    blocks = by_place(blocks)
     for k, out in enumerate(outs):
         for i in range(2):
             for j in range(2):
-                blocks[2 * i + j][at + k] = out[j * HALF : (j + 1) * HALF, i * 128 : (i + 1) * 128]
+                blocks[i, j][at + k] = out[j * HALF : (j + 1) * HALF, i * 128 : (i + 1) * 128]
 
 
 STEP = 8
+CHUNKS = 2
 
 
 def own_bits():
@@ -160,7 +170,9 @@
     return [hi >> k % hi_bits & 1 for k in range(4)]
 
 
-def first_kernel(x_ref, gates, o00, o01, o10, o11, spread, turned, w1_ref):
+def first_kernel(x_ref, gates, *refs):
+    *outs, spread, turned, w1_ref = refs
+    count = outs[0].shape[0]
     own = own_bits()
     late = product(gate_of(gates, 3, 0), gate_of(gates, 2, 0))
     early = product(gate_of(gates, 1, 0), gate_of(gates, 0, 0))
@@ -180,7 +192,8 @@
     for k in range(0, HALF, STEP):
         rows = slice(k * G, (k + STEP) * G)
         x = jnp.concatenate([turned[0, rows, :], turned[1, rows, :]], axis=1).astype(BF).reshape(STEP, G, 4 * G)
-        store_blocks(both_gates(x, w1_ref[...], g), k, (o00, o01, o10, o11))
+        part = 4 * (k // count)
+        store_blocks(both_gates(x, w1_ref[...], g), k % count, outs[part : part + 4])
 
 
 def weights_kernel(top, gates, w1_ref, g_ref, w_ref):
@@ -192,21 +205,25 @@
 
 
 def middle_kernel(*refs):
-    *ins, w1_ref, g_ref, o00, o01, o10, o11 = refs
-    for k in range(0, HALF, STEP):
-        halves = [jnp.concatenate([x[i, k : k + STEP] for x in ins], axis=1) for i in range(2)]
+    *ins, w1_ref, g_ref, o0, o1, o2, o3 = refs
+    order = [APART.index(o) for o in range(4)] if len(ins) > 1 else [0]
+    for k in range(0, o0.shape[0], STEP):
+        ordered = [ins[at] for at in order]
+        halves = [jnp.concatenate([x[i, k : k + STEP] for x in ordered], axis=1) for i in range(2)]
         x = jnp.concatenate(halves, axis=2)
-        store_blocks(both_gates(x, w1_ref[...], g_ref[...]), k, (o00, o01, o10, o11))
-
-
-def last_kernel(b00, b01, b10, b11, w_ref, o_ref, wide, spread):
+        store_blocks(both_gates(x, w1_ref[...], g_ref[...]), k, (o0, o1, o2, o3))
+
+
+def last_kernel(*refs):
+    *ins, w_ref, o_ref, wide, spread = refs
     bit = own_bits()[3]
-    blocks = ((b00, b01), (b10, b11))
+    count = ins[0].shape[0]
     for k in range(HALF):
+        blocks = by_place(ins[4 * (k // count) : 4 * (k // count) + 4])
         for j in range(2):
             rows = pl.ds(pl.multiple_of(k * G + (bit ^ j) * HALF, HALF), HALF)
             for i in range(2):
-                wide[i, rows, :] = blocks[i][j][k].astype(F32)
+                wide[i, rows, :] = blocks[i, j][k % count].astype(F32)
     for k in range(G // 8):
         halves = [
             jnp.concatenate([wide[i, pl.ds(k * 8 + q, HALF, stride=G), :] for q in range(8)], axis=0) for i in range(2)
@@ -220,17 +237,17 @@
         o_ref[k * 512 : (k + 1) * 512, :] = spread[k * 512 : (k + 1) * 512, :].astype(BF)
 
 
-def pick_kernel(regroup, b00, b01, b10, b11, *outs):
-    blocks = ((b00, b01), (b10, b11))
+def pick_kernel(regroup, b0, b1, b2, b3, *outs):
+    blocks = by_place((b0, b1, b2, b3))
     own = own_bits()[1]
     lo = lax.axis_index("lo")
     rows = outs[0].shape[2]
-    for o, out in enumerate(outs):
+    for o, out in zip(APART, outs):
         t = regroup[lo ^ o]
         j = t >> 1 ^ own
         at = pl.ds(pl.multiple_of((t & 1) * rows, rows), rows)
         for i in range(2):
-            out[i] = jnp.where(j == 0, blocks[i][0][:, at, :], blocks[i][1][:, at, :])
+            out[i] = jnp.where(j == 0, blocks[i, 0][:, at, :], blocks[i, 1][:, at, :])
 
 
 VMEM = pl.BlockSpec(memory_space=pltpu.VMEM)
@@ -249,12 +266,28 @@
 
 
 def exchange(blocks, b_bit, a_bit):
-    size = lax.axis_size("hi")
     out = []
-    for at, block in enumerate(blocks):
-        apart = (at >> 1 << b_bit) | ((at & 1) << a_bit)
-        out.append(lax.ppermute(block, "hi", [(d, d ^ apart) for d in range(size)]) if apart else block)
+    for (i, j), block in zip(PLACES, blocks):
+        apart = i << b_bit | j << a_bit
+        pairs = [(d, d ^ apart) for d in range(lax.axis_size("hi"))]
+        out.append(lax.ppermute(block, "hi", pairs) if apart else block)
     return out
+
+
+def regrouped(blocks, regroup, bit, groups, top):
+    count = blocks[0].shape[0]
+    if groups == 4:
+        part = jax.ShapeDtypeStruct((2, count, top, 128), BF)
+        parts = call(pick_kernel, [part] * groups, (regroup, *blocks), specs=[SMEM] + [VMEM] * 4)
+        pairs = [[(d, d ^ o) for d in range(groups)] for o in APART]
+        return [lax.ppermute(x, "lo", to) if o else x for o, x, to in zip(APART, parts, pairs)]
+    own = lax.axis_index("hi") >> bit & 1
+    blocks = by_place(blocks)
+    halves = [jnp.stack([blocks[i, 0], blocks[i, 1]], axis=1) for i in range(2)]
+    both = jnp.stack([jnp.where(own == 0, half, jnp.flip(half, 1)) for half in halves])
+    both = jnp.take(both.reshape(2, count, groups, top, 128), regroup, axis=2)
+    both = lax.all_to_all(both, "lo", split_axis=2, concat_axis=2, tiled=True)
+    return [both.reshape(2, count, G, 128)]
 
 
 def on_device(state, gates, regroup):
@@ -264,32 +297,24 @@
     top = G // groups
     whole = 2 * state.shape[1] // 128
 
-    block = jax.ShapeDtypeStruct((HALF, HALF, 128), BF)
+    count = HALF // CHUNKS
+    block = jax.ShapeDtypeStruct((count, HALF, 128), BF)
     turned = pltpu.VMEM((2, HALF * G, 128), F32)
     spread = pltpu.VMEM((whole, 128), F32)
     x = state.reshape(2, -1, 128).transpose(1, 0, 2).reshape(whole, 128)
-    blocks = call(first_kernel, [block] * 4, (x, gates), scratch=[spread, turned, pltpu.VMEM((4 * G, 8 * G), BF)])
-    blocks = exchange(blocks, bits[0], bits[1])
+    scratch = [spread, turned, pltpu.VMEM((4 * G, 8 * G), BF)]
+    blocks = call(first_kernel, [block] * (4 * CHUNKS), (x, gates), scratch=scratch)
     shapes = [jax.ShapeDtypeStruct(shape, BF) for shape in ((4 * G, 8 * G), (G, 2 * G), (4 * G, 4 * G))]
     w1, g, w = call(functools.partial(weights_kernel, top if groups == 4 else 0), shapes, (gates,))
 
-    if groups == 4:
-        part = jax.ShapeDtypeStruct((2, HALF, top, 128), BF)
-        parts = call(pick_kernel, [part] * groups, (regroup, *blocks), specs=[SMEM] + [VMEM] * 4)
-        parts = [parts[0]] + [
-            lax.ppermute(parts[o], "lo", [(d, d ^ o) for d in range(groups)]) for o in range(1, groups)
-        ]
-    else:
-        own = lax.axis_index("hi") >> bits[1] & 1
-        halves = [jnp.stack(blocks[2 * i : 2 * i + 2], 1) for i in range(2)]
-        both = jnp.stack([jnp.where(own == 0, half, jnp.flip(half, 1)) for half in halves])
-        both = jnp.take(both.reshape(2, HALF, groups, top, 128), regroup, axis=2)
-        both = lax.all_to_all(both, "lo", split_axis=2, concat_axis=2, tiled=True)
-        parts = [both.reshape(2, HALF, G, 128)]
-    blocks = call(middle_kernel, [block] * 4, (*parts, w1, g))
-    blocks = exchange(blocks, bits[2], bits[3])
-
-    out = call(last_kernel, jax.ShapeDtypeStruct((whole, 128), BF), (*blocks, w), scratch=[turned, spread])
+    done = []
+    for chunk in range(CHUNKS):
+        mine = exchange(blocks[4 * chunk : 4 * chunk + 4], bits[0], bits[1])
+        parts = regrouped(mine, regroup, bits[1], groups, top)
+        mine = call(middle_kernel, [block] * 4, (*parts, w1, g))
+        done += exchange(mine, bits[2], bits[3])
+
+    out = call(last_kernel, jax.ShapeDtypeStruct((whole, 128), BF), (*done, w), scratch=[turned, spread])
     return out.reshape(-1, 2, 128).transpose(1, 0, 2).reshape(state.shape)
 
 

time: 70.3 us -> 60.3 us (0.86)
  waiting for transfers between devices: 46 us -> 20.1 us
  starting transfers between devices: 11 us -> 26.2 us
    ppermute x9 -> x18, waiting for transfers between devices: 46 us -> 20.1 us  [the longest x12 18.4 us: exchange(): out.append(lax.ppermute(block, 'hi', pairs) if apart else block)]
    ppermute x9 -> x18, starting transfers between devices: 11 us -> 26.2 us  [the longest x12 21.8 us: exchange(): out.append(lax.ppermute(block, 'hi', pairs) if apart else block)]
    pallas_call x5 -> x7, Pallas kernels: 10.8 us -> 11.5 us  [call(): pl.pallas_call(kernel, out_shape=outs, in_specs=specs or [VMEM] * len(arg...]
  transfers between devices with their start and end apart: 9 -> 18, of which waited for: 7 -> 7; matrix products, arithmetic and copies ran while one was open for 0% -> 0% of each run, Pallas kernels for 1% -> 6%
where the time goes in v2:
time: 60.3 us; the launch traced here: 60.1 us
  starting transfers between devices  26.2 us (43%)
  waiting for transfers between devices  20.1 us (33%)
  Pallas kernels  11.5 us (19%)
  local copies, waits for them, and re-layouts  2.23 us (4%)
    ppermute x12, starting transfers between devices, exchange(): out.append(lax.ppermute(block, 'hi', pairs) if apart else block)  21.8 us
    ppermute x12, waiting for transfers between devices, exchange(): out.append(lax.ppermute(block, 'hi', pairs) if apart else block)  18.4 us
    pallas_call x7, Pallas kernels, call(): pl.pallas_call(kernel, out_shape=outs, in_specs=specs or [VMEM] * len(arg...  11.5 us
    ppermute x6, starting transfers between devices, regrouped(): lax.ppermute(x, 'lo', to)  4.41 us
    unnamed x8, local copies, waits for them, and re-layouts  2.23 us
    ppermute x6, waiting for transfers between devices, regrouped(): lax.ppermute(x, 'lo', to)  1.77 us
  transfers between devices with their start and end apart: 18, of which 7 were waited for; matrix products, arithmetic and copies ran while one was open for 0% of the time, Pallas kernels for 6%

profile of v2, /device:TPU:0, one launch (start us, length us, event | category | flops | bytes accessed | tf_op | source)
XLA Modules:
  0.0 60.1 jit_solution(17273690225734768914)
XLA Ops:
  0.0 1.0 %copy-done = bf16[4,3,2,64,64]{4,3,2,1,0:T(8,128)(2,1)S(1)} copy-done((bf16[4,3,2,64,64]{4,3,2,1,0:T(8,128)(2,1)S(1)}, bf16[4,3,2,64,64]{4,3,2,1,0:T(8,128)(2,1)}, u32[]{:S(2)}) %copy-start) | copy-done | bytes 196632
  1.0 1.2 %copy-done.2 = bf16[2,262144]{1,0:T(2,128)(2,1)S(1)} copy-done((bf16[2,262144]{1,0:T(2,128)(2,1)S(1)}, bf16[2,262144]{1,0:T(2,128)(2,1)}, u32[]{:S(2)}) %copy-start.2) | copy-done | bytes 1048600
  2.2 3.5 %shard_map.37 = (bf16[16,32,128]{2,1,0:T(8,128)(2,1)S(1)}, bf16[16,32,128]{2,1,0:T(8,128)(2,1)S(1)}, bf16[16,32,128]{2,1,0:T(8,128)(2,1)S(1)}, bf16[16,32,128]{2...) custom-call(bf16[4096,128]{1,0:T(8,128)(2,1)S(1)} %bitcast.10, ...), custom_call_target="tpu_custom_call" | custom-call | tf_op jit(solution)/shard_map/pallas_call | solution.py:258
  5.7 0.0 copy-start.1
  5.7 3.0 %collective-permute-start = (bf16[16,32,128]{2,1,0:T(8,128)(2,1)S(1)}, bf16[16,32,128]{2,1,0:T(8,128)(2,1)S(1)}, u32[]{:S(2)}, u32[]{:S(2)}) collective-permute-start(bf16[16,32,128]{2,1,0:T(8,128)(2,1)S(1)} %get-tuple-element.32), channel_id=1, source_target_pairs={{0,4},{4,0},{8,12},{12,8},{16,20},{20,16},{24,28},{28,24},{1,5},{5... | collective-permute-start | bytes 393224 | tf_op jit(solution)/shard_map/ppermute | solution.py:273
  8.8 1.5 %collective-permute-start.1 = (bf16[16,32,128]{2,1,0:T(8,128)(2,1)S(1)}, bf16[16,32,128]{2,1,0:T(8,128)(2,1)S(1)}, u32[]{:S(2)}, u32[]{:S(2)}) collective-permute-start(bf16[16,32,128]{2,1,0:T(8,128)(2,1)S(1)} %get-tuple-element.33), channel_id=1, source_target_pairs={{0,12},{4,8},{8,4},{12,0},{16,28},{20,24},{24,20},{28,16},{1,13},{... | collective-permute-start | bytes 393224 | tf_op jit(solution)/shard_map/ppermute | solution.py:273
  10.3 0.1 collective-permute-start.2
  10.4 1.9 %collective-permute-start.9 = (bf16[16,32,128]{2,1,0:T(8,128)(2,1)S(1)}, bf16[16,32,128]{2,1,0:T(8,128)(2,1)S(1)}, u32[]{:S(2)}, u32[]{:S(2)}) collective-permute-start(bf16[16,32,128]{2,1,0:T(8,128)(2,1)S(1)} %get-tuple-element.46), channel_id=1, source_target_pairs={{0,4},{4,0},{8,12},{12,8},{16,20},{20,16},{24,28},{28,24},{1,5},{5... | collective-permute-start | bytes 393224 | tf_op jit(solution)/shard_map/ppermute | solution.py:273
  12.3 1.5 %collective-permute-start.10 = (bf16[16,32,128]{2,1,0:T(8,128)(2,1)S(1)}, bf16[16,32,128]{2,1,0:T(8,128)(2,1)S(1)}, u32[]{:S(2)}, u32[]{:S(2)}) collective-permute-start(bf16[16,32,128]{2,1,0:T(8,128)(2,1)S(1)} %get-tuple-element.47), channel_id=1, source_target_pairs={{0,12},{4,8},{8,4},{12,0},{16,28},{20,24},{24,20},{28,16},{1,13},{... | collective-permute-start | bytes 393224 | tf_op jit(solution)/shard_map/ppermute | solution.py:273
  13.8 2.4 %collective-permute-done.b0 = bf16[16,32,128]{2,1,0:T(8,128)(2,1)S(1)} collective-permute-done((bf16[16,32,128]{2,1,0:T(8,128)(2,1)S(1)}, bf16[16,32,128]{2,1,0:T(8,128)(2,1)S(1)}, u32[]{:S(2)}, u32[]{:S(2)}) %collective-permute-start) | collective-permute-done | bytes 131104 | tf_op jit(solution)/shard_map/ppermute | solution.py:273
  16.1 1.8 %collective-permute-start.11 = (bf16[16,32,128]{2,1,0:T(8,128)(2,1)S(1)}, bf16[16,32,128]{2,1,0:T(8,128)(2,1)S(1)}, u32[]{:S(2)}, u32[]{:S(2)}) collective-permute-start(bf16[16,32,128]{2,1,0:T(8,128)(2,1)S(1)} %get-tuple-element.48), channel_id=1, source_target_pairs={{0,8},{4,12},{8,0},{12,4},{16,24},{20,28},{24,16},{28,20},{1,9},{5... | collective-permute-start | bytes 393224 | tf_op jit(solution)/shard_map/ppermute | solution.py:273
  18.0 0.0 collective-permute-done.1.b1
  18.0 0.0 collective-permute-done.2.b2
  18.0 0.0 copy-done.3
  18.0 0.7 %shard_map.38 = (bf16[2,16,16,128]{3,2,1,0:T(8,128)(2,1)S(1)}, bf16[2,16,16,128]{3,2,1,0:T(8,128)(2,1)S(1)}, bf16[2,16,16,128]{3,2,1,0:T(8,128)(2,1)S(1)}, bf16[2,16,16,128]{3,2,1,0:T(8,128)(2,1)S(1)}) custom-call(s32[4]{0:T(128)S(1)} %copy-done.3, bf16[16,32,128]{2,1,0:T(8,128)(2,1)S(1)} %collective-permute-done.b0, ...), custom_call_target="tpu_custom_call" | custom-call | tf_op jit(solution)/shard_map/pallas_call | solution.py:258
  18.7 1.6 %collective-permute-start.3 = (bf16[2,16,16,128]{3,2,1,0:T(8,128)(2,1)S(1)}, bf16[2,16,16,128]{3,2,1,0:T(8,128)(2,1)S(1)}, u32[]{:S(2)}, u32[]{:S(2)}) collective-permute-start(bf16[2,16,16,128]{3,2,1,0:T(8,128)(2,1)S(1)} %get-tuple-element.36), channel_id=1, source_target_pairs={{0,2},{1,3},{2,0},{3,1},{4,6},{5,7},{6,4},{7,5},{8,10},{9,11},{10,... | collective-permute-start | bytes 393224 | tf_op jit(solution)/shard_map/ppermute | solution.py:283
  20.2 0.0 collective-permute-start.4
  20.2 0.0 collective-permute-done.9.b0
  20.2 0.6 %collective-permute-start.5 = (bf16[2,16,16,128]{3,2,1,0:T(8,128)(2,1)S(1)}, bf16[2,16,16,128]{3,2,1,0:T(8,128)(2,1)S(1)}, u32[]{:S(2)}, u32[]{:S(2)}) collective-permute-start(bf16[2,16,16,128]{3,2,1,0:T(8,128)(2,1)S(1)} %get-tuple-element.38), channel_id=1, source_target_pairs={{0,1},{1,0},{2,3},{3,2},{4,5},{5,4},{6,7},{7,6},{8,9},{9,8},{10,11... | collective-permute-start | bytes 393224 | tf_op jit(solution)/shard_map/ppermute | solution.py:283
  20.9 0.0 copy-done.1
  20.9 0.9 %shard_map.39 = (bf16[256,512]{1,0:T(8,128)(2,1)S(1)}, bf16[64,128]{1,0:T(8,128)(2,1)S(1)}, bf16[256,256]{1,0:T(8,128)(2,1)S(1)}) custom-call(bf16[4,3,2,64,64]{4,3,2,1,0:T(8,128)(2,1)S(1)} %copy-done.1), custom_call_target="tpu_custom_call" | custom-call | tf_op jit(solution)/shard_map/pallas_call | solution.py:258
  21.8 0.0 collective-permute-done.10.b1
  21.8 0.3 collective-permute-done.11.b2
  22.0 0.7 %shard_map.41 = (bf16[2,16,16,128]{3,2,1,0:T(8,128)(2,1)S(1)}, bf16[2,16,16,128]{3,2,1,0:T(8,128)(2,1)S(1)}, bf16[2,16,16,128]{3,2,1,0:T(8,128)(2,1)S(1)}, bf16[2,16,16,128]{3,2,1,0:T(8,128)(2,1)S(1)}) custom-call(s32[4]{0:T(128)S(1)} %copy-done.3, bf16[16,32,128]{2,1,0:T(8,128)(2,1)S(1)} %collective-permute-done.9.b0, ...), custom_call_target="tpu_custom_call" | custom-call | tf_op jit(solution)/shard_map/pallas_call | solution.py:258
  22.8 1.7 %collective-permute-start.12 = (bf16[2,16,16,128]{3,2,1,0:T(8,128)(2,1)S(1)}, bf16[2,16,16,128]{3,2,1,0:T(8,128)(2,1)S(1)}, u32[]{:S(2)}, u32[]{:S(2)}) collective-permute-start(bf16[2,16,16,128]{3,2,1,0:T(8,128)(2,1)S(1)} %get-tuple-element.50), channel_id=1, source_target_pairs={{0,2},{1,3},{2,0},{3,1},{4,6},{5,7},{6,4},{7,5},{8,10},{9,11},{10,... | collective-permute-start | bytes 393224 | tf_op jit(solution)/shard_map/ppermute | solution.py:283
  24.4 0.0 collective-permute-start.13
  24.4 0.0 collective-permute-done.3.refs_0_
  24.4 0.5 collective-permute-start.14
  25.0 1.8 %collective-permute-done.4.refs_1_ = bf16[2,16,16,128]{3,2,1,0:T(8,128)(2,1)S(1)} collective-permute-done((bf16[2,16,16,128]{3,2,1,0:T(8,128)(2,1)S(1)}, bf16[2,16,16,128]{3,2,1,0:T(8,128)(2,1)S(1)}, u32[]{:S(2)}, u32[]{:S(2)}) %collective-permute-start.4) | collective-permute-done | bytes 131104 | tf_op jit(solution)/shard_map/ppermute | solution.py:283
  26.7 0.0 collective-permute-done.5.refs_2_
  26.7 0.7 %shard_map.40 = (bf16[16,32,128]{2,1,0:T(8,128)(2,1)S(1)}, bf16[16,32,128]{2,1,0:T(8,128)(2,1)S(1)}, bf16[16,32,128]{2,1,0:T(8,128)(2,1)S(1)}, bf16[16,32,128]{2,1,0:T(8,128)(2,1)S(1)}) custom-call(bf16[2,16,16,128]{3,2,1,0:T(8,128)(2,1)S(1)} %collective-permute-done.3.refs_0_, bf16[2,16,16,128]{3,2,1,0:T(8,128)(2,1)S(1)} %collective-permute-done.4.refs_1_, ...), custom_call_target="tpu_custom_call" | custom-call | tf_op jit(solution)/shard_map/pallas_call | solution.py:258
  27.5 2.7 %collective-permute-start.6 = (bf16[16,32,128]{2,1,0:T(8,128)(2,1)S(1)}, bf16[16,32,128]{2,1,0:T(8,128)(2,1)S(1)}, u32[]{:S(2)}, u32[]{:S(2)}) collective-permute-start(bf16[16,32,128]{2,1,0:T(8,128)(2,1)S(1)} %get-tuple-element.42), channel_id=1, source_target_pairs={{0,16},{4,20},{8,24},{12,28},{16,0},{20,4},{24,8},{28,12},{1,17},{... | collective-permute-start | bytes 393224 | tf_op jit(solution)/shard_map/ppermute | solution.py:273
  30.1 2.7 %collective-permute-start.7 = (bf16[16,32,128]{2,1,0:T(8,128)(2,1)S(1)}, bf16[16,32,128]{2,1,0:T(8,128)(2,1)S(1)}, u32[]{:S(2)}, u32[]{:S(2)}) collective-permute-start(bf16[16,32,128]{2,1,0:T(8,128)(2,1)S(1)} %get-tuple-element.43), channel_id=1, source_target_pairs={{0,20},{4,16},{8,28},{12,24},{16,4},{20,0},{24,12},{28,8},{1,21},{... | collective-permute-start | bytes 393224 | tf_op jit(solution)/shard_map/ppermute | solution.py:273
  32.9 0.0 collective-permute-done.12.refs_0_
  32.9 0.2 collective-permute-start.8
  33.1 0.0 collective-permute-done.13.refs_1_
  33.1 0.0 collective-permute-done.14.refs_2_
  33.1 0.7 %shard_map.42 = (bf16[16,32,128]{2,1,0:T(8,128)(2,1)S(1)}, bf16[16,32,128]{2,1,0:T(8,128)(2,1)S(1)}, bf16[16,32,128]{2,1,0:T(8,128)(2,1)S(1)}, bf16[16,32,128]{2,1,0:T(8,128)(2,1)S(1)}) custom-call(bf16[2,16,16,128]{3,2,1,0:T(8,128)(2,1)S(1)} %collective-permute-done.12.refs_0_, bf16[2,16,16,128]{3,2,1,0:T(8,128)(2,1)S(1)} %collective-permute-done.13.refs_1_, ...), custom_call_target="tpu_custom_call" | custom-call | tf_op jit(solution)/shard_map/pallas_call | solution.py:258
  33.8 2.4 %collective-permute-start.15 = (bf16[16,32,128]{2,1,0:T(8,128)(2,1)S(1)}, bf16[16,32,128]{2,1,0:T(8,128)(2,1)S(1)}, u32[]{:S(2)}, u32[]{:S(2)}) collective-permute-start(bf16[16,32,128]{2,1,0:T(8,128)(2,1)S(1)} %get-tuple-element.54), channel_id=1, source_target_pairs={{0,16},{4,20},{8,24},{12,28},{16,0},{20,4},{24,8},{28,12},{1,17},{... | collective-permute-start | bytes 393224 | tf_op jit(solution)/shard_map/ppermute | solution.py:273
  36.3 1.8 %collective-permute-start.16 = (bf16[16,32,128]{2,1,0:T(8,128)(2,1)S(1)}, bf16[16,32,128]{2,1,0:T(8,128)(2,1)S(1)}, u32[]{:S(2)}, u32[]{:S(2)}) collective-permute-start(bf16[16,32,128]{2,1,0:T(8,128)(2,1)S(1)} %get-tuple-element.55), channel_id=1, source_target_pairs={{0,20},{4,16},{8,28},{12,24},{16,4},{20,0},{24,12},{28,8},{1,21},{... | collective-permute-start | bytes 393224 | tf_op jit(solution)/shard_map/ppermute | solution.py:273
  38.1 7.9 %collective-permute-done.6.refs_0_ = bf16[16,32,128]{2,1,0:T(8,128)(2,1)S(1)} collective-permute-done((bf16[16,32,128]{2,1,0:T(8,128)(2,1)S(1)}, bf16[16,32,128]{2,1,0:T(8,128)(2,1)S(1)}, u32[]{:S(2)}, u32[]{:S(2)}) %collective-permute-start.6) | collective-permute-done | bytes 131104 | tf_op jit(solution)/shard_map/ppermute | solution.py:273
  46.0 2.1 %collective-permute-start.17 = (bf16[16,32,128]{2,1,0:T(8,128)(2,1)S(1)}, bf16[16,32,128]{2,1,0:T(8,128)(2,1)S(1)}, u32[]{:S(2)}, u32[]{:S(2)}) collective-permute-start(bf16[16,32,128]{2,1,0:T(8,128)(2,1)S(1)} %get-tuple-element.56), channel_id=1, source_target_pairs={{0,4},{4,0},{8,12},{12,8},{16,20},{20,16},{24,28},{28,24},{1,5},{5... | collective-permute-start | bytes 393224 | tf_op jit(solution)/shard_map/ppermute | solution.py:273
  48.1 2.3 %collective-permute-done.7.refs_1_ = bf16[16,32,128]{2,1,0:T(8,128)(2,1)S(1)} collective-permute-done((bf16[16,32,128]{2,1,0:T(8,128)(2,1)S(1)}, bf16[16,32,128]{2,1,0:T(8,128)(2,1)S(1)}, u32[]{:S(2)}, u32[]{:S(2)}) %collective-permute-start.7) | collective-permute-done | bytes 131104 | tf_op jit(solution)/shard_map/ppermute | solution.py:273
  50.3 0.0 collective-permute-done.8.refs_2_
  50.3 1.3 %collective-permute-done.15.refs_4_ = bf16[16,32,128]{2,1,0:T(8,128)(2,1)S(1)} collective-permute-done((bf16[16,32,128]{2,1,0:T(8,128)(2,1)S(1)}, bf16[16,32,128]{2,1,0:T(8,128)(2,1)S(1)}, u32[]{:S(2)}, u32[]{:S(2)}) %collective-permute-start.15) | collective-permute-done | bytes 131104 | tf_op jit(solution)/shard_map/ppermute | solution.py:273
  51.6 4.2 %collective-permute-done.16.refs_5_ = bf16[16,32,128]{2,1,0:T(8,128)(2,1)S(1)} collective-permute-done((bf16[16,32,128]{2,1,0:T(8,128)(2,1)S(1)}, bf16[16,32,128]{2,1,0:T(8,128)(2,1)S(1)}, u32[]{:S(2)}, u32[]{:S(2)}) %collective-permute-start.16) | collective-permute-done | bytes 131104 | tf_op jit(solution)/shard_map/ppermute | solution.py:273
  55.9 0.0 collective-permute-done.17.refs_6_
  55.9 4.3 %shard_map.43 = bf16[4096,128]{1,0:T(8,128)(2,1)} custom-call(bf16[16,32,128]{2,1,0:T(8,128)(2,1)S(1)} %collective-permute-done.6.refs_0_, bf16[16,32,128]{2,1,0:T(8,128)(2,1)S(1)} %collective-permute-done.7.refs_1_, bf16[16,32,128]{2,1,0:T(8,128)(2,1)S(1)} %collective-permute-done.8.refs_2_, bf16[16,32,128]{2,1,0:T(8,128)(2,1)S(1)} %get-tuple-element.45.refs_3_, ...), custom_call_target="tpu_custom_call" | custom-call | tf_op jit(solution)/shard_map/pallas_call | solution.py:258
  (3 shorter events, 0.0 us)
Async XLA Ops:
  0.0 1.0 %copy-start = (bf16[4,3,2,64,64]{4,3,2,1,0:T(8,128)(2,1)S(1)}, bf16[4,3,2,64,64]{4,3,2,1,0:T(8,128)(2,1)}, u32[]{:S(2)}) copy-start(bf16[4,3,2,64,64]{4,3,2,1,0:T(8,128)(2,1)} %gates.3) | copy-start | bytes 589828
  1.0 1.2 %copy-start.2 = (bf16[2,262144]{1,0:T(2,128)(2,1)S(1)}, bf16[2,262144]{1,0:T(2,128)(2,1)}, u32[]{:S(2)}) copy-start(bf16[2,262144]{1,0:T(2,128)(2,1)} %param.3) | copy-start | bytes 3145732
  2.2 15.7 %copy-start.3 = (s32[4]{0:T(128)S(1)}, s32[4]{0:T(128)}, u32[]{:S(2)}) copy-start(s32[4]{0:T(128)} %regroup.3) | copy-start | bytes 52
  5.7 15.2 %copy-start.1 = (bf16[4,3,2,64,64]{4,3,2,1,0:T(8,128)(2,1)S(1)}, bf16[4,3,2,64,64]{4,3,2,1,0:T(8,128)(2,1)}, u32[]{:S(2)}) copy-start(bf16[4,3,2,64,64]{4,3,2,1,0:T(8,128)(2,1)} %gates.3) | copy-start | bytes 589828
  5.7 10.4 %collective-permute-start = (bf16[16,32,128]{2,1,0:T(8,128)(2,1)S(1)}, bf16[16,32,128]{2,1,0:T(8,128)(2,1)S(1)}, u32[]{:S(2)}, u32[]{:S(2)}) collective-permute-start(bf16[16,32,128]{2,1,0:T(8,128)(2,1)S(1)} %get-tuple-element.32), channel_id=1, source_target_pairs={{0,4},{4,0},{8,12},{12,8},{16,20},{20,16},{24,28},{28,24},{1,5},{5... | collective-permute-start | bytes 393224 | tf_op jit(solution)/shard_map/ppermute | solution.py:273
  8.8 9.2 %collective-permute-start.1 = (bf16[16,32,128]{2,1,0:T(8,128)(2,1)S(1)}, bf16[16,32,128]{2,1,0:T(8,128)(2,1)S(1)}, u32[]{:S(2)}, u32[]{:S(2)}) collective-permute-start(bf16[16,32,128]{2,1,0:T(8,128)(2,1)S(1)} %get-tuple-element.33), channel_id=1, source_target_pairs={{0,12},{4,8},{8,4},{12,0},{16,28},{20,24},{24,20},{28,16},{1,13},{... | collective-permute-start | bytes 393224 | tf_op jit(solution)/shard_map/ppermute | solution.py:273
  10.3 7.7 %collective-permute-start.2 = (bf16[16,32,128]{2,1,0:T(8,128)(2,1)S(1)}, bf16[16,32,128]{2,1,0:T(8,128)(2,1)S(1)}, u32[]{:S(2)}, u32[]{:S(2)}) collective-permute-start(bf16[16,32,128]{2,1,0:T(8,128)(2,1)S(1)} %get-tuple-element.34), channel_id=1, source_target_pairs={{0,8},{4,12},{8,0},{12,4},{16,24},{20,28},{24,16},{28,20},{1,9},{5... | collective-permute-start | bytes 393224 | tf_op jit(solution)/shard_map/ppermute | solution.py:273
  10.4 9.9 %collective-permute-start.9 = (bf16[16,32,128]{2,1,0:T(8,128)(2,1)S(1)}, bf16[16,32,128]{2,1,0:T(8,128)(2,1)S(1)}, u32[]{:S(2)}, u32[]{:S(2)}) collective-permute-start(bf16[16,32,128]{2,1,0:T(8,128)(2,1)S(1)} %get-tuple-element.46), channel_id=1, source_target_pairs={{0,4},{4,0},{8,12},{12,8},{16,20},{20,16},{24,28},{28,24},{1,5},{5... | collective-permute-start | bytes 393224 | tf_op jit(solution)/shard_map/ppermute | solution.py:273
  12.3 9.5 %collective-permute-start.10 = (bf16[16,32,128]{2,1,0:T(8,128)(2,1)S(1)}, bf16[16,32,128]{2,1,0:T(8,128)(2,1)S(1)}, u32[]{:S(2)}, u32[]{:S(2)}) collective-permute-start(bf16[16,32,128]{2,1,0:T(8,128)(2,1)S(1)} %get-tuple-element.47), channel_id=1, source_target_pairs={{0,12},{4,8},{8,4},{12,0},{16,28},{20,24},{24,20},{28,16},{1,13},{... | collective-permute-start | bytes 393224 | tf_op jit(solution)/shard_map/ppermute | solution.py:273
  16.1 5.9 %collective-permute-start.11 = (bf16[16,32,128]{2,1,0:T(8,128)(2,1)S(1)}, bf16[16,32,128]{2,1,0:T(8,128)(2,1)S(1)}, u32[]{:S(2)}, u32[]{:S(2)}) collective-permute-start(bf16[16,32,128]{2,1,0:T(8,128)(2,1)S(1)} %get-tuple-element.48), channel_id=1, source_target_pairs={{0,8},{4,12},{8,0},{12,4},{16,24},{20,28},{24,16},{28,20},{1,9},{5... | collective-permute-start | bytes 393224 | tf_op jit(solution)/shard_map/ppermute | solution.py:273
  18.7 5.7 %collective-permute-start.3 = (bf16[2,16,16,128]{3,2,1,0:T(8,128)(2,1)S(1)}, bf16[2,16,16,128]{3,2,1,0:T(8,128)(2,1)S(1)}, u32[]{:S(2)}, u32[]{:S(2)}) collective-permute-start(bf16[2,16,16,128]{3,2,1,0:T(8,128)(2,1)S(1)} %get-tuple-element.36), channel_id=1, source_target_pairs={{0,2},{1,3},{2,0},{3,1},{4,6},{5,7},{6,4},{7,5},{8,10},{9,11},{10,... | collective-permute-start | bytes 393224 | tf_op jit(solution)/shard_map/ppermute | solution.py:283
  20.2 6.5 %collective-permute-start.4 = (bf16[2,16,16,128]{3,2,1,0:T(8,128)(2,1)S(1)}, bf16[2,16,16,128]{3,2,1,0:T(8,128)(2,1)S(1)}, u32[]{:S(2)}, u32[]{:S(2)}) collective-permute-start(bf16[2,16,16,128]{3,2,1,0:T(8,128)(2,1)S(1)} %get-tuple-element.37), channel_id=1, source_target_pairs={{0,3},{1,2},{2,1},{3,0},{4,7},{5,6},{6,5},{7,4},{8,11},{9,10},{10,... | collective-permute-start | bytes 393224 | tf_op jit(solution)/shard_map/ppermute | solution.py:283
  20.2 6.5 %collective-permute-start.5 = (bf16[2,16,16,128]{3,2,1,0:T(8,128)(2,1)S(1)}, bf16[2,16,16,128]{3,2,1,0:T(8,128)(2,1)S(1)}, u32[]{:S(2)}, u32[]{:S(2)}) collective-permute-start(bf16[2,16,16,128]{3,2,1,0:T(8,128)(2,1)S(1)} %get-tuple-element.38), channel_id=1, source_target_pairs={{0,1},{1,0},{2,3},{3,2},{4,5},{5,4},{6,7},{7,6},{8,9},{9,8},{10,11... | collective-permute-start | bytes 393224 | tf_op jit(solution)/shard_map/ppermute | solution.py:283
  22.8 10.1 %collective-permute-start.12 = (bf16[2,16,16,128]{3,2,1,0:T(8,128)(2,1)S(1)}, bf16[2,16,16,128]{3,2,1,0:T(8,128)(2,1)S(1)}, u32[]{:S(2)}, u32[]{:S(2)}) collective-permute-start(bf16[2,16,16,128]{3,2,1,0:T(8,128)(2,1)S(1)} %get-tuple-element.50), channel_id=1, source_target_pairs={{0,2},{1,3},{2,0},{3,1},{4,6},{5,7},{6,4},{7,5},{8,10},{9,11},{10,... | collective-permute-start | bytes 393224 | tf_op jit(solution)/shard_map/ppermute | solution.py:283
  24.4 8.7 %collective-permute-start.13 = (bf16[2,16,16,128]{3,2,1,0:T(8,128)(2,1)S(1)}, bf16[2,16,16,128]{3,2,1,0:T(8,128)(2,1)S(1)}, u32[]{:S(2)}, u32[]{:S(2)}) collective-permute-start(bf16[2,16,16,128]{3,2,1,0:T(8,128)(2,1)S(1)} %get-tuple-element.51), channel_id=1, source_target_pairs={{0,3},{1,2},{2,1},{3,0},{4,7},{5,6},{6,5},{7,4},{8,11},{9,10},{10,... | collective-permute-start | bytes 393224 | tf_op jit(solution)/shard_map/ppermute | solution.py:283
  24.4 8.7 %collective-permute-start.14 = (bf16[2,16,16,128]{3,2,1,0:T(8,128)(2,1)S(1)}, bf16[2,16,16,128]{3,2,1,0:T(8,128)(2,1)S(1)}, u32[]{:S(2)}, u32[]{:S(2)}) collective-permute-start(bf16[2,16,16,128]{3,2,1,0:T(8,128)(2,1)S(1)} %get-tuple-element.52), channel_id=1, source_target_pairs={{0,1},{1,0},{2,3},{3,2},{4,5},{5,4},{6,7},{7,6},{8,9},{9,8},{10,11... | collective-permute-start | bytes 393224 | tf_op jit(solution)/shard_map/ppermute | solution.py:283
  27.5 18.5 %collective-permute-start.6 = (bf16[16,32,128]{2,1,0:T(8,128)(2,1)S(1)}, bf16[16,32,128]{2,1,0:T(8,128)(2,1)S(1)}, u32[]{:S(2)}, u32[]{:S(2)}) collective-permute-start(bf16[16,32,128]{2,1,0:T(8,128)(2,1)S(1)} %get-tuple-element.42), channel_id=1, source_target_pairs={{0,16},{4,20},{8,24},{12,28},{16,0},{20,4},{24,8},{28,12},{1,17},{... | collective-permute-start | bytes 393224 | tf_op jit(solution)/shard_map/ppermute | solution.py:273
  30.1 20.2 %collective-permute-start.7 = (bf16[16,32,128]{2,1,0:T(8,128)(2,1)S(1)}, bf16[16,32,128]{2,1,0:T(8,128)(2,1)S(1)}, u32[]{:S(2)}, u32[]{:S(2)}) collective-permute-start(bf16[16,32,128]{2,1,0:T(8,128)(2,1)S(1)} %get-tuple-element.43), channel_id=1, source_target_pairs={{0,20},{4,16},{8,28},{12,24},{16,4},{20,0},{24,12},{28,8},{1,21},{... | collective-permute-start | bytes 393224 | tf_op jit(solution)/shard_map/ppermute | solution.py:273
  32.9 17.5 %collective-permute-start.8 = (bf16[16,32,128]{2,1,0:T(8,128)(2,1)S(1)}, bf16[16,32,128]{2,1,0:T(8,128)(2,1)S(1)}, u32[]{:S(2)}, u32[]{:S(2)}) collective-permute-start(bf16[16,32,128]{2,1,0:T(8,128)(2,1)S(1)} %get-tuple-element.44), channel_id=1, source_target_pairs={{0,4},{4,0},{8,12},{12,8},{16,20},{20,16},{24,28},{28,24},{1,5},{5... | collective-permute-start | bytes 393224 | tf_op jit(solution)/shard_map/ppermute | solution.py:273
  33.8 17.8 %collective-permute-start.15 = (bf16[16,32,128]{2,1,0:T(8,128)(2,1)S(1)}, bf16[16,32,128]{2,1,0:T(8,128)(2,1)S(1)}, u32[]{:S(2)}, u32[]{:S(2)}) collective-permute-start(bf16[16,32,128]{2,1,0:T(8,128)(2,1)S(1)} %get-tuple-element.54), channel_id=1, source_target_pairs={{0,16},{4,20},{8,24},{12,28},{16,0},{20,4},{24,8},{28,12},{1,17},{... | collective-permute-start | bytes 393224 | tf_op jit(solution)/shard_map/ppermute | solution.py:273
  36.3 19.6 %collective-permute-start.16 = (bf16[16,32,128]{2,1,0:T(8,128)(2,1)S(1)}, bf16[16,32,128]{2,1,0:T(8,128)(2,1)S(1)}, u32[]{:S(2)}, u32[]{:S(2)}) collective-permute-start(bf16[16,32,128]{2,1,0:T(8,128)(2,1)S(1)} %get-tuple-element.55), channel_id=1, source_target_pairs={{0,20},{4,16},{8,28},{12,24},{16,4},{20,0},{24,12},{28,8},{1,21},{... | collective-permute-start | bytes 393224 | tf_op jit(solution)/shard_map/ppermute | solution.py:273
  46.0 9.9 %collective-permute-start.17 = (bf16[16,32,128]{2,1,0:T(8,128)(2,1)S(1)}, bf16[16,32,128]{2,1,0:T(8,128)(2,1)S(1)}, u32[]{:S(2)}, u32[]{:S(2)}) collective-permute-start(bf16[16,32,128]{2,1,0:T(8,128)(2,1)S(1)} %get-tuple-element.56), channel_id=1, source_target_pairs={{0,4},{4,0},{8,12},{12,8},{16,20},{20,16},{24,28},{28,24},{1,5},{5... | collective-permute-start | bytes 393224 | tf_op jit(solution)/shard_map/ppermute | solution.py:273

commit v3 on v2

--- a/solution.py
+++ b/solution.py
@@ -160,8 +160,8 @@
                 blocks[i, j][at + k] = out[j * HALF : (j + 1) * HALF, i * 128 : (i + 1) * 128]
 
 
-STEP = 8
-CHUNKS = 2
+STEP = 4
+EARLY = 12
 
 
 def own_bits():
@@ -172,11 +172,11 @@
 
 def first_kernel(x_ref, gates, *refs):
     *outs, spread, turned, w1_ref = refs
-    count = outs[0].shape[0]
+    early = outs[0].shape[0]
     own = own_bits()
     late = product(gate_of(gates, 3, 0), gate_of(gates, 2, 0))
-    early = product(gate_of(gates, 1, 0), gate_of(gates, 0, 0))
-    w0 = first_weights(wide_product(late, early))
+    soon = product(gate_of(gates, 1, 0), gate_of(gates, 0, 0))
+    w0 = first_weights(wide_product(late, soon))
     w1_ref[...] = right_weights(gate_of(gates, 0, 1), True, 0, own[0])
     g = left_weights(product(gate_of(gates, 1, 2), gate_of(gates, 0, 2)), 0, own[1])
 
@@ -192,38 +192,68 @@
     for k in range(0, HALF, STEP):
         rows = slice(k * G, (k + STEP) * G)
         x = jnp.concatenate([turned[0, rows, :], turned[1, rows, :]], axis=1).astype(BF).reshape(STEP, G, 4 * G)
-        part = 4 * (k // count)
-        store_blocks(both_gates(x, w1_ref[...], g), k % count, outs[part : part + 4])
-
-
-def weights_kernel(top, gates, w1_ref, g_ref, w_ref):
+        made = both_gates(x, w1_ref[...], g)
+        if k >= early:
+            store_blocks(made, k - early, outs[4:])
+        else:
+            store_blocks(made, k, outs[:4])
+
+
+def lanes_kernel(b0, b1, b2, b3, w1_ref, moving, staying):
+    blocks = by_place((b0, b1, b2, b3))
+    w = w1_ref[:, : 4 * G]
+    for j in range(2):
+        for k in range(0, b0.shape[0], STEP):
+            x = jnp.concatenate([blocks[i, j][k : k + STEP] for i in range(2)], axis=2).reshape(STEP * HALF, 4 * G)
+            y = dot(x, w).astype(BF)
+            staying[j, k : k + STEP] = y[:, :128].reshape(STEP, HALF, 128)
+            moving[j, k : k + STEP] = y[:, 128:].reshape(STEP, HALF, 128)
+
+
+def rows_kernel(*refs):
+    *ins, w1_ref, g_ref, m0, m1, s0, s1 = refs
+    for k in range(0, m0.shape[0], STEP):
+        made = both_gates(joined(ins, k), w1_ref[...], g_ref[...])
+        for at, out in enumerate(made):
+            for i in range(2):
+                lanes = slice(i * 128, (i + 1) * 128)
+                (s0, s1)[i][k + at] = out[:HALF, lanes]
+                (m0, m1)[i][k + at] = out[HALF:, lanes]
+
+
+def weights_kernel(top, gates, w1_ref, i_ref, g_ref, w_ref):
     own = own_bits()
     w1_ref[...] = right_weights(product(gate_of(gates, 2, 1), gate_of(gates, 1, 1)), False, own[0], own[2])
+    k, a = iotas(G, 2 * G)
+    i_ref[...] = right_weights(ones(k == a), False, 0, 0)
     step = top * lax.axis_index("lo") if top else 0
     g_ref[...] = left_weights(product(gate_of(gates, 3, 2), gate_of(gates, 2, 2)), step, own[3])
     w_ref[...] = last_weights(gate_of(gates, 3, 1), own[2])
 
 
+def joined(ins, k):
+    order = [APART.index(o) for o in range(4)] if len(ins) > 1 else [0]
+    halves = [jnp.concatenate([ins[at][i, k : k + STEP] for at in order], axis=1) for i in range(2)]
+    return jnp.concatenate(halves, axis=2)
+
+
 def middle_kernel(*refs):
     *ins, w1_ref, g_ref, o0, o1, o2, o3 = refs
-    order = [APART.index(o) for o in range(4)] if len(ins) > 1 else [0]
     for k in range(0, o0.shape[0], STEP):
-        ordered = [ins[at] for at in order]
-        halves = [jnp.concatenate([x[i, k : k + STEP] for x in ordered], axis=1) for i in range(2)]
-        x = jnp.concatenate(halves, axis=2)
-        store_blocks(both_gates(x, w1_ref[...], g_ref[...]), k, (o0, o1, o2, o3))
-
-
-def last_kernel(*refs):
-    *ins, w_ref, o_ref, wide, spread = refs
+        store_blocks(both_gates(joined(ins, k), w1_ref[...], g_ref[...]), k, (o0, o1, o2, o3))
+
+
+def last_kernel(m0, m1, s0, s1, b0, b1, b2, b3, w_ref, o_ref, wide, spread):
     bit = own_bits()[3]
-    count = ins[0].shape[0]
+    blocks = by_place((b0, b1, b2, b3))
+    early = m0.shape[0]
+    firsts = ((s0, m0), (s1, m1))
     for k in range(HALF):
-        blocks = by_place(ins[4 * (k // count) : 4 * (k // count) + 4])
         for j in range(2):
             rows = pl.ds(pl.multiple_of(k * G + (bit ^ j) * HALF, HALF), HALF)
             for i in range(2):
-                wide[i, rows, :] = blocks[i, j][k % count].astype(F32)
+                block = blocks[i, j][k - early] if k >= early else firsts[i][j][k]
+                wide[i, rows, :] = block.astype(F32)
     for k in range(G // 8):
         halves = [
             jnp.concatenate([wide[i, pl.ds(k * 8 + q, HALF, stride=G), :] for q in range(8)], axis=0) for i in range(2)
@@ -237,8 +267,13 @@
         o_ref[k * 512 : (k + 1) * 512, :] = spread[k * 512 : (k + 1) * 512, :].astype(BF)
 
 
-def pick_kernel(regroup, b0, b1, b2, b3, *outs):
-    blocks = by_place((b0, b1, b2, b3))
+def pick_kernel(groups, regroup, *refs):
+    ins, outs = refs[:-groups], refs[-groups:]
+    if len(ins) == 4:
+        blocks = by_place(ins)
+    else:
+        moved, stayed = ins
+        blocks = {(i, j): (stayed, moved)[i].at[j] for i, j in PLACES}
     own = own_bits()[1]
     lo = lax.axis_index("lo")
     rows = outs[0].shape[2]
@@ -254,36 +289,48 @@
 SMEM = pl.BlockSpec(memory_space=pltpu.SMEM)
 
 
-def call(kernel, outs, args, specs=None, scratch=()):
+def call(kernel, outs, args, specs=None, scratch=(), after=()):
+    specs = specs or [VMEM] * len(args)
+
+    def body(*refs):
+        kernel(*refs[: len(args)], *refs[len(args) + len(after) :])
+
     return pl.pallas_call(
-        kernel,
+        body,
         out_shape=outs,
-        in_specs=specs or [VMEM] * len(args),
+        in_specs=specs + [pl.BlockSpec(memory_space=pl.ANY)] * len(after),
         out_specs=jax.tree.map(lambda _: VMEM, outs),
         scratch_shapes=scratch,
+        cost_estimate=pl.CostEstimate(flops=1, bytes_accessed=1, transcendentals=0),
         compiler_params=pltpu.CompilerParams(vmem_limit_bytes=40 * 2**20),
-    )(*args)
+    )(*args, *after)
+
+
+def swapped(x, apart):
+    return lax.ppermute(x, "hi", [(d, d ^ apart) for d in range(lax.axis_size("hi"))])
 
 
 def exchange(blocks, b_bit, a_bit):
     out = []
     for (i, j), block in zip(PLACES, blocks):
         apart = i << b_bit | j << a_bit
-        pairs = [(d, d ^ apart) for d in range(lax.axis_size("hi"))]
-        out.append(lax.ppermute(block, "hi", pairs) if apart else block)
+        out.append(swapped(block, apart) if apart else block)
     return out
 
 
-def regrouped(blocks, regroup, bit, groups, top):
-    count = blocks[0].shape[0]
+def regrouped(blocks, regroup, bit, groups, top, after=()):
+    count = blocks[0].shape[-3]
     if groups == 4:
         part = jax.ShapeDtypeStruct((2, count, top, 128), BF)
-        parts = call(pick_kernel, [part] * groups, (regroup, *blocks), specs=[SMEM] + [VMEM] * 4)
+        parts = call(functools.partial(pick_kernel, groups), [part] * groups, (regroup, *blocks), [SMEM] + [VMEM] * len(blocks), after=after)
         pairs = [[(d, d ^ o) for d in range(groups)] for o in APART]
         return [lax.ppermute(x, "lo", to) if o else x for o, x, to in zip(APART, parts, pairs)]
     own = lax.axis_index("hi") >> bit & 1
-    blocks = by_place(blocks)
-    halves = [jnp.stack([blocks[i, 0], blocks[i, 1]], axis=1) for i in range(2)]
+    if len(blocks) == 4:
+        blocks = by_place(blocks)
+        halves = [jnp.stack([blocks[i, 0], blocks[i, 1]], axis=1) for i in range(2)]
+    else:
+        halves = [jnp.moveaxis(x, 0, 1) for x in blocks[::-1]]
     both = jnp.stack([jnp.where(own == 0, half, jnp.flip(half, 1)) for half in halves])
     both = jnp.take(both.reshape(2, count, groups, top, 128), regroup, axis=2)
     both = lax.all_to_all(both, "lo", split_axis=2, concat_axis=2, tiled=True)
@@ -297,24 +344,35 @@
     top = G // groups
     whole = 2 * state.shape[1] // 128
 
-    count = HALF // CHUNKS
-    block = jax.ShapeDtypeStruct((count, HALF, 128), BF)
+    block = jax.ShapeDtypeStruct((HALF - EARLY, HALF, 128), BF)
+    early_block = jax.ShapeDtypeStruct((EARLY, HALF, 128), BF)
+    early_half = jax.ShapeDtypeStruct((2, EARLY, HALF, 128), BF)
     turned = pltpu.VMEM((2, HALF * G, 128), F32)
     spread = pltpu.VMEM((whole, 128), F32)
+    lanes, rows = (4 * G, 8 * G), (G, 2 * G)
+
     x = state.reshape(2, -1, 128).transpose(1, 0, 2).reshape(whole, 128)
-    scratch = [spread, turned, pltpu.VMEM((4 * G, 8 * G), BF)]
-    blocks = call(first_kernel, [block] * (4 * CHUNKS), (x, gates), scratch=scratch)
-    shapes = [jax.ShapeDtypeStruct(shape, BF) for shape in ((4 * G, 8 * G), (G, 2 * G), (4 * G, 4 * G))]
-    w1, g, w = call(functools.partial(weights_kernel, top if groups == 4 else 0), shapes, (gates,))
-
-    done = []
-    for chunk in range(CHUNKS):
-        mine = exchange(blocks[4 * chunk : 4 * chunk + 4], bits[0], bits[1])
-        parts = regrouped(mine, regroup, bits[1], groups, top)
-        mine = call(middle_kernel, [block] * 4, (*parts, w1, g))
-        done += exchange(mine, bits[2], bits[3])
-
-    out = call(last_kernel, jax.ShapeDtypeStruct((whole, 128), BF), (*done, w), scratch=[turned, spread])
+    scratch = [spread, turned, pltpu.VMEM(lanes, BF)]
+    made = call(first_kernel, [early_block] * 4 + [block] * 4, (x, gates), scratch=scratch)
+    early = exchange(made[:4], bits[0], bits[1])
+    late = exchange(made[4:], bits[0], bits[1])
+    shapes = [jax.ShapeDtypeStruct(shape, BF) for shape in (lanes, lanes, rows, (4 * G, 4 * G))]
+    w1, w_i, g, w = call(functools.partial(weights_kernel, top if groups == 4 else 0), shapes, (gates,))
+
+    moving, staying = call(lanes_kernel, [early_half] * 2, (*early, w1))
+    early = [swapped(moving, 1 << bits[2]), staying]
+
+    late = regrouped(late, regroup, bits[1], groups, top, after=[staying])
+    late = call(middle_kernel, [block] * 4, (*late, w1, g))
+    sent = late[3:]
+    late = exchange(late, bits[2], bits[3])
+
+    early = regrouped(early, regroup, bits[1], groups, top, after=sent)
+    m0, m1, *early = call(rows_kernel, [early_block] * 4, (*early, w_i, g))
+    early = [swapped(m0, 1 << bits[3]), swapped(m1, 1 << bits[3]), *early]
+
+    args = (*early, *late, w)
+    out = call(last_kernel, jax.ShapeDtypeStruct((whole, 128), BF), args, scratch=[turned, spread])
     return out.reshape(-1, 2, 128).transpose(1, 0, 2).reshape(state.shape)
 
 

time: 60.3 us -> 62.8 us (1.041)
  waiting for transfers between devices: 20.1 us -> 23.4 us
  starting transfers between devices: 26.2 us -> 23.2 us
  Pallas kernels: 11.5 us -> 13.1 us
  local copies, waits for them, and re-layouts: 2.23 us -> 2.87 us
    ppermute x6, waiting for transfers between devices: 1.77 us -> 7.09 us  [regrouped(): lax.ppermute(x, 'lo', to)]
    ppermute x12, starting transfers between devices: 21.8 us -> 18.8 us  [swapped(): lax.ppermute(x, 'hi', [(d, d ^ apart) for d in range(lax.axis_size('hi'))])]
    ppermute x12, waiting for transfers between devices: 18.4 us -> 16.3 us  [swapped(): lax.ppermute(x, 'hi', [(d, d ^ apart) for d in range(lax.axis_size('hi'))])]
    pallas_call x7 -> x8, Pallas kernels: 11.5 us -> 13.1 us  [call(): pl.pallas_call(body, out_shape=outs, in_specs=specs + [pl.BlockSpec(memor...]
    unnamed x8, local copies, waits for them, and re-layouts: 2.23 us -> 2.87 us
  transfers between devices with their start and end apart: 18 -> 18, of which waited for: 7 -> 9; matrix products, arithmetic and copies ran while one was open for 0% -> 0% of each run, Pallas kernels for 6% -> 7%
where the time goes in v3:
time: 62.8 us; the launch traced here: 62.6 us
  waiting for transfers between devices  23.4 us (37%)
  starting transfers between devices  23.2 us (37%)
  Pallas kernels  13.1 us (21%)
  local copies, waits for them, and re-layouts  2.87 us (5%)
    ppermute x12, starting transfers between devices, swapped(): lax.ppermute(x, 'hi', [(d, d ^ apart) for d in range(lax.axis_size('hi'))])  18.8 us
    ppermute x12, waiting for transfers between devices, swapped(): lax.ppermute(x, 'hi', [(d, d ^ apart) for d in range(lax.axis_size('hi'))])  16.3 us
    pallas_call x8, Pallas kernels, call(): pl.pallas_call(body, out_shape=outs, in_specs=specs + [pl.BlockSpec(memor...  13.1 us
    ppermute x6, waiting for transfers between devices, regrouped(): lax.ppermute(x, 'lo', to)  7.09 us
    ppermute x6, starting transfers between devices, regrouped(): lax.ppermute(x, 'lo', to)  4.44 us
    unnamed x8, local copies, waits for them, and re-layouts  2.87 us
  transfers between devices with their start and end apart: 18, of which 9 were waited for; matrix products, arithmetic and copies ran while one was open for 0% of the time, Pallas kernels for 7%

profile of v3, /device:TPU:0, one launch (start us, length us, event | category | flops | bytes accessed | tf_op | source)
XLA Modules:
  0.0 62.6 jit_solution(7159977298468089539)
XLA Ops:
  0.0 1.0 %copy-done = bf16[4,3,2,64,64]{4,3,2,1,0:T(8,128)(2,1)S(1)} copy-done((bf16[4,3,2,64,64]{4,3,2,1,0:T(8,128)(2,1)S(1)}, bf16[4,3,2,64,64]{4,3,2,1,0:T(8,128)(2,1)}, u32[]{:S(2)}) %copy-start) | copy-done | bytes 196632
  1.0 1.2 %copy-done.2 = bf16[2,262144]{1,0:T(2,128)(2,1)S(1)} copy-done((bf16[2,262144]{1,0:T(2,128)(2,1)S(1)}, bf16[2,262144]{1,0:T(2,128)(2,1)}, u32[]{:S(2)}) %copy-start.2) | copy-done | bytes 1048600
  2.2 4.1 %shard_map.37 = (bf16[12,32,128]{2,1,0:T(8,128)(2,1)S(1)}, bf16[12,32,128]{2,1,0:T(8,128)(2,1)S(1)}, bf16[12,32,128]{2,1,0:T(8,128)(2,1)S(1)}, bf16[12,32,128]{2...) custom-call(bf16[4096,128]{1,0:T(8,128)(2,1)S(1)} %bitcast.10, ...), custom_call_target="tpu_custom_call" | custom-call | flops 1 | bytes 1 | tf_op jit(solution)/shard_map/pallas_call | solution.py:298
  6.3 3.0 %collective-permute-start = (bf16[12,32,128]{2,1,0:T(8,128)(2,1)S(1)}, bf16[12,32,128]{2,1,0:T(8,128)(2,1)S(1)}, u32[]{:S(2)}, u32[]{:S(2)}) collective-permute-start(bf16[12,32,128]{2,1,0:T(8,128)(2,1)S(1)} %get-tuple-element.35), channel_id=1, source_target_pairs={{0,4},{4,0},{8,12},{12,8},{16,20},{20,16},{24,28},{28,24},{1,5},{5... | collective-permute-start | bytes 294920 | tf_op jit(solution)/shard_map/ppermute | solution.py:310
  9.3 0.1 collective-permute-start.4
  9.4 3.0 %collective-permute-start.5 = (bf16[20,32,128]{2,1,0:T(8,128)(2,1)S(1)}, bf16[20,32,128]{2,1,0:T(8,128)(2,1)S(1)}, u32[]{:S(2)}, u32[]{:S(2)}) collective-permute-start(bf16[20,32,128]{2,1,0:T(8,128)(2,1)S(1)} %get-tuple-element.43), channel_id=1, source_target_pairs={{0,12},{4,8},{8,4},{12,0},{16,28},{20,24},{24,20},{28,16},{1,13},{... | collective-permute-start | bytes 491528 | tf_op jit(solution)/shard_map/ppermute | solution.py:310
  12.4 0.5 collective-permute-start.6
  12.8 1.5 %collective-permute-start.1 = (bf16[12,32,128]{2,1,0:T(8,128)(2,1)S(1)}, bf16[12,32,128]{2,1,0:T(8,128)(2,1)S(1)}, u32[]{:S(2)}, u32[]{:S(2)}) collective-permute-start(bf16[12,32,128]{2,1,0:T(8,128)(2,1)S(1)} %get-tuple-element.36), channel_id=1, source_target_pairs={{0,12},{4,8},{8,4},{12,0},{16,28},{20,24},{24,20},{28,16},{1,13},{... | collective-permute-start | bytes 294920 | tf_op jit(solution)/shard_map/ppermute | solution.py:310
  14.3 0.9 %collective-permute-done.refs_0_ = bf16[12,32,128]{2,1,0:T(8,128)(2,1)S(1)} collective-permute-done((bf16[12,32,128]{2,1,0:T(8,128)(2,1)S(1)}, bf16[12,32,128]{2,1,0:T(8,128)(2,1)S(1)}, u32[]{:S(2)}, u32[]{:S(2)}) %collective-permute-start) | collective-permute-done | bytes 98336 | tf_op jit(solution)/shard_map/ppermute | solution.py:310
  15.2 2.3 %collective-permute-start.2 = (bf16[12,32,128]{2,1,0:T(8,128)(2,1)S(1)}, bf16[12,32,128]{2,1,0:T(8,128)(2,1)S(1)}, u32[]{:S(2)}, u32[]{:S(2)}) collective-permute-start(bf16[12,32,128]{2,1,0:T(8,128)(2,1)S(1)} %get-tuple-element.37), channel_id=1, source_target_pairs={{0,8},{4,12},{8,0},{12,4},{16,24},{20,28},{24,16},{28,20},{1,9},{5... | collective-permute-start | bytes 294920 | tf_op jit(solution)/shard_map/ppermute | solution.py:310
  17.5 1.0 %shard_map.38 = (bf16[256,512]{1,0:T(8,128)(2,1)S(1)}, bf16[256,512]{1,0:T(8,128)(2,1)S(1)}, bf16[64,128]{1,0:T(8,128)(2,1)S(1)}, bf16[256,256]{1,0:T(8,128)(2,1)S(1)}) custom-call(bf16[4,3,2,64,64]{4,3,2,1,0:T(8,128)(2,1)S(1)} %copy-done.1), custom_call_target="tpu_custom_call" | custom-call | flops 1 | bytes 1 | tf_op jit(solution)/shard_map/pallas_call | solution.py:298
  18.5 4.2 %collective-permute-done.1.refs_1_ = bf16[12,32,128]{2,1,0:T(8,128)(2,1)S(1)} collective-permute-done((bf16[12,32,128]{2,1,0:T(8,128)(2,1)S(1)}, bf16[12,32,128]{2,1,0:T(8,128)(2,1)S(1)}, u32[]{:S(2)}, u32[]{:S(2)}) %collective-permute-start.1) | collective-permute-done | bytes 98336 | tf_op jit(solution)/shard_map/ppermute | solution.py:310
  22.7 1.2 %collective-permute-done.2.refs_2_ = bf16[12,32,128]{2,1,0:T(8,128)(2,1)S(1)} collective-permute-done((bf16[12,32,128]{2,1,0:T(8,128)(2,1)S(1)}, bf16[12,32,128]{2,1,0:T(8,128)(2,1)S(1)}, u32[]{:S(2)}, u32[]{:S(2)}) %collective-permute-start.2) | collective-permute-done | bytes 98336 | tf_op jit(solution)/shard_map/ppermute | solution.py:310
  23.9 0.3 shard_map.39
  24.2 2.7 %collective-permute-start.3 = (bf16[2,12,32,128]{3,2,1,0:T(8,128)(2,1)S(1)}, bf16[2,12,32,128]{3,2,1,0:T(8,128)(2,1)S(1)}, u32[]{:S(2)}, u32[]{:S(2)}) collective-permute-start(bf16[2,12,32,128]{3,2,1,0:T(8,128)(2,1)S(1)} %get-tuple-element.40), channel_id=1, source_target_pairs={{0,16},{4,20},{8,24},{12,28},{16,0},{20,4},{24,8},{28,12},{1,17},{... | collective-permute-start | bytes 589832 | tf_op jit(solution)/shard_map/ppermute | solution.py:310
  26.9 0.0 collective-permute-done.4.refs_1_
  26.9 0.0 collective-permute-done.5.refs_2_
  26.9 0.0 collective-permute-done.6.refs_3_
  26.9 0.0 copy-start.3
  26.9 0.6 %copy-done.3 = s32[4]{0:T(128)S(1)} copy-done((s32[4]{0:T(128)S(1)}, s32[4]{0:T(128)}, u32[]{:S(2)}) %copy-start.3) | copy-done | bytes 40
  27.5 0.7 %shard_map.40 = (bf16[2,20,16,128]{3,2,1,0:T(8,128)(2,1)S(1)}, bf16[2,20,16,128]{3,2,1,0:T(8,128)(2,1)S(1)}, bf16[2,20,16,128]{3,2,1,0:T(8,128)(2,1)S(1)}, bf16[2,20,16,128]{3,2,1,0:T(8,128)(2,1)S(1)}) custom-call(s32[4]{0:T(128)S(1)} %copy-done.3, bf16[20,32,128]{2,1,0:T(8,128)(2,1)S(1)} %collective-permute-done.4.refs_1_, ...), custom_call_target="tpu_custom_call" | custom-call | flops 1 | bytes 1 | tf_op jit(solution)/shard_map/pallas_call | solution.py:298
  28.3 1.6 %collective-permute-start.7 = (bf16[2,20,16,128]{3,2,1,0:T(8,128)(2,1)S(1)}, bf16[2,20,16,128]{3,2,1,0:T(8,128)(2,1)S(1)}, u32[]{:S(2)}, u32[]{:S(2)}) collective-permute-start(bf16[2,20,16,128]{3,2,1,0:T(8,128)(2,1)S(1)} %get-tuple-element.46), channel_id=1, source_target_pairs={{0,2},{1,3},{2,0},{3,1},{4,6},{5,7},{6,4},{7,5},{8,10},{9,11},{10,... | collective-permute-start | bytes 491528 | tf_op jit(solution)/shard_map/ppermute | solution.py:327
  29.8 0.0 collective-permute-start.8
  29.8 0.6 %collective-permute-start.9 = (bf16[2,20,16,128]{3,2,1,0:T(8,128)(2,1)S(1)}, bf16[2,20,16,128]{3,2,1,0:T(8,128)(2,1)S(1)}, u32[]{:S(2)}, u32[]{:S(2)}) collective-permute-start(bf16[2,20,16,128]{3,2,1,0:T(8,128)(2,1)S(1)} %get-tuple-element.48), channel_id=1, source_target_pairs={{0,1},{1,0},{2,3},{3,2},{4,5},{5,4},{6,7},{7,6},{8,9},{9,8},{10,11... | collective-permute-start | bytes 491528 | tf_op jit(solution)/shard_map/ppermute | solution.py:327
  30.5 4.0 %collective-permute-done.7.refs_0_ = bf16[2,20,16,128]{3,2,1,0:T(8,128)(2,1)S(1)} collective-permute-done((bf16[2,20,16,128]{3,2,1,0:T(8,128)(2,1)S(1)}, bf16[2,20,16,128]{3,2,1,0:T(8,128)(2,1)S(1)}, u32[]{:S(2)}, u32[]{:S(2)}) %collective-permute-start.7) | collective-permute-done | bytes 163872 | tf_op jit(solution)/shard_map/ppermute | solution.py:327
  34.5 1.8 %collective-permute-done.8.refs_1_ = bf16[2,20,16,128]{3,2,1,0:T(8,128)(2,1)S(1)} collective-permute-done((bf16[2,20,16,128]{3,2,1,0:T(8,128)(2,1)S(1)}, bf16[2,20,16,128]{3,2,1,0:T(8,128)(2,1)S(1)}, u32[]{:S(2)}, u32[]{:S(2)}) %collective-permute-start.8) | collective-permute-done | bytes 163872 | tf_op jit(solution)/shard_map/ppermute | solution.py:327
  36.3 0.0 collective-permute-done.9.refs_2_
  36.3 1.2 %shard_map.41 = (bf16[20,32,128]{2,1,0:T(8,128)(2,1)S(1)}, bf16[20,32,128]{2,1,0:T(8,128)(2,1)S(1)}, bf16[20,32,128]{2,1,0:T(8,128)(2,1)S(1)}, bf16[20,32,128]{2,1,0:T(8,128)(2,1)S(1)}) custom-call(bf16[2,20,16,128]{3,2,1,0:T(8,128)(2,1)S(1)} %collective-permute-done.7.refs_0_, bf16[2,20,16,128]{3,2,1,0:T(8,128)(2,1)S(1)} %collective-permute-done.8.refs_1_, ...), custom_call_target="tpu_custom_call" | custom-call | flops 1 | bytes 1 | tf_op jit(solution)/shard_map/pallas_call | solution.py:298
  37.6 0.0 collective-permute-done.3.refs_1_
  37.6 0.7 %shard_map.42 = (bf16[2,12,16,128]{3,2,1,0:T(8,128)(2,1)S(1)}, bf16[2,12,16,128]{3,2,1,0:T(8,128)(2,1)S(1)}, bf16[2,12,16,128]{3,2,1,0:T(8,128)(2,1)S(1)}, bf16[2,12,16,128]{3,2,1,0:T(8,128)(2,1)S(1)}) custom-call(s32[4]{0:T(128)S(1)} %copy-done.3, bf16[2,12,32,128]{3,2,1,0:T(8,128)(2,1)S(1)} %collective-permute-done.3.refs_1_, ...), custom_call_target="tpu_custom_call" | custom-call | flops 1 | bytes 1 | tf_op jit(solution)/shard_map/pallas_call | solution.py:298
  38.2 0.6 %collective-permute-start.10 = (bf16[2,12,16,128]{3,2,1,0:T(8,128)(2,1)S(1)}, bf16[2,12,16,128]{3,2,1,0:T(8,128)(2,1)S(1)}, u32[]{:S(2)}, u32[]{:S(2)}) collective-permute-start(bf16[2,12,16,128]{3,2,1,0:T(8,128)(2,1)S(1)} %get-tuple-element.52), channel_id=1, source_target_pairs={{0,2},{1,3},{2,0},{3,1},{4,6},{5,7},{6,4},{7,5},{8,10},{9,11},{10,... | collective-permute-start | bytes 294920 | tf_op jit(solution)/shard_map/ppermute | solution.py:327
  38.9 1.5 %collective-permute-start.11 = (bf16[2,12,16,128]{3,2,1,0:T(8,128)(2,1)S(1)}, bf16[2,12,16,128]{3,2,1,0:T(8,128)(2,1)S(1)}, u32[]{:S(2)}, u32[]{:S(2)}) collective-permute-start(bf16[2,12,16,128]{3,2,1,0:T(8,128)(2,1)S(1)} %get-tuple-element.53), channel_id=1, source_target_pairs={{0,3},{1,2},{2,1},{3,0},{4,7},{5,6},{6,5},{7,4},{8,11},{9,10},{10,... | collective-permute-start | bytes 294920 | tf_op jit(solution)/shard_map/ppermute | solution.py:327
  40.3 0.1 collective-permute-start.12
  40.5 0.3 collective-permute-start.15
  40.8 2.5 %collective-permute-start.16 = (bf16[20,32,128]{2,1,0:T(8,128)(2,1)S(1)}, bf16[20,32,128]{2,1,0:T(8,128)(2,1)S(1)}, u32[]{:S(2)}, u32[]{:S(2)}) collective-permute-start(bf16[20,32,128]{2,1,0:T(8,128)(2,1)S(1)} %get-tuple-element.62), channel_id=1, source_target_pairs={{0,20},{4,16},{8,28},{12,24},{16,4},{20,0},{24,12},{28,8},{1,21},{... | collective-permute-start | bytes 491528 | tf_op jit(solution)/shard_map/ppermute | solution.py:310
  43.3 0.7 %collective-permute-done.10.refs_0_ = bf16[2,12,16,128]{3,2,1,0:T(8,128)(2,1)S(1)} collective-permute-done((bf16[2,12,16,128]{3,2,1,0:T(8,128)(2,1)S(1)}, bf16[2,12,16,128]{3,2,1,0:T(8,128)(2,1)S(1)}, u32[]{:S(2)}, u32[]{:S(2)}) %collective-permute-start.10) | collective-permute-done | bytes 98336 | tf_op jit(solution)/shard_map/ppermute | solution.py:327
  44.0 0.9 %collective-permute-start.17 = (bf16[20,32,128]{2,1,0:T(8,128)(2,1)S(1)}, bf16[20,32,128]{2,1,0:T(8,128)(2,1)S(1)}, u32[]{:S(2)}, u32[]{:S(2)}) collective-permute-start(bf16[20,32,128]{2,1,0:T(8,128)(2,1)S(1)} %get-tuple-element.63), channel_id=1, source_target_pairs={{0,4},{4,0},{8,12},{12,8},{16,20},{20,16},{24,28},{28,24},{1,5},{5... | collective-permute-start | bytes 491528 | tf_op jit(solution)/shard_map/ppermute | solution.py:310
  44.9 0.6 collective-permute-done.11.refs_1_
  45.5 0.0 collective-permute-done.12.refs_2_
  45.5 0.8 %shard_map.43 = (bf16[12,32,128]{2,1,0:T(8,128)(2,1)S(1)}, bf16[12,32,128]{2,1,0:T(8,128)(2,1)S(1)}, bf16[12,32,128]{2,1,0:T(8,128)(2,1)S(1)}, bf16[12,32,128]{2,1,0:T(8,128)(2,1)S(1)}) custom-call(bf16[2,12,16,128]{3,2,1,0:T(8,128)(2,1)S(1)} %collective-permute-done.10.refs_0_, bf16[2,12,16,128]{3,2,1,0:T(8,128)(2,1)S(1)} %collective-permute-done.11.refs_1_, ...), custom_call_target="tpu_custom_call" | custom-call | flops 1 | bytes 1 | tf_op jit(solution)/shard_map/pallas_call | solution.py:298
  46.3 0.6 collective-permute-start.13
  46.9 1.5 %collective-permute-start.14 = (bf16[12,32,128]{2,1,0:T(8,128)(2,1)S(1)}, bf16[12,32,128]{2,1,0:T(8,128)(2,1)S(1)}, u32[]{:S(2)}, u32[]{:S(2)}) collective-permute-start(bf16[12,32,128]{2,1,0:T(8,128)(2,1)S(1)} %get-tuple-element.58), channel_id=1, source_target_pairs={{0,4},{4,0},{8,12},{12,8},{16,20},{20,16},{24,28},{28,24},{1,5},{5... | collective-permute-start | bytes 294920 | tf_op jit(solution)/shard_map/ppermute | solution.py:310
  48.4 7.0 %collective-permute-done.15.refs_4_ = bf16[20,32,128]{2,1,0:T(8,128)(2,1)S(1)} collective-permute-done((bf16[20,32,128]{2,1,0:T(8,128)(2,1)S(1)}, bf16[20,32,128]{2,1,0:T(8,128)(2,1)S(1)}, u32[]{:S(2)}, u32[]{:S(2)}) %collective-permute-start.15) | collective-permute-done | bytes 163872 | tf_op jit(solution)/shard_map/ppermute | solution.py:310
  55.4 2.9 %collective-permute-done.16.refs_5_ = bf16[20,32,128]{2,1,0:T(8,128)(2,1)S(1)} collective-permute-done((bf16[20,32,128]{2,1,0:T(8,128)(2,1)S(1)}, bf16[20,32,128]{2,1,0:T(8,128)(2,1)S(1)}, u32[]{:S(2)}, u32[]{:S(2)}) %collective-permute-start.16) | collective-permute-done | bytes 163872 | tf_op jit(solution)/shard_map/ppermute | solution.py:310
  58.4 0.0 collective-permute-done.17.refs_6_
  58.4 0.0 collective-permute-done.13.refs_0_
  58.4 0.0 collective-permute-done.14.refs_1_
  58.4 4.3 %shard_map.44 = bf16[4096,128]{1,0:T(8,128)(2,1)} custom-call(bf16[12,32,128]{2,1,0:T(8,128)(2,1)S(1)} %collective-permute-done.13.refs_0_, bf16[12,32,128]{2,1,0:T(8,128)(2,1)S(1)} %collective-permute-done.14.refs_1_, bf16[12,32,128]{2,1,0:T(8,128)(2,1)S(1)} %get-tuple-element.59.refs_2_, bf16[12,32,128]{2,1,0:T(8,128)(2,1)S(1)} %get-tuple-element.60.refs_3_, ...), custom_call_target="tpu_custom_call" | custom-call | flops 1 | bytes 1 | tf_op jit(solution)/shard_map/pallas_call | solution.py:298
  (4 shorter events, 0.0 us)
Async XLA Ops:
  0.0 1.0 %copy-start = (bf16[4,3,2,64,64]{4,3,2,1,0:T(8,128)(2,1)S(1)}, bf16[4,3,2,64,64]{4,3,2,1,0:T(8,128)(2,1)}, u32[]{:S(2)}) copy-start(bf16[4,3,2,64,64]{4,3,2,1,0:T(8,128)(2,1)} %refs_0_.3) | copy-start | bytes 589828
  1.0 1.2 %copy-start.2 = (bf16[2,262144]{1,0:T(2,128)(2,1)S(1)}, bf16[2,262144]{1,0:T(2,128)(2,1)}, u32[]{:S(2)}) copy-start(bf16[2,262144]{1,0:T(2,128)(2,1)} %param.3) | copy-start | bytes 3145732
  2.2 15.2 %copy-start.1 = (bf16[4,3,2,64,64]{4,3,2,1,0:T(8,128)(2,1)S(1)}, bf16[4,3,2,64,64]{4,3,2,1,0:T(8,128)(2,1)}, u32[]{:S(2)}) copy-start(bf16[4,3,2,64,64]{4,3,2,1,0:T(8,128)(2,1)} %refs_0_.3) | copy-start | bytes 589828
  6.3 8.9 %collective-permute-start = (bf16[12,32,128]{2,1,0:T(8,128)(2,1)S(1)}, bf16[12,32,128]{2,1,0:T(8,128)(2,1)S(1)}, u32[]{:S(2)}, u32[]{:S(2)}) collective-permute-start(bf16[12,32,128]{2,1,0:T(8,128)(2,1)S(1)} %get-tuple-element.35), channel_id=1, source_target_pairs={{0,4},{4,0},{8,12},{12,8},{16,20},{20,16},{24,28},{28,24},{1,5},{5... | collective-permute-start | bytes 294920 | tf_op jit(solution)/shard_map/ppermute | solution.py:310
  9.3 17.5 %collective-permute-start.4 = (bf16[20,32,128]{2,1,0:T(8,128)(2,1)S(1)}, bf16[20,32,128]{2,1,0:T(8,128)(2,1)S(1)}, u32[]{:S(2)}, u32[]{:S(2)}) collective-permute-start(bf16[20,32,128]{2,1,0:T(8,128)(2,1)S(1)} %get-tuple-element.42), channel_id=1, source_target_pairs={{0,4},{4,0},{8,12},{12,8},{16,20},{20,16},{24,28},{28,24},{1,5},{5... | collective-permute-start | bytes 491528 | tf_op jit(solution)/shard_map/ppermute | solution.py:310
  9.4 17.5 %collective-permute-start.5 = (bf16[20,32,128]{2,1,0:T(8,128)(2,1)S(1)}, bf16[20,32,128]{2,1,0:T(8,128)(2,1)S(1)}, u32[]{:S(2)}, u32[]{:S(2)}) collective-permute-start(bf16[20,32,128]{2,1,0:T(8,128)(2,1)S(1)} %get-tuple-element.43), channel_id=1, source_target_pairs={{0,12},{4,8},{8,4},{12,0},{16,28},{20,24},{24,20},{28,16},{1,13},{... | collective-permute-start | bytes 491528 | tf_op jit(solution)/shard_map/ppermute | solution.py:310
  12.4 14.5 %collective-permute-start.6 = (bf16[20,32,128]{2,1,0:T(8,128)(2,1)S(1)}, bf16[20,32,128]{2,1,0:T(8,128)(2,1)S(1)}, u32[]{:S(2)}, u32[]{:S(2)}) collective-permute-start(bf16[20,32,128]{2,1,0:T(8,128)(2,1)S(1)} %get-tuple-element.44), channel_id=1, source_target_pairs={{0,8},{4,12},{8,0},{12,4},{16,24},{20,28},{24,16},{28,20},{1,9},{5... | collective-permute-start | bytes 491528 | tf_op jit(solution)/shard_map/ppermute | solution.py:310
  12.8 9.9 %collective-permute-start.1 = (bf16[12,32,128]{2,1,0:T(8,128)(2,1)S(1)}, bf16[12,32,128]{2,1,0:T(8,128)(2,1)S(1)}, u32[]{:S(2)}, u32[]{:S(2)}) collective-permute-start(bf16[12,32,128]{2,1,0:T(8,128)(2,1)S(1)} %get-tuple-element.36), channel_id=1, source_target_pairs={{0,12},{4,8},{8,4},{12,0},{16,28},{20,24},{24,20},{28,16},{1,13},{... | collective-permute-start | bytes 294920 | tf_op jit(solution)/shard_map/ppermute | solution.py:310
  15.2 8.7 %collective-permute-start.2 = (bf16[12,32,128]{2,1,0:T(8,128)(2,1)S(1)}, bf16[12,32,128]{2,1,0:T(8,128)(2,1)S(1)}, u32[]{:S(2)}, u32[]{:S(2)}) collective-permute-start(bf16[12,32,128]{2,1,0:T(8,128)(2,1)S(1)} %get-tuple-element.37), channel_id=1, source_target_pairs={{0,8},{4,12},{8,0},{12,4},{16,24},{20,28},{24,16},{28,20},{1,9},{5... | collective-permute-start | bytes 294920 | tf_op jit(solution)/shard_map/ppermute | solution.py:310
  24.2 13.4 %collective-permute-start.3 = (bf16[2,12,32,128]{3,2,1,0:T(8,128)(2,1)S(1)}, bf16[2,12,32,128]{3,2,1,0:T(8,128)(2,1)S(1)}, u32[]{:S(2)}, u32[]{:S(2)}) collective-permute-start(bf16[2,12,32,128]{3,2,1,0:T(8,128)(2,1)S(1)} %get-tuple-element.40), channel_id=1, source_target_pairs={{0,16},{4,20},{8,24},{12,28},{16,0},{20,4},{24,8},{28,12},{1,17},{... | collective-permute-start | bytes 589832 | tf_op jit(solution)/shard_map/ppermute | solution.py:310
  26.9 0.7 %copy-start.3 = (s32[4]{0:T(128)S(1)}, s32[4]{0:T(128)}, u32[]{:S(2)}) copy-start(s32[4]{0:T(128)} %refs_0_.5) | copy-start | bytes 52
  28.3 6.2 %collective-permute-start.7 = (bf16[2,20,16,128]{3,2,1,0:T(8,128)(2,1)S(1)}, bf16[2,20,16,128]{3,2,1,0:T(8,128)(2,1)S(1)}, u32[]{:S(2)}, u32[]{:S(2)}) collective-permute-start(bf16[2,20,16,128]{3,2,1,0:T(8,128)(2,1)S(1)} %get-tuple-element.46), channel_id=1, source_target_pairs={{0,2},{1,3},{2,0},{3,1},{4,6},{5,7},{6,4},{7,5},{8,10},{9,11},{10,... | collective-permute-start | bytes 491528 | tf_op jit(solution)/shard_map/ppermute | solution.py:327
  29.8 6.5 %collective-permute-start.8 = (bf16[2,20,16,128]{3,2,1,0:T(8,128)(2,1)S(1)}, bf16[2,20,16,128]{3,2,1,0:T(8,128)(2,1)S(1)}, u32[]{:S(2)}, u32[]{:S(2)}) collective-permute-start(bf16[2,20,16,128]{3,2,1,0:T(8,128)(2,1)S(1)} %get-tuple-element.47), channel_id=1, source_target_pairs={{0,3},{1,2},{2,1},{3,0},{4,7},{5,6},{6,5},{7,4},{8,11},{9,10},{10,... | collective-permute-start | bytes 491528 | tf_op jit(solution)/shard_map/ppermute | solution.py:327
  29.8 6.5 %collective-permute-start.9 = (bf16[2,20,16,128]{3,2,1,0:T(8,128)(2,1)S(1)}, bf16[2,20,16,128]{3,2,1,0:T(8,128)(2,1)S(1)}, u32[]{:S(2)}, u32[]{:S(2)}) collective-permute-start(bf16[2,20,16,128]{3,2,1,0:T(8,128)(2,1)S(1)} %get-tuple-element.48), channel_id=1, source_target_pairs={{0,1},{1,0},{2,3},{3,2},{4,5},{5,4},{6,7},{7,6},{8,9},{9,8},{10,11... | collective-permute-start | bytes 491528 | tf_op jit(solution)/shard_map/ppermute | solution.py:327
  38.2 5.7 %collective-permute-start.10 = (bf16[2,12,16,128]{3,2,1,0:T(8,128)(2,1)S(1)}, bf16[2,12,16,128]{3,2,1,0:T(8,128)(2,1)S(1)}, u32[]{:S(2)}, u32[]{:S(2)}) collective-permute-start(bf16[2,12,16,128]{3,2,1,0:T(8,128)(2,1)S(1)} %get-tuple-element.52), channel_id=1, source_target_pairs={{0,2},{1,3},{2,0},{3,1},{4,6},{5,7},{6,4},{7,5},{8,10},{9,11},{10,... | collective-permute-start | bytes 294920 | tf_op jit(solution)/shard_map/ppermute | solution.py:327
  38.9 6.6 %collective-permute-start.11 = (bf16[2,12,16,128]{3,2,1,0:T(8,128)(2,1)S(1)}, bf16[2,12,16,128]{3,2,1,0:T(8,128)(2,1)S(1)}, u32[]{:S(2)}, u32[]{:S(2)}) collective-permute-start(bf16[2,12,16,128]{3,2,1,0:T(8,128)(2,1)S(1)} %get-tuple-element.53), channel_id=1, source_target_pairs={{0,3},{1,2},{2,1},{3,0},{4,7},{5,6},{6,5},{7,4},{8,11},{9,10},{10,... | collective-permute-start | bytes 294920 | tf_op jit(solution)/shard_map/ppermute | solution.py:327
  40.3 5.2 %collective-permute-start.12 = (bf16[2,12,16,128]{3,2,1,0:T(8,128)(2,1)S(1)}, bf16[2,12,16,128]{3,2,1,0:T(8,128)(2,1)S(1)}, u32[]{:S(2)}, u32[]{:S(2)}) collective-permute-start(bf16[2,12,16,128]{3,2,1,0:T(8,128)(2,1)S(1)} %get-tuple-element.54), channel_id=1, source_target_pairs={{0,1},{1,0},{2,3},{3,2},{4,5},{5,4},{6,7},{7,6},{8,9},{9,8},{10,11... | collective-permute-start | bytes 294920 | tf_op jit(solution)/shard_map/ppermute | solution.py:327
  40.5 15.0 %collective-permute-start.15 = (bf16[20,32,128]{2,1,0:T(8,128)(2,1)S(1)}, bf16[20,32,128]{2,1,0:T(8,128)(2,1)S(1)}, u32[]{:S(2)}, u32[]{:S(2)}) collective-permute-start(bf16[20,32,128]{2,1,0:T(8,128)(2,1)S(1)} %get-tuple-element.61), channel_id=1, source_target_pairs={{0,16},{4,20},{8,24},{12,28},{16,0},{20,4},{24,8},{28,12},{1,17},{... | collective-permute-start | bytes 491528 | tf_op jit(solution)/shard_map/ppermute | solution.py:310
  40.8 17.5 %collective-permute-start.16 = (bf16[20,32,128]{2,1,0:T(8,128)(2,1)S(1)}, bf16[20,32,128]{2,1,0:T(8,128)(2,1)S(1)}, u32[]{:S(2)}, u32[]{:S(2)}) collective-permute-start(bf16[20,32,128]{2,1,0:T(8,128)(2,1)S(1)} %get-tuple-element.62), channel_id=1, source_target_pairs={{0,20},{4,16},{8,28},{12,24},{16,4},{20,0},{24,12},{28,8},{1,21},{... | collective-permute-start | bytes 491528 | tf_op jit(solution)/shard_map/ppermute | solution.py:310
  44.0 14.4 %collective-permute-start.17 = (bf16[20,32,128]{2,1,0:T(8,128)(2,1)S(1)}, bf16[20,32,128]{2,1,0:T(8,128)(2,1)S(1)}, u32[]{:S(2)}, u32[]{:S(2)}) collective-permute-start(bf16[20,32,128]{2,1,0:T(8,128)(2,1)S(1)} %get-tuple-element.63), channel_id=1, source_target_pairs={{0,4},{4,0},{8,12},{12,8},{16,20},{20,16},{24,28},{28,24},{1,5},{5... | collective-permute-start | bytes 491528 | tf_op jit(solution)/shard_map/ppermute | solution.py:310
  46.3 12.1 %collective-permute-start.13 = (bf16[12,32,128]{2,1,0:T(8,128)(2,1)S(1)}, bf16[12,32,128]{2,1,0:T(8,128)(2,1)S(1)}, u32[]{:S(2)}, u32[]{:S(2)}) collective-permute-start(bf16[12,32,128]{2,1,0:T(8,128)(2,1)S(1)} %get-tuple-element.57), channel_id=1, source_target_pairs={{0,4},{4,0},{8,12},{12,8},{16,20},{20,16},{24,28},{28,24},{1,5},{5... | collective-permute-start | bytes 294920 | tf_op jit(solution)/shard_map/ppermute | solution.py:310
  46.9 11.5 %collective-permute-start.14 = (bf16[12,32,128]{2,1,0:T(8,128)(2,1)S(1)}, bf16[12,32,128]{2,1,0:T(8,128)(2,1)S(1)}, u32[]{:S(2)}, u32[]{:S(2)}) collective-permute-start(bf16[12,32,128]{2,1,0:T(8,128)(2,1)S(1)} %get-tuple-element.58), channel_id=1, source_target_pairs={{0,4},{4,0},{8,12},{12,8},{16,20},{20,16},{24,28},{28,24},{1,5},{5... | collective-permute-start | bytes 294920 | tf_op jit(solution)/shard_map/ppermute | solution.py:310

commit v4 on v3

--- a/solution.py
+++ b/solution.py
@@ -160,8 +160,9 @@
                 blocks[i, j][at + k] = out[j * HALF : (j + 1) * HALF, i * 128 : (i + 1) * 128]
 
 
-STEP = 4
+STEP = 8
 EARLY = 12
+COST = 2 * 10**9
 
 
 def own_bits():
@@ -170,15 +171,18 @@
     return [hi >> k % hi_bits & 1 for k in range(4)]
 
 
-def first_kernel(x_ref, gates, *refs):
-    *outs, spread, turned, w1_ref = refs
-    early = outs[0].shape[0]
+def steps(size):
+    return [(k, min(STEP, size - k)) for k in range(0, size, STEP)]
+
+
+def first_kernel(x_ref, gates, o0, o1, o2, o3, rest, w1_ref, g_ref, spread, turned):
+    early = o0.shape[0]
     own = own_bits()
     late = product(gate_of(gates, 3, 0), gate_of(gates, 2, 0))
     soon = product(gate_of(gates, 1, 0), gate_of(gates, 0, 0))
     w0 = first_weights(wide_product(late, soon))
     w1_ref[...] = right_weights(gate_of(gates, 0, 1), True, 0, own[0])
-    g = left_weights(product(gate_of(gates, 1, 2), gate_of(gates, 0, 2)), 0, own[1])
+    g_ref[...] = left_weights(product(gate_of(gates, 1, 2), gate_of(gates, 0, 2)), 0, own[1])
 
     for k in range(G // 8):
         spread[k * 512 : (k + 1) * 512, :] = x_ref[k * 512 : (k + 1) * 512, :].astype(F32)
@@ -189,31 +193,36 @@
             for n in range(2):
                 turned[n, pl.ds(k * 8 + q, HALF, stride=G), :] = tiles[q][n]
 
-    for k in range(0, HALF, STEP):
-        rows = slice(k * G, (k + STEP) * G)
-        x = jnp.concatenate([turned[0, rows, :], turned[1, rows, :]], axis=1).astype(BF).reshape(STEP, G, 4 * G)
-        made = both_gates(x, w1_ref[...], g)
-        if k >= early:
-            store_blocks(made, k - early, outs[4:])
-        else:
-            store_blocks(made, k, outs[:4])
+    for k, n in steps(early):
+        rows = slice(k * G, (k + n) * G)
+        x = jnp.concatenate([turned[0, rows, :], turned[1, rows, :]], axis=1).astype(BF).reshape(n, G, 4 * G)
+        store_blocks(both_gates(x, w1_ref[...], g_ref[...]), k, (o0, o1, o2, o3))
+    for n in range(2):
+        rest[n] = turned[n, early * G :, :].astype(BF)
+
+
+def second_kernel(rest, w1_ref, g_ref, o0, o1, o2, o3):
+    for k, n in steps(o0.shape[0]):
+        rows = slice(k * G, (k + n) * G)
+        x = jnp.concatenate([rest[0, rows, :], rest[1, rows, :]], axis=1).reshape(n, G, 4 * G)
+        store_blocks(both_gates(x, w1_ref[...], g_ref[...]), k, (o0, o1, o2, o3))
 
 
 def lanes_kernel(b0, b1, b2, b3, w1_ref, moving, staying):
     blocks = by_place((b0, b1, b2, b3))
     w = w1_ref[:, : 4 * G]
     for j in range(2):
-        for k in range(0, b0.shape[0], STEP):
-            x = jnp.concatenate([blocks[i, j][k : k + STEP] for i in range(2)], axis=2).reshape(STEP * HALF, 4 * G)
+        for k, n in steps(b0.shape[0]):
+            x = jnp.concatenate([blocks[i, j][k : k + n] for i in range(2)], axis=2).reshape(n * HALF, 4 * G)
             y = dot(x, w).astype(BF)
-            staying[j, k : k + STEP] = y[:, :128].reshape(STEP, HALF, 128)
-            moving[j, k : k + STEP] = y[:, 128:].reshape(STEP, HALF, 128)
+            staying[j, k : k + n] = y[:, :128].reshape(n, HALF, 128)
+            moving[j, k : k + n] = y[:, 128:].reshape(n, HALF, 128)
 
 
 def rows_kernel(*refs):
     *ins, w1_ref, g_ref, m0, m1, s0, s1 = refs
-    for k in range(0, m0.shape[0], STEP):
-        made = both_gates(joined(ins, k), w1_ref[...], g_ref[...])
+    for k, n in steps(m0.shape[0]):
+        made = both_gates(joined(ins, k, n), w1_ref[...], g_ref[...])
         for at, out in enumerate(made):
             for i in range(2):
                 lanes = slice(i * 128, (i + 1) * 128)
@@ -231,16 +240,16 @@
     w_ref[...] = last_weights(gate_of(gates, 3, 1), own[2])
 
 
-def joined(ins, k):
+def joined(ins, k, n):
     order = [APART.index(o) for o in range(4)] if len(ins) > 1 else [0]
-    halves = [jnp.concatenate([ins[at][i, k : k + STEP] for at in order], axis=1) for i in range(2)]
+    halves = [jnp.concatenate([ins[at][i, k : k + n] for at in order], axis=1) for i in range(2)]
     return jnp.concatenate(halves, axis=2)
 
 
 def middle_kernel(*refs):
     *ins, w1_ref, g_ref, o0, o1, o2, o3 = refs
-    for k in range(0, o0.shape[0], STEP):
-        store_blocks(both_gates(joined(ins, k), w1_ref[...], g_ref[...]), k, (o0, o1, o2, o3))
+    for k, n in steps(o0.shape[0]):
+        store_blocks(both_gates(joined(ins, k, n), w1_ref[...], g_ref[...]), k, (o0, o1, o2, o3))
 
 
 def last_kernel(m0, m1, s0, s1, b0, b1, b2, b3, w_ref, o_ref, wide, spread):
@@ -289,7 +298,7 @@
 SMEM = pl.BlockSpec(memory_space=pltpu.SMEM)
 
 
-def call(kernel, outs, args, specs=None, scratch=(), after=()):
+def call(kernel, outs, args, specs=None, scratch=(), after=(), flops=1):
     specs = specs or [VMEM] * len(args)
 
     def body(*refs):
@@ -301,7 +310,7 @@
         in_specs=specs + [pl.BlockSpec(memory_space=pl.ANY)] * len(after),
         out_specs=jax.tree.map(lambda _: VMEM, outs),
         scratch_shapes=scratch,
-        cost_estimate=pl.CostEstimate(flops=1, bytes_accessed=1, transcendentals=0),
+        cost_estimate=pl.CostEstimate(flops=flops, bytes_accessed=1, transcendentals=0),
         compiler_params=pltpu.CompilerParams(vmem_limit_bytes=40 * 2**20),
     )(*args, *after)
 
@@ -352,14 +361,20 @@
     lanes, rows = (4 * G, 8 * G), (G, 2 * G)
 
     x = state.reshape(2, -1, 128).transpose(1, 0, 2).reshape(whole, 128)
-    scratch = [spread, turned, pltpu.VMEM(lanes, BF)]
-    made = call(first_kernel, [early_block] * 4 + [block] * 4, (x, gates), scratch=scratch)
-    early = exchange(made[:4], bits[0], bits[1])
-    late = exchange(made[4:], bits[0], bits[1])
+    rest = jax.ShapeDtypeStruct((2, (HALF - EARLY) * G, 128), BF)
+    *early, rest, w1, g = call(
+        first_kernel,
+        [early_block] * 4 + [rest, jax.ShapeDtypeStruct(lanes, BF), jax.ShapeDtypeStruct(rows, BF)],
+        (x, gates),
+        scratch=[spread, turned],
+    )
+    early = exchange(early, bits[0], bits[1])
+    late = call(second_kernel, [block] * 4, (rest, w1, g))
+    late = exchange(late, bits[0], bits[1])
     shapes = [jax.ShapeDtypeStruct(shape, BF) for shape in (lanes, lanes, rows, (4 * G, 4 * G))]
     w1, w_i, g, w = call(functools.partial(weights_kernel, top if groups == 4 else 0), shapes, (gates,))
 
-    moving, staying = call(lanes_kernel, [early_half] * 2, (*early, w1))
+    moving, staying = call(lanes_kernel, [early_half] * 2, (*early, w1), flops=COST)
     early = [swapped(moving, 1 << bits[2]), staying]
 
     late = regrouped(late, regroup, bits[1], groups, top, after=[staying])
@@ -368,7 +383,7 @@
     late = exchange(late, bits[2], bits[3])
 
     early = regrouped(early, regroup, bits[1], groups, top, after=sent)
-    m0, m1, *early = call(rows_kernel, [early_block] * 4, (*early, w_i, g))
+    m0, m1, *early = call(rows_kernel, [early_block] * 4, (*early, w_i, g), after=late[:1])
     early = [swapped(m0, 1 << bits[3]), swapped(m1, 1 << bits[3]), *early]
 
     args = (*early, *late, w)

time: 62.8 us -> 65.2 us (1.038)
  waiting for transfers between devices: 23.4 us -> 25.4 us
    ppermute x12, waiting for transfers between devices: 16.3 us -> 19 us  [swapped(): lax.ppermute(x, 'hi', [(d, d ^ apart) for d in range(lax.axis_size('hi'))])]
    ppermute x6, waiting for transfers between devices: 7.09 us -> 6.39 us  [regrouped(): lax.ppermute(x, 'lo', to)]
    pallas_call x8 -> x9, Pallas kernels: 13.1 us -> 13.4 us  [call(): pl.pallas_call(body, out_shape=outs, in_specs=specs + [pl.BlockSpec(memor...]
  transfers between devices with their start and end apart: 18 -> 18, of which waited for: 9 -> 10; matrix products, arithmetic and copies ran while one was open for 0% -> 0% of each run, Pallas kernels for 7% -> 8%
where the time goes in v4:
time: 65.2 us; the launch traced here: 65 us
  waiting for transfers between devices  25.4 us (39%)
  starting transfers between devices  23.3 us (36%)
  Pallas kernels  13.4 us (21%)
  local copies, waits for them, and re-layouts  2.88 us (4%)
    ppermute x12, waiting for transfers between devices, swapped(): lax.ppermute(x, 'hi', [(d, d ^ apart) for d in range(lax.axis_size('hi'))])  19 us
    ppermute x12, starting transfers between devices, swapped(): lax.ppermute(x, 'hi', [(d, d ^ apart) for d in range(lax.axis_size('hi'))])  18.9 us
    pallas_call x9, Pallas kernels, call(): pl.pallas_call(body, out_shape=outs, in_specs=specs + [pl.BlockSpec(memor...  13.4 us
    ppermute x6, waiting for transfers between devices, regrouped(): lax.ppermute(x, 'lo', to)  6.39 us
    ppermute x6, starting transfers between devices, regrouped(): lax.ppermute(x, 'lo', to)  4.41 us
    unnamed x8, local copies, waits for them, and re-layouts  2.88 us
  transfers between devices with their start and end apart: 18, of which 10 were waited for; matrix products, arithmetic and copies ran while one was open for 0% of the time, Pallas kernels for 8%

profile of v4, /device:TPU:0, one launch (start us, length us, event | category | flops | bytes accessed | tf_op | source)
XLA Modules:
  0.0 65.0 jit_solution(8729899747216721549)
XLA Ops:
  0.0 1.0 %copy-done = bf16[4,3,2,64,64]{4,3,2,1,0:T(8,128)(2,1)S(1)} copy-done((bf16[4,3,2,64,64]{4,3,2,1,0:T(8,128)(2,1)S(1)}, bf16[4,3,2,64,64]{4,3,2,1,0:T(8,128)(2,1)}, u32[]{:S(2)}) %copy-start) | copy-done | bytes 196632
  1.0 1.2 %copy-done.2 = bf16[2,262144]{1,0:T(2,128)(2,1)S(1)} copy-done((bf16[2,262144]{1,0:T(2,128)(2,1)S(1)}, bf16[2,262144]{1,0:T(2,128)(2,1)}, u32[]{:S(2)}) %copy-start.2) | copy-done | bytes 1048600
  2.2 3.9 %shard_map.37 = (bf16[12,32,128]{2,1,0:T(8,128)(2,1)S(1)}, bf16[12,32,128]{2,1,0:T(8,128)(2,1)S(1)}, bf16[12,32,128]{2,1,0:T(8,128)(2,1)S(1)}, bf16[12,32,128]{2...) custom-call(bf16[4096,128]{1,0:T(8,128)(2,1)S(1)} %bitcast.10, ...), custom_call_target="tpu_custom_call" | custom-call | flops 1 | bytes 1 | tf_op jit(solution)/shard_map/pallas_call | solution.py:307
  6.1 3.0 %collective-permute-start = (bf16[12,32,128]{2,1,0:T(8,128)(2,1)S(1)}, bf16[12,32,128]{2,1,0:T(8,128)(2,1)S(1)}, u32[]{:S(2)}, u32[]{:S(2)}) collective-permute-start(bf16[12,32,128]{2,1,0:T(8,128)(2,1)S(1)} %get-tuple-element.38), channel_id=1, source_target_pairs={{0,4},{4,0},{8,12},{12,8},{16,20},{20,16},{24,28},{28,24},{1,5},{5... | collective-permute-start | bytes 294920 | tf_op jit(solution)/shard_map/ppermute | solution.py:319
  9.2 1.5 %collective-permute-start.1 = (bf16[12,32,128]{2,1,0:T(8,128)(2,1)S(1)}, bf16[12,32,128]{2,1,0:T(8,128)(2,1)S(1)}, u32[]{:S(2)}, u32[]{:S(2)}) collective-permute-start(bf16[12,32,128]{2,1,0:T(8,128)(2,1)S(1)} %get-tuple-element.39), channel_id=1, source_target_pairs={{0,12},{4,8},{8,4},{12,0},{16,28},{20,24},{24,20},{28,16},{1,13},{... | collective-permute-start | bytes 294920 | tf_op jit(solution)/shard_map/ppermute | solution.py:319
  10.7 0.1 collective-permute-start.2
  10.7 0.9 %shard_map.40 = (bf16[20,32,128]{2,1,0:T(8,128)(2,1)S(1)}, bf16[20,32,128]{2,1,0:T(8,128)(2,1)S(1)}, bf16[20,32,128]{2,1,0:T(8,128)(2,1)S(1)}, bf16[20,32,128]{2,1,0:T(8,128)(2,1)S(1)}) custom-call(bf16[2,1280,128]{2,1,0:T(8,128)(2,1)S(1)} %get-tuple-element.45.refs_0_, bf16[256,512]{1,0:T(8,128)(2,1)S(1)} %get-tuple-element.46.refs_1_, ...), custom_call_target="tpu_custom_call" | custom-call | flops 1 | bytes 1 | tf_op jit(solution)/shard_map/pallas_call | solution.py:307
  11.7 2.0 %collective-permute-start.4 = (bf16[20,32,128]{2,1,0:T(8,128)(2,1)S(1)}, bf16[20,32,128]{2,1,0:T(8,128)(2,1)S(1)}, u32[]{:S(2)}, u32[]{:S(2)}) collective-permute-start(bf16[20,32,128]{2,1,0:T(8,128)(2,1)S(1)} %get-tuple-element.48), channel_id=1, source_target_pairs={{0,4},{4,0},{8,12},{12,8},{16,20},{20,16},{24,28},{28,24},{1,5},{5... | collective-permute-start | bytes 491528 | tf_op jit(solution)/shard_map/ppermute | solution.py:319
  13.7 1.5 %collective-permute-start.5 = (bf16[20,32,128]{2,1,0:T(8,128)(2,1)S(1)}, bf16[20,32,128]{2,1,0:T(8,128)(2,1)S(1)}, u32[]{:S(2)}, u32[]{:S(2)}) collective-permute-start(bf16[20,32,128]{2,1,0:T(8,128)(2,1)S(1)} %get-tuple-element.49), channel_id=1, source_target_pairs={{0,12},{4,8},{8,4},{12,0},{16,28},{20,24},{24,20},{28,16},{1,13},{... | collective-permute-start | bytes 491528 | tf_op jit(solution)/shard_map/ppermute | solution.py:319
  15.2 1.0 %shard_map.38 = (bf16[256,512]{1,0:T(8,128)(2,1)S(1)}, bf16[256,512]{1,0:T(8,128)(2,1)S(1)}, bf16[64,128]{1,0:T(8,128)(2,1)S(1)}, bf16[256,256]{1,0:T(8,128)(2,1)S(1)}) custom-call(bf16[4,3,2,64,64]{4,3,2,1,0:T(8,128)(2,1)S(1)} %copy-done.1), custom_call_target="tpu_custom_call" | custom-call | flops 1 | bytes 1 | tf_op jit(solution)/shard_map/pallas_call | solution.py:307
  16.2 0.0 collective-permute-done.refs_0_
  16.2 0.1 collective-permute-start.6
  16.4 0.0 collective-permute-done.1.refs_1_
  16.4 0.0 collective-permute-done.2.refs_2_
  16.4 0.3 shard_map.39
  16.7 3.0 %collective-permute-start.3 = (bf16[2,12,32,128]{3,2,1,0:T(8,128)(2,1)S(1)}, bf16[2,12,32,128]{3,2,1,0:T(8,128)(2,1)S(1)}, u32[]{:S(2)}, u32[]{:S(2)}) collective-permute-start(bf16[2,12,32,128]{3,2,1,0:T(8,128)(2,1)S(1)} %get-tuple-element.43), channel_id=1, source_target_pairs={{0,16},{4,20},{8,24},{12,28},{16,0},{20,4},{24,8},{28,12},{1,17},{... | collective-permute-start | bytes 589832 | tf_op jit(solution)/shard_map/ppermute | solution.py:319
  19.7 1.1 %collective-permute-done.4.refs_1_ = bf16[20,32,128]{2,1,0:T(8,128)(2,1)S(1)} collective-permute-done((bf16[20,32,128]{2,1,0:T(8,128)(2,1)S(1)}, bf16[20,32,128]{2,1,0:T(8,128)(2,1)S(1)}, u32[]{:S(2)}, u32[]{:S(2)}) %collective-permute-start.4) | collective-permute-done | bytes 163872 | tf_op jit(solution)/shard_map/ppermute | solution.py:319
  20.8 5.2 %collective-permute-done.5.refs_2_ = bf16[20,32,128]{2,1,0:T(8,128)(2,1)S(1)} collective-permute-done((bf16[20,32,128]{2,1,0:T(8,128)(2,1)S(1)}, bf16[20,32,128]{2,1,0:T(8,128)(2,1)S(1)}, u32[]{:S(2)}, u32[]{:S(2)}) %collective-permute-start.5) | collective-permute-done | bytes 163872 | tf_op jit(solution)/shard_map/ppermute | solution.py:319
  25.9 0.7 %collective-permute-done.6.refs_3_ = bf16[20,32,128]{2,1,0:T(8,128)(2,1)S(1)} collective-permute-done((bf16[20,32,128]{2,1,0:T(8,128)(2,1)S(1)}, bf16[20,32,128]{2,1,0:T(8,128)(2,1)S(1)}, u32[]{:S(2)}, u32[]{:S(2)}) %collective-permute-start.6) | collective-permute-done | bytes 163872 | tf_op jit(solution)/shard_map/ppermute | solution.py:319
  26.7 0.7 %copy-done.3 = s32[4]{0:T(128)S(1)} copy-done((s32[4]{0:T(128)S(1)}, s32[4]{0:T(128)}, u32[]{:S(2)}) %copy-start.3) | copy-done | bytes 40
  27.3 0.7 %shard_map.41 = (bf16[2,20,16,128]{3,2,1,0:T(8,128)(2,1)S(1)}, bf16[2,20,16,128]{3,2,1,0:T(8,128)(2,1)S(1)}, bf16[2,20,16,128]{3,2,1,0:T(8,128)(2,1)S(1)}, bf16[2,20,16,128]{3,2,1,0:T(8,128)(2,1)S(1)}) custom-call(s32[4]{0:T(128)S(1)} %copy-done.3, bf16[20,32,128]{2,1,0:T(8,128)(2,1)S(1)} %collective-permute-done.4.refs_1_, ...), custom_call_target="tpu_custom_call" | custom-call | flops 1 | bytes 1 | tf_op jit(solution)/shard_map/pallas_call | solution.py:307
  28.1 1.8 %collective-permute-start.7 = (bf16[2,20,16,128]{3,2,1,0:T(8,128)(2,1)S(1)}, bf16[2,20,16,128]{3,2,1,0:T(8,128)(2,1)S(1)}, u32[]{:S(2)}, u32[]{:S(2)}) collective-permute-start(bf16[2,20,16,128]{3,2,1,0:T(8,128)(2,1)S(1)} %get-tuple-element.52), channel_id=1, source_target_pairs={{0,2},{1,3},{2,0},{3,1},{4,6},{5,7},{6,4},{7,5},{8,10},{9,11},{10,... | collective-permute-start | bytes 491528 | tf_op jit(solution)/shard_map/ppermute | solution.py:336
  29.9 0.0 collective-permute-start.8
  29.9 0.4 collective-permute-start.9
  30.3 3.9 %collective-permute-done.7.refs_0_ = bf16[2,20,16,128]{3,2,1,0:T(8,128)(2,1)S(1)} collective-permute-done((bf16[2,20,16,128]{3,2,1,0:T(8,128)(2,1)S(1)}, bf16[2,20,16,128]{3,2,1,0:T(8,128)(2,1)S(1)}, u32[]{:S(2)}, u32[]{:S(2)}) %collective-permute-start.7) | collective-permute-done | bytes 163872 | tf_op jit(solution)/shard_map/ppermute | solution.py:336
  34.2 2.2 %collective-permute-done.8.refs_1_ = bf16[2,20,16,128]{3,2,1,0:T(8,128)(2,1)S(1)} collective-permute-done((bf16[2,20,16,128]{3,2,1,0:T(8,128)(2,1)S(1)}, bf16[2,20,16,128]{3,2,1,0:T(8,128)(2,1)S(1)}, u32[]{:S(2)}, u32[]{:S(2)}) %collective-permute-start.8) | collective-permute-done | bytes 163872 | tf_op jit(solution)/shard_map/ppermute | solution.py:336
  36.4 0.0 collective-permute-done.9.refs_2_
  36.4 0.9 %shard_map.42 = (bf16[20,32,128]{2,1,0:T(8,128)(2,1)S(1)}, bf16[20,32,128]{2,1,0:T(8,128)(2,1)S(1)}, bf16[20,32,128]{2,1,0:T(8,128)(2,1)S(1)}, bf16[20,32,128]{2,1,0:T(8,128)(2,1)S(1)}) custom-call(bf16[2,20,16,128]{3,2,1,0:T(8,128)(2,1)S(1)} %collective-permute-done.7.refs_0_, bf16[2,20,16,128]{3,2,1,0:T(8,128)(2,1)S(1)} %collective-permute-done.8.refs_1_, ...), custom_call_target="tpu_custom_call" | custom-call | flops 1 | bytes 1 | tf_op jit(solution)/shard_map/pallas_call | solution.py:307
  37.4 0.7 %collective-permute-start.13 = (bf16[20,32,128]{2,1,0:T(8,128)(2,1)S(1)}, bf16[20,32,128]{2,1,0:T(8,128)(2,1)S(1)}, u32[]{:S(2)}, u32[]{:S(2)}) collective-permute-start(bf16[20,32,128]{2,1,0:T(8,128)(2,1)S(1)} %get-tuple-element.63), channel_id=1, source_target_pairs={{0,16},{4,20},{8,24},{12,28},{16,0},{20,4},{24,8},{28,12},{1,17},{... | collective-permute-start | bytes 491528 | tf_op jit(solution)/shard_map/ppermute | solution.py:319
  38.1 0.0 collective-permute-done.3.refs_1_
  38.1 0.7 %shard_map.43 = (bf16[2,12,16,128]{3,2,1,0:T(8,128)(2,1)S(1)}, bf16[2,12,16,128]{3,2,1,0:T(8,128)(2,1)S(1)}, bf16[2,12,16,128]{3,2,1,0:T(8,128)(2,1)S(1)}, bf16[2,12,16,128]{3,2,1,0:T(8,128)(2,1)S(1)}) custom-call(s32[4]{0:T(128)S(1)} %copy-done.3, bf16[2,12,32,128]{3,2,1,0:T(8,128)(2,1)S(1)} %collective-permute-done.3.refs_1_, ...), custom_call_target="tpu_custom_call" | custom-call | flops 1 | bytes 1 | tf_op jit(solution)/shard_map/pallas_call | solution.py:307
  38.8 0.7 %collective-permute-start.10 = (bf16[2,12,16,128]{3,2,1,0:T(8,128)(2,1)S(1)}, bf16[2,12,16,128]{3,2,1,0:T(8,128)(2,1)S(1)}, u32[]{:S(2)}, u32[]{:S(2)}) collective-permute-start(bf16[2,12,16,128]{3,2,1,0:T(8,128)(2,1)S(1)} %get-tuple-element.58), channel_id=1, source_target_pairs={{0,2},{1,3},{2,0},{3,1},{4,6},{5,7},{6,4},{7,5},{8,10},{9,11},{10,... | collective-permute-start | bytes 294920 | tf_op jit(solution)/shard_map/ppermute | solution.py:336
  39.4 1.2 %collective-permute-start.11 = (bf16[2,12,16,128]{3,2,1,0:T(8,128)(2,1)S(1)}, bf16[2,12,16,128]{3,2,1,0:T(8,128)(2,1)S(1)}, u32[]{:S(2)}, u32[]{:S(2)}) collective-permute-start(bf16[2,12,16,128]{3,2,1,0:T(8,128)(2,1)S(1)} %get-tuple-element.59), channel_id=1, source_target_pairs={{0,3},{1,2},{2,1},{3,0},{4,7},{5,6},{6,5},{7,4},{8,11},{9,10},{10,... | collective-permute-start | bytes 294920 | tf_op jit(solution)/shard_map/ppermute | solution.py:336
  40.6 0.3 collective-permute-start.12
  41.0 3.2 %collective-permute-start.16 = (bf16[20,32,128]{2,1,0:T(8,128)(2,1)S(1)}, bf16[20,32,128]{2,1,0:T(8,128)(2,1)S(1)}, u32[]{:S(2)}, u32[]{:S(2)}) collective-permute-start(bf16[20,32,128]{2,1,0:T(8,128)(2,1)S(1)} %get-tuple-element.68), channel_id=1, source_target_pairs={{0,20},{4,16},{8,28},{12,24},{16,4},{20,0},{24,12},{28,8},{1,21},{... | collective-permute-start | bytes 491528 | tf_op jit(solution)/shard_map/ppermute | solution.py:319
  44.2 0.2 collective-permute-done.10.refs_0_
  44.4 1.5 %collective-permute-start.17 = (bf16[20,32,128]{2,1,0:T(8,128)(2,1)S(1)}, bf16[20,32,128]{2,1,0:T(8,128)(2,1)S(1)}, u32[]{:S(2)}, u32[]{:S(2)}) collective-permute-start(bf16[20,32,128]{2,1,0:T(8,128)(2,1)S(1)} %get-tuple-element.69), channel_id=1, source_target_pairs={{0,4},{4,0},{8,12},{12,8},{16,20},{20,16},{24,28},{28,24},{1,5},{5... | collective-permute-start | bytes 491528 | tf_op jit(solution)/shard_map/ppermute | solution.py:319
  46.0 0.0 collective-permute-done.11.refs_1_
  46.0 0.0 collective-permute-done.12.refs_2_
  46.0 6.2 %collective-permute-done.13.refs_6_.refs_4_ = bf16[20,32,128]{2,1,0:T(8,128)(2,1)S(1)} collective-permute-done((bf16[20,32,128]{2,1,0:T(8,128)(2,1)S(1)}, bf16[20,32,128]{2,1,0:T(8,128)(2,1)S(1)}, u32[]{:S(2)}, u32[]{:S(2)}) %collective-permute-start.13) | collective-permute-done | bytes 163872 | tf_op jit(solution)/shard_map/ppermute | solution.py:319
  52.1 0.7 %shard_map.44 = (bf16[12,32,128]{2,1,0:T(8,128)(2,1)S(1)}, bf16[12,32,128]{2,1,0:T(8,128)(2,1)S(1)}, bf16[12,32,128]{2,1,0:T(8,128)(2,1)S(1)}, bf16[12,32,128]{2,1,0:T(8,128)(2,1)S(1)}) custom-call(bf16[2,12,16,128]{3,2,1,0:T(8,128)(2,1)S(1)} %collective-permute-done.10.refs_0_, bf16[2,12,16,128]{3,2,1,0:T(8,128)(2,1)S(1)} %collective-permute-done.11.refs_1_, ...), custom_call_target="tpu_custom_call" | custom-call | flops 1 | bytes 1 | tf_op jit(solution)/shard_map/pallas_call | solution.py:307
  52.8 1.5 %collective-permute-start.14 = (bf16[12,32,128]{2,1,0:T(8,128)(2,1)S(1)}, bf16[12,32,128]{2,1,0:T(8,128)(2,1)S(1)}, u32[]{:S(2)}, u32[]{:S(2)}) collective-permute-start(bf16[12,32,128]{2,1,0:T(8,128)(2,1)S(1)} %get-tuple-element.64), channel_id=1, source_target_pairs={{0,4},{4,0},{8,12},{12,8},{16,20},{20,16},{24,28},{28,24},{1,5},{5... | collective-permute-start | bytes 294920 | tf_op jit(solution)/shard_map/ppermute | solution.py:319
  54.3 0.6 collective-permute-start.15
  54.9 1.7 %collective-permute-done.16.refs_5_ = bf16[20,32,128]{2,1,0:T(8,128)(2,1)S(1)} collective-permute-done((bf16[20,32,128]{2,1,0:T(8,128)(2,1)S(1)}, bf16[20,32,128]{2,1,0:T(8,128)(2,1)S(1)}, u32[]{:S(2)}, u32[]{:S(2)}) %collective-permute-start.16) | collective-permute-done | bytes 163872 | tf_op jit(solution)/shard_map/ppermute | solution.py:319
  56.6 0.0 collective-permute-done.17.refs_6_
  56.6 2.1 %collective-permute-done.14.refs_0_ = bf16[12,32,128]{2,1,0:T(8,128)(2,1)S(1)} collective-permute-done((bf16[12,32,128]{2,1,0:T(8,128)(2,1)S(1)}, bf16[12,32,128]{2,1,0:T(8,128)(2,1)S(1)}, u32[]{:S(2)}, u32[]{:S(2)}) %collective-permute-start.14) | collective-permute-done | bytes 98336 | tf_op jit(solution)/shard_map/ppermute | solution.py:319
  58.7 2.0 %collective-permute-done.15.refs_1_ = bf16[12,32,128]{2,1,0:T(8,128)(2,1)S(1)} collective-permute-done((bf16[12,32,128]{2,1,0:T(8,128)(2,1)S(1)}, bf16[12,32,128]{2,1,0:T(8,128)(2,1)S(1)}, u32[]{:S(2)}, u32[]{:S(2)}) %collective-permute-start.15) | collective-permute-done | bytes 98336 | tf_op jit(solution)/shard_map/ppermute | solution.py:319
  60.8 4.3 %shard_map.45 = bf16[4096,128]{1,0:T(8,128)(2,1)} custom-call(bf16[12,32,128]{2,1,0:T(8,128)(2,1)S(1)} %collective-permute-done.14.refs_0_, bf16[12,32,128]{2,1,0:T(8,128)(2,1)S(1)} %collective-permute-done.15.refs_1_, bf16[12,32,128]{2,1,0:T(8,128)(2,1)S(1)} %get-tuple-element.66.refs_2_, bf16[12,32,128]{2,1,0:T(8,128)(2,1)S(1)} %get-tuple-element.67.refs_3_, ...), custom_call_target="tpu_custom_call" | custom-call | flops 1 | bytes 1 | tf_op jit(solution)/shard_map/pallas_call | solution.py:307
  (5 shorter events, 0.0 us)
Async XLA Ops:
  0.0 1.0 %copy-start = (bf16[4,3,2,64,64]{4,3,2,1,0:T(8,128)(2,1)S(1)}, bf16[4,3,2,64,64]{4,3,2,1,0:T(8,128)(2,1)}, u32[]{:S(2)}) copy-start(bf16[4,3,2,64,64]{4,3,2,1,0:T(8,128)(2,1)} %refs_0_.3) | copy-start | bytes 589828
  1.0 1.2 %copy-start.2 = (bf16[2,262144]{1,0:T(2,128)(2,1)S(1)}, bf16[2,262144]{1,0:T(2,128)(2,1)}, u32[]{:S(2)}) copy-start(bf16[2,262144]{1,0:T(2,128)(2,1)} %param.3) | copy-start | bytes 3145732
  6.1 10.1 %collective-permute-start = (bf16[12,32,128]{2,1,0:T(8,128)(2,1)S(1)}, bf16[12,32,128]{2,1,0:T(8,128)(2,1)S(1)}, u32[]{:S(2)}, u32[]{:S(2)}) collective-permute-start(bf16[12,32,128]{2,1,0:T(8,128)(2,1)S(1)} %get-tuple-element.38), channel_id=1, source_target_pairs={{0,4},{4,0},{8,12},{12,8},{16,20},{20,16},{24,28},{28,24},{1,5},{5... | collective-permute-start | bytes 294920 | tf_op jit(solution)/shard_map/ppermute | solution.py:319
  9.2 7.2 %collective-permute-start.1 = (bf16[12,32,128]{2,1,0:T(8,128)(2,1)S(1)}, bf16[12,32,128]{2,1,0:T(8,128)(2,1)S(1)}, u32[]{:S(2)}, u32[]{:S(2)}) collective-permute-start(bf16[12,32,128]{2,1,0:T(8,128)(2,1)S(1)} %get-tuple-element.39), channel_id=1, source_target_pairs={{0,12},{4,8},{8,4},{12,0},{16,28},{20,24},{24,20},{28,16},{1,13},{... | collective-permute-start | bytes 294920 | tf_op jit(solution)/shard_map/ppermute | solution.py:319
  10.7 5.7 %collective-permute-start.2 = (bf16[12,32,128]{2,1,0:T(8,128)(2,1)S(1)}, bf16[12,32,128]{2,1,0:T(8,128)(2,1)S(1)}, u32[]{:S(2)}, u32[]{:S(2)}) collective-permute-start(bf16[12,32,128]{2,1,0:T(8,128)(2,1)S(1)} %get-tuple-element.40), channel_id=1, source_target_pairs={{0,8},{4,12},{8,0},{12,4},{16,24},{20,28},{24,16},{28,20},{1,9},{5... | collective-permute-start | bytes 294920 | tf_op jit(solution)/shard_map/ppermute | solution.py:319
  10.7 4.4 %copy-start.1 = (bf16[4,3,2,64,64]{4,3,2,1,0:T(8,128)(2,1)S(1)}, bf16[4,3,2,64,64]{4,3,2,1,0:T(8,128)(2,1)}, u32[]{:S(2)}) copy-start(bf16[4,3,2,64,64]{4,3,2,1,0:T(8,128)(2,1)} %refs_0_.3) | copy-start | bytes 589828
  11.7 9.1 %collective-permute-start.4 = (bf16[20,32,128]{2,1,0:T(8,128)(2,1)S(1)}, bf16[20,32,128]{2,1,0:T(8,128)(2,1)S(1)}, u32[]{:S(2)}, u32[]{:S(2)}) collective-permute-start(bf16[20,32,128]{2,1,0:T(8,128)(2,1)S(1)} %get-tuple-element.48), channel_id=1, source_target_pairs={{0,4},{4,0},{8,12},{12,8},{16,20},{20,16},{24,28},{28,24},{1,5},{5... | collective-permute-start | bytes 491528 | tf_op jit(solution)/shard_map/ppermute | solution.py:319
  13.7 12.2 %collective-permute-start.5 = (bf16[20,32,128]{2,1,0:T(8,128)(2,1)S(1)}, bf16[20,32,128]{2,1,0:T(8,128)(2,1)S(1)}, u32[]{:S(2)}, u32[]{:S(2)}) collective-permute-start(bf16[20,32,128]{2,1,0:T(8,128)(2,1)S(1)} %get-tuple-element.49), channel_id=1, source_target_pairs={{0,12},{4,8},{8,4},{12,0},{16,28},{20,24},{24,20},{28,16},{1,13},{... | collective-permute-start | bytes 491528 | tf_op jit(solution)/shard_map/ppermute | solution.py:319
  16.2 10.4 %collective-permute-start.6 = (bf16[20,32,128]{2,1,0:T(8,128)(2,1)S(1)}, bf16[20,32,128]{2,1,0:T(8,128)(2,1)S(1)}, u32[]{:S(2)}, u32[]{:S(2)}) collective-permute-start(bf16[20,32,128]{2,1,0:T(8,128)(2,1)S(1)} %get-tuple-element.50), channel_id=1, source_target_pairs={{0,8},{4,12},{8,0},{12,4},{16,24},{20,28},{24,16},{28,20},{1,9},{5... | collective-permute-start | bytes 491528 | tf_op jit(solution)/shard_map/ppermute | solution.py:319
  16.7 21.4 %collective-permute-start.3 = (bf16[2,12,32,128]{3,2,1,0:T(8,128)(2,1)S(1)}, bf16[2,12,32,128]{3,2,1,0:T(8,128)(2,1)S(1)}, u32[]{:S(2)}, u32[]{:S(2)}) collective-permute-start(bf16[2,12,32,128]{3,2,1,0:T(8,128)(2,1)S(1)} %get-tuple-element.43), channel_id=1, source_target_pairs={{0,16},{4,20},{8,24},{12,28},{16,0},{20,4},{24,8},{28,12},{1,17},{... | collective-permute-start | bytes 589832 | tf_op jit(solution)/shard_map/ppermute | solution.py:319
  26.7 0.7 %copy-start.3 = (s32[4]{0:T(128)S(1)}, s32[4]{0:T(128)}, u32[]{:S(2)}) copy-start(s32[4]{0:T(128)} %refs_0_.5) | copy-start | bytes 52
  28.1 6.1 %collective-permute-start.7 = (bf16[2,20,16,128]{3,2,1,0:T(8,128)(2,1)S(1)}, bf16[2,20,16,128]{3,2,1,0:T(8,128)(2,1)S(1)}, u32[]{:S(2)}, u32[]{:S(2)}) collective-permute-start(bf16[2,20,16,128]{3,2,1,0:T(8,128)(2,1)S(1)} %get-tuple-element.52), channel_id=1, source_target_pairs={{0,2},{1,3},{2,0},{3,1},{4,6},{5,7},{6,4},{7,5},{8,10},{9,11},{10,... | collective-permute-start | bytes 491528 | tf_op jit(solution)/shard_map/ppermute | solution.py:336
  29.9 6.5 %collective-permute-start.8 = (bf16[2,20,16,128]{3,2,1,0:T(8,128)(2,1)S(1)}, bf16[2,20,16,128]{3,2,1,0:T(8,128)(2,1)S(1)}, u32[]{:S(2)}, u32[]{:S(2)}) collective-permute-start(bf16[2,20,16,128]{3,2,1,0:T(8,128)(2,1)S(1)} %get-tuple-element.53), channel_id=1, source_target_pairs={{0,3},{1,2},{2,1},{3,0},{4,7},{5,6},{6,5},{7,4},{8,11},{9,10},{10,... | collective-permute-start | bytes 491528 | tf_op jit(solution)/shard_map/ppermute | solution.py:336
  29.9 6.5 %collective-permute-start.9 = (bf16[2,20,16,128]{3,2,1,0:T(8,128)(2,1)S(1)}, bf16[2,20,16,128]{3,2,1,0:T(8,128)(2,1)S(1)}, u32[]{:S(2)}, u32[]{:S(2)}) collective-permute-start(bf16[2,20,16,128]{3,2,1,0:T(8,128)(2,1)S(1)} %get-tuple-element.54), channel_id=1, source_target_pairs={{0,1},{1,0},{2,3},{3,2},{4,5},{5,4},{6,7},{7,6},{8,9},{9,8},{10,11... | collective-permute-start | bytes 491528 | tf_op jit(solution)/shard_map/ppermute | solution.py:336
  37.4 14.8 %collective-permute-start.13 = (bf16[20,32,128]{2,1,0:T(8,128)(2,1)S(1)}, bf16[20,32,128]{2,1,0:T(8,128)(2,1)S(1)}, u32[]{:S(2)}, u32[]{:S(2)}) collective-permute-start(bf16[20,32,128]{2,1,0:T(8,128)(2,1)S(1)} %get-tuple-element.63), channel_id=1, source_target_pairs={{0,16},{4,20},{8,24},{12,28},{16,0},{20,4},{24,8},{28,12},{1,17},{... | collective-permute-start | bytes 491528 | tf_op jit(solution)/shard_map/ppermute | solution.py:319
  38.8 5.7 %collective-permute-start.10 = (bf16[2,12,16,128]{3,2,1,0:T(8,128)(2,1)S(1)}, bf16[2,12,16,128]{3,2,1,0:T(8,128)(2,1)S(1)}, u32[]{:S(2)}, u32[]{:S(2)}) collective-permute-start(bf16[2,12,16,128]{3,2,1,0:T(8,128)(2,1)S(1)} %get-tuple-element.58), channel_id=1, source_target_pairs={{0,2},{1,3},{2,0},{3,1},{4,6},{5,7},{6,4},{7,5},{8,10},{9,11},{10,... | collective-permute-start | bytes 294920 | tf_op jit(solution)/shard_map/ppermute | solution.py:336
  39.4 6.5 %collective-permute-start.11 = (bf16[2,12,16,128]{3,2,1,0:T(8,128)(2,1)S(1)}, bf16[2,12,16,128]{3,2,1,0:T(8,128)(2,1)S(1)}, u32[]{:S(2)}, u32[]{:S(2)}) collective-permute-start(bf16[2,12,16,128]{3,2,1,0:T(8,128)(2,1)S(1)} %get-tuple-element.59), channel_id=1, source_target_pairs={{0,3},{1,2},{2,1},{3,0},{4,7},{5,6},{6,5},{7,4},{8,11},{9,10},{10,... | collective-permute-start | bytes 294920 | tf_op jit(solution)/shard_map/ppermute | solution.py:336
  40.6 5.3 %collective-permute-start.12 = (bf16[2,12,16,128]{3,2,1,0:T(8,128)(2,1)S(1)}, bf16[2,12,16,128]{3,2,1,0:T(8,128)(2,1)S(1)}, u32[]{:S(2)}, u32[]{:S(2)}) collective-permute-start(bf16[2,12,16,128]{3,2,1,0:T(8,128)(2,1)S(1)} %get-tuple-element.60), channel_id=1, source_target_pairs={{0,1},{1,0},{2,3},{3,2},{4,5},{5,4},{6,7},{7,6},{8,9},{9,8},{10,11... | collective-permute-start | bytes 294920 | tf_op jit(solution)/shard_map/ppermute | solution.py:336
  41.0 15.7 %collective-permute-start.16 = (bf16[20,32,128]{2,1,0:T(8,128)(2,1)S(1)}, bf16[20,32,128]{2,1,0:T(8,128)(2,1)S(1)}, u32[]{:S(2)}, u32[]{:S(2)}) collective-permute-start(bf16[20,32,128]{2,1,0:T(8,128)(2,1)S(1)} %get-tuple-element.68), channel_id=1, source_target_pairs={{0,20},{4,16},{8,28},{12,24},{16,4},{20,0},{24,12},{28,8},{1,21},{... | collective-permute-start | bytes 491528 | tf_op jit(solution)/shard_map/ppermute | solution.py:319
  44.4 12.2 %collective-permute-start.17 = (bf16[20,32,128]{2,1,0:T(8,128)(2,1)S(1)}, bf16[20,32,128]{2,1,0:T(8,128)(2,1)S(1)}, u32[]{:S(2)}, u32[]{:S(2)}) collective-permute-start(bf16[20,32,128]{2,1,0:T(8,128)(2,1)S(1)} %get-tuple-element.69), channel_id=1, source_target_pairs={{0,4},{4,0},{8,12},{12,8},{16,20},{20,16},{24,28},{28,24},{1,5},{5... | collective-permute-start | bytes 491528 | tf_op jit(solution)/shard_map/ppermute | solution.py:319
  52.8 5.9 %collective-permute-start.14 = (bf16[12,32,128]{2,1,0:T(8,128)(2,1)S(1)}, bf16[12,32,128]{2,1,0:T(8,128)(2,1)S(1)}, u32[]{:S(2)}, u32[]{:S(2)}) collective-permute-start(bf16[12,32,128]{2,1,0:T(8,128)(2,1)S(1)} %get-tuple-element.64), channel_id=1, source_target_pairs={{0,4},{4,0},{8,12},{12,8},{16,20},{20,16},{24,28},{28,24},{1,5},{5... | collective-permute-start | bytes 294920 | tf_op jit(solution)/shard_map/ppermute | solution.py:319
  54.3 6.4 %collective-permute-start.15 = (bf16[12,32,128]{2,1,0:T(8,128)(2,1)S(1)}, bf16[12,32,128]{2,1,0:T(8,128)(2,1)S(1)}, u32[]{:S(2)}, u32[]{:S(2)}) collective-permute-start(bf16[12,32,128]{2,1,0:T(8,128)(2,1)S(1)} %get-tuple-element.65), channel_id=1, source_target_pairs={{0,4},{4,0},{8,12},{12,8},{16,20},{20,16},{24,28},{28,24},{1,5},{5... | collective-permute-start | bytes 294920 | tf_op jit(solution)/shard_map/ppermute | solution.py:319

commit v5 on v4

--- a/solution.py
+++ b/solution.py
@@ -208,33 +208,9 @@
         store_blocks(both_gates(x, w1_ref[...], g_ref[...]), k, (o0, o1, o2, o3))
 
 
-def lanes_kernel(b0, b1, b2, b3, w1_ref, moving, staying):
-    blocks = by_place((b0, b1, b2, b3))
-    w = w1_ref[:, : 4 * G]
-    for j in range(2):
-        for k, n in steps(b0.shape[0]):
-            x = jnp.concatenate([blocks[i, j][k : k + n] for i in range(2)], axis=2).reshape(n * HALF, 4 * G)
-            y = dot(x, w).astype(BF)
-            staying[j, k : k + n] = y[:, :128].reshape(n, HALF, 128)
-            moving[j, k : k + n] = y[:, 128:].reshape(n, HALF, 128)
-
-
-def rows_kernel(*refs):
-    *ins, w1_ref, g_ref, m0, m1, s0, s1 = refs
-    for k, n in steps(m0.shape[0]):
-        made = both_gates(joined(ins, k, n), w1_ref[...], g_ref[...])
-        for at, out in enumerate(made):
-            for i in range(2):
-                lanes = slice(i * 128, (i + 1) * 128)
-                (s0, s1)[i][k + at] = out[:HALF, lanes]
-                (m0, m1)[i][k + at] = out[HALF:, lanes]
-
-
-def weights_kernel(top, gates, w1_ref, i_ref, g_ref, w_ref):
+def weights_kernel(top, gates, w1_ref, g_ref, w_ref):
     own = own_bits()
     w1_ref[...] = right_weights(product(gate_of(gates, 2, 1), gate_of(gates, 1, 1)), False, own[0], own[2])
-    k, a = iotas(G, 2 * G)
-    i_ref[...] = right_weights(ones(k == a), False, 0, 0)
     step = top * lax.axis_index("lo") if top else 0
     g_ref[...] = left_weights(product(gate_of(gates, 3, 2), gate_of(gates, 2, 2)), step, own[3])
     w_ref[...] = last_weights(gate_of(gates, 3, 1), own[2])
@@ -252,22 +228,25 @@
         store_blocks(both_gates(joined(ins, k, n), w1_ref[...], g_ref[...]), k, (o0, o1, o2, o3))
 
 
-def last_kernel(m0, m1, s0, s1, b0, b1, b2, b3, w_ref, o_ref, wide, spread):
+def gather_rows(first, ins, wide):
     bit = own_bits()[3]
-    blocks = by_place((b0, b1, b2, b3))
-    early = m0.shape[0]
-    firsts = ((s0, m0), (s1, m1))
-    for k in range(HALF):
+    blocks = by_place(ins)
+    for k in range(ins[0].shape[0]):
         for j in range(2):
-            rows = pl.ds(pl.multiple_of(k * G + (bit ^ j) * HALF, HALF), HALF)
+            rows = pl.ds((bit ^ j) * (HALF * HALF) + first + k, HALF, stride=HALF)
             for i in range(2):
-                block = blocks[i, j][k - early] if k >= early else firsts[i][j][k]
-                wide[i, rows, :] = block.astype(F32)
+                wide[i, rows, :] = blocks[i, j][k].astype(F32)
+
+
+def gather_kernel(b0, b1, b2, b3, wide):
+    gather_rows(0, (b0, b1, b2, b3), wide)
+
+
+def last_kernel(_, b0, b1, b2, b3, w_ref, o_ref, wide, spread):
+    gather_rows(HALF - b0.shape[0], (b0, b1, b2, b3), wide)
     for k in range(G // 8):
-        halves = [
-            jnp.concatenate([wide[i, pl.ds(k * 8 + q, HALF, stride=G), :] for q in range(8)], axis=0) for i in range(2)
-        ]
-        x = jnp.concatenate(halves, axis=1).astype(BF)
+        rows = slice(k * 256, (k + 1) * 256)
+        x = jnp.concatenate([wide[i, rows, :] for i in range(2)], axis=1).astype(BF)
         r = turned_dot(w_ref[...], x)
         tiles = turn([r[g * HALF : (g + 1) * HALF] for g in range(8)])
         for q in range(8):
@@ -278,11 +257,7 @@
 
 def pick_kernel(groups, regroup, *refs):
     ins, outs = refs[:-groups], refs[-groups:]
-    if len(ins) == 4:
-        blocks = by_place(ins)
-    else:
-        moved, stayed = ins
-        blocks = {(i, j): (stayed, moved)[i].at[j] for i, j in PLACES}
+    blocks = by_place(ins)
     own = own_bits()[1]
     lo = lax.axis_index("lo")
     rows = outs[0].shape[2]
@@ -298,7 +273,7 @@
 SMEM = pl.BlockSpec(memory_space=pltpu.SMEM)
 
 
-def call(kernel, outs, args, specs=None, scratch=(), after=(), flops=1):
+def call(kernel, outs, args, specs=None, scratch=(), after=(), flops=1, aliases={}):
     specs = specs or [VMEM] * len(args)
 
     def body(*refs):
@@ -310,6 +285,7 @@
         in_specs=specs + [pl.BlockSpec(memory_space=pl.ANY)] * len(after),
         out_specs=jax.tree.map(lambda _: VMEM, outs),
         scratch_shapes=scratch,
+        input_output_aliases=aliases,
         cost_estimate=pl.CostEstimate(flops=flops, bytes_accessed=1, transcendentals=0),
         compiler_params=pltpu.CompilerParams(vmem_limit_bytes=40 * 2**20),
     )(*args, *after)
@@ -327,19 +303,16 @@
     return out
 
 
-def regrouped(blocks, regroup, bit, groups, top, after=()):
+def regrouped(blocks, regroup, bit, groups, top, flops=1, after=()):
     count = blocks[0].shape[-3]
     if groups == 4:
         part = jax.ShapeDtypeStruct((2, count, top, 128), BF)
-        parts = call(functools.partial(pick_kernel, groups), [part] * groups, (regroup, *blocks), [SMEM] + [VMEM] * len(blocks), after=after)
+        parts = call(functools.partial(pick_kernel, groups), [part] * groups, (regroup, *blocks), [SMEM] + [VMEM] * 4, after=after, flops=flops)
         pairs = [[(d, d ^ o) for d in range(groups)] for o in APART]
         return [lax.ppermute(x, "lo", to) if o else x for o, x, to in zip(APART, parts, pairs)]
     own = lax.axis_index("hi") >> bit & 1
-    if len(blocks) == 4:
-        blocks = by_place(blocks)
-        halves = [jnp.stack([blocks[i, 0], blocks[i, 1]], axis=1) for i in range(2)]
-    else:
-        halves = [jnp.moveaxis(x, 0, 1) for x in blocks[::-1]]
+    blocks = by_place(blocks)
+    halves = [jnp.stack([blocks[i, 0], blocks[i, 1]], axis=1) for i in range(2)]
     both = jnp.stack([jnp.where(own == 0, half, jnp.flip(half, 1)) for half in halves])
     both = jnp.take(both.reshape(2, count, groups, top, 128), regroup, axis=2)
     both = lax.all_to_all(both, "lo", split_axis=2, concat_axis=2, tiled=True)
@@ -355,7 +328,6 @@
 
     block = jax.ShapeDtypeStruct((HALF - EARLY, HALF, 128), BF)
     early_block = jax.ShapeDtypeStruct((EARLY, HALF, 128), BF)
-    early_half = jax.ShapeDtypeStruct((2, EARLY, HALF, 128), BF)
     turned = pltpu.VMEM((2, HALF * G, 128), F32)
     spread = pltpu.VMEM((whole, 128), F32)
     lanes, rows = (4 * G, 8 * G), (G, 2 * G)
@@ -371,23 +343,20 @@
     early = exchange(early, bits[0], bits[1])
     late = call(second_kernel, [block] * 4, (rest, w1, g))
     late = exchange(late, bits[0], bits[1])
-    shapes = [jax.ShapeDtypeStruct(shape, BF) for shape in (lanes, lanes, rows, (4 * G, 4 * G))]
-    w1, w_i, g, w = call(functools.partial(weights_kernel, top if groups == 4 else 0), shapes, (gates,))
-
-    moving, staying = call(lanes_kernel, [early_half] * 2, (*early, w1), flops=COST)
-    early = [swapped(moving, 1 << bits[2]), staying]
-
-    late = regrouped(late, regroup, bits[1], groups, top, after=[staying])
-    late = call(middle_kernel, [block] * 4, (*late, w1, g))
-    sent = late[3:]
+    shapes = [jax.ShapeDtypeStruct(shape, BF) for shape in (lanes, rows, (4 * G, 4 * G))]
+    w1, g, w = call(functools.partial(weights_kernel, top if groups == 4 else 0), shapes, (gates,))
+
+    early = regrouped(early, regroup, bits[1], groups, top, COST)
+    late = regrouped(late, regroup, bits[1], groups, top, after=early[3:])
+    early = call(middle_kernel, [early_block] * 4, (*early, w1, g), flops=COST)
+    late = call(middle_kernel, [block] * 4, (*late, w1, g), after=early[3:])
+    early = exchange(early, bits[2], bits[3])
     late = exchange(late, bits[2], bits[3])
 
-    early = regrouped(early, regroup, bits[1], groups, top, after=sent)
-    m0, m1, *early = call(rows_kernel, [early_block] * 4, (*early, w_i, g), after=late[:1])
-    early = [swapped(m0, 1 << bits[3]), swapped(m1, 1 << bits[3]), *early]
-
-    args = (*early, *late, w)
-    out = call(last_kernel, jax.ShapeDtypeStruct((whole, 128), BF), args, scratch=[turned, spread])
+    wide = jax.ShapeDtypeStruct((2, HALF * G, 128), F32)
+    early = call(gather_kernel, wide, early, flops=COST)
+    shapes = [jax.ShapeDtypeStruct((whole, 128), BF), wide]
+    out, _ = call(last_kernel, shapes, (early, *late, w), scratch=[spread], aliases={0: 1})
     return out.reshape(-1, 2, 128).transpose(1, 0, 2).reshape(state.shape)
 
 

time: 65.2 us -> 58.4 us (0.90)
  waiting for transfers between devices: 25.4 us -> 18.9 us
  Pallas kernels: 13.4 us -> 14.4 us
  starting transfers between devices: 23.3 us -> 22.6 us
    ppermute x6, waiting for transfers between devices: 6.39 us -> 1.08 us  [regrouped(): lax.ppermute(x, 'lo', to)]
    ppermute x12, waiting for transfers between devices: 19 us -> 17.8 us  [swapped(): lax.ppermute(x, 'hi', [(d, d ^ apart) for d in range(lax.axis_size('hi'))])]
    pallas_call x9, Pallas kernels: 13.4 us -> 14.4 us  [call(): pl.pallas_call(body, out_shape=outs, in_specs=specs + [pl.BlockSpec(memor...]
  transfers between devices with their start and end apart: 18 -> 18, of which waited for: 10 -> 8; matrix products, arithmetic and copies ran while one was open for 0% -> 0% of each run, Pallas kernels for 8% -> 10%
where the time goes in v5:
time: 58.4 us; the launch traced here: 58.3 us
  starting transfers between devices  22.6 us (39%)
  waiting for transfers between devices  18.9 us (32%)
  Pallas kernels  14.4 us (25%)
  local copies, waits for them, and re-layouts  2.24 us (4%)
    ppermute x12, starting transfers between devices, swapped(): lax.ppermute(x, 'hi', [(d, d ^ apart) for d in range(lax.axis_size('hi'))])  18.6 us
    ppermute x12, waiting for transfers between devices, swapped(): lax.ppermute(x, 'hi', [(d, d ^ apart) for d in range(lax.axis_size('hi'))])  17.8 us
    pallas_call x9, Pallas kernels, call(): pl.pallas_call(body, out_shape=outs, in_specs=specs + [pl.BlockSpec(memor...  14.4 us
    ppermute x6, starting transfers between devices, regrouped(): lax.ppermute(x, 'lo', to)  4.05 us
    unnamed x8, local copies, waits for them, and re-layouts  2.24 us
  transfers between devices with their start and end apart: 18, of which 8 were waited for; matrix products, arithmetic and copies ran while one was open for 0% of the time, Pallas kernels for 10%

profile of v5, /device:TPU:0, one launch (start us, length us, event | category | flops | bytes accessed | tf_op | source)
XLA Modules:
  0.0 58.3 jit_solution(9085722306287639901)
XLA Ops:
  0.0 1.0 %copy-done = bf16[4,3,2,64,64]{4,3,2,1,0:T(8,128)(2,1)S(1)} copy-done((bf16[4,3,2,64,64]{4,3,2,1,0:T(8,128)(2,1)S(1)}, bf16[4,3,2,64,64]{4,3,2,1,0:T(8,128)(2,1)}, u32[]{:S(2)}) %copy-start) | copy-done | bytes 196632
  1.0 1.2 %copy-done.2 = bf16[2,262144]{1,0:T(2,128)(2,1)S(1)} copy-done((bf16[2,262144]{1,0:T(2,128)(2,1)S(1)}, bf16[2,262144]{1,0:T(2,128)(2,1)}, u32[]{:S(2)}) %copy-start.2) | copy-done | bytes 1048600
  2.2 3.9 %shard_map.37 = (bf16[12,32,128]{2,1,0:T(8,128)(2,1)S(1)}, bf16[12,32,128]{2,1,0:T(8,128)(2,1)S(1)}, bf16[12,32,128]{2,1,0:T(8,128)(2,1)S(1)}, bf16[12,32,128]{2...) custom-call(bf16[4096,128]{1,0:T(8,128)(2,1)S(1)} %bitcast.10, ...), custom_call_target="tpu_custom_call" | custom-call | flops 1 | bytes 1 | tf_op jit(solution)/shard_map/pallas_call | solution.py:282
  6.2 3.0 %collective-permute-start = (bf16[12,32,128]{2,1,0:T(8,128)(2,1)S(1)}, bf16[12,32,128]{2,1,0:T(8,128)(2,1)S(1)}, u32[]{:S(2)}, u32[]{:S(2)}) collective-permute-start(bf16[12,32,128]{2,1,0:T(8,128)(2,1)S(1)} %get-tuple-element.36), channel_id=1, source_target_pairs={{0,4},{4,0},{8,12},{12,8},{16,20},{20,16},{24,28},{28,24},{1,5},{5... | collective-permute-start | bytes 294920 | tf_op jit(solution)/shard_map/ppermute | solution.py:295
  9.2 1.5 %collective-permute-start.1 = (bf16[12,32,128]{2,1,0:T(8,128)(2,1)S(1)}, bf16[12,32,128]{2,1,0:T(8,128)(2,1)S(1)}, u32[]{:S(2)}, u32[]{:S(2)}) collective-permute-start(bf16[12,32,128]{2,1,0:T(8,128)(2,1)S(1)} %get-tuple-element.37), channel_id=1, source_target_pairs={{0,12},{4,8},{8,4},{12,0},{16,28},{20,24},{24,20},{28,16},{1,13},{... | collective-permute-start | bytes 294920 | tf_op jit(solution)/shard_map/ppermute | solution.py:295
  10.7 0.1 collective-permute-start.2
  10.8 0.9 %shard_map.42 = (bf16[20,32,128]{2,1,0:T(8,128)(2,1)S(1)}, bf16[20,32,128]{2,1,0:T(8,128)(2,1)S(1)}, bf16[20,32,128]{2,1,0:T(8,128)(2,1)S(1)}, bf16[20,32,128]{2,1,0:T(8,128)(2,1)S(1)}) custom-call(bf16[2,1280,128]{2,1,0:T(8,128)(2,1)S(1)} %get-tuple-element.50.refs_0_, bf16[256,512]{1,0:T(8,128)(2,1)S(1)} %get-tuple-element.51.refs_1_, ...), custom_call_target="tpu_custom_call" | custom-call | flops 1 | bytes 1 | tf_op jit(solution)/shard_map/pallas_call | solution.py:282
  11.7 2.0 %collective-permute-start.9 = (bf16[20,32,128]{2,1,0:T(8,128)(2,1)S(1)}, bf16[20,32,128]{2,1,0:T(8,128)(2,1)S(1)}, u32[]{:S(2)}, u32[]{:S(2)}) collective-permute-start(bf16[20,32,128]{2,1,0:T(8,128)(2,1)S(1)} %get-tuple-element.53), channel_id=1, source_target_pairs={{0,4},{4,0},{8,12},{12,8},{16,20},{20,16},{24,28},{28,24},{1,5},{5... | collective-permute-start | bytes 491528 | tf_op jit(solution)/shard_map/ppermute | solution.py:295
  13.7 1.5 %collective-permute-start.10 = (bf16[20,32,128]{2,1,0:T(8,128)(2,1)S(1)}, bf16[20,32,128]{2,1,0:T(8,128)(2,1)S(1)}, u32[]{:S(2)}, u32[]{:S(2)}) collective-permute-start(bf16[20,32,128]{2,1,0:T(8,128)(2,1)S(1)} %get-tuple-element.54), channel_id=1, source_target_pairs={{0,12},{4,8},{8,4},{12,0},{16,28},{20,24},{24,20},{28,16},{1,13},{... | collective-permute-start | bytes 491528 | tf_op jit(solution)/shard_map/ppermute | solution.py:295
  15.2 0.0 collective-permute-done.refs_1_
  15.2 0.1 collective-permute-start.11
  15.3 0.5 collective-permute-done.1.refs_2_
  15.7 0.4 collective-permute-done.2.refs_3_
  16.2 0.0 copy-done.3
  16.2 0.7 %shard_map.38 = (bf16[2,12,16,128]{3,2,1,0:T(8,128)(2,1)S(1)}, bf16[2,12,16,128]{3,2,1,0:T(8,128)(2,1)S(1)}, bf16[2,12,16,128]{3,2,1,0:T(8,128)(2,1)S(1)}, bf16[2,12,16,128]{3,2,1,0:T(8,128)(2,1)S(1)}) custom-call(s32[4]{0:T(128)S(1)} %copy-done.3, bf16[12,32,128]{2,1,0:T(8,128)(2,1)S(1)} %collective-permute-done.refs_1_, ...), custom_call_target="tpu_custom_call" | custom-call | flops 2000000000 | bytes 1 | tf_op jit(solution)/shard_map/pallas_call | solution.py:282
  16.8 1.8 %collective-permute-start.3 = (bf16[2,12,16,128]{3,2,1,0:T(8,128)(2,1)S(1)}, bf16[2,12,16,128]{3,2,1,0:T(8,128)(2,1)S(1)}, u32[]{:S(2)}, u32[]{:S(2)}) collective-permute-start(bf16[2,12,16,128]{3,2,1,0:T(8,128)(2,1)S(1)} %get-tuple-element.40), channel_id=1, source_target_pairs={{0,2},{1,3},{2,0},{3,1},{4,6},{5,7},{6,4},{7,5},{8,10},{9,11},{10,... | collective-permute-start | bytes 294920 | tf_op jit(solution)/shard_map/ppermute | solution.py:312
  18.7 0.0 collective-permute-start.4
  18.7 3.0 %collective-permute-done.9.refs_1_ = bf16[20,32,128]{2,1,0:T(8,128)(2,1)S(1)} collective-permute-done((bf16[20,32,128]{2,1,0:T(8,128)(2,1)S(1)}, bf16[20,32,128]{2,1,0:T(8,128)(2,1)S(1)}, u32[]{:S(2)}, u32[]{:S(2)}) %collective-permute-start.9) | collective-permute-done | bytes 163872 | tf_op jit(solution)/shard_map/ppermute | solution.py:295
  21.7 0.0 collective-permute-start.5
  21.7 0.9 %shard_map.39 = (bf16[256,512]{1,0:T(8,128)(2,1)S(1)}, bf16[64,128]{1,0:T(8,128)(2,1)S(1)}, bf16[256,256]{1,0:T(8,128)(2,1)S(1)}) custom-call(bf16[4,3,2,64,64]{4,3,2,1,0:T(8,128)(2,1)S(1)} %copy-done.1), custom_call_target="tpu_custom_call" | custom-call | flops 1 | bytes 1 | tf_op jit(solution)/shard_map/pallas_call | solution.py:282
  22.6 0.0 collective-permute-done.10.refs_2_
  22.6 0.0 collective-permute-done.11.refs_3_
  22.6 0.7 %shard_map.43 = (bf16[2,20,16,128]{3,2,1,0:T(8,128)(2,1)S(1)}, bf16[2,20,16,128]{3,2,1,0:T(8,128)(2,1)S(1)}, bf16[2,20,16,128]{3,2,1,0:T(8,128)(2,1)S(1)}, bf16[2,20,16,128]{3,2,1,0:T(8,128)(2,1)S(1)}) custom-call(s32[4]{0:T(128)S(1)} %copy-done.3, bf16[20,32,128]{2,1,0:T(8,128)(2,1)S(1)} %collective-permute-done.9.refs_1_, ...), custom_call_target="tpu_custom_call" | custom-call | flops 1 | bytes 1 | tf_op jit(solution)/shard_map/pallas_call | solution.py:282
  23.3 1.7 %collective-permute-start.12 = (bf16[2,20,16,128]{3,2,1,0:T(8,128)(2,1)S(1)}, bf16[2,20,16,128]{3,2,1,0:T(8,128)(2,1)S(1)}, u32[]{:S(2)}, u32[]{:S(2)}) collective-permute-start(bf16[2,20,16,128]{3,2,1,0:T(8,128)(2,1)S(1)} %get-tuple-element.57), channel_id=1, source_target_pairs={{0,2},{1,3},{2,0},{3,1},{4,6},{5,7},{6,4},{7,5},{8,10},{9,11},{10,... | collective-permute-start | bytes 491528 | tf_op jit(solution)/shard_map/ppermute | solution.py:312
  25.0 0.2 collective-permute-start.13
  25.3 0.0 collective-permute-done.3.refs_0_
  25.3 0.3 collective-permute-start.14
  25.5 0.0 collective-permute-done.4.refs_1_
  25.5 0.0 collective-permute-done.5.refs_2_
  25.5 0.7 %shard_map.40 = (bf16[12,32,128]{2,1,0:T(8,128)(2,1)S(1)}, bf16[12,32,128]{2,1,0:T(8,128)(2,1)S(1)}, bf16[12,32,128]{2,1,0:T(8,128)(2,1)S(1)}, bf16[12,32,128]{2,1,0:T(8,128)(2,1)S(1)}) custom-call(bf16[2,12,16,128]{3,2,1,0:T(8,128)(2,1)S(1)} %collective-permute-done.3.refs_0_, bf16[2,12,16,128]{3,2,1,0:T(8,128)(2,1)S(1)} %collective-permute-done.4.refs_1_, ...), custom_call_target="tpu_custom_call" | custom-call | flops 2000000000 | bytes 1 | tf_op jit(solution)/shard_map/pallas_call | solution.py:282
  26.2 2.8 %collective-permute-start.6 = (bf16[12,32,128]{2,1,0:T(8,128)(2,1)S(1)}, bf16[12,32,128]{2,1,0:T(8,128)(2,1)S(1)}, u32[]{:S(2)}, u32[]{:S(2)}) collective-permute-start(bf16[12,32,128]{2,1,0:T(8,128)(2,1)S(1)} %get-tuple-element.46), channel_id=1, source_target_pairs={{0,16},{4,20},{8,24},{12,28},{16,0},{20,4},{24,8},{28,12},{1,17},{... | collective-permute-start | bytes 294920 | tf_op jit(solution)/shard_map/ppermute | solution.py:295
  29.0 1.3 %collective-permute-start.7 = (bf16[12,32,128]{2,1,0:T(8,128)(2,1)S(1)}, bf16[12,32,128]{2,1,0:T(8,128)(2,1)S(1)}, u32[]{:S(2)}, u32[]{:S(2)}) collective-permute-start(bf16[12,32,128]{2,1,0:T(8,128)(2,1)S(1)} %get-tuple-element.47), channel_id=1, source_target_pairs={{0,20},{4,16},{8,28},{12,24},{16,4},{20,0},{24,12},{28,8},{1,21},{... | collective-permute-start | bytes 294920 | tf_op jit(solution)/shard_map/ppermute | solution.py:295
  30.3 0.1 collective-permute-done.12.refs_0_
  30.4 1.7 %collective-permute-start.8 = (bf16[12,32,128]{2,1,0:T(8,128)(2,1)S(1)}, bf16[12,32,128]{2,1,0:T(8,128)(2,1)S(1)}, u32[]{:S(2)}, u32[]{:S(2)}) collective-permute-start(bf16[12,32,128]{2,1,0:T(8,128)(2,1)S(1)} %get-tuple-element.48), channel_id=1, source_target_pairs={{0,4},{4,0},{8,12},{12,8},{16,20},{20,16},{24,28},{28,24},{1,5},{5... | collective-permute-start | bytes 294920 | tf_op jit(solution)/shard_map/ppermute | solution.py:295
  32.1 1.0 %collective-permute-done.13.refs_1_ = bf16[2,20,16,128]{3,2,1,0:T(8,128)(2,1)S(1)} collective-permute-done((bf16[2,20,16,128]{3,2,1,0:T(8,128)(2,1)S(1)}, bf16[2,20,16,128]{3,2,1,0:T(8,128)(2,1)S(1)}, u32[]{:S(2)}, u32[]{:S(2)}) %collective-permute-start.13) | collective-permute-done | bytes 163872 | tf_op jit(solution)/shard_map/ppermute | solution.py:312
  33.1 0.0 collective-permute-done.14.refs_2_
  33.1 0.9 %shard_map.44 = (bf16[20,32,128]{2,1,0:T(8,128)(2,1)S(1)}, bf16[20,32,128]{2,1,0:T(8,128)(2,1)S(1)}, bf16[20,32,128]{2,1,0:T(8,128)(2,1)S(1)}, bf16[20,32,128]{2,1,0:T(8,128)(2,1)S(1)}) custom-call(bf16[2,20,16,128]{3,2,1,0:T(8,128)(2,1)S(1)} %collective-permute-done.12.refs_0_, bf16[2,20,16,128]{3,2,1,0:T(8,128)(2,1)S(1)} %collective-permute-done.13.refs_1_, ...), custom_call_target="tpu_custom_call" | custom-call | flops 1 | bytes 1 | tf_op jit(solution)/shard_map/pallas_call | solution.py:282
  34.1 2.7 %collective-permute-start.15 = (bf16[20,32,128]{2,1,0:T(8,128)(2,1)S(1)}, bf16[20,32,128]{2,1,0:T(8,128)(2,1)S(1)}, u32[]{:S(2)}, u32[]{:S(2)}) collective-permute-start(bf16[20,32,128]{2,1,0:T(8,128)(2,1)S(1)} %get-tuple-element.61), channel_id=1, source_target_pairs={{0,16},{4,20},{8,24},{12,28},{16,0},{20,4},{24,8},{28,12},{1,17},{... | collective-permute-start | bytes 491528 | tf_op jit(solution)/shard_map/ppermute | solution.py:295
  36.8 0.4 collective-permute-start.16
  37.1 0.0 collective-permute-done.6.refs_0_
  37.1 1.5 %collective-permute-start.17 = (bf16[20,32,128]{2,1,0:T(8,128)(2,1)S(1)}, bf16[20,32,128]{2,1,0:T(8,128)(2,1)S(1)}, u32[]{:S(2)}, u32[]{:S(2)}) collective-permute-start(bf16[20,32,128]{2,1,0:T(8,128)(2,1)S(1)} %get-tuple-element.63), channel_id=1, source_target_pairs={{0,4},{4,0},{8,12},{12,8},{16,20},{20,16},{24,28},{28,24},{1,5},{5... | collective-permute-start | bytes 491528 | tf_op jit(solution)/shard_map/ppermute | solution.py:295
  38.7 8.1 %collective-permute-done.7.refs_1_ = bf16[12,32,128]{2,1,0:T(8,128)(2,1)S(1)} collective-permute-done((bf16[12,32,128]{2,1,0:T(8,128)(2,1)S(1)}, bf16[12,32,128]{2,1,0:T(8,128)(2,1)S(1)}, u32[]{:S(2)}, u32[]{:S(2)}) %collective-permute-start.7) | collective-permute-done | bytes 98336 | tf_op jit(solution)/shard_map/ppermute | solution.py:295
  46.8 0.0 collective-permute-done.8.refs_2_
  46.8 0.8 %shard_map.41.refs_0_ = f32[2,2048,128]{2,1,0:T(8,128)S(1)} custom-call(bf16[12,32,128]{2,1,0:T(8,128)(2,1)S(1)} %collective-permute-done.6.refs_0_, bf16[12,32,128]{2,1,0:T(8,128)(2,1)S(1)} %collective-permute-done.7.refs_1_, bf16[12,32,128]{2,1,0:T(8,128)(2,1)S(1)} %collective-permute-done.8.refs_2_, bf16[12,32,128]{2,1,0:T(8,128)(2,1)S(1)} %get-tuple-element.49.refs_3_.refs_6_), custom_call_target="tpu_custom_call" | custom-call | flops 2000000000 | bytes 1 | tf_op jit(solution)/shard_map/pallas_call | solution.py:282
  47.6 1.7 %collective-permute-done.15.refs_1_ = bf16[20,32,128]{2,1,0:T(8,128)(2,1)S(1)} collective-permute-done((bf16[20,32,128]{2,1,0:T(8,128)(2,1)S(1)}, bf16[20,32,128]{2,1,0:T(8,128)(2,1)S(1)}, u32[]{:S(2)}, u32[]{:S(2)}) %collective-permute-start.15) | collective-permute-done | bytes 163872 | tf_op jit(solution)/shard_map/ppermute | solution.py:295
  49.3 4.1 %collective-permute-done.16.refs_2_ = bf16[20,32,128]{2,1,0:T(8,128)(2,1)S(1)} collective-permute-done((bf16[20,32,128]{2,1,0:T(8,128)(2,1)S(1)}, bf16[20,32,128]{2,1,0:T(8,128)(2,1)S(1)}, u32[]{:S(2)}, u32[]{:S(2)}) %collective-permute-start.16) | collective-permute-done | bytes 163872 | tf_op jit(solution)/shard_map/ppermute | solution.py:295
  53.4 0.0 collective-permute-done.17.refs_3_
  53.4 4.9 %shard_map.45 = (bf16[4096,128]{1,0:T(8,128)(2,1)}, f32[2,2048,128]{2,1,0:T(8,128)S(1)}) custom-call(f32[2,2048,128]{2,1,0:T(8,128)S(1)} %shard_map.41.refs_0_, bf16[20,32,128]{2,1,0:T(8,128)(2,1)S(1)} %collective-permute-done.15.refs_1_, bf16[20,32,128]{2,1,0:T(8,128)(2,1)S(1)} %collective-permute-done.16.refs_2_, ...), custom_call_target="tpu_custom_call", output_to_operand_aliasing={{1}: (0, {})} | custom-call | flops 1 | bytes 1 | tf_op jit(solution)/shard_map/pallas_call | solution.py:282
  (5 shorter events, 0.0 us)
Async XLA Ops:
  0.0 16.2 %copy-start.3 = (s32[4]{0:T(128)S(1)}, s32[4]{0:T(128)}, u32[]{:S(2)}) copy-start(s32[4]{0:T(128)} %refs_0_.5) | copy-start | bytes 52
  0.0 1.0 %copy-start = (bf16[4,3,2,64,64]{4,3,2,1,0:T(8,128)(2,1)S(1)}, bf16[4,3,2,64,64]{4,3,2,1,0:T(8,128)(2,1)}, u32[]{:S(2)}) copy-start(bf16[4,3,2,64,64]{4,3,2,1,0:T(8,128)(2,1)} %refs_0_.4) | copy-start | bytes 589828
  1.0 1.2 %copy-start.2 = (bf16[2,262144]{1,0:T(2,128)(2,1)S(1)}, bf16[2,262144]{1,0:T(2,128)(2,1)}, u32[]{:S(2)}) copy-start(bf16[2,262144]{1,0:T(2,128)(2,1)} %param.3) | copy-start | bytes 3145732
  6.2 9.0 %collective-permute-start = (bf16[12,32,128]{2,1,0:T(8,128)(2,1)S(1)}, bf16[12,32,128]{2,1,0:T(8,128)(2,1)S(1)}, u32[]{:S(2)}, u32[]{:S(2)}) collective-permute-start(bf16[12,32,128]{2,1,0:T(8,128)(2,1)S(1)} %get-tuple-element.36), channel_id=1, source_target_pairs={{0,4},{4,0},{8,12},{12,8},{16,20},{20,16},{24,28},{28,24},{1,5},{5... | collective-permute-start | bytes 294920 | tf_op jit(solution)/shard_map/ppermute | solution.py:295
  9.2 6.5 %collective-permute-start.1 = (bf16[12,32,128]{2,1,0:T(8,128)(2,1)S(1)}, bf16[12,32,128]{2,1,0:T(8,128)(2,1)S(1)}, u32[]{:S(2)}, u32[]{:S(2)}) collective-permute-start(bf16[12,32,128]{2,1,0:T(8,128)(2,1)S(1)} %get-tuple-element.37), channel_id=1, source_target_pairs={{0,12},{4,8},{8,4},{12,0},{16,28},{20,24},{24,20},{28,16},{1,13},{... | collective-permute-start | bytes 294920 | tf_op jit(solution)/shard_map/ppermute | solution.py:295
  10.7 5.5 %collective-permute-start.2 = (bf16[12,32,128]{2,1,0:T(8,128)(2,1)S(1)}, bf16[12,32,128]{2,1,0:T(8,128)(2,1)S(1)}, u32[]{:S(2)}, u32[]{:S(2)}) collective-permute-start(bf16[12,32,128]{2,1,0:T(8,128)(2,1)S(1)} %get-tuple-element.38), channel_id=1, source_target_pairs={{0,8},{4,12},{8,0},{12,4},{16,24},{20,28},{24,16},{28,20},{1,9},{5... | collective-permute-start | bytes 294920 | tf_op jit(solution)/shard_map/ppermute | solution.py:295
  11.7 10.0 %collective-permute-start.9 = (bf16[20,32,128]{2,1,0:T(8,128)(2,1)S(1)}, bf16[20,32,128]{2,1,0:T(8,128)(2,1)S(1)}, u32[]{:S(2)}, u32[]{:S(2)}) collective-permute-start(bf16[20,32,128]{2,1,0:T(8,128)(2,1)S(1)} %get-tuple-element.53), channel_id=1, source_target_pairs={{0,4},{4,0},{8,12},{12,8},{16,20},{20,16},{24,28},{28,24},{1,5},{5... | collective-permute-start | bytes 491528 | tf_op jit(solution)/shard_map/ppermute | solution.py:295
  13.7 8.9 %collective-permute-start.10 = (bf16[20,32,128]{2,1,0:T(8,128)(2,1)S(1)}, bf16[20,32,128]{2,1,0:T(8,128)(2,1)S(1)}, u32[]{:S(2)}, u32[]{:S(2)}) collective-permute-start(bf16[20,32,128]{2,1,0:T(8,128)(2,1)S(1)} %get-tuple-element.54), channel_id=1, source_target_pairs={{0,12},{4,8},{8,4},{12,0},{16,28},{20,24},{24,20},{28,16},{1,13},{... | collective-permute-start | bytes 491528 | tf_op jit(solution)/shard_map/ppermute | solution.py:295
  15.2 7.4 %collective-permute-start.11 = (bf16[20,32,128]{2,1,0:T(8,128)(2,1)S(1)}, bf16[20,32,128]{2,1,0:T(8,128)(2,1)S(1)}, u32[]{:S(2)}, u32[]{:S(2)}) collective-permute-start(bf16[20,32,128]{2,1,0:T(8,128)(2,1)S(1)} %get-tuple-element.55), channel_id=1, source_target_pairs={{0,8},{4,12},{8,0},{12,4},{16,24},{20,28},{24,16},{28,20},{1,9},{5... | collective-permute-start | bytes 491528 | tf_op jit(solution)/shard_map/ppermute | solution.py:295
  16.2 5.5 %copy-start.1 = (bf16[4,3,2,64,64]{4,3,2,1,0:T(8,128)(2,1)S(1)}, bf16[4,3,2,64,64]{4,3,2,1,0:T(8,128)(2,1)}, u32[]{:S(2)}) copy-start(bf16[4,3,2,64,64]{4,3,2,1,0:T(8,128)(2,1)} %refs_0_.4) | copy-start | bytes 589828
  16.8 8.4 %collective-permute-start.3 = (bf16[2,12,16,128]{3,2,1,0:T(8,128)(2,1)S(1)}, bf16[2,12,16,128]{3,2,1,0:T(8,128)(2,1)S(1)}, u32[]{:S(2)}, u32[]{:S(2)}) collective-permute-start(bf16[2,12,16,128]{3,2,1,0:T(8,128)(2,1)S(1)} %get-tuple-element.40), channel_id=1, source_target_pairs={{0,2},{1,3},{2,0},{3,1},{4,6},{5,7},{6,4},{7,5},{8,10},{9,11},{10,... | collective-permute-start | bytes 294920 | tf_op jit(solution)/shard_map/ppermute | solution.py:312
  18.7 6.9 %collective-permute-start.4 = (bf16[2,12,16,128]{3,2,1,0:T(8,128)(2,1)S(1)}, bf16[2,12,16,128]{3,2,1,0:T(8,128)(2,1)S(1)}, u32[]{:S(2)}, u32[]{:S(2)}) collective-permute-start(bf16[2,12,16,128]{3,2,1,0:T(8,128)(2,1)S(1)} %get-tuple-element.41), channel_id=1, source_target_pairs={{0,3},{1,2},{2,1},{3,0},{4,7},{5,6},{6,5},{7,4},{8,11},{9,10},{10,... | collective-permute-start | bytes 294920 | tf_op jit(solution)/shard_map/ppermute | solution.py:312
  21.7 3.9 %collective-permute-start.5 = (bf16[2,12,16,128]{3,2,1,0:T(8,128)(2,1)S(1)}, bf16[2,12,16,128]{3,2,1,0:T(8,128)(2,1)S(1)}, u32[]{:S(2)}, u32[]{:S(2)}) collective-permute-start(bf16[2,12,16,128]{3,2,1,0:T(8,128)(2,1)S(1)} %get-tuple-element.42), channel_id=1, source_target_pairs={{0,1},{1,0},{2,3},{3,2},{4,5},{5,4},{6,7},{7,6},{8,9},{9,8},{10,11... | collective-permute-start | bytes 294920 | tf_op jit(solution)/shard_map/ppermute | solution.py:312
  23.3 7.1 %collective-permute-start.12 = (bf16[2,20,16,128]{3,2,1,0:T(8,128)(2,1)S(1)}, bf16[2,20,16,128]{3,2,1,0:T(8,128)(2,1)S(1)}, u32[]{:S(2)}, u32[]{:S(2)}) collective-permute-start(bf16[2,20,16,128]{3,2,1,0:T(8,128)(2,1)S(1)} %get-tuple-element.57), channel_id=1, source_target_pairs={{0,2},{1,3},{2,0},{3,1},{4,6},{5,7},{6,4},{7,5},{8,10},{9,11},{10,... | collective-permute-start | bytes 491528 | tf_op jit(solution)/shard_map/ppermute | solution.py:312
  25.0 8.1 %collective-permute-start.13 = (bf16[2,20,16,128]{3,2,1,0:T(8,128)(2,1)S(1)}, bf16[2,20,16,128]{3,2,1,0:T(8,128)(2,1)S(1)}, u32[]{:S(2)}, u32[]{:S(2)}) collective-permute-start(bf16[2,20,16,128]{3,2,1,0:T(8,128)(2,1)S(1)} %get-tuple-element.58), channel_id=1, source_target_pairs={{0,3},{1,2},{2,1},{3,0},{4,7},{5,6},{6,5},{7,4},{8,11},{9,10},{10,... | collective-permute-start | bytes 491528 | tf_op jit(solution)/shard_map/ppermute | solution.py:312
  25.3 7.9 %collective-permute-start.14 = (bf16[2,20,16,128]{3,2,1,0:T(8,128)(2,1)S(1)}, bf16[2,20,16,128]{3,2,1,0:T(8,128)(2,1)S(1)}, u32[]{:S(2)}, u32[]{:S(2)}) collective-permute-start(bf16[2,20,16,128]{3,2,1,0:T(8,128)(2,1)S(1)} %get-tuple-element.59), channel_id=1, source_target_pairs={{0,1},{1,0},{2,3},{3,2},{4,5},{5,4},{6,7},{7,6},{8,9},{9,8},{10,11... | collective-permute-start | bytes 491528 | tf_op jit(solution)/shard_map/ppermute | solution.py:312
  26.2 10.9 %collective-permute-start.6 = (bf16[12,32,128]{2,1,0:T(8,128)(2,1)S(1)}, bf16[12,32,128]{2,1,0:T(8,128)(2,1)S(1)}, u32[]{:S(2)}, u32[]{:S(2)}) collective-permute-start(bf16[12,32,128]{2,1,0:T(8,128)(2,1)S(1)} %get-tuple-element.46), channel_id=1, source_target_pairs={{0,16},{4,20},{8,24},{12,28},{16,0},{20,4},{24,8},{28,12},{1,17},{... | collective-permute-start | bytes 294920 | tf_op jit(solution)/shard_map/ppermute | solution.py:295
  29.0 17.8 %collective-permute-start.7 = (bf16[12,32,128]{2,1,0:T(8,128)(2,1)S(1)}, bf16[12,32,128]{2,1,0:T(8,128)(2,1)S(1)}, u32[]{:S(2)}, u32[]{:S(2)}) collective-permute-start(bf16[12,32,128]{2,1,0:T(8,128)(2,1)S(1)} %get-tuple-element.47), channel_id=1, source_target_pairs={{0,20},{4,16},{8,28},{12,24},{16,4},{20,0},{24,12},{28,8},{1,21},{... | collective-permute-start | bytes 294920 | tf_op jit(solution)/shard_map/ppermute | solution.py:295
  30.4 16.4 %collective-permute-start.8 = (bf16[12,32,128]{2,1,0:T(8,128)(2,1)S(1)}, bf16[12,32,128]{2,1,0:T(8,128)(2,1)S(1)}, u32[]{:S(2)}, u32[]{:S(2)}) collective-permute-start(bf16[12,32,128]{2,1,0:T(8,128)(2,1)S(1)} %get-tuple-element.48), channel_id=1, source_target_pairs={{0,4},{4,0},{8,12},{12,8},{16,20},{20,16},{24,28},{28,24},{1,5},{5... | collective-permute-start | bytes 294920 | tf_op jit(solution)/shard_map/ppermute | solution.py:295
  34.1 15.2 %collective-permute-start.15 = (bf16[20,32,128]{2,1,0:T(8,128)(2,1)S(1)}, bf16[20,32,128]{2,1,0:T(8,128)(2,1)S(1)}, u32[]{:S(2)}, u32[]{:S(2)}) collective-permute-start(bf16[20,32,128]{2,1,0:T(8,128)(2,1)S(1)} %get-tuple-element.61), channel_id=1, source_target_pairs={{0,16},{4,20},{8,24},{12,28},{16,0},{20,4},{24,8},{28,12},{1,17},{... | collective-permute-start | bytes 491528 | tf_op jit(solution)/shard_map/ppermute | solution.py:295
  36.8 16.6 %collective-permute-start.16 = (bf16[20,32,128]{2,1,0:T(8,128)(2,1)S(1)}, bf16[20,32,128]{2,1,0:T(8,128)(2,1)S(1)}, u32[]{:S(2)}, u32[]{:S(2)}) collective-permute-start(bf16[20,32,128]{2,1,0:T(8,128)(2,1)S(1)} %get-tuple-element.62), channel_id=1, source_target_pairs={{0,20},{4,16},{8,28},{12,24},{16,4},{20,0},{24,12},{28,8},{1,21},{... | collective-permute-start | bytes 491528 | tf_op jit(solution)/shard_map/ppermute | solution.py:295
  37.1 16.2 %collective-permute-start.17 = (bf16[20,32,128]{2,1,0:T(8,128)(2,1)S(1)}, bf16[20,32,128]{2,1,0:T(8,128)(2,1)S(1)}, u32[]{:S(2)}, u32[]{:S(2)}) collective-permute-start(bf16[20,32,128]{2,1,0:T(8,128)(2,1)S(1)} %get-tuple-element.63), channel_id=1, source_target_pairs={{0,4},{4,0},{8,12},{12,8},{16,20},{20,16},{24,28},{28,24},{1,5},{5... | collective-permute-start | bytes 491528 | tf_op jit(solution)/shard_map/ppermute | solution.py:295

commit v6 on v5

--- a/solution.py
+++ b/solution.py
@@ -161,7 +161,7 @@
 
 
 STEP = 8
-EARLY = 12
+EARLY = 14
 COST = 2 * 10**9
 
 
@@ -228,23 +228,24 @@
         store_blocks(both_gates(joined(ins, k, n), w1_ref[...], g_ref[...]), k, (o0, o1, o2, o3))
 
 
-def gather_rows(first, ins, wide):
-    bit = own_bits()[3]
-    blocks = by_place(ins)
-    for k in range(ins[0].shape[0]):
-        for j in range(2):
-            rows = pl.ds((bit ^ j) * (HALF * HALF) + first + k, HALF, stride=HALF)
-            for i in range(2):
-                wide[i, rows, :] = blocks[i, j][k].astype(F32)
-
-
-def gather_kernel(b0, b1, b2, b3, wide):
-    gather_rows(0, (b0, b1, b2, b3), wide)
-
-
-def last_kernel(_, b0, b1, b2, b3, w_ref, o_ref, wide, spread):
-    gather_rows(HALF - b0.shape[0], (b0, b1, b2, b3), wide)
-    for k in range(G // 8):
+def gather_rows(first, pair, wide):
+    for k in range(pair[0].shape[0]):
+        for i in range(2):
+            wide[i, pl.ds(first + k, HALF, stride=HALF), :] = pair[i][k].astype(F32)
+
+
+def gather_kernel(b0, b1, b2, b3, *wides):
+    blocks = by_place((b0, b1, b2, b3))
+    for j, wide in enumerate(wides):
+        gather_rows(0, (blocks[0, j], blocks[1, j]), wide)
+
+
+def last_kernel(j, *refs):
+    moved, stayed, w_ref, o_ref, wide, spread, made, sems = refs[-8:]
+    gather_rows(HALF - moved.shape[0], (stayed, moved), wide)
+    start = (own_bits()[3] ^ j) * (o_ref.shape[0] // 2)
+    copies = []
+    for k in range(HALF // 8):
         rows = slice(k * 256, (k + 1) * 256)
         x = jnp.concatenate([wide[i, rows, :] for i in range(2)], axis=1).astype(BF)
         r = turned_dot(w_ref[...], x)
@@ -252,7 +253,13 @@
         for q in range(8):
             for n in range(2):
                 spread[pl.ds((k * 8 + q) * G + n, HALF, stride=2), :] = tiles[q][n]
-        o_ref[k * 512 : (k + 1) * 512, :] = spread[k * 512 : (k + 1) * 512, :].astype(BF)
+        rows = slice(k * 512, (k + 1) * 512)
+        made[rows, :] = spread[rows, :].astype(BF)
+        to = pl.ds(pl.multiple_of(start + k * 512, 512), 512)
+        copies.append(pltpu.make_async_copy(made.at[rows], o_ref.at[to], sems.at[k]))
+        copies[-1].start()
+    for copy in copies:
+        copy.wait()
 
 
 def pick_kernel(groups, regroup, *refs):
@@ -270,10 +277,11 @@
 
 
 VMEM = pl.BlockSpec(memory_space=pltpu.VMEM)
+ANY = pl.BlockSpec(memory_space=pl.ANY)
 SMEM = pl.BlockSpec(memory_space=pltpu.SMEM)
 
 
-def call(kernel, outs, args, specs=None, scratch=(), after=(), flops=1, aliases={}):
+def call(kernel, outs, args, specs=None, scratch=(), after=(), flops=1, aliases={}, out_specs=None):
     specs = specs or [VMEM] * len(args)
 
     def body(*refs):
@@ -282,8 +290,8 @@
     return pl.pallas_call(
         body,
         out_shape=outs,
-        in_specs=specs + [pl.BlockSpec(memory_space=pl.ANY)] * len(after),
-        out_specs=jax.tree.map(lambda _: VMEM, outs),
+        in_specs=specs + [ANY] * len(after),
+        out_specs=out_specs or jax.tree.map(lambda _: VMEM, outs),
         scratch_shapes=scratch,
         input_output_aliases=aliases,
         cost_estimate=pl.CostEstimate(flops=flops, bytes_accessed=1, transcendentals=0),
@@ -353,10 +361,19 @@
     early = exchange(early, bits[2], bits[3])
     late = exchange(late, bits[2], bits[3])
 
-    wide = jax.ShapeDtypeStruct((2, HALF * G, 128), F32)
-    early = call(gather_kernel, wide, early, flops=COST)
+    wide = jax.ShapeDtypeStruct((2, HALF * HALF, 128), F32)
+    wides = call(gather_kernel, [wide] * 2, early, flops=COST)
+    late = by_place(late)
+    scratch = [pltpu.VMEM((whole // 2, 128), F32), pltpu.VMEM((whole // 2, 128), BF), pltpu.SemaphoreType.DMA((HALF // 8,))]
     shapes = [jax.ShapeDtypeStruct((whole, 128), BF), wide]
-    out, _ = call(last_kernel, shapes, (early, *late, w), scratch=[spread], aliases={0: 1})
+    out = []
+    for j in range(2):
+        args = (*out, wides[j], late[1, j], late[0, j], w)
+        aliases = {0: 0, 1: 1} if out else {0: 1}
+        specs = [ANY] * len(out) + [VMEM] * 4
+        kernel = functools.partial(last_kernel, j)
+        out = call(kernel, shapes, args, specs, scratch, aliases=aliases, out_specs=[ANY, VMEM])[:1]
+    (out,) = out
     return out.reshape(-1, 2, 128).transpose(1, 0, 2).reshape(state.shape)
 
 

time: 58.4 us -> 55.5 us (0.950)
  waiting for transfers between devices: 18.9 us -> 16.4 us
  Pallas kernels: 14.4 us -> 13.8 us
    ppermute x12, waiting for transfers between devices: 17.8 us -> 16.4 us  [swapped(): lax.ppermute(x, 'hi', [(d, d ^ apart) for d in range(lax.axis_size('hi'))])]
    ppermute x6, waiting for transfers between devices: 1.08 us -> 0.02 us  [regrouped(): lax.ppermute(x, 'lo', to)]
    pallas_call x9 -> x10, Pallas kernels: 14.4 us -> 13.8 us  [call(): pl.pallas_call(body, out_shape=outs, in_specs=specs + [ANY] * len(after),...]
  transfers between devices with their start and end apart: 18 -> 18, of which waited for: 8 -> 8; matrix products, arithmetic and copies ran while one was open for 0% -> 0% of each run, Pallas kernels for 10% -> 14%
where the time goes in v6:
time: 55.5 us; the launch traced here: 55.3 us
  starting transfers between devices  22.8 us (41%)
  waiting for transfers between devices  16.4 us (30%)
  Pallas kernels  13.8 us (25%)
  local copies, waits for them, and re-layouts  2.23 us (4%)
    ppermute x12, starting transfers between devices, swapped(): lax.ppermute(x, 'hi', [(d, d ^ apart) for d in range(lax.axis_size('hi'))])  18.7 us
    ppermute x12, waiting for transfers between devices, swapped(): lax.ppermute(x, 'hi', [(d, d ^ apart) for d in range(lax.axis_size('hi'))])  16.4 us
    pallas_call x10, Pallas kernels, call(): pl.pallas_call(body, out_shape=outs, in_specs=specs + [ANY] * len(after),...  13.8 us
    ppermute x6, starting transfers between devices, regrouped(): lax.ppermute(x, 'lo', to)  4.1 us
    unnamed x8, local copies, waits for them, and re-layouts  2.23 us
  transfers between devices with their start and end apart: 18, of which 8 were waited for; matrix products, arithmetic and copies ran while one was open for 0% of the time, Pallas kernels for 14%

profile of v6, /device:TPU:0, one launch (start us, length us, event | category | flops | bytes accessed | tf_op | source)
XLA Modules:
  0.0 55.3 jit_solution(13799560598741424060)
XLA Ops:
  0.0 1.0 %copy-done = bf16[4,3,2,64,64]{4,3,2,1,0:T(8,128)(2,1)S(1)} copy-done((bf16[4,3,2,64,64]{4,3,2,1,0:T(8,128)(2,1)S(1)}, bf16[4,3,2,64,64]{4,3,2,1,0:T(8,128)(2,1)}, u32[]{:S(2)}) %copy-start) | copy-done | bytes 196632
  1.0 1.2 %copy-done.2 = bf16[2,262144]{1,0:T(2,128)(2,1)S(1)} copy-done((bf16[2,262144]{1,0:T(2,128)(2,1)S(1)}, bf16[2,262144]{1,0:T(2,128)(2,1)}, u32[]{:S(2)}) %copy-start.2) | copy-done | bytes 1048600
  2.2 3.9 %shard_map.37 = (bf16[14,32,128]{2,1,0:T(8,128)(2,1)S(1)}, bf16[14,32,128]{2,1,0:T(8,128)(2,1)S(1)}, bf16[14,32,128]{2,1,0:T(8,128)(2,1)S(1)}, bf16[14,32,128]{2...) custom-call(bf16[4096,128]{1,0:T(8,128)(2,1)S(1)} %bitcast.10, ...), custom_call_target="tpu_custom_call" | custom-call | flops 1 | bytes 1 | tf_op jit(solution)/shard_map/pallas_call | solution.py:290
  6.2 3.0 %collective-permute-start = (bf16[14,32,128]{2,1,0:T(8,128)(2,1)S(1)}, bf16[14,32,128]{2,1,0:T(8,128)(2,1)S(1)}, u32[]{:S(2)}, u32[]{:S(2)}) collective-permute-start(bf16[14,32,128]{2,1,0:T(8,128)(2,1)S(1)} %get-tuple-element.39), channel_id=1, source_target_pairs={{0,4},{4,0},{8,12},{12,8},{16,20},{20,16},{24,28},{28,24},{1,5},{5... | collective-permute-start | bytes 344072 | tf_op jit(solution)/shard_map/ppermute | solution.py:303
  9.2 1.5 %collective-permute-start.1 = (bf16[14,32,128]{2,1,0:T(8,128)(2,1)S(1)}, bf16[14,32,128]{2,1,0:T(8,128)(2,1)S(1)}, u32[]{:S(2)}, u32[]{:S(2)}) collective-permute-start(bf16[14,32,128]{2,1,0:T(8,128)(2,1)S(1)} %get-tuple-element.40), channel_id=1, source_target_pairs={{0,12},{4,8},{8,4},{12,0},{16,28},{20,24},{24,20},{28,16},{1,13},{... | collective-permute-start | bytes 344072 | tf_op jit(solution)/shard_map/ppermute | solution.py:303
  10.7 0.1 collective-permute-start.2
  10.8 0.9 %shard_map.42 = (bf16[18,32,128]{2,1,0:T(8,128)(2,1)S(1)}, bf16[18,32,128]{2,1,0:T(8,128)(2,1)S(1)}, bf16[18,32,128]{2,1,0:T(8,128)(2,1)S(1)}, bf16[18,32,128]{2,1,0:T(8,128)(2,1)S(1)}) custom-call(bf16[2,1152,128]{2,1,0:T(8,128)(2,1)S(1)} %get-tuple-element.54.refs_0_, bf16[256,512]{1,0:T(8,128)(2,1)S(1)} %get-tuple-element.55.refs_1_, ...), custom_call_target="tpu_custom_call" | custom-call | flops 1 | bytes 1 | tf_op jit(solution)/shard_map/pallas_call | solution.py:290
  11.7 2.0 %collective-permute-start.9 = (bf16[18,32,128]{2,1,0:T(8,128)(2,1)S(1)}, bf16[18,32,128]{2,1,0:T(8,128)(2,1)S(1)}, u32[]{:S(2)}, u32[]{:S(2)}) collective-permute-start(bf16[18,32,128]{2,1,0:T(8,128)(2,1)S(1)} %get-tuple-element.57), channel_id=1, source_target_pairs={{0,4},{4,0},{8,12},{12,8},{16,20},{20,16},{24,28},{28,24},{1,5},{5... | collective-permute-start | bytes 442376 | tf_op jit(solution)/shard_map/ppermute | solution.py:303
  13.7 1.5 %collective-permute-start.10 = (bf16[18,32,128]{2,1,0:T(8,128)(2,1)S(1)}, bf16[18,32,128]{2,1,0:T(8,128)(2,1)S(1)}, u32[]{:S(2)}, u32[]{:S(2)}) collective-permute-start(bf16[18,32,128]{2,1,0:T(8,128)(2,1)S(1)} %get-tuple-element.58), channel_id=1, source_target_pairs={{0,12},{4,8},{8,4},{12,0},{16,28},{20,24},{24,20},{28,16},{1,13},{... | collective-permute-start | bytes 442376 | tf_op jit(solution)/shard_map/ppermute | solution.py:303
  15.2 0.0 collective-permute-done.refs_1_
  15.2 1.1 %collective-permute-start.11 = (bf16[18,32,128]{2,1,0:T(8,128)(2,1)S(1)}, bf16[18,32,128]{2,1,0:T(8,128)(2,1)S(1)}, u32[]{:S(2)}, u32[]{:S(2)}) collective-permute-start(bf16[18,32,128]{2,1,0:T(8,128)(2,1)S(1)} %get-tuple-element.59), channel_id=1, source_target_pairs={{0,8},{4,12},{8,0},{12,4},{16,24},{20,28},{24,16},{28,20},{1,9},{5... | collective-permute-start | bytes 442376 | tf_op jit(solution)/shard_map/ppermute | solution.py:303
  16.3 0.0 collective-permute-done.1.refs_2_
  16.3 1.0 %collective-permute-done.2.refs_3_ = bf16[14,32,128]{2,1,0:T(8,128)(2,1)S(1)} collective-permute-done((bf16[14,32,128]{2,1,0:T(8,128)(2,1)S(1)}, bf16[14,32,128]{2,1,0:T(8,128)(2,1)S(1)}, u32[]{:S(2)}, u32[]{:S(2)}) %collective-permute-start.2) | collective-permute-done | bytes 114720 | tf_op jit(solution)/shard_map/ppermute | solution.py:303
  17.2 0.7 %shard_map.38 = (bf16[2,14,16,128]{3,2,1,0:T(8,128)(2,1)S(1)}, bf16[2,14,16,128]{3,2,1,0:T(8,128)(2,1)S(1)}, bf16[2,14,16,128]{3,2,1,0:T(8,128)(2,1)S(1)}, bf16[2,14,16,128]{3,2,1,0:T(8,128)(2,1)S(1)}) custom-call(s32[4]{0:T(128)S(1)} %copy-done.3, bf16[14,32,128]{2,1,0:T(8,128)(2,1)S(1)} %collective-permute-done.refs_1_, ...), custom_call_target="tpu_custom_call" | custom-call | flops 2000000000 | bytes 1 | tf_op jit(solution)/shard_map/pallas_call | solution.py:290
  17.9 1.9 %collective-permute-start.3 = (bf16[2,14,16,128]{3,2,1,0:T(8,128)(2,1)S(1)}, bf16[2,14,16,128]{3,2,1,0:T(8,128)(2,1)S(1)}, u32[]{:S(2)}, u32[]{:S(2)}) collective-permute-start(bf16[2,14,16,128]{3,2,1,0:T(8,128)(2,1)S(1)} %get-tuple-element.43), channel_id=1, source_target_pairs={{0,2},{1,3},{2,0},{3,1},{4,6},{5,7},{6,4},{7,5},{8,10},{9,11},{10,... | collective-permute-start | bytes 344072 | tf_op jit(solution)/shard_map/ppermute | solution.py:320
  19.8 0.0 collective-permute-start.4
  19.8 0.8 %collective-permute-done.9.refs_1_ = bf16[18,32,128]{2,1,0:T(8,128)(2,1)S(1)} collective-permute-done((bf16[18,32,128]{2,1,0:T(8,128)(2,1)S(1)}, bf16[18,32,128]{2,1,0:T(8,128)(2,1)S(1)}, u32[]{:S(2)}, u32[]{:S(2)}) %collective-permute-start.9) | collective-permute-done | bytes 147488 | tf_op jit(solution)/shard_map/ppermute | solution.py:303
  20.6 0.0 collective-permute-start.5
  20.6 0.9 %shard_map.39 = (bf16[256,512]{1,0:T(8,128)(2,1)S(1)}, bf16[64,128]{1,0:T(8,128)(2,1)S(1)}, bf16[256,256]{1,0:T(8,128)(2,1)S(1)}) custom-call(bf16[4,3,2,64,64]{4,3,2,1,0:T(8,128)(2,1)S(1)} %copy-done.1), custom_call_target="tpu_custom_call" | custom-call | flops 1 | bytes 1 | tf_op jit(solution)/shard_map/pallas_call | solution.py:290
  21.5 0.2 collective-permute-done.10.refs_2_
  21.7 0.7 %collective-permute-done.11.refs_3_ = bf16[18,32,128]{2,1,0:T(8,128)(2,1)S(1)} collective-permute-done((bf16[18,32,128]{2,1,0:T(8,128)(2,1)S(1)}, bf16[18,32,128]{2,1,0:T(8,128)(2,1)S(1)}, u32[]{:S(2)}, u32[]{:S(2)}) %collective-permute-start.11) | collective-permute-done | bytes 147488 | tf_op jit(solution)/shard_map/ppermute | solution.py:303
  22.5 0.7 %shard_map.43 = (bf16[2,18,16,128]{3,2,1,0:T(8,128)(2,1)S(1)}, bf16[2,18,16,128]{3,2,1,0:T(8,128)(2,1)S(1)}, bf16[2,18,16,128]{3,2,1,0:T(8,128)(2,1)S(1)}, bf16[2,18,16,128]{3,2,1,0:T(8,128)(2,1)S(1)}) custom-call(s32[4]{0:T(128)S(1)} %copy-done.3, bf16[18,32,128]{2,1,0:T(8,128)(2,1)S(1)} %collective-permute-done.9.refs_1_, ...), custom_call_target="tpu_custom_call" | custom-call | flops 1 | bytes 1 | tf_op jit(solution)/shard_map/pallas_call | solution.py:290
  23.2 1.7 %collective-permute-start.12 = (bf16[2,18,16,128]{3,2,1,0:T(8,128)(2,1)S(1)}, bf16[2,18,16,128]{3,2,1,0:T(8,128)(2,1)S(1)}, u32[]{:S(2)}, u32[]{:S(2)}) collective-permute-start(bf16[2,18,16,128]{3,2,1,0:T(8,128)(2,1)S(1)} %get-tuple-element.61), channel_id=1, source_target_pairs={{0,2},{1,3},{2,0},{3,1},{4,6},{5,7},{6,4},{7,5},{8,10},{9,11},{10,... | collective-permute-start | bytes 442376 | tf_op jit(solution)/shard_map/ppermute | solution.py:320
  24.9 0.0 collective-permute-start.13
  24.9 0.0 collective-permute-done.3.refs_0_
  24.9 0.5 collective-permute-start.14
  25.4 0.0 collective-permute-done.4.refs_1_
  25.4 0.0 collective-permute-done.5.refs_2_
  25.4 0.7 %shard_map.40 = (bf16[14,32,128]{2,1,0:T(8,128)(2,1)S(1)}, bf16[14,32,128]{2,1,0:T(8,128)(2,1)S(1)}, bf16[14,32,128]{2,1,0:T(8,128)(2,1)S(1)}, bf16[14,32,128]{2,1,0:T(8,128)(2,1)S(1)}) custom-call(bf16[2,14,16,128]{3,2,1,0:T(8,128)(2,1)S(1)} %collective-permute-done.3.refs_0_, bf16[2,14,16,128]{3,2,1,0:T(8,128)(2,1)S(1)} %collective-permute-done.4.refs_1_, ...), custom_call_target="tpu_custom_call" | custom-call | flops 2000000000 | bytes 1 | tf_op jit(solution)/shard_map/pallas_call | solution.py:290
  26.1 2.8 %collective-permute-start.6 = (bf16[14,32,128]{2,1,0:T(8,128)(2,1)S(1)}, bf16[14,32,128]{2,1,0:T(8,128)(2,1)S(1)}, u32[]{:S(2)}, u32[]{:S(2)}) collective-permute-start(bf16[14,32,128]{2,1,0:T(8,128)(2,1)S(1)} %get-tuple-element.49), channel_id=1, source_target_pairs={{0,16},{4,20},{8,24},{12,28},{16,0},{20,4},{24,8},{28,12},{1,17},{... | collective-permute-start | bytes 344072 | tf_op jit(solution)/shard_map/ppermute | solution.py:303
  28.9 1.3 %collective-permute-start.7 = (bf16[14,32,128]{2,1,0:T(8,128)(2,1)S(1)}, bf16[14,32,128]{2,1,0:T(8,128)(2,1)S(1)}, u32[]{:S(2)}, u32[]{:S(2)}) collective-permute-start(bf16[14,32,128]{2,1,0:T(8,128)(2,1)S(1)} %get-tuple-element.50), channel_id=1, source_target_pairs={{0,20},{4,16},{8,28},{12,24},{16,4},{20,0},{24,12},{28,8},{1,21},{... | collective-permute-start | bytes 344072 | tf_op jit(solution)/shard_map/ppermute | solution.py:303
  30.2 0.0 collective-permute-done.12.refs_0_
  30.2 1.4 %collective-permute-start.8 = (bf16[14,32,128]{2,1,0:T(8,128)(2,1)S(1)}, bf16[14,32,128]{2,1,0:T(8,128)(2,1)S(1)}, u32[]{:S(2)}, u32[]{:S(2)}) collective-permute-start(bf16[14,32,128]{2,1,0:T(8,128)(2,1)S(1)} %get-tuple-element.51), channel_id=1, source_target_pairs={{0,4},{4,0},{8,12},{12,8},{16,20},{20,16},{24,28},{28,24},{1,5},{5... | collective-permute-start | bytes 344072 | tf_op jit(solution)/shard_map/ppermute | solution.py:303
  31.6 0.0 collective-permute-done.13.refs_1_
  31.6 0.0 collective-permute-done.14.refs_2_
  31.6 0.9 %shard_map.44 = (bf16[18,32,128]{2,1,0:T(8,128)(2,1)S(1)}, bf16[18,32,128]{2,1,0:T(8,128)(2,1)S(1)}, bf16[18,32,128]{2,1,0:T(8,128)(2,1)S(1)}, bf16[18,32,128]{2,1,0:T(8,128)(2,1)S(1)}) custom-call(bf16[2,18,16,128]{3,2,1,0:T(8,128)(2,1)S(1)} %collective-permute-done.12.refs_0_, bf16[2,18,16,128]{3,2,1,0:T(8,128)(2,1)S(1)} %collective-permute-done.13.refs_1_, ...), custom_call_target="tpu_custom_call" | custom-call | flops 1 | bytes 1 | tf_op jit(solution)/shard_map/pallas_call | solution.py:290
  32.5 2.7 %collective-permute-start.15 = (bf16[18,32,128]{2,1,0:T(8,128)(2,1)S(1)}, bf16[18,32,128]{2,1,0:T(8,128)(2,1)S(1)}, u32[]{:S(2)}, u32[]{:S(2)}) collective-permute-start(bf16[18,32,128]{2,1,0:T(8,128)(2,1)S(1)} %get-tuple-element.65), channel_id=1, source_target_pairs={{0,16},{4,20},{8,24},{12,28},{16,0},{20,4},{24,8},{28,12},{1,17},{... | collective-permute-start | bytes 442376 | tf_op jit(solution)/shard_map/ppermute | solution.py:303
  35.2 1.4 %collective-permute-start.16 = (bf16[18,32,128]{2,1,0:T(8,128)(2,1)S(1)}, bf16[18,32,128]{2,1,0:T(8,128)(2,1)S(1)}, u32[]{:S(2)}, u32[]{:S(2)}) collective-permute-start(bf16[18,32,128]{2,1,0:T(8,128)(2,1)S(1)} %get-tuple-element.70), channel_id=1, source_target_pairs={{0,20},{4,16},{8,28},{12,24},{16,4},{20,0},{24,12},{28,8},{1,21},{... | collective-permute-start | bytes 442376 | tf_op jit(solution)/shard_map/ppermute | solution.py:303
  36.5 4.6 %collective-permute-done.6.refs_0_ = bf16[14,32,128]{2,1,0:T(8,128)(2,1)S(1)} collective-permute-done((bf16[14,32,128]{2,1,0:T(8,128)(2,1)S(1)}, bf16[14,32,128]{2,1,0:T(8,128)(2,1)S(1)}, u32[]{:S(2)}, u32[]{:S(2)}) %collective-permute-start.6) | collective-permute-done | bytes 114720 | tf_op jit(solution)/shard_map/ppermute | solution.py:303
  41.1 0.0 collective-permute-start.17
  41.1 6.7 %collective-permute-done.7.refs_1_ = bf16[14,32,128]{2,1,0:T(8,128)(2,1)S(1)} collective-permute-done((bf16[14,32,128]{2,1,0:T(8,128)(2,1)S(1)}, bf16[14,32,128]{2,1,0:T(8,128)(2,1)S(1)}, u32[]{:S(2)}, u32[]{:S(2)}) %collective-permute-start.7) | collective-permute-done | bytes 114720 | tf_op jit(solution)/shard_map/ppermute | solution.py:303
  47.8 0.0 collective-permute-done.8.refs_2_
  47.8 0.9 %shard_map.41 = (f32[2,1024,128]{2,1,0:T(8,128)S(1)}, f32[2,1024,128]{2,1,0:T(8,128)S(1)}) custom-call(bf16[14,32,128]{2,1,0:T(8,128)(2,1)S(1)} %collective-permute-done.6.refs_0_, bf16[14,32,128]{2,1,0:T(8,128)(2,1)S(1)} %collective-permute-done.7.refs_1_, bf16[14,32,128]{2,1,0:T(8,128)(2,1)S(1)} %collective-permute-done.8.refs_2_, ...), custom_call_target="tpu_custom_call" | custom-call | flops 2000000000 | bytes 1 | tf_op jit(solution)/shard_map/pallas_call | solution.py:290
  48.7 1.1 %collective-permute-done.15.refs_1_ = bf16[18,32,128]{2,1,0:T(8,128)(2,1)S(1)} collective-permute-done((bf16[18,32,128]{2,1,0:T(8,128)(2,1)S(1)}, bf16[18,32,128]{2,1,0:T(8,128)(2,1)S(1)}, u32[]{:S(2)}, u32[]{:S(2)}) %collective-permute-start.15) | collective-permute-done | bytes 147488 | tf_op jit(solution)/shard_map/ppermute | solution.py:303
  49.9 2.1 %shard_map.45 = (bf16[4096,128]{1,0:T(8,128)(2,1)}, f32[2,1024,128]{2,1,0:T(8,128)S(1)}) custom-call(f32[2,1024,128]{2,1,0:T(8,128)S(1)} %get-tuple-element.53.refs_0_, bf16[18,32,128]{2,1,0:T(8,128)(2,1)S(1)} %collective-permute-done.15.refs_1_, bf16[18,32,128]{2,1,0:T(8,128)(2,1)S(1)} %get-tuple-element.66.refs_2_, ...), custom_call_target="tpu_custom_call", output_to_operand_aliasing={{1}: (0, {})} | custom-call | flops 1 | bytes 1 | tf_op jit(solution)/shard_map/pallas_call | solution.py:290
  52.0 1.2 %collective-permute-done.16.refs_2_ = bf16[18,32,128]{2,1,0:T(8,128)(2,1)S(1)} collective-permute-done((bf16[18,32,128]{2,1,0:T(8,128)(2,1)S(1)}, bf16[18,32,128]{2,1,0:T(8,128)(2,1)S(1)}, u32[]{:S(2)}, u32[]{:S(2)}) %collective-permute-start.16) | collective-permute-done | bytes 147488 | tf_op jit(solution)/shard_map/ppermute | solution.py:303
  53.2 0.0 collective-permute-done.17.refs_3_
  53.2 2.1 %shard_map.46 = (bf16[4096,128]{1,0:T(8,128)(2,1)}, f32[2,1024,128]{2,1,0:T(8,128)S(1)}) custom-call(bf16[4096,128]{1,0:T(8,128)(2,1)} %get-tuple-element.68.refs_0_, f32[2,1024,128]{2,1,0:T(8,128)S(1)} %get-tuple-element.69.refs_1_, bf16[18,32,128]{2,1,0:T(8,128)(2,1)S(1)} %collective-permute-done.16.refs_2_, ...), custom_call_target="tpu_custom_call", output_to_operand_aliasing={{0}: (0, {}), {1}: (1, {})} | custom-call | flops 1 | bytes 1 | tf_op jit(solution)/shard_map/pallas_call | solution.py:290
  (6 shorter events, 0.0 us)
Async XLA Ops:
  0.0 1.0 %copy-start = (bf16[4,3,2,64,64]{4,3,2,1,0:T(8,128)(2,1)S(1)}, bf16[4,3,2,64,64]{4,3,2,1,0:T(8,128)(2,1)}, u32[]{:S(2)}) copy-start(bf16[4,3,2,64,64]{4,3,2,1,0:T(8,128)(2,1)} %refs_0_.4) | copy-start | bytes 589828
  1.0 1.2 %copy-start.2 = (bf16[2,262144]{1,0:T(2,128)(2,1)S(1)}, bf16[2,262144]{1,0:T(2,128)(2,1)}, u32[]{:S(2)}) copy-start(bf16[2,262144]{1,0:T(2,128)(2,1)} %param.3) | copy-start | bytes 3145732
  6.2 9.0 %collective-permute-start = (bf16[14,32,128]{2,1,0:T(8,128)(2,1)S(1)}, bf16[14,32,128]{2,1,0:T(8,128)(2,1)S(1)}, u32[]{:S(2)}, u32[]{:S(2)}) collective-permute-start(bf16[14,32,128]{2,1,0:T(8,128)(2,1)S(1)} %get-tuple-element.39), channel_id=1, source_target_pairs={{0,4},{4,0},{8,12},{12,8},{16,20},{20,16},{24,28},{28,24},{1,5},{5... | collective-permute-start | bytes 344072 | tf_op jit(solution)/shard_map/ppermute | solution.py:303
  9.2 7.1 %collective-permute-start.1 = (bf16[14,32,128]{2,1,0:T(8,128)(2,1)S(1)}, bf16[14,32,128]{2,1,0:T(8,128)(2,1)S(1)}, u32[]{:S(2)}, u32[]{:S(2)}) collective-permute-start(bf16[14,32,128]{2,1,0:T(8,128)(2,1)S(1)} %get-tuple-element.40), channel_id=1, source_target_pairs={{0,12},{4,8},{8,4},{12,0},{16,28},{20,24},{24,20},{28,16},{1,13},{... | collective-permute-start | bytes 344072 | tf_op jit(solution)/shard_map/ppermute | solution.py:303
  10.7 6.5 %collective-permute-start.2 = (bf16[14,32,128]{2,1,0:T(8,128)(2,1)S(1)}, bf16[14,32,128]{2,1,0:T(8,128)(2,1)S(1)}, u32[]{:S(2)}, u32[]{:S(2)}) collective-permute-start(bf16[14,32,128]{2,1,0:T(8,128)(2,1)S(1)} %get-tuple-element.41), channel_id=1, source_target_pairs={{0,8},{4,12},{8,0},{12,4},{16,24},{20,28},{24,16},{28,20},{1,9},{5... | collective-permute-start | bytes 344072 | tf_op jit(solution)/shard_map/ppermute | solution.py:303
  11.7 8.9 %collective-permute-start.9 = (bf16[18,32,128]{2,1,0:T(8,128)(2,1)S(1)}, bf16[18,32,128]{2,1,0:T(8,128)(2,1)S(1)}, u32[]{:S(2)}, u32[]{:S(2)}) collective-permute-start(bf16[18,32,128]{2,1,0:T(8,128)(2,1)S(1)} %get-tuple-element.57), channel_id=1, source_target_pairs={{0,4},{4,0},{8,12},{12,8},{16,20},{20,16},{24,28},{28,24},{1,5},{5... | collective-permute-start | bytes 442376 | tf_op jit(solution)/shard_map/ppermute | solution.py:303
  13.7 8.1 %collective-permute-start.10 = (bf16[18,32,128]{2,1,0:T(8,128)(2,1)S(1)}, bf16[18,32,128]{2,1,0:T(8,128)(2,1)S(1)}, u32[]{:S(2)}, u32[]{:S(2)}) collective-permute-start(bf16[18,32,128]{2,1,0:T(8,128)(2,1)S(1)} %get-tuple-element.58), channel_id=1, source_target_pairs={{0,12},{4,8},{8,4},{12,0},{16,28},{20,24},{24,20},{28,16},{1,13},{... | collective-permute-start | bytes 442376 | tf_op jit(solution)/shard_map/ppermute | solution.py:303
  15.2 2.0 %copy-start.3 = (s32[4]{0:T(128)S(1)}, s32[4]{0:T(128)}, u32[]{:S(2)}) copy-start(s32[4]{0:T(128)} %refs_0_.5) | copy-start | bytes 52
  15.2 7.3 %collective-permute-start.11 = (bf16[18,32,128]{2,1,0:T(8,128)(2,1)S(1)}, bf16[18,32,128]{2,1,0:T(8,128)(2,1)S(1)}, u32[]{:S(2)}, u32[]{:S(2)}) collective-permute-start(bf16[18,32,128]{2,1,0:T(8,128)(2,1)S(1)} %get-tuple-element.59), channel_id=1, source_target_pairs={{0,8},{4,12},{8,0},{12,4},{16,24},{20,28},{24,16},{28,20},{1,9},{5... | collective-permute-start | bytes 442376 | tf_op jit(solution)/shard_map/ppermute | solution.py:303
  17.2 3.4 %copy-start.1 = (bf16[4,3,2,64,64]{4,3,2,1,0:T(8,128)(2,1)S(1)}, bf16[4,3,2,64,64]{4,3,2,1,0:T(8,128)(2,1)}, u32[]{:S(2)}) copy-start(bf16[4,3,2,64,64]{4,3,2,1,0:T(8,128)(2,1)} %refs_0_.4) | copy-start | bytes 589828
  17.9 7.0 %collective-permute-start.3 = (bf16[2,14,16,128]{3,2,1,0:T(8,128)(2,1)S(1)}, bf16[2,14,16,128]{3,2,1,0:T(8,128)(2,1)S(1)}, u32[]{:S(2)}, u32[]{:S(2)}) collective-permute-start(bf16[2,14,16,128]{3,2,1,0:T(8,128)(2,1)S(1)} %get-tuple-element.43), channel_id=1, source_target_pairs={{0,2},{1,3},{2,0},{3,1},{4,6},{5,7},{6,4},{7,5},{8,10},{9,11},{10,... | collective-permute-start | bytes 344072 | tf_op jit(solution)/shard_map/ppermute | solution.py:320
  19.8 5.6 %collective-permute-start.4 = (bf16[2,14,16,128]{3,2,1,0:T(8,128)(2,1)S(1)}, bf16[2,14,16,128]{3,2,1,0:T(8,128)(2,1)S(1)}, u32[]{:S(2)}, u32[]{:S(2)}) collective-permute-start(bf16[2,14,16,128]{3,2,1,0:T(8,128)(2,1)S(1)} %get-tuple-element.44), channel_id=1, source_target_pairs={{0,3},{1,2},{2,1},{3,0},{4,7},{5,6},{6,5},{7,4},{8,11},{9,10},{10,... | collective-permute-start | bytes 344072 | tf_op jit(solution)/shard_map/ppermute | solution.py:320
  20.6 4.8 %collective-permute-start.5 = (bf16[2,14,16,128]{3,2,1,0:T(8,128)(2,1)S(1)}, bf16[2,14,16,128]{3,2,1,0:T(8,128)(2,1)S(1)}, u32[]{:S(2)}, u32[]{:S(2)}) collective-permute-start(bf16[2,14,16,128]{3,2,1,0:T(8,128)(2,1)S(1)} %get-tuple-element.45), channel_id=1, source_target_pairs={{0,1},{1,0},{2,3},{3,2},{4,5},{5,4},{6,7},{7,6},{8,9},{9,8},{10,11... | collective-permute-start | bytes 344072 | tf_op jit(solution)/shard_map/ppermute | solution.py:320
  23.2 7.0 %collective-permute-start.12 = (bf16[2,18,16,128]{3,2,1,0:T(8,128)(2,1)S(1)}, bf16[2,18,16,128]{3,2,1,0:T(8,128)(2,1)S(1)}, u32[]{:S(2)}, u32[]{:S(2)}) collective-permute-start(bf16[2,18,16,128]{3,2,1,0:T(8,128)(2,1)S(1)} %get-tuple-element.61), channel_id=1, source_target_pairs={{0,2},{1,3},{2,0},{3,1},{4,6},{5,7},{6,4},{7,5},{8,10},{9,11},{10,... | collective-permute-start | bytes 442376 | tf_op jit(solution)/shard_map/ppermute | solution.py:320
  24.9 6.7 %collective-permute-start.13 = (bf16[2,18,16,128]{3,2,1,0:T(8,128)(2,1)S(1)}, bf16[2,18,16,128]{3,2,1,0:T(8,128)(2,1)S(1)}, u32[]{:S(2)}, u32[]{:S(2)}) collective-permute-start(bf16[2,18,16,128]{3,2,1,0:T(8,128)(2,1)S(1)} %get-tuple-element.62), channel_id=1, source_target_pairs={{0,3},{1,2},{2,1},{3,0},{4,7},{5,6},{6,5},{7,4},{8,11},{9,10},{10,... | collective-permute-start | bytes 442376 | tf_op jit(solution)/shard_map/ppermute | solution.py:320
  24.9 6.7 %collective-permute-start.14 = (bf16[2,18,16,128]{3,2,1,0:T(8,128)(2,1)S(1)}, bf16[2,18,16,128]{3,2,1,0:T(8,128)(2,1)S(1)}, u32[]{:S(2)}, u32[]{:S(2)}) collective-permute-start(bf16[2,18,16,128]{3,2,1,0:T(8,128)(2,1)S(1)} %get-tuple-element.63), channel_id=1, source_target_pairs={{0,1},{1,0},{2,3},{3,2},{4,5},{5,4},{6,7},{7,6},{8,9},{9,8},{10,11... | collective-permute-start | bytes 442376 | tf_op jit(solution)/shard_map/ppermute | solution.py:320
  26.1 15.0 %collective-permute-start.6 = (bf16[14,32,128]{2,1,0:T(8,128)(2,1)S(1)}, bf16[14,32,128]{2,1,0:T(8,128)(2,1)S(1)}, u32[]{:S(2)}, u32[]{:S(2)}) collective-permute-start(bf16[14,32,128]{2,1,0:T(8,128)(2,1)S(1)} %get-tuple-element.49), channel_id=1, source_target_pairs={{0,16},{4,20},{8,24},{12,28},{16,0},{20,4},{24,8},{28,12},{1,17},{... | collective-permute-start | bytes 344072 | tf_op jit(solution)/shard_map/ppermute | solution.py:303
  28.9 19.0 %collective-permute-start.7 = (bf16[14,32,128]{2,1,0:T(8,128)(2,1)S(1)}, bf16[14,32,128]{2,1,0:T(8,128)(2,1)S(1)}, u32[]{:S(2)}, u32[]{:S(2)}) collective-permute-start(bf16[14,32,128]{2,1,0:T(8,128)(2,1)S(1)} %get-tuple-element.50), channel_id=1, source_target_pairs={{0,20},{4,16},{8,28},{12,24},{16,4},{20,0},{24,12},{28,8},{1,21},{... | collective-permute-start | bytes 344072 | tf_op jit(solution)/shard_map/ppermute | solution.py:303
  30.2 17.7 %collective-permute-start.8 = (bf16[14,32,128]{2,1,0:T(8,128)(2,1)S(1)}, bf16[14,32,128]{2,1,0:T(8,128)(2,1)S(1)}, u32[]{:S(2)}, u32[]{:S(2)}) collective-permute-start(bf16[14,32,128]{2,1,0:T(8,128)(2,1)S(1)} %get-tuple-element.51), channel_id=1, source_target_pairs={{0,4},{4,0},{8,12},{12,8},{16,20},{20,16},{24,28},{28,24},{1,5},{5... | collective-permute-start | bytes 344072 | tf_op jit(solution)/shard_map/ppermute | solution.py:303
  32.5 17.4 %collective-permute-start.15 = (bf16[18,32,128]{2,1,0:T(8,128)(2,1)S(1)}, bf16[18,32,128]{2,1,0:T(8,128)(2,1)S(1)}, u32[]{:S(2)}, u32[]{:S(2)}) collective-permute-start(bf16[18,32,128]{2,1,0:T(8,128)(2,1)S(1)} %get-tuple-element.65), channel_id=1, source_target_pairs={{0,16},{4,20},{8,24},{12,28},{16,0},{20,4},{24,8},{28,12},{1,17},{... | collective-permute-start | bytes 442376 | tf_op jit(solution)/shard_map/ppermute | solution.py:303
  35.2 18.1 %collective-permute-start.16 = (bf16[18,32,128]{2,1,0:T(8,128)(2,1)S(1)}, bf16[18,32,128]{2,1,0:T(8,128)(2,1)S(1)}, u32[]{:S(2)}, u32[]{:S(2)}) collective-permute-start(bf16[18,32,128]{2,1,0:T(8,128)(2,1)S(1)} %get-tuple-element.70), channel_id=1, source_target_pairs={{0,20},{4,16},{8,28},{12,24},{16,4},{20,0},{24,12},{28,8},{1,21},{... | collective-permute-start | bytes 442376 | tf_op jit(solution)/shard_map/ppermute | solution.py:303
  41.1 12.1 %collective-permute-start.17 = (bf16[18,32,128]{2,1,0:T(8,128)(2,1)S(1)}, bf16[18,32,128]{2,1,0:T(8,128)(2,1)S(1)}, u32[]{:S(2)}, u32[]{:S(2)}) collective-permute-start(bf16[18,32,128]{2,1,0:T(8,128)(2,1)S(1)} %get-tuple-element.71), channel_id=1, source_target_pairs={{0,4},{4,0},{8,12},{12,8},{16,20},{20,16},{24,28},{28,24},{1,5},{5... | collective-permute-start | bytes 442376 | tf_op jit(solution)/shard_map/ppermute | solution.py:303

commit v7 on v6

--- a/solution.py
+++ b/solution.py
@@ -52,13 +52,14 @@
     return dot(jnp.concatenate([lh, lh, ll], axis=1), jnp.concatenate([eh, el, eh], axis=0))
 
 
-def first_weights(gate):
+def first_weights(gate, part):
     real = jnp.concatenate([gate[:, :G], gate[:, :G]], axis=1)
     imag = jnp.concatenate([gate[:, G:], gate[:, G:]], axis=1)
-    low = iotas(HALF, 2 * G)[1] < G
+    low = iotas(HALF // 2, 2 * G)[1] < G
     rows = []
     for ch in range(2):
-        r, i = (x[ch * HALF : (ch + 1) * HALF] for x in (real, imag))
+        start = ch * HALF + part * HALF // 2
+        r, i = (x[start : start + HALF // 2] for x in (real, imag))
         for pair in ((r, -i), (i, r)):
             for mask in (low, ~low):
                 rows.append(jnp.concatenate([jnp.where(mask, x, 0.0) for x in pair], axis=1))
@@ -160,8 +161,10 @@
                 blocks[i, j][at + k] = out[j * HALF : (j + 1) * HALF, i * 128 : (i + 1) * 128]
 
 
-STEP = 8
-EARLY = 14
+STEP = 22
+PITCH = G + 1
+NARROW = HALF + 1
+EARLY = 12
 COST = 2 * 10**9
 
 
@@ -172,40 +175,53 @@
 
 
 def steps(size):
-    return [(k, min(STEP, size - k)) for k in range(0, size, STEP)]
-
-
-def first_kernel(x_ref, gates, o0, o1, o2, o3, rest, w1_ref, g_ref, spread, turned):
+    parts = -(-size // STEP)
+    ends = [size * k // parts for k in range(parts + 1)]
+    return [(k, end - k) for k, end in zip(ends, ends[1:])]
+
+
+def split_rows(k, x, w, turned):
+    r = turned_dot(w, x)
+    some = HALF // 2
+    tiles = turn([r[g * some : (g + 1) * some] for g in range(8)])
+    for q in range(8):
+        for n in range(2):
+            turned[n, pl.ds(k * 8 + q, some, stride=PITCH), :] = tiles[q][n]
+
+
+def rows_of(turned, first, last):
+    halves = [jnp.stack([turned[i, cp * PITCH : cp * PITCH + G, :] for cp in range(first, last)]) for i in range(2)]
+    return jnp.concatenate(halves, axis=2).astype(BF)
+
+
+def first_kernel(x_ref, gates, o0, o1, o2, o3, mixed, rest, w0_ref, w1_ref, g_ref, spread, turned):
     early = o0.shape[0]
     own = own_bits()
     late = product(gate_of(gates, 3, 0), gate_of(gates, 2, 0))
     soon = product(gate_of(gates, 1, 0), gate_of(gates, 0, 0))
-    w0 = first_weights(wide_product(late, soon))
+    gate = wide_product(late, soon)
+    w0 = first_weights(gate, 0)
+    w0_ref[...] = first_weights(gate, 1)
     w1_ref[...] = right_weights(gate_of(gates, 0, 1), True, 0, own[0])
     g_ref[...] = left_weights(product(gate_of(gates, 1, 2), gate_of(gates, 0, 2)), 0, own[1])
 
     for k in range(G // 8):
         spread[k * 512 : (k + 1) * 512, :] = x_ref[k * 512 : (k + 1) * 512, :].astype(F32)
         x = jnp.concatenate([spread[pl.ds(k * 512 + p, 256, stride=2), :] for p in range(2)], axis=1).astype(BF)
-        r = turned_dot(w0, x)
-        tiles = turn([r[g * HALF : (g + 1) * HALF] for g in range(8)])
-        for q in range(8):
-            for n in range(2):
-                turned[n, pl.ds(k * 8 + q, HALF, stride=G), :] = tiles[q][n]
-
-    for k, n in steps(early):
-        rows = slice(k * G, (k + n) * G)
-        x = jnp.concatenate([turned[0, rows, :], turned[1, rows, :]], axis=1).astype(BF).reshape(n, G, 4 * G)
-        store_blocks(both_gates(x, w1_ref[...], g_ref[...]), k, (o0, o1, o2, o3))
-    for n in range(2):
-        rest[n] = turned[n, early * G :, :].astype(BF)
-
-
-def second_kernel(rest, w1_ref, g_ref, o0, o1, o2, o3):
-    for k, n in steps(o0.shape[0]):
-        rows = slice(k * G, (k + n) * G)
-        x = jnp.concatenate([rest[0, rows, :], rest[1, rows, :]], axis=1).reshape(n, G, 4 * G)
-        store_blocks(both_gates(x, w1_ref[...], g_ref[...]), k, (o0, o1, o2, o3))
+        mixed[k * 256 : (k + 1) * 256, :] = x
+        split_rows(k, x, w0, turned)
+
+    store_blocks(both_gates(rows_of(turned, 0, early), w1_ref[...], g_ref[...]), 0, (o0, o1, o2, o3))
+    rest[...] = rows_of(turned, early, HALF // 2)
+
+
+def second_kernel(mixed, rest, w0_ref, w1_ref, g_ref, o0, o1, o2, o3, turned):
+    blocks = (o0, o1, o2, o3)
+    store_blocks(both_gates(rest[...], w1_ref[...], g_ref[...]), 0, blocks)
+    for k in range(G // 8):
+        split_rows(k, mixed[k * 256 : (k + 1) * 256, :], w0_ref[...], turned)
+    made = both_gates(rows_of(turned, 0, HALF // 2), w1_ref[...], g_ref[...])
+    store_blocks(made, rest.shape[0], blocks)
 
 
 def weights_kernel(top, gates, w1_ref, g_ref, w_ref):
@@ -231,7 +247,7 @@
 def gather_rows(first, pair, wide):
     for k in range(pair[0].shape[0]):
         for i in range(2):
-            wide[i, pl.ds(first + k, HALF, stride=HALF), :] = pair[i][k].astype(F32)
+            wide[i, pl.ds(first + k, HALF, stride=NARROW), :] = pair[i][k].astype(F32)
 
 
 def gather_kernel(b0, b1, b2, b3, *wides):
@@ -246,8 +262,9 @@
     start = (own_bits()[3] ^ j) * (o_ref.shape[0] // 2)
     copies = []
     for k in range(HALF // 8):
-        rows = slice(k * 256, (k + 1) * 256)
-        x = jnp.concatenate([wide[i, rows, :] for i in range(2)], axis=1).astype(BF)
+        starts = [(k * 8 + q) * NARROW for q in range(8)]
+        halves = [jnp.concatenate([wide[i, at : at + HALF, :] for at in starts], axis=0) for i in range(2)]
+        x = jnp.concatenate(halves, axis=1).astype(BF)
         r = turned_dot(w_ref[...], x)
         tiles = turn([r[g * HALF : (g + 1) * HALF] for g in range(8)])
         for q in range(8):
@@ -336,20 +353,16 @@
 
     block = jax.ShapeDtypeStruct((HALF - EARLY, HALF, 128), BF)
     early_block = jax.ShapeDtypeStruct((EARLY, HALF, 128), BF)
-    turned = pltpu.VMEM((2, HALF * G, 128), F32)
+    turned = pltpu.VMEM((2, HALF // 2 * PITCH, 128), F32)
     spread = pltpu.VMEM((whole, 128), F32)
     lanes, rows = (4 * G, 8 * G), (G, 2 * G)
 
     x = state.reshape(2, -1, 128).transpose(1, 0, 2).reshape(whole, 128)
-    rest = jax.ShapeDtypeStruct((2, (HALF - EARLY) * G, 128), BF)
-    *early, rest, w1, g = call(
-        first_kernel,
-        [early_block] * 4 + [rest, jax.ShapeDtypeStruct(lanes, BF), jax.ShapeDtypeStruct(rows, BF)],
-        (x, gates),
-        scratch=[spread, turned],
-    )
+    shapes = [(whole // 2, 4 * G), (HALF // 2 - EARLY, G, 4 * G), (2 * G, 4 * G), lanes, rows]
+    shapes = [jax.ShapeDtypeStruct(shape, BF) for shape in shapes]
+    *early, mixed, rest, w0, w1, g = call(first_kernel, [early_block] * 4 + shapes, (x, gates), scratch=[spread, turned])
     early = exchange(early, bits[0], bits[1])
-    late = call(second_kernel, [block] * 4, (rest, w1, g))
+    late = call(second_kernel, [block] * 4, (mixed, rest, w0, w1, g), scratch=[turned])
     late = exchange(late, bits[0], bits[1])
     shapes = [jax.ShapeDtypeStruct(shape, BF) for shape in (lanes, rows, (4 * G, 4 * G))]
     w1, g, w = call(functools.partial(weights_kernel, top if groups == 4 else 0), shapes, (gates,))
@@ -361,7 +374,7 @@
     early = exchange(early, bits[2], bits[3])
     late = exchange(late, bits[2], bits[3])
 
-    wide = jax.ShapeDtypeStruct((2, HALF * HALF, 128), F32)
+    wide = jax.ShapeDtypeStruct((2, HALF * NARROW, 128), F32)
     wides = call(gather_kernel, [wide] * 2, early, flops=COST)
     late = by_place(late)
     scratch = [pltpu.VMEM((whole // 2, 128), F32), pltpu.VMEM((whole // 2, 128), BF), pltpu.SemaphoreType.DMA((HALF // 8,))]

time: 55.5 us -> 53.5 us (0.964)
  Pallas kernels: 13.8 us -> 10.8 us
  waiting for transfers between devices: 16.4 us -> 17.5 us
    pallas_call x10, Pallas kernels: 13.8 us -> 10.8 us  [call(): pl.pallas_call(body, out_shape=outs, in_specs=specs + [ANY] * len(after),...]
    ppermute x6, waiting for transfers between devices: 0.02 us -> 1.37 us  [regrouped(): lax.ppermute(x, 'lo', to)]
  transfers between devices with their start and end apart: 18 -> 18, of which waited for: 8 -> 6; matrix products, arithmetic and copies ran while one was open for 0% -> 0% of each run, Pallas kernels for 14% -> 13%
where the time goes in v7:
time: 53.5 us; the launch traced here: 53.3 us
  starting transfers between devices  22.7 us (42%)
  waiting for transfers between devices  17.5 us (33%)
  Pallas kernels  10.8 us (20%)
  local copies, waits for them, and re-layouts  2.23 us (4%)
    ppermute x12, starting transfers between devices, swapped(): lax.ppermute(x, 'hi', [(d, d ^ apart) for d in range(lax.axis_size('hi'))])  18.5 us
    ppermute x12, waiting for transfers between devices, swapped(): lax.ppermute(x, 'hi', [(d, d ^ apart) for d in range(lax.axis_size('hi'))])  16.1 us
    pallas_call x10, Pallas kernels, call(): pl.pallas_call(body, out_shape=outs, in_specs=specs + [ANY] * len(after),...  10.8 us
    ppermute x6, starting transfers between devices, regrouped(): lax.ppermute(x, 'lo', to)  4.17 us
    unnamed x8, local copies, waits for them, and re-layouts  2.23 us
    ppermute x6, waiting for transfers between devices, regrouped(): lax.ppermute(x, 'lo', to)  1.37 us
  transfers between devices with their start and end apart: 18, of which 6 were waited for; matrix products, arithmetic and copies ran while one was open for 0% of the time, Pallas kernels for 13%

profile of v7, /device:TPU:0, one launch (start us, length us, event | category | flops | bytes accessed | tf_op | source)
XLA Modules:
  0.0 53.3 jit_solution(9414464700022379935)
XLA Ops:
  0.0 1.0 %copy-done = bf16[4,3,2,64,64]{4,3,2,1,0:T(8,128)(2,1)S(1)} copy-done((bf16[4,3,2,64,64]{4,3,2,1,0:T(8,128)(2,1)S(1)}, bf16[4,3,2,64,64]{4,3,2,1,0:T(8,128)(2,1)}, u32[]{:S(2)}) %copy-start) | copy-done | bytes 196632
  1.0 1.2 %copy-done.2 = bf16[2,262144]{1,0:T(2,128)(2,1)S(1)} copy-done((bf16[2,262144]{1,0:T(2,128)(2,1)S(1)}, bf16[2,262144]{1,0:T(2,128)(2,1)}, u32[]{:S(2)}) %copy-start.2) | copy-done | bytes 1048600
  2.2 2.1 %shard_map.37 = (bf16[12,32,128]{2,1,0:T(8,128)(2,1)S(1)}, bf16[12,32,128]{2,1,0:T(8,128)(2,1)S(1)}, bf16[12,32,128]{2,1,0:T(8,128)(2,1)S(1)}, bf16[12,32,128]{2...) custom-call(bf16[4096,128]{1,0:T(8,128)(2,1)S(1)} %bitcast.10, ...), custom_call_target="tpu_custom_call" | custom-call | flops 1 | bytes 1 | tf_op jit(solution)/shard_map/pallas_call | solution.py:307
  4.4 0.0 copy-start.3
  4.4 3.0 %collective-permute-start = (bf16[12,32,128]{2,1,0:T(8,128)(2,1)S(1)}, bf16[12,32,128]{2,1,0:T(8,128)(2,1)S(1)}, u32[]{:S(2)}, u32[]{:S(2)}) collective-permute-start(bf16[12,32,128]{2,1,0:T(8,128)(2,1)S(1)} %get-tuple-element.41), channel_id=1, source_target_pairs={{0,4},{4,0},{8,12},{12,8},{16,20},{20,16},{24,28},{28,24},{1,5},{5... | collective-permute-start | bytes 294920 | tf_op jit(solution)/shard_map/ppermute | solution.py:320
  7.4 1.5 %collective-permute-start.1 = (bf16[12,32,128]{2,1,0:T(8,128)(2,1)S(1)}, bf16[12,32,128]{2,1,0:T(8,128)(2,1)S(1)}, u32[]{:S(2)}, u32[]{:S(2)}) collective-permute-start(bf16[12,32,128]{2,1,0:T(8,128)(2,1)S(1)} %get-tuple-element.42), channel_id=1, source_target_pairs={{0,12},{4,8},{8,4},{12,0},{16,28},{20,24},{24,20},{28,16},{1,13},{... | collective-permute-start | bytes 294920 | tf_op jit(solution)/shard_map/ppermute | solution.py:320
  8.9 0.1 collective-permute-start.2
  9.0 1.5 %shard_map.42 = (bf16[20,32,128]{2,1,0:T(8,128)(2,1)S(1)}, bf16[20,32,128]{2,1,0:T(8,128)(2,1)S(1)}, bf16[20,32,128]{2,1,0:T(8,128)(2,1)S(1)}, bf16[20,32,128]{2,1,0:T(8,128)(2,1)S(1)}) custom-call(bf16[2048,256]{1,0:T(8,128)(2,1)S(1)} %get-tuple-element.56.refs_0_, bf16[4,64,256]{2,1,0:T(8,128)(2,1)S(1)} %get-tuple-element.57.refs_1_, ...), custom_call_target="tpu_custom_call" | custom-call | flops 1 | bytes 1 | tf_op jit(solution)/shard_map/pallas_call | solution.py:307
  10.5 2.0 %collective-permute-start.9 = (bf16[20,32,128]{2,1,0:T(8,128)(2,1)S(1)}, bf16[20,32,128]{2,1,0:T(8,128)(2,1)S(1)}, u32[]{:S(2)}, u32[]{:S(2)}) collective-permute-start(bf16[20,32,128]{2,1,0:T(8,128)(2,1)S(1)} %get-tuple-element.61), channel_id=1, source_target_pairs={{0,4},{4,0},{8,12},{12,8},{16,20},{20,16},{24,28},{28,24},{1,5},{5... | collective-permute-start | bytes 491528 | tf_op jit(solution)/shard_map/ppermute | solution.py:320
  12.5 1.5 %collective-permute-start.10 = (bf16[20,32,128]{2,1,0:T(8,128)(2,1)S(1)}, bf16[20,32,128]{2,1,0:T(8,128)(2,1)S(1)}, u32[]{:S(2)}, u32[]{:S(2)}) collective-permute-start(bf16[20,32,128]{2,1,0:T(8,128)(2,1)S(1)} %get-tuple-element.62), channel_id=1, source_target_pairs={{0,12},{4,8},{8,4},{12,0},{16,28},{20,24},{24,20},{28,16},{1,13},{... | collective-permute-start | bytes 491528 | tf_op jit(solution)/shard_map/ppermute | solution.py:320
  14.0 0.0 collective-permute-done.refs_1_
  14.0 0.1 collective-permute-start.11
  14.0 0.0 collective-permute-done.1.refs_2_
  14.0 0.0 collective-permute-done.2.refs_3_
  14.0 0.0 copy-start.1
  14.1 0.7 %shard_map.38 = (bf16[2,12,16,128]{3,2,1,0:T(8,128)(2,1)S(1)}, bf16[2,12,16,128]{3,2,1,0:T(8,128)(2,1)S(1)}, bf16[2,12,16,128]{3,2,1,0:T(8,128)(2,1)S(1)}, bf16[2,12,16,128]{3,2,1,0:T(8,128)(2,1)S(1)}) custom-call(s32[4]{0:T(128)S(1)} %copy-done.3, bf16[12,32,128]{2,1,0:T(8,128)(2,1)S(1)} %collective-permute-done.refs_1_, ...), custom_call_target="tpu_custom_call" | custom-call | flops 2000000000 | bytes 1 | tf_op jit(solution)/shard_map/pallas_call | solution.py:307
  14.7 1.9 %collective-permute-start.3 = (bf16[2,12,16,128]{3,2,1,0:T(8,128)(2,1)S(1)}, bf16[2,12,16,128]{3,2,1,0:T(8,128)(2,1)S(1)}, u32[]{:S(2)}, u32[]{:S(2)}) collective-permute-start(bf16[2,12,16,128]{3,2,1,0:T(8,128)(2,1)S(1)} %get-tuple-element.45), channel_id=1, source_target_pairs={{0,2},{1,3},{2,0},{3,1},{4,6},{5,7},{6,4},{7,5},{8,10},{9,11},{10,... | collective-permute-start | bytes 294920 | tf_op jit(solution)/shard_map/ppermute | solution.py:337
  16.7 0.0 collective-permute-start.4
  16.7 3.3 %collective-permute-done.9.refs_1_ = bf16[20,32,128]{2,1,0:T(8,128)(2,1)S(1)} collective-permute-done((bf16[20,32,128]{2,1,0:T(8,128)(2,1)S(1)}, bf16[20,32,128]{2,1,0:T(8,128)(2,1)S(1)}, u32[]{:S(2)}, u32[]{:S(2)}) %collective-permute-start.9) | collective-permute-done | bytes 163872 | tf_op jit(solution)/shard_map/ppermute | solution.py:320
  19.9 0.9 %shard_map.39 = (bf16[256,512]{1,0:T(8,128)(2,1)S(1)}, bf16[64,128]{1,0:T(8,128)(2,1)S(1)}, bf16[256,256]{1,0:T(8,128)(2,1)S(1)}) custom-call(bf16[4,3,2,64,64]{4,3,2,1,0:T(8,128)(2,1)S(1)} %copy-done.1), custom_call_target="tpu_custom_call" | custom-call | flops 1 | bytes 1 | tf_op jit(solution)/shard_map/pallas_call | solution.py:307
  20.8 0.0 collective-permute-done.10.refs_2_
  20.8 0.0 collective-permute-done.11.refs_3_
  20.8 0.7 %shard_map.43 = (bf16[2,20,16,128]{3,2,1,0:T(8,128)(2,1)S(1)}, bf16[2,20,16,128]{3,2,1,0:T(8,128)(2,1)S(1)}, bf16[2,20,16,128]{3,2,1,0:T(8,128)(2,1)S(1)}, bf16[2,20,16,128]{3,2,1,0:T(8,128)(2,1)S(1)}) custom-call(s32[4]{0:T(128)S(1)} %copy-done.3, bf16[20,32,128]{2,1,0:T(8,128)(2,1)S(1)} %collective-permute-done.9.refs_1_, ...), custom_call_target="tpu_custom_call" | custom-call | flops 1 | bytes 1 | tf_op jit(solution)/shard_map/pallas_call | solution.py:307
  21.6 1.9 %collective-permute-start.12 = (bf16[2,20,16,128]{3,2,1,0:T(8,128)(2,1)S(1)}, bf16[2,20,16,128]{3,2,1,0:T(8,128)(2,1)S(1)}, u32[]{:S(2)}, u32[]{:S(2)}) collective-permute-start(bf16[2,20,16,128]{3,2,1,0:T(8,128)(2,1)S(1)} %get-tuple-element.65), channel_id=1, source_target_pairs={{0,2},{1,3},{2,0},{3,1},{4,6},{5,7},{6,4},{7,5},{8,10},{9,11},{10,... | collective-permute-start | bytes 491528 | tf_op jit(solution)/shard_map/ppermute | solution.py:337
  23.5 0.2 collective-permute-start.13
  23.7 0.1 collective-permute-start.14
  23.8 0.0 collective-permute-done.4.refs_1_
  23.8 0.0 collective-permute-done.5.refs_2_
  23.8 0.5 shard_map.40
  24.3 3.0 %collective-permute-start.6 = (bf16[12,32,128]{2,1,0:T(8,128)(2,1)S(1)}, bf16[12,32,128]{2,1,0:T(8,128)(2,1)S(1)}, u32[]{:S(2)}, u32[]{:S(2)}) collective-permute-start(bf16[12,32,128]{2,1,0:T(8,128)(2,1)S(1)} %get-tuple-element.51), channel_id=1, source_target_pairs={{0,16},{4,20},{8,24},{12,28},{16,0},{20,4},{24,8},{28,12},{1,17},{... | collective-permute-start | bytes 294920 | tf_op jit(solution)/shard_map/ppermute | solution.py:320
  27.3 1.1 %collective-permute-start.7 = (bf16[12,32,128]{2,1,0:T(8,128)(2,1)S(1)}, bf16[12,32,128]{2,1,0:T(8,128)(2,1)S(1)}, u32[]{:S(2)}, u32[]{:S(2)}) collective-permute-start(bf16[12,32,128]{2,1,0:T(8,128)(2,1)S(1)} %get-tuple-element.52), channel_id=1, source_target_pairs={{0,20},{4,16},{8,28},{12,24},{16,4},{20,0},{24,12},{28,8},{1,21},{... | collective-permute-start | bytes 294920 | tf_op jit(solution)/shard_map/ppermute | solution.py:320
  28.4 0.2 collective-permute-done.12.refs_0_
  28.6 1.8 %collective-permute-start.8 = (bf16[12,32,128]{2,1,0:T(8,128)(2,1)S(1)}, bf16[12,32,128]{2,1,0:T(8,128)(2,1)S(1)}, u32[]{:S(2)}, u32[]{:S(2)}) collective-permute-start(bf16[12,32,128]{2,1,0:T(8,128)(2,1)S(1)} %get-tuple-element.53), channel_id=1, source_target_pairs={{0,4},{4,0},{8,12},{12,8},{16,20},{20,16},{24,28},{28,24},{1,5},{5... | collective-permute-start | bytes 294920 | tf_op jit(solution)/shard_map/ppermute | solution.py:320
  30.4 1.2 %collective-permute-done.13.refs_1_ = bf16[2,20,16,128]{3,2,1,0:T(8,128)(2,1)S(1)} collective-permute-done((bf16[2,20,16,128]{3,2,1,0:T(8,128)(2,1)S(1)}, bf16[2,20,16,128]{3,2,1,0:T(8,128)(2,1)S(1)}, u32[]{:S(2)}, u32[]{:S(2)}) %collective-permute-start.13) | collective-permute-done | bytes 163872 | tf_op jit(solution)/shard_map/ppermute | solution.py:337
  31.6 0.0 collective-permute-done.14.refs_2_
  31.6 0.7 %shard_map.44 = (bf16[20,32,128]{2,1,0:T(8,128)(2,1)S(1)}, bf16[20,32,128]{2,1,0:T(8,128)(2,1)S(1)}, bf16[20,32,128]{2,1,0:T(8,128)(2,1)S(1)}, bf16[20,32,128]{2,1,0:T(8,128)(2,1)S(1)}) custom-call(bf16[2,20,16,128]{3,2,1,0:T(8,128)(2,1)S(1)} %collective-permute-done.12.refs_0_, bf16[2,20,16,128]{3,2,1,0:T(8,128)(2,1)S(1)} %collective-permute-done.13.refs_1_, ...), custom_call_target="tpu_custom_call" | custom-call | flops 1 | bytes 1 | tf_op jit(solution)/shard_map/pallas_call | solution.py:307
  32.2 2.8 %collective-permute-start.15 = (bf16[20,32,128]{2,1,0:T(8,128)(2,1)S(1)}, bf16[20,32,128]{2,1,0:T(8,128)(2,1)S(1)}, u32[]{:S(2)}, u32[]{:S(2)}) collective-permute-start(bf16[20,32,128]{2,1,0:T(8,128)(2,1)S(1)} %get-tuple-element.69), channel_id=1, source_target_pairs={{0,16},{4,20},{8,24},{12,28},{16,0},{20,4},{24,8},{28,12},{1,17},{... | collective-permute-start | bytes 491528 | tf_op jit(solution)/shard_map/ppermute | solution.py:320
  35.1 0.2 collective-permute-start.16
  35.2 0.0 collective-permute-done.6.refs_0_
  35.2 1.5 %collective-permute-start.17 = (bf16[20,32,128]{2,1,0:T(8,128)(2,1)S(1)}, bf16[20,32,128]{2,1,0:T(8,128)(2,1)S(1)}, u32[]{:S(2)}, u32[]{:S(2)}) collective-permute-start(bf16[20,32,128]{2,1,0:T(8,128)(2,1)S(1)} %get-tuple-element.75), channel_id=1, source_target_pairs={{0,4},{4,0},{8,12},{12,8},{16,20},{20,16},{24,28},{28,24},{1,5},{5... | collective-permute-start | bytes 491528 | tf_op jit(solution)/shard_map/ppermute | solution.py:320
  36.7 8.2 %collective-permute-done.7.refs_1_ = bf16[12,32,128]{2,1,0:T(8,128)(2,1)S(1)} collective-permute-done((bf16[12,32,128]{2,1,0:T(8,128)(2,1)S(1)}, bf16[12,32,128]{2,1,0:T(8,128)(2,1)S(1)}, u32[]{:S(2)}, u32[]{:S(2)}) %collective-permute-start.7) | collective-permute-done | bytes 98336 | tf_op jit(solution)/shard_map/ppermute | solution.py:320
  45.0 0.0 collective-permute-done.8.refs_2_
  45.0 0.1 shard_map.41
  45.0 2.7 %collective-permute-done.15.refs_1_ = bf16[20,32,128]{2,1,0:T(8,128)(2,1)S(1)} collective-permute-done((bf16[20,32,128]{2,1,0:T(8,128)(2,1)S(1)}, bf16[20,32,128]{2,1,0:T(8,128)(2,1)S(1)}, u32[]{:S(2)}, u32[]{:S(2)}) %collective-permute-start.15) | collective-permute-done | bytes 163872 | tf_op jit(solution)/shard_map/ppermute | solution.py:320
  47.7 1.8 %shard_map.45 = (bf16[4096,128]{1,0:T(8,128)(2,1)}, f32[2,1056,128]{2,1,0:T(8,128)S(1)}) custom-call(f32[2,1056,128]{2,1,0:T(8,128)S(1)} %get-tuple-element.55.refs_0_, bf16[20,32,128]{2,1,0:T(8,128)(2,1)S(1)} %collective-permute-done.15.refs_1_, bf16[20,32,128]{2,1,0:T(8,128)(2,1)S(1)} %get-tuple-element.70.refs_2_, ...), custom_call_target="tpu_custom_call", output_to_operand_aliasing={{1}: (0, {})} | custom-call | flops 1 | bytes 1 | tf_op jit(solution)/shard_map/pallas_call | solution.py:307
  49.6 1.9 %collective-permute-done.16.refs_2_ = bf16[20,32,128]{2,1,0:T(8,128)(2,1)S(1)} collective-permute-done((bf16[20,32,128]{2,1,0:T(8,128)(2,1)S(1)}, bf16[20,32,128]{2,1,0:T(8,128)(2,1)S(1)}, u32[]{:S(2)}, u32[]{:S(2)}) %collective-permute-start.16) | collective-permute-done | bytes 163872 | tf_op jit(solution)/shard_map/ppermute | solution.py:320
  51.5 0.0 collective-permute-done.17.refs_3_
  51.5 1.8 %shard_map.46 = (bf16[4096,128]{1,0:T(8,128)(2,1)}, f32[2,1056,128]{2,1,0:T(8,128)S(1)}) custom-call(bf16[4096,128]{1,0:T(8,128)(2,1)} %get-tuple-element.72.refs_0_, f32[2,1056,128]{2,1,0:T(8,128)S(1)} %get-tuple-element.73.refs_1_, bf16[20,32,128]{2,1,0:T(8,128)(2,1)S(1)} %collective-permute-done.16.refs_2_, ...), custom_call_target="tpu_custom_call", output_to_operand_aliasing={{0}: (0, {}), {1}: (1, {})} | custom-call | flops 1 | bytes 1 | tf_op jit(solution)/shard_map/pallas_call | solution.py:307
  (6 shorter events, 0.0 us)
Async XLA Ops:
  0.0 1.0 %copy-start = (bf16[4,3,2,64,64]{4,3,2,1,0:T(8,128)(2,1)S(1)}, bf16[4,3,2,64,64]{4,3,2,1,0:T(8,128)(2,1)}, u32[]{:S(2)}) copy-start(bf16[4,3,2,64,64]{4,3,2,1,0:T(8,128)(2,1)} %refs_0_.4) | copy-start | bytes 589828
  1.0 1.2 %copy-start.2 = (bf16[2,262144]{1,0:T(2,128)(2,1)S(1)}, bf16[2,262144]{1,0:T(2,128)(2,1)}, u32[]{:S(2)}) copy-start(bf16[2,262144]{1,0:T(2,128)(2,1)} %param.3) | copy-start | bytes 3145732
  4.4 9.7 %copy-start.3 = (s32[4]{0:T(128)S(1)}, s32[4]{0:T(128)}, u32[]{:S(2)}) copy-start(s32[4]{0:T(128)} %refs_0_.5) | copy-start | bytes 52
  4.4 9.6 %collective-permute-start = (bf16[12,32,128]{2,1,0:T(8,128)(2,1)S(1)}, bf16[12,32,128]{2,1,0:T(8,128)(2,1)S(1)}, u32[]{:S(2)}, u32[]{:S(2)}) collective-permute-start(bf16[12,32,128]{2,1,0:T(8,128)(2,1)S(1)} %get-tuple-element.41), channel_id=1, source_target_pairs={{0,4},{4,0},{8,12},{12,8},{16,20},{20,16},{24,28},{28,24},{1,5},{5... | collective-permute-start | bytes 294920 | tf_op jit(solution)/shard_map/ppermute | solution.py:320
  7.4 6.6 %collective-permute-start.1 = (bf16[12,32,128]{2,1,0:T(8,128)(2,1)S(1)}, bf16[12,32,128]{2,1,0:T(8,128)(2,1)S(1)}, u32[]{:S(2)}, u32[]{:S(2)}) collective-permute-start(bf16[12,32,128]{2,1,0:T(8,128)(2,1)S(1)} %get-tuple-element.42), channel_id=1, source_target_pairs={{0,12},{4,8},{8,4},{12,0},{16,28},{20,24},{24,20},{28,16},{1,13},{... | collective-permute-start | bytes 294920 | tf_op jit(solution)/shard_map/ppermute | solution.py:320
  8.9 5.1 %collective-permute-start.2 = (bf16[12,32,128]{2,1,0:T(8,128)(2,1)S(1)}, bf16[12,32,128]{2,1,0:T(8,128)(2,1)S(1)}, u32[]{:S(2)}, u32[]{:S(2)}) collective-permute-start(bf16[12,32,128]{2,1,0:T(8,128)(2,1)S(1)} %get-tuple-element.43), channel_id=1, source_target_pairs={{0,8},{4,12},{8,0},{12,4},{16,24},{20,28},{24,16},{28,20},{1,9},{5... | collective-permute-start | bytes 294920 | tf_op jit(solution)/shard_map/ppermute | solution.py:320
  10.5 9.5 %collective-permute-start.9 = (bf16[20,32,128]{2,1,0:T(8,128)(2,1)S(1)}, bf16[20,32,128]{2,1,0:T(8,128)(2,1)S(1)}, u32[]{:S(2)}, u32[]{:S(2)}) collective-permute-start(bf16[20,32,128]{2,1,0:T(8,128)(2,1)S(1)} %get-tuple-element.61), channel_id=1, source_target_pairs={{0,4},{4,0},{8,12},{12,8},{16,20},{20,16},{24,28},{28,24},{1,5},{5... | collective-permute-start | bytes 491528 | tf_op jit(solution)/shard_map/ppermute | solution.py:320
  12.5 8.4 %collective-permute-start.10 = (bf16[20,32,128]{2,1,0:T(8,128)(2,1)S(1)}, bf16[20,32,128]{2,1,0:T(8,128)(2,1)S(1)}, u32[]{:S(2)}, u32[]{:S(2)}) collective-permute-start(bf16[20,32,128]{2,1,0:T(8,128)(2,1)S(1)} %get-tuple-element.62), channel_id=1, source_target_pairs={{0,12},{4,8},{8,4},{12,0},{16,28},{20,24},{24,20},{28,16},{1,13},{... | collective-permute-start | bytes 491528 | tf_op jit(solution)/shard_map/ppermute | solution.py:320
  14.0 6.9 %collective-permute-start.11 = (bf16[20,32,128]{2,1,0:T(8,128)(2,1)S(1)}, bf16[20,32,128]{2,1,0:T(8,128)(2,1)S(1)}, u32[]{:S(2)}, u32[]{:S(2)}) collective-permute-start(bf16[20,32,128]{2,1,0:T(8,128)(2,1)S(1)} %get-tuple-element.63), channel_id=1, source_target_pairs={{0,8},{4,12},{8,0},{12,4},{16,24},{20,28},{24,16},{28,20},{1,9},{5... | collective-permute-start | bytes 491528 | tf_op jit(solution)/shard_map/ppermute | solution.py:320
  14.0 5.9 %copy-start.1 = (bf16[4,3,2,64,64]{4,3,2,1,0:T(8,128)(2,1)S(1)}, bf16[4,3,2,64,64]{4,3,2,1,0:T(8,128)(2,1)}, u32[]{:S(2)}) copy-start(bf16[4,3,2,64,64]{4,3,2,1,0:T(8,128)(2,1)} %refs_0_.4) | copy-start | bytes 589828
  14.7 8.9 %collective-permute-start.3 = (bf16[2,12,16,128]{3,2,1,0:T(8,128)(2,1)S(1)}, bf16[2,12,16,128]{3,2,1,0:T(8,128)(2,1)S(1)}, u32[]{:S(2)}, u32[]{:S(2)}) collective-permute-start(bf16[2,12,16,128]{3,2,1,0:T(8,128)(2,1)S(1)} %get-tuple-element.45), channel_id=1, source_target_pairs={{0,2},{1,3},{2,0},{3,1},{4,6},{5,7},{6,4},{7,5},{8,10},{9,11},{10,... | collective-permute-start | bytes 294920 | tf_op jit(solution)/shard_map/ppermute | solution.py:337
  16.7 7.2 %collective-permute-start.4 = (bf16[2,12,16,128]{3,2,1,0:T(8,128)(2,1)S(1)}, bf16[2,12,16,128]{3,2,1,0:T(8,128)(2,1)S(1)}, u32[]{:S(2)}, u32[]{:S(2)}) collective-permute-start(bf16[2,12,16,128]{3,2,1,0:T(8,128)(2,1)S(1)} %get-tuple-element.46), channel_id=1, source_target_pairs={{0,3},{1,2},{2,1},{3,0},{4,7},{5,6},{6,5},{7,4},{8,11},{9,10},{10,... | collective-permute-start | bytes 294920 | tf_op jit(solution)/shard_map/ppermute | solution.py:337
  19.9 3.9 %collective-permute-start.5 = (bf16[2,12,16,128]{3,2,1,0:T(8,128)(2,1)S(1)}, bf16[2,12,16,128]{3,2,1,0:T(8,128)(2,1)S(1)}, u32[]{:S(2)}, u32[]{:S(2)}) collective-permute-start(bf16[2,12,16,128]{3,2,1,0:T(8,128)(2,1)S(1)} %get-tuple-element.47), channel_id=1, source_target_pairs={{0,1},{1,0},{2,3},{3,2},{4,5},{5,4},{6,7},{7,6},{8,9},{9,8},{10,11... | collective-permute-start | bytes 294920 | tf_op jit(solution)/shard_map/ppermute | solution.py:337
  21.6 7.0 %collective-permute-start.12 = (bf16[2,20,16,128]{3,2,1,0:T(8,128)(2,1)S(1)}, bf16[2,20,16,128]{3,2,1,0:T(8,128)(2,1)S(1)}, u32[]{:S(2)}, u32[]{:S(2)}) collective-permute-start(bf16[2,20,16,128]{3,2,1,0:T(8,128)(2,1)S(1)} %get-tuple-element.65), channel_id=1, source_target_pairs={{0,2},{1,3},{2,0},{3,1},{4,6},{5,7},{6,4},{7,5},{8,10},{9,11},{10,... | collective-permute-start | bytes 491528 | tf_op jit(solution)/shard_map/ppermute | solution.py:337
  23.5 8.1 %collective-permute-start.13 = (bf16[2,20,16,128]{3,2,1,0:T(8,128)(2,1)S(1)}, bf16[2,20,16,128]{3,2,1,0:T(8,128)(2,1)S(1)}, u32[]{:S(2)}, u32[]{:S(2)}) collective-permute-start(bf16[2,20,16,128]{3,2,1,0:T(8,128)(2,1)S(1)} %get-tuple-element.66), channel_id=1, source_target_pairs={{0,3},{1,2},{2,1},{3,0},{4,7},{5,6},{6,5},{7,4},{8,11},{9,10},{10,... | collective-permute-start | bytes 491528 | tf_op jit(solution)/shard_map/ppermute | solution.py:337
  23.7 7.9 %collective-permute-start.14 = (bf16[2,20,16,128]{3,2,1,0:T(8,128)(2,1)S(1)}, bf16[2,20,16,128]{3,2,1,0:T(8,128)(2,1)S(1)}, u32[]{:S(2)}, u32[]{:S(2)}) collective-permute-start(bf16[2,20,16,128]{3,2,1,0:T(8,128)(2,1)S(1)} %get-tuple-element.67), channel_id=1, source_target_pairs={{0,1},{1,0},{2,3},{3,2},{4,5},{5,4},{6,7},{7,6},{8,9},{9,8},{10,11... | collective-permute-start | bytes 491528 | tf_op jit(solution)/shard_map/ppermute | solution.py:337
  24.3 10.9 %collective-permute-start.6 = (bf16[12,32,128]{2,1,0:T(8,128)(2,1)S(1)}, bf16[12,32,128]{2,1,0:T(8,128)(2,1)S(1)}, u32[]{:S(2)}, u32[]{:S(2)}) collective-permute-start(bf16[12,32,128]{2,1,0:T(8,128)(2,1)S(1)} %get-tuple-element.51), channel_id=1, source_target_pairs={{0,16},{4,20},{8,24},{12,28},{16,0},{20,4},{24,8},{28,12},{1,17},{... | collective-permute-start | bytes 294920 | tf_op jit(solution)/shard_map/ppermute | solution.py:320
  27.3 17.7 %collective-permute-start.7 = (bf16[12,32,128]{2,1,0:T(8,128)(2,1)S(1)}, bf16[12,32,128]{2,1,0:T(8,128)(2,1)S(1)}, u32[]{:S(2)}, u32[]{:S(2)}) collective-permute-start(bf16[12,32,128]{2,1,0:T(8,128)(2,1)S(1)} %get-tuple-element.52), channel_id=1, source_target_pairs={{0,20},{4,16},{8,28},{12,24},{16,4},{20,0},{24,12},{28,8},{1,21},{... | collective-permute-start | bytes 294920 | tf_op jit(solution)/shard_map/ppermute | solution.py:320
  28.6 16.3 %collective-permute-start.8 = (bf16[12,32,128]{2,1,0:T(8,128)(2,1)S(1)}, bf16[12,32,128]{2,1,0:T(8,128)(2,1)S(1)}, u32[]{:S(2)}, u32[]{:S(2)}) collective-permute-start(bf16[12,32,128]{2,1,0:T(8,128)(2,1)S(1)} %get-tuple-element.53), channel_id=1, source_target_pairs={{0,4},{4,0},{8,12},{12,8},{16,20},{20,16},{24,28},{28,24},{1,5},{5... | collective-permute-start | bytes 294920 | tf_op jit(solution)/shard_map/ppermute | solution.py:320
  32.2 15.5 %collective-permute-start.15 = (bf16[20,32,128]{2,1,0:T(8,128)(2,1)S(1)}, bf16[20,32,128]{2,1,0:T(8,128)(2,1)S(1)}, u32[]{:S(2)}, u32[]{:S(2)}) collective-permute-start(bf16[20,32,128]{2,1,0:T(8,128)(2,1)S(1)} %get-tuple-element.69), channel_id=1, source_target_pairs={{0,16},{4,20},{8,24},{12,28},{16,0},{20,4},{24,8},{28,12},{1,17},{... | collective-permute-start | bytes 491528 | tf_op jit(solution)/shard_map/ppermute | solution.py:320
  35.1 16.4 %collective-permute-start.16 = (bf16[20,32,128]{2,1,0:T(8,128)(2,1)S(1)}, bf16[20,32,128]{2,1,0:T(8,128)(2,1)S(1)}, u32[]{:S(2)}, u32[]{:S(2)}) collective-permute-start(bf16[20,32,128]{2,1,0:T(8,128)(2,1)S(1)} %get-tuple-element.74), channel_id=1, source_target_pairs={{0,20},{4,16},{8,28},{12,24},{16,4},{20,0},{24,12},{28,8},{1,21},{... | collective-permute-start | bytes 491528 | tf_op jit(solution)/shard_map/ppermute | solution.py:320
  35.2 16.2 %collective-permute-start.17 = (bf16[20,32,128]{2,1,0:T(8,128)(2,1)S(1)}, bf16[20,32,128]{2,1,0:T(8,128)(2,1)S(1)}, u32[]{:S(2)}, u32[]{:S(2)}) collective-permute-start(bf16[20,32,128]{2,1,0:T(8,128)(2,1)S(1)} %get-tuple-element.75), channel_id=1, source_target_pairs={{0,4},{4,0},{8,12},{12,8},{16,20},{20,16},{24,28},{28,24},{1,5},{5... | collective-permute-start | bytes 491528 | tf_op jit(solution)/shard_map/ppermute | solution.py:320

commit v8 on v7

--- a/solution.py
+++ b/solution.py
@@ -164,7 +164,7 @@
 STEP = 22
 PITCH = G + 1
 NARROW = HALF + 1
-EARLY = 12
+EARLY = 13
 COST = 2 * 10**9
 
 
@@ -181,12 +181,12 @@
 
 
 def split_rows(k, x, w, turned):
-    r = turned_dot(w, x)
+    r = turned_dot(w, x).astype(BF)
     some = HALF // 2
     tiles = turn([r[g * some : (g + 1) * some] for g in range(8)])
     for q in range(8):
         for n in range(2):
-            turned[n, pl.ds(k * 8 + q, some, stride=PITCH), :] = tiles[q][n]
+            turned[n, pl.ds(k * 8 + q, some, stride=PITCH), :] = tiles[q][n].astype(F32)
 
 
 def rows_of(turned, first, last):
@@ -215,21 +215,22 @@
     rest[...] = rows_of(turned, early, HALF // 2)
 
 
-def second_kernel(mixed, rest, w0_ref, w1_ref, g_ref, o0, o1, o2, o3, turned):
-    blocks = (o0, o1, o2, o3)
+def later_weights(top, gates, w1_ref, g_ref, w_ref):
+    own = own_bits()
+    w1_ref[...] = right_weights(product(gate_of(gates, 2, 1), gate_of(gates, 1, 1)), False, own[0], own[2])
+    step = top * lax.axis_index("lo") if top else 0
+    g_ref[...] = left_weights(product(gate_of(gates, 3, 2), gate_of(gates, 2, 2)), step, own[3])
+    w_ref[...] = last_weights(gate_of(gates, 3, 1), own[2])
+
+
+def second_kernel(top, mixed, rest, w0_ref, w1_ref, g_ref, gates, *refs):
+    *blocks, turned = refs[:4] + refs[7:]
+    later_weights(top, gates, *refs[4:7])
     store_blocks(both_gates(rest[...], w1_ref[...], g_ref[...]), 0, blocks)
     for k in range(G // 8):
         split_rows(k, mixed[k * 256 : (k + 1) * 256, :], w0_ref[...], turned)
     made = both_gates(rows_of(turned, 0, HALF // 2), w1_ref[...], g_ref[...])
     store_blocks(made, rest.shape[0], blocks)
-
-
-def weights_kernel(top, gates, w1_ref, g_ref, w_ref):
-    own = own_bits()
-    w1_ref[...] = right_weights(product(gate_of(gates, 2, 1), gate_of(gates, 1, 1)), False, own[0], own[2])
-    step = top * lax.axis_index("lo") if top else 0
-    g_ref[...] = left_weights(product(gate_of(gates, 3, 2), gate_of(gates, 2, 2)), step, own[3])
-    w_ref[...] = last_weights(gate_of(gates, 3, 1), own[2])
 
 
 def joined(ins, k, n):
@@ -265,11 +266,11 @@
         starts = [(k * 8 + q) * NARROW for q in range(8)]
         halves = [jnp.concatenate([wide[i, at : at + HALF, :] for at in starts], axis=0) for i in range(2)]
         x = jnp.concatenate(halves, axis=1).astype(BF)
-        r = turned_dot(w_ref[...], x)
+        r = turned_dot(w_ref[...], x).astype(BF)
         tiles = turn([r[g * HALF : (g + 1) * HALF] for g in range(8)])
         for q in range(8):
             for n in range(2):
-                spread[pl.ds((k * 8 + q) * G + n, HALF, stride=2), :] = tiles[q][n]
+                spread[pl.ds((k * 8 + q) * G + n, HALF, stride=2), :] = tiles[q][n].astype(F32)
         rows = slice(k * 512, (k + 1) * 512)
         made[rows, :] = spread[rows, :].astype(BF)
         to = pl.ds(pl.multiple_of(start + k * 512, 512), 512)
@@ -362,11 +363,10 @@
     shapes = [jax.ShapeDtypeStruct(shape, BF) for shape in shapes]
     *early, mixed, rest, w0, w1, g = call(first_kernel, [early_block] * 4 + shapes, (x, gates), scratch=[spread, turned])
     early = exchange(early, bits[0], bits[1])
-    late = call(second_kernel, [block] * 4, (mixed, rest, w0, w1, g), scratch=[turned])
+    shapes = [jax.ShapeDtypeStruct(shape, BF) for shape in (lanes, rows, (4 * G, 4 * G))]
+    kernel = functools.partial(second_kernel, top if groups == 4 else 0)
+    *late, w1, g, w = call(kernel, [block] * 4 + shapes, (mixed, rest, w0, w1, g, gates), scratch=[turned])
     late = exchange(late, bits[0], bits[1])
-    shapes = [jax.ShapeDtypeStruct(shape, BF) for shape in (lanes, rows, (4 * G, 4 * G))]
-    w1, g, w = call(functools.partial(weights_kernel, top if groups == 4 else 0), shapes, (gates,))
-
     early = regrouped(early, regroup, bits[1], groups, top, COST)
     late = regrouped(late, regroup, bits[1], groups, top, after=early[3:])
     early = call(middle_kernel, [early_block] * 4, (*early, w1, g), flops=COST)

time: 53.5 us -> 53 us (level)
  starting transfers between devices: 22.7 us -> 27.2 us
  waiting for transfers between devices: 17.5 us -> 13.8 us
  Pallas kernels: 10.8 us -> 9.49 us
    ppermute x12, starting transfers between devices: 18.5 us -> 23.1 us  [swapped(): lax.ppermute(x, 'hi', [(d, d ^ apart) for d in range(lax.axis_size('hi'))])]
    ppermute x12, waiting for transfers between devices: 16.1 us -> 13.5 us  [swapped(): lax.ppermute(x, 'hi', [(d, d ^ apart) for d in range(lax.axis_size('hi'))])]
    pallas_call x10 -> x9, Pallas kernels: 10.8 us -> 9.49 us  [call(): pl.pallas_call(body, out_shape=outs, in_specs=specs + [ANY] * len(after),...]
    ppermute x6, waiting for transfers between devices: 1.37 us -> 0.29 us  [regrouped(): lax.ppermute(x, 'lo', to)]
  transfers between devices with their start and end apart: 18 -> 18, of which waited for: 6 -> 8; matrix products, arithmetic and copies ran while one was open for 0% -> 0% of each run, Pallas kernels for 13% -> 12%
where the time goes in v8:
time: 53 us; the launch traced here: 52.8 us
  starting transfers between devices  27.2 us (51%)
  waiting for transfers between devices  13.8 us (26%)
  Pallas kernels  9.49 us (18%)
  local copies, waits for them, and re-layouts  2.23 us (4%)
    ppermute x12, starting transfers between devices, swapped(): lax.ppermute(x, 'hi', [(d, d ^ apart) for d in range(lax.axis_size('hi'))])  23.1 us
    ppermute x12, waiting for transfers between devices, swapped(): lax.ppermute(x, 'hi', [(d, d ^ apart) for d in range(lax.axis_size('hi'))])  13.5 us
    pallas_call x9, Pallas kernels, call(): pl.pallas_call(body, out_shape=outs, in_specs=specs + [ANY] * len(after),...  9.49 us
    ppermute x6, starting transfers between devices, regrouped(): lax.ppermute(x, 'lo', to)  4.15 us
    unnamed x8, local copies, waits for them, and re-layouts  2.23 us
  transfers between devices with their start and end apart: 18, of which 8 were waited for; matrix products, arithmetic and copies ran while one was open for 0% of the time, Pallas kernels for 12%

profile of v8, /device:TPU:0, one launch (start us, length us, event | category | flops | bytes accessed | tf_op | source)
XLA Modules:
  0.0 52.8 jit_solution(9725370524881475834)
XLA Ops:
  0.0 1.0 %copy-done = bf16[4,3,2,64,64]{4,3,2,1,0:T(8,128)(2,1)S(1)} copy-done((bf16[4,3,2,64,64]{4,3,2,1,0:T(8,128)(2,1)S(1)}, bf16[4,3,2,64,64]{4,3,2,1,0:T(8,128)(2,1)}, u32[]{:S(2)}) %copy-start) | copy-done | bytes 196632
  1.0 1.2 %copy-done.2 = bf16[2,262144]{1,0:T(2,128)(2,1)S(1)} copy-done((bf16[2,262144]{1,0:T(2,128)(2,1)S(1)}, bf16[2,262144]{1,0:T(2,128)(2,1)}, u32[]{:S(2)}) %copy-start.2) | copy-done | bytes 1048600
  2.2 2.0 %shard_map.37 = (bf16[13,32,128]{2,1,0:T(8,128)(2,1)S(1)}, bf16[13,32,128]{2,1,0:T(8,128)(2,1)S(1)}, bf16[13,32,128]{2,1,0:T(8,128)(2,1)S(1)}, bf16[13,32,128]{2...) custom-call(bf16[4096,128]{1,0:T(8,128)(2,1)S(1)} %bitcast.10, ...), custom_call_target="tpu_custom_call" | custom-call | flops 1 | bytes 1 | tf_op jit(solution)/shard_map/pallas_call | solution.py:308
  4.2 0.0 copy-start.3
  4.2 3.0 %collective-permute-start = (bf16[13,32,128]{2,1,0:T(8,128)(2,1)S(1)}, bf16[13,32,128]{2,1,0:T(8,128)(2,1)S(1)}, u32[]{:S(2)}, u32[]{:S(2)}) collective-permute-start(bf16[13,32,128]{2,1,0:T(8,128)(2,1)S(1)} %get-tuple-element.41), channel_id=1, source_target_pairs={{0,4},{4,0},{8,12},{12,8},{16,20},{20,16},{24,28},{28,24},{1,5},{5... | collective-permute-start | bytes 319496 | tf_op jit(solution)/shard_map/ppermute | solution.py:321
  7.3 1.5 %collective-permute-start.1 = (bf16[13,32,128]{2,1,0:T(8,128)(2,1)S(1)}, bf16[13,32,128]{2,1,0:T(8,128)(2,1)S(1)}, u32[]{:S(2)}, u32[]{:S(2)}) collective-permute-start(bf16[13,32,128]{2,1,0:T(8,128)(2,1)S(1)} %get-tuple-element.42), channel_id=1, source_target_pairs={{0,12},{4,8},{8,4},{12,0},{16,28},{20,24},{24,20},{28,16},{1,13},{... | collective-permute-start | bytes 319496 | tf_op jit(solution)/shard_map/ppermute | solution.py:321
  8.8 0.1 collective-permute-start.2
  8.9 2.1 %shard_map.39 = (bf16[19,32,128]{2,1,0:T(8,128)(2,1)S(1)}, bf16[19,32,128]{2,1,0:T(8,128)(2,1)S(1)}, bf16[19,32,128]{2,1,0:T(8,128)(2,1)S(1)}, bf16[19,32,128]{2...) custom-call(bf16[2048,256]{1,0:T(8,128)(2,1)S(1)} %get-tuple-element, ...), custom_call_target="tpu_custom_call" | custom-call | flops 1 | bytes 1 | tf_op jit(solution)/shard_map/pallas_call | solution.py:308
  11.0 2.0 %collective-permute-start.9 = (bf16[19,32,128]{2,1,0:T(8,128)(2,1)S(1)}, bf16[19,32,128]{2,1,0:T(8,128)(2,1)S(1)}, u32[]{:S(2)}, u32[]{:S(2)}) collective-permute-start(bf16[19,32,128]{2,1,0:T(8,128)(2,1)S(1)} %get-tuple-element.61), channel_id=1, source_target_pairs={{0,4},{4,0},{8,12},{12,8},{16,20},{20,16},{24,28},{28,24},{1,5},{5... | collective-permute-start | bytes 466952 | tf_op jit(solution)/shard_map/ppermute | solution.py:321
  13.0 1.5 %collective-permute-start.10 = (bf16[19,32,128]{2,1,0:T(8,128)(2,1)S(1)}, bf16[19,32,128]{2,1,0:T(8,128)(2,1)S(1)}, u32[]{:S(2)}, u32[]{:S(2)}) collective-permute-start(bf16[19,32,128]{2,1,0:T(8,128)(2,1)S(1)} %get-tuple-element.62), channel_id=1, source_target_pairs={{0,12},{4,8},{8,4},{12,0},{16,28},{20,24},{24,20},{28,16},{1,13},{... | collective-permute-start | bytes 466952 | tf_op jit(solution)/shard_map/ppermute | solution.py:321
  14.5 0.0 collective-permute-done.refs_1_
  14.5 0.1 collective-permute-start.11
  14.6 0.0 collective-permute-done.1.refs_2_
  14.6 0.0 collective-permute-done.2.refs_3_
  14.6 0.7 %shard_map.38 = (bf16[2,13,16,128]{3,2,1,0:T(8,128)(2,1)S(1)}, bf16[2,13,16,128]{3,2,1,0:T(8,128)(2,1)S(1)}, bf16[2,13,16,128]{3,2,1,0:T(8,128)(2,1)S(1)}, bf16[2,13,16,128]{3,2,1,0:T(8,128)(2,1)S(1)}) custom-call(s32[4]{0:T(128)S(1)} %copy-done.3, bf16[13,32,128]{2,1,0:T(8,128)(2,1)S(1)} %collective-permute-done.refs_1_, ...), custom_call_target="tpu_custom_call" | custom-call | flops 2000000000 | bytes 1 | tf_op jit(solution)/shard_map/pallas_call | solution.py:308
  15.3 1.9 %collective-permute-start.3 = (bf16[2,13,16,128]{3,2,1,0:T(8,128)(2,1)S(1)}, bf16[2,13,16,128]{3,2,1,0:T(8,128)(2,1)S(1)}, u32[]{:S(2)}, u32[]{:S(2)}) collective-permute-start(bf16[2,13,16,128]{3,2,1,0:T(8,128)(2,1)S(1)} %get-tuple-element.45), channel_id=1, source_target_pairs={{0,2},{1,3},{2,0},{3,1},{4,6},{5,7},{6,4},{7,5},{8,10},{9,11},{10,... | collective-permute-start | bytes 319496 | tf_op jit(solution)/shard_map/ppermute | solution.py:338
  17.2 0.0 collective-permute-start.4
  17.2 2.3 %collective-permute-done.9.refs_1_ = bf16[19,32,128]{2,1,0:T(8,128)(2,1)S(1)} collective-permute-done((bf16[19,32,128]{2,1,0:T(8,128)(2,1)S(1)}, bf16[19,32,128]{2,1,0:T(8,128)(2,1)S(1)}, u32[]{:S(2)}, u32[]{:S(2)}) %collective-permute-start.9) | collective-permute-done | bytes 155680 | tf_op jit(solution)/shard_map/ppermute | solution.py:321
  19.5 0.0 collective-permute-start.5
  19.5 0.8 %collective-permute-done.10.refs_2_ = bf16[19,32,128]{2,1,0:T(8,128)(2,1)S(1)} collective-permute-done((bf16[19,32,128]{2,1,0:T(8,128)(2,1)S(1)}, bf16[19,32,128]{2,1,0:T(8,128)(2,1)S(1)}, u32[]{:S(2)}, u32[]{:S(2)}) %collective-permute-start.10) | collective-permute-done | bytes 155680 | tf_op jit(solution)/shard_map/ppermute | solution.py:321
  20.2 0.6 %collective-permute-done.11.refs_3_ = bf16[19,32,128]{2,1,0:T(8,128)(2,1)S(1)} collective-permute-done((bf16[19,32,128]{2,1,0:T(8,128)(2,1)S(1)}, bf16[19,32,128]{2,1,0:T(8,128)(2,1)S(1)}, u32[]{:S(2)}, u32[]{:S(2)}) %collective-permute-start.11) | collective-permute-done | bytes 155680 | tf_op jit(solution)/shard_map/ppermute | solution.py:321
  20.8 0.7 %shard_map.42 = (bf16[2,19,16,128]{3,2,1,0:T(8,128)(2,1)S(1)}, bf16[2,19,16,128]{3,2,1,0:T(8,128)(2,1)S(1)}, bf16[2,19,16,128]{3,2,1,0:T(8,128)(2,1)S(1)}, bf16[2,19,16,128]{3,2,1,0:T(8,128)(2,1)S(1)}) custom-call(s32[4]{0:T(128)S(1)} %copy-done.3, bf16[19,32,128]{2,1,0:T(8,128)(2,1)S(1)} %collective-permute-done.9.refs_1_, ...), custom_call_target="tpu_custom_call" | custom-call | flops 1 | bytes 1 | tf_op jit(solution)/shard_map/pallas_call | solution.py:308
  21.6 1.7 %collective-permute-start.12 = (bf16[2,19,16,128]{3,2,1,0:T(8,128)(2,1)S(1)}, bf16[2,19,16,128]{3,2,1,0:T(8,128)(2,1)S(1)}, u32[]{:S(2)}, u32[]{:S(2)}) collective-permute-start(bf16[2,19,16,128]{3,2,1,0:T(8,128)(2,1)S(1)} %get-tuple-element.65), channel_id=1, source_target_pairs={{0,2},{1,3},{2,0},{3,1},{4,6},{5,7},{6,4},{7,5},{8,10},{9,11},{10,... | collective-permute-start | bytes 466952 | tf_op jit(solution)/shard_map/ppermute | solution.py:338
  23.2 0.0 collective-permute-start.13
  23.2 0.0 collective-permute-done.3.refs_0_
  23.2 0.6 %collective-permute-start.14 = (bf16[2,19,16,128]{3,2,1,0:T(8,128)(2,1)S(1)}, bf16[2,19,16,128]{3,2,1,0:T(8,128)(2,1)S(1)}, u32[]{:S(2)}, u32[]{:S(2)}) collective-permute-start(bf16[2,19,16,128]{3,2,1,0:T(8,128)(2,1)S(1)} %get-tuple-element.67), channel_id=1, source_target_pairs={{0,1},{1,0},{2,3},{3,2},{4,5},{5,4},{6,7},{7,6},{8,9},{9,8},{10,11... | collective-permute-start | bytes 466952 | tf_op jit(solution)/shard_map/ppermute | solution.py:338
  23.8 0.0 collective-permute-done.4.refs_1_
  23.8 0.0 collective-permute-done.5.refs_2_
  23.8 0.5 shard_map.40
  24.3 2.8 %collective-permute-start.6 = (bf16[13,32,128]{2,1,0:T(8,128)(2,1)S(1)}, bf16[13,32,128]{2,1,0:T(8,128)(2,1)S(1)}, u32[]{:S(2)}, u32[]{:S(2)}) collective-permute-start(bf16[13,32,128]{2,1,0:T(8,128)(2,1)S(1)} %get-tuple-element.56), channel_id=1, source_target_pairs={{0,16},{4,20},{8,24},{12,28},{16,0},{20,4},{24,8},{28,12},{1,17},{... | collective-permute-start | bytes 319496 | tf_op jit(solution)/shard_map/ppermute | solution.py:321
  27.1 1.3 %collective-permute-start.7 = (bf16[13,32,128]{2,1,0:T(8,128)(2,1)S(1)}, bf16[13,32,128]{2,1,0:T(8,128)(2,1)S(1)}, u32[]{:S(2)}, u32[]{:S(2)}) collective-permute-start(bf16[13,32,128]{2,1,0:T(8,128)(2,1)S(1)} %get-tuple-element.57), channel_id=1, source_target_pairs={{0,20},{4,16},{8,28},{12,24},{16,4},{20,0},{24,12},{28,8},{1,21},{... | collective-permute-start | bytes 319496 | tf_op jit(solution)/shard_map/ppermute | solution.py:321
  28.4 0.0 collective-permute-done.12.refs_0_
  28.4 0.9 %collective-permute-start.8 = (bf16[13,32,128]{2,1,0:T(8,128)(2,1)S(1)}, bf16[13,32,128]{2,1,0:T(8,128)(2,1)S(1)}, u32[]{:S(2)}, u32[]{:S(2)}) collective-permute-start(bf16[13,32,128]{2,1,0:T(8,128)(2,1)S(1)} %get-tuple-element.58), channel_id=1, source_target_pairs={{0,4},{4,0},{8,12},{12,8},{16,20},{20,16},{24,28},{28,24},{1,5},{5... | collective-permute-start | bytes 319496 | tf_op jit(solution)/shard_map/ppermute | solution.py:321
  29.3 0.3 collective-permute-done.13.refs_1_
  29.5 0.0 collective-permute-done.14.refs_2_
  29.6 0.6 %shard_map.43 = (bf16[19,32,128]{2,1,0:T(8,128)(2,1)S(1)}, bf16[19,32,128]{2,1,0:T(8,128)(2,1)S(1)}, bf16[19,32,128]{2,1,0:T(8,128)(2,1)S(1)}, bf16[19,32,128]{2,1,0:T(8,128)(2,1)S(1)}) custom-call(bf16[2,19,16,128]{3,2,1,0:T(8,128)(2,1)S(1)} %collective-permute-done.12.refs_0_, bf16[2,19,16,128]{3,2,1,0:T(8,128)(2,1)S(1)} %collective-permute-done.13.refs_1_, ...), custom_call_target="tpu_custom_call" | custom-call | flops 1 | bytes 1 | tf_op jit(solution)/shard_map/pallas_call | solution.py:308
  30.2 2.7 %collective-permute-start.15 = (bf16[19,32,128]{2,1,0:T(8,128)(2,1)S(1)}, bf16[19,32,128]{2,1,0:T(8,128)(2,1)S(1)}, u32[]{:S(2)}, u32[]{:S(2)}) collective-permute-start(bf16[19,32,128]{2,1,0:T(8,128)(2,1)S(1)} %get-tuple-element.69), channel_id=1, source_target_pairs={{0,16},{4,20},{8,24},{12,28},{16,0},{20,4},{24,8},{28,12},{1,17},{... | collective-permute-start | bytes 466952 | tf_op jit(solution)/shard_map/ppermute | solution.py:321
  32.9 1.3 %collective-permute-start.16 = (bf16[19,32,128]{2,1,0:T(8,128)(2,1)S(1)}, bf16[19,32,128]{2,1,0:T(8,128)(2,1)S(1)}, u32[]{:S(2)}, u32[]{:S(2)}) collective-permute-start(bf16[19,32,128]{2,1,0:T(8,128)(2,1)S(1)} %get-tuple-element.74), channel_id=1, source_target_pairs={{0,20},{4,16},{8,28},{12,24},{16,4},{20,0},{24,12},{28,8},{1,21},{... | collective-permute-start | bytes 466952 | tf_op jit(solution)/shard_map/ppermute | solution.py:321
  34.1 1.5 %collective-permute-done.6.refs_0_ = bf16[13,32,128]{2,1,0:T(8,128)(2,1)S(1)} collective-permute-done((bf16[13,32,128]{2,1,0:T(8,128)(2,1)S(1)}, bf16[13,32,128]{2,1,0:T(8,128)(2,1)S(1)}, u32[]{:S(2)}, u32[]{:S(2)}) %collective-permute-start.6) | collective-permute-done | bytes 106528 | tf_op jit(solution)/shard_map/ppermute | solution.py:321
  35.7 6.0 %collective-permute-start.17 = (bf16[19,32,128]{2,1,0:T(8,128)(2,1)S(1)}, bf16[19,32,128]{2,1,0:T(8,128)(2,1)S(1)}, u32[]{:S(2)}, u32[]{:S(2)}) collective-permute-start(bf16[19,32,128]{2,1,0:T(8,128)(2,1)S(1)} %get-tuple-element.75), channel_id=1, source_target_pairs={{0,4},{4,0},{8,12},{12,8},{16,20},{20,16},{24,28},{28,24},{1,5},{5... | collective-permute-start | bytes 466952 | tf_op jit(solution)/shard_map/ppermute | solution.py:321
  41.7 4.0 %collective-permute-done.7.refs_1_ = bf16[13,32,128]{2,1,0:T(8,128)(2,1)S(1)} collective-permute-done((bf16[13,32,128]{2,1,0:T(8,128)(2,1)S(1)}, bf16[13,32,128]{2,1,0:T(8,128)(2,1)S(1)}, u32[]{:S(2)}, u32[]{:S(2)}) %collective-permute-start.7) | collective-permute-done | bytes 106528 | tf_op jit(solution)/shard_map/ppermute | solution.py:321
  45.7 0.0 collective-permute-done.8.refs_2_
  45.7 0.1 shard_map.41
  45.8 2.2 %collective-permute-done.15.refs_1_ = bf16[19,32,128]{2,1,0:T(8,128)(2,1)S(1)} collective-permute-done((bf16[19,32,128]{2,1,0:T(8,128)(2,1)S(1)}, bf16[19,32,128]{2,1,0:T(8,128)(2,1)S(1)}, u32[]{:S(2)}, u32[]{:S(2)}) %collective-permute-start.15) | collective-permute-done | bytes 155680 | tf_op jit(solution)/shard_map/ppermute | solution.py:321
  48.0 1.4 %shard_map.44 = (bf16[4096,128]{1,0:T(8,128)(2,1)}, f32[2,1056,128]{2,1,0:T(8,128)S(1)}) custom-call(f32[2,1056,128]{2,1,0:T(8,128)S(1)} %get-tuple-element.60.refs_0_, bf16[19,32,128]{2,1,0:T(8,128)(2,1)S(1)} %collective-permute-done.15.refs_1_, bf16[19,32,128]{2,1,0:T(8,128)(2,1)S(1)} %get-tuple-element.70.refs_2_, ...), custom_call_target="tpu_custom_call", output_to_operand_aliasing={{1}: (0, {})} | custom-call | flops 1 | bytes 1 | tf_op jit(solution)/shard_map/pallas_call | solution.py:308
  49.3 2.1 %collective-permute-done.16.refs_2_ = bf16[19,32,128]{2,1,0:T(8,128)(2,1)S(1)} collective-permute-done((bf16[19,32,128]{2,1,0:T(8,128)(2,1)S(1)}, bf16[19,32,128]{2,1,0:T(8,128)(2,1)S(1)}, u32[]{:S(2)}, u32[]{:S(2)}) %collective-permute-start.16) | collective-permute-done | bytes 155680 | tf_op jit(solution)/shard_map/ppermute | solution.py:321
  51.4 0.0 collective-permute-done.17.refs_3_
  51.4 1.4 %shard_map.45 = (bf16[4096,128]{1,0:T(8,128)(2,1)}, f32[2,1056,128]{2,1,0:T(8,128)S(1)}) custom-call(bf16[4096,128]{1,0:T(8,128)(2,1)} %get-tuple-element.72.refs_0_, f32[2,1056,128]{2,1,0:T(8,128)S(1)} %get-tuple-element.73.refs_1_, bf16[19,32,128]{2,1,0:T(8,128)(2,1)S(1)} %collective-permute-done.16.refs_2_, ...), custom_call_target="tpu_custom_call", output_to_operand_aliasing={{0}: (0, {}), {1}: (1, {})} | custom-call | flops 1 | bytes 1 | tf_op jit(solution)/shard_map/pallas_call | solution.py:308
  (5 shorter events, 0.0 us)
Async XLA Ops:
  0.0 1.0 %copy-start = (bf16[4,3,2,64,64]{4,3,2,1,0:T(8,128)(2,1)S(1)}, bf16[4,3,2,64,64]{4,3,2,1,0:T(8,128)(2,1)}, u32[]{:S(2)}) copy-start(bf16[4,3,2,64,64]{4,3,2,1,0:T(8,128)(2,1)} %refs_5_.1) | copy-start | bytes 589828
  1.0 1.2 %copy-start.2 = (bf16[2,262144]{1,0:T(2,128)(2,1)S(1)}, bf16[2,262144]{1,0:T(2,128)(2,1)}, u32[]{:S(2)}) copy-start(bf16[2,262144]{1,0:T(2,128)(2,1)} %param.3) | copy-start | bytes 3145732
  2.2 6.6 %copy-start.1 = (bf16[4,3,2,64,64]{4,3,2,1,0:T(8,128)(2,1)S(1)}, bf16[4,3,2,64,64]{4,3,2,1,0:T(8,128)(2,1)}, u32[]{:S(2)}) copy-start(bf16[4,3,2,64,64]{4,3,2,1,0:T(8,128)(2,1)} %refs_5_.1) | copy-start | bytes 589828
  4.2 10.3 %copy-start.3 = (s32[4]{0:T(128)S(1)}, s32[4]{0:T(128)}, u32[]{:S(2)}) copy-start(s32[4]{0:T(128)} %refs_0_.3) | copy-start | bytes 52
  4.2 10.3 %collective-permute-start = (bf16[13,32,128]{2,1,0:T(8,128)(2,1)S(1)}, bf16[13,32,128]{2,1,0:T(8,128)(2,1)S(1)}, u32[]{:S(2)}, u32[]{:S(2)}) collective-permute-start(bf16[13,32,128]{2,1,0:T(8,128)(2,1)S(1)} %get-tuple-element.41), channel_id=1, source_target_pairs={{0,4},{4,0},{8,12},{12,8},{16,20},{20,16},{24,28},{28,24},{1,5},{5... | collective-permute-start | bytes 319496 | tf_op jit(solution)/shard_map/ppermute | solution.py:321
  7.3 7.3 %collective-permute-start.1 = (bf16[13,32,128]{2,1,0:T(8,128)(2,1)S(1)}, bf16[13,32,128]{2,1,0:T(8,128)(2,1)S(1)}, u32[]{:S(2)}, u32[]{:S(2)}) collective-permute-start(bf16[13,32,128]{2,1,0:T(8,128)(2,1)S(1)} %get-tuple-element.42), channel_id=1, source_target_pairs={{0,12},{4,8},{8,4},{12,0},{16,28},{20,24},{24,20},{28,16},{1,13},{... | collective-permute-start | bytes 319496 | tf_op jit(solution)/shard_map/ppermute | solution.py:321
  8.8 5.8 %collective-permute-start.2 = (bf16[13,32,128]{2,1,0:T(8,128)(2,1)S(1)}, bf16[13,32,128]{2,1,0:T(8,128)(2,1)S(1)}, u32[]{:S(2)}, u32[]{:S(2)}) collective-permute-start(bf16[13,32,128]{2,1,0:T(8,128)(2,1)S(1)} %get-tuple-element.43), channel_id=1, source_target_pairs={{0,8},{4,12},{8,0},{12,4},{16,24},{20,28},{24,16},{28,20},{1,9},{5... | collective-permute-start | bytes 319496 | tf_op jit(solution)/shard_map/ppermute | solution.py:321
  11.0 8.5 %collective-permute-start.9 = (bf16[19,32,128]{2,1,0:T(8,128)(2,1)S(1)}, bf16[19,32,128]{2,1,0:T(8,128)(2,1)S(1)}, u32[]{:S(2)}, u32[]{:S(2)}) collective-permute-start(bf16[19,32,128]{2,1,0:T(8,128)(2,1)S(1)} %get-tuple-element.61), channel_id=1, source_target_pairs={{0,4},{4,0},{8,12},{12,8},{16,20},{20,16},{24,28},{28,24},{1,5},{5... | collective-permute-start | bytes 466952 | tf_op jit(solution)/shard_map/ppermute | solution.py:321
  13.0 7.3 %collective-permute-start.10 = (bf16[19,32,128]{2,1,0:T(8,128)(2,1)S(1)}, bf16[19,32,128]{2,1,0:T(8,128)(2,1)S(1)}, u32[]{:S(2)}, u32[]{:S(2)}) collective-permute-start(bf16[19,32,128]{2,1,0:T(8,128)(2,1)S(1)} %get-tuple-element.62), channel_id=1, source_target_pairs={{0,12},{4,8},{8,4},{12,0},{16,28},{20,24},{24,20},{28,16},{1,13},{... | collective-permute-start | bytes 466952 | tf_op jit(solution)/shard_map/ppermute | solution.py:321
  14.5 6.3 %collective-permute-start.11 = (bf16[19,32,128]{2,1,0:T(8,128)(2,1)S(1)}, bf16[19,32,128]{2,1,0:T(8,128)(2,1)S(1)}, u32[]{:S(2)}, u32[]{:S(2)}) collective-permute-start(bf16[19,32,128]{2,1,0:T(8,128)(2,1)S(1)} %get-tuple-element.63), channel_id=1, source_target_pairs={{0,8},{4,12},{8,0},{12,4},{16,24},{20,28},{24,16},{28,20},{1,9},{5... | collective-permute-start | bytes 466952 | tf_op jit(solution)/shard_map/ppermute | solution.py:321
  15.3 8.0 %collective-permute-start.3 = (bf16[2,13,16,128]{3,2,1,0:T(8,128)(2,1)S(1)}, bf16[2,13,16,128]{3,2,1,0:T(8,128)(2,1)S(1)}, u32[]{:S(2)}, u32[]{:S(2)}) collective-permute-start(bf16[2,13,16,128]{3,2,1,0:T(8,128)(2,1)S(1)} %get-tuple-element.45), channel_id=1, source_target_pairs={{0,2},{1,3},{2,0},{3,1},{4,6},{5,7},{6,4},{7,5},{8,10},{9,11},{10,... | collective-permute-start | bytes 319496 | tf_op jit(solution)/shard_map/ppermute | solution.py:338
  17.2 6.6 %collective-permute-start.4 = (bf16[2,13,16,128]{3,2,1,0:T(8,128)(2,1)S(1)}, bf16[2,13,16,128]{3,2,1,0:T(8,128)(2,1)S(1)}, u32[]{:S(2)}, u32[]{:S(2)}) collective-permute-start(bf16[2,13,16,128]{3,2,1,0:T(8,128)(2,1)S(1)} %get-tuple-element.46), channel_id=1, source_target_pairs={{0,3},{1,2},{2,1},{3,0},{4,7},{5,6},{6,5},{7,4},{8,11},{9,10},{10,... | collective-permute-start | bytes 319496 | tf_op jit(solution)/shard_map/ppermute | solution.py:338
  19.5 4.3 %collective-permute-start.5 = (bf16[2,13,16,128]{3,2,1,0:T(8,128)(2,1)S(1)}, bf16[2,13,16,128]{3,2,1,0:T(8,128)(2,1)S(1)}, u32[]{:S(2)}, u32[]{:S(2)}) collective-permute-start(bf16[2,13,16,128]{3,2,1,0:T(8,128)(2,1)S(1)} %get-tuple-element.47), channel_id=1, source_target_pairs={{0,1},{1,0},{2,3},{3,2},{4,5},{5,4},{6,7},{7,6},{8,9},{9,8},{10,11... | collective-permute-start | bytes 319496 | tf_op jit(solution)/shard_map/ppermute | solution.py:338
  21.6 6.8 %collective-permute-start.12 = (bf16[2,19,16,128]{3,2,1,0:T(8,128)(2,1)S(1)}, bf16[2,19,16,128]{3,2,1,0:T(8,128)(2,1)S(1)}, u32[]{:S(2)}, u32[]{:S(2)}) collective-permute-start(bf16[2,19,16,128]{3,2,1,0:T(8,128)(2,1)S(1)} %get-tuple-element.65), channel_id=1, source_target_pairs={{0,2},{1,3},{2,0},{3,1},{4,6},{5,7},{6,4},{7,5},{8,10},{9,11},{10,... | collective-permute-start | bytes 466952 | tf_op jit(solution)/shard_map/ppermute | solution.py:338
  23.2 6.3 %collective-permute-start.13 = (bf16[2,19,16,128]{3,2,1,0:T(8,128)(2,1)S(1)}, bf16[2,19,16,128]{3,2,1,0:T(8,128)(2,1)S(1)}, u32[]{:S(2)}, u32[]{:S(2)}) collective-permute-start(bf16[2,19,16,128]{3,2,1,0:T(8,128)(2,1)S(1)} %get-tuple-element.66), channel_id=1, source_target_pairs={{0,3},{1,2},{2,1},{3,0},{4,7},{5,6},{6,5},{7,4},{8,11},{9,10},{10,... | collective-permute-start | bytes 466952 | tf_op jit(solution)/shard_map/ppermute | solution.py:338
  23.2 6.3 %collective-permute-start.14 = (bf16[2,19,16,128]{3,2,1,0:T(8,128)(2,1)S(1)}, bf16[2,19,16,128]{3,2,1,0:T(8,128)(2,1)S(1)}, u32[]{:S(2)}, u32[]{:S(2)}) collective-permute-start(bf16[2,19,16,128]{3,2,1,0:T(8,128)(2,1)S(1)} %get-tuple-element.67), channel_id=1, source_target_pairs={{0,1},{1,0},{2,3},{3,2},{4,5},{5,4},{6,7},{7,6},{8,9},{9,8},{10,11... | collective-permute-start | bytes 466952 | tf_op jit(solution)/shard_map/ppermute | solution.py:338
  24.3 11.4 %collective-permute-start.6 = (bf16[13,32,128]{2,1,0:T(8,128)(2,1)S(1)}, bf16[13,32,128]{2,1,0:T(8,128)(2,1)S(1)}, u32[]{:S(2)}, u32[]{:S(2)}) collective-permute-start(bf16[13,32,128]{2,1,0:T(8,128)(2,1)S(1)} %get-tuple-element.56), channel_id=1, source_target_pairs={{0,16},{4,20},{8,24},{12,28},{16,0},{20,4},{24,8},{28,12},{1,17},{... | collective-permute-start | bytes 319496 | tf_op jit(solution)/shard_map/ppermute | solution.py:321
  27.1 18.6 %collective-permute-start.7 = (bf16[13,32,128]{2,1,0:T(8,128)(2,1)S(1)}, bf16[13,32,128]{2,1,0:T(8,128)(2,1)S(1)}, u32[]{:S(2)}, u32[]{:S(2)}) collective-permute-start(bf16[13,32,128]{2,1,0:T(8,128)(2,1)S(1)} %get-tuple-element.57), channel_id=1, source_target_pairs={{0,20},{4,16},{8,28},{12,24},{16,4},{20,0},{24,12},{28,8},{1,21},{... | collective-permute-start | bytes 319496 | tf_op jit(solution)/shard_map/ppermute | solution.py:321
  28.4 17.3 %collective-permute-start.8 = (bf16[13,32,128]{2,1,0:T(8,128)(2,1)S(1)}, bf16[13,32,128]{2,1,0:T(8,128)(2,1)S(1)}, u32[]{:S(2)}, u32[]{:S(2)}) collective-permute-start(bf16[13,32,128]{2,1,0:T(8,128)(2,1)S(1)} %get-tuple-element.58), channel_id=1, source_target_pairs={{0,4},{4,0},{8,12},{12,8},{16,20},{20,16},{24,28},{28,24},{1,5},{5... | collective-permute-start | bytes 319496 | tf_op jit(solution)/shard_map/ppermute | solution.py:321
  30.2 17.8 %collective-permute-start.15 = (bf16[19,32,128]{2,1,0:T(8,128)(2,1)S(1)}, bf16[19,32,128]{2,1,0:T(8,128)(2,1)S(1)}, u32[]{:S(2)}, u32[]{:S(2)}) collective-permute-start(bf16[19,32,128]{2,1,0:T(8,128)(2,1)S(1)} %get-tuple-element.69), channel_id=1, source_target_pairs={{0,16},{4,20},{8,24},{12,28},{16,0},{20,4},{24,8},{28,12},{1,17},{... | collective-permute-start | bytes 466952 | tf_op jit(solution)/shard_map/ppermute | solution.py:321
  32.9 18.6 %collective-permute-start.16 = (bf16[19,32,128]{2,1,0:T(8,128)(2,1)S(1)}, bf16[19,32,128]{2,1,0:T(8,128)(2,1)S(1)}, u32[]{:S(2)}, u32[]{:S(2)}) collective-permute-start(bf16[19,32,128]{2,1,0:T(8,128)(2,1)S(1)} %get-tuple-element.74), channel_id=1, source_target_pairs={{0,20},{4,16},{8,28},{12,24},{16,4},{20,0},{24,12},{28,8},{1,21},{... | collective-permute-start | bytes 466952 | tf_op jit(solution)/shard_map/ppermute | solution.py:321
  35.7 15.7 %collective-permute-start.17 = (bf16[19,32,128]{2,1,0:T(8,128)(2,1)S(1)}, bf16[19,32,128]{2,1,0:T(8,128)(2,1)S(1)}, u32[]{:S(2)}, u32[]{:S(2)}) collective-permute-start(bf16[19,32,128]{2,1,0:T(8,128)(2,1)S(1)} %get-tuple-element.75), channel_id=1, source_target_pairs={{0,4},{4,0},{8,12},{12,8},{16,20},{20,16},{24,28},{28,24},{1,5},{5... | collective-permute-start | bytes 466952 | tf_op jit(solution)/shard_map/ppermute | solution.py:321

commit v9 on v8

--- a/solution.py
+++ b/solution.py
@@ -66,24 +66,30 @@
     return jnp.concatenate(rows, axis=0).astype(BF)
 
 
+def columns(size):
+    return lax.broadcasted_iota(jnp.int32, (1, size), 1)
+
+
+def placed(rows, to, minus):
+    at = iotas(rows, to.shape[1])[0]
+    return jnp.where(at == to, (1 - 2 * minus).astype(F32), 0.0).astype(BF)
+
+
 def right_weights(gate, low, in_bit, out_bit):
     k, b = iotas(G, G)
     order = ((k & (HALF - 1)) << 1 | k >> GQ - 1) if low else k ^ in_bit * HALF
     gate = gate.astype(BF)
     t = turned_dot(ones(b == order), jnp.concatenate([gate[:, :G], gate[:, G:]], axis=0)).astype(BF)
-    at, n = iotas(2 * G, 8 * G)
+    n = columns(8 * G)
     bit = lambda i: n >> i & 1
     to = ((bit(7) ^ out_bit) << GQ - 1) | n & (HALF - 1)
     turn_i = bit(8)
     part = bit(5) ^ turn_i
     sign_i = turn_i & (1 - bit(5))
-    ch = iotas(G, 8 * G)[1] >> 6 & 1
     made = []
     for p in range(2):
-        minus = sign_i ^ ((1 - part) & p)
-        place = jnp.where(at == to + (part ^ p) * G, (1 - 2 * minus).astype(F32), 0.0).astype(BF)
-        y = dot(t, place)
-        made.append([jnp.where(ch == c, y, 0.0).astype(BF) for c in range(2)])
+        y = dot(t, placed(2 * G, to + (part ^ p) * G, sign_i ^ ((1 - part) & p)))
+        made.append([jnp.where(bit(6) == c, y, 0.0).astype(BF) for c in range(2)])
     if low:
         rows = [made[p][c] for c in range(2) for p in range(2)]
     else:
@@ -101,15 +107,13 @@
 def last_weights(gate, in_bit):
     k, b = iotas(G, G)
     t = dot(ones(b == ((k & (HALF - 1)) << 1 | k >> GQ - 1)), gate).astype(BF)
-    at, n = iotas(2 * G, 4 * G)
+    n = columns(4 * G)
     p_in = n >> 5 & 1
     b_in = ((n >> 7 ^ in_bit) << GQ - 1) | n & (HALF - 1)
-    ch = iotas(HALF, 4 * G)[1] >> 6 & 1
+    ch = n >> 6 & 1
     rows = []
     for p in range(2):
-        minus = (1 - p) * p_in
-        place = jnp.where(at == b_in + (p_in ^ p) * G, (1 - 2 * minus).astype(F32), 0.0).astype(BF)
-        y = dot(t, place)
+        y = dot(t, placed(2 * G, b_in + (p_in ^ p) * G, (1 - p) * p_in))
         for b0 in range(2):
             for c in range(2):
                 rows.append(jnp.where(ch == c, y[b0 * HALF : (b0 + 1) * HALF], 0.0).astype(BF))
@@ -194,22 +198,24 @@
     return jnp.concatenate(halves, axis=2).astype(BF)
 
 
-def first_kernel(x_ref, gates, o0, o1, o2, o3, mixed, rest, w0_ref, w1_ref, g_ref, spread, turned):
-    early = o0.shape[0]
+def first_weights_kernel(gates, early_w0_ref, w0_ref, w1_ref, g_ref):
     own = own_bits()
     late = product(gate_of(gates, 3, 0), gate_of(gates, 2, 0))
     soon = product(gate_of(gates, 1, 0), gate_of(gates, 0, 0))
     gate = wide_product(late, soon)
-    w0 = first_weights(gate, 0)
+    early_w0_ref[...] = first_weights(gate, 0)
     w0_ref[...] = first_weights(gate, 1)
     w1_ref[...] = right_weights(gate_of(gates, 0, 1), True, 0, own[0])
     g_ref[...] = left_weights(product(gate_of(gates, 1, 2), gate_of(gates, 0, 2)), 0, own[1])
 
+
+def first_kernel(x_ref, w0_ref, w1_ref, g_ref, o0, o1, o2, o3, mixed, rest, spread, turned):
+    early = o0.shape[0]
     for k in range(G // 8):
         spread[k * 512 : (k + 1) * 512, :] = x_ref[k * 512 : (k + 1) * 512, :].astype(F32)
         x = jnp.concatenate([spread[pl.ds(k * 512 + p, 256, stride=2), :] for p in range(2)], axis=1).astype(BF)
         mixed[k * 256 : (k + 1) * 256, :] = x
-        split_rows(k, x, w0, turned)
+        split_rows(k, x, w0_ref[...], turned)
 
     store_blocks(both_gates(rows_of(turned, 0, early), w1_ref[...], g_ref[...]), 0, (o0, o1, o2, o3))
     rest[...] = rows_of(turned, early, HALF // 2)
@@ -359,9 +365,10 @@
     lanes, rows = (4 * G, 8 * G), (G, 2 * G)
 
     x = state.reshape(2, -1, 128).transpose(1, 0, 2).reshape(whole, 128)
-    shapes = [(whole // 2, 4 * G), (HALF // 2 - EARLY, G, 4 * G), (2 * G, 4 * G), lanes, rows]
-    shapes = [jax.ShapeDtypeStruct(shape, BF) for shape in shapes]
-    *early, mixed, rest, w0, w1, g = call(first_kernel, [early_block] * 4 + shapes, (x, gates), scratch=[spread, turned])
+    shapes = [jax.ShapeDtypeStruct(shape, BF) for shape in ((2 * G, 4 * G), (2 * G, 4 * G), lanes, rows)]
+    early_w0, w0, w1, g = call(first_weights_kernel, shapes, (gates,), flops=COST)
+    shapes = [jax.ShapeDtypeStruct(shape, BF) for shape in ((whole // 2, 4 * G), (HALF // 2 - EARLY, G, 4 * G))]
+    *early, mixed, rest = call(first_kernel, [early_block] * 4 + shapes, (x, early_w0, w1, g), scratch=[spread, turned])
     early = exchange(early, bits[0], bits[1])
     shapes = [jax.ShapeDtypeStruct(shape, BF) for shape in (lanes, rows, (4 * G, 4 * G))]
     kernel = functools.partial(second_kernel, top if groups == 4 else 0)

time: 53 us -> 52.1 us (0.983)
  local copies, waits for them, and re-layouts: 2.23 us -> 1.1 us
    unnamed x8, local copies, waits for them, and re-layouts: 2.23 us -> 1.1 us
    pallas_call x9 -> x10, Pallas kernels: 9.49 us -> 9.78 us  [call(): pl.pallas_call(body, out_shape=outs, in_specs=specs + [ANY] * len(after),...]
where the time goes in v9:
time: 52.1 us; the launch traced here: 52 us
  starting transfers between devices  27.2 us (52%)
  waiting for transfers between devices  13.7 us (26%)
  Pallas kernels  9.78 us (19%)
  local copies, waits for them, and re-layouts  1.1 us (2%)
    ppermute x12, starting transfers between devices, swapped(): lax.ppermute(x, 'hi', [(d, d ^ apart) for d in range(lax.axis_size('hi'))])  23.1 us
    ppermute x12, waiting for transfers between devices, swapped(): lax.ppermute(x, 'hi', [(d, d ^ apart) for d in range(lax.axis_size('hi'))])  13.4 us
    pallas_call x10, Pallas kernels, call(): pl.pallas_call(body, out_shape=outs, in_specs=specs + [ANY] * len(after),...  9.78 us
    ppermute x6, starting transfers between devices, regrouped(): lax.ppermute(x, 'lo', to)  4.16 us
    unnamed x8, local copies, waits for them, and re-layouts  1.1 us
  transfers between devices with their start and end apart: 18, of which 8 were waited for; matrix products, arithmetic and copies ran while one was open for 0% of the time, Pallas kernels for 12%

profile of v9, /device:TPU:0, one launch (start us, length us, event | category | flops | bytes accessed | tf_op | source)
XLA Modules:
  0.0 52.0 jit_solution(2500179136382689602)
XLA Ops:
  0.0 1.1 %copy-done.1 = bf16[4,3,2,64,64]{4,3,2,1,0:T(8,128)(2,1)S(1)} copy-done((bf16[4,3,2,64,64]{4,3,2,1,0:T(8,128)(2,1)S(1)}, bf16[4,3,2,64,64]{4,3,2,1,0:T(8,128)(2,1)}, u32[]{:S(2)}) %copy-start.1) | copy-done | bytes 196632
  1.1 1.0 %shard_map.37 = (bf16[128,256]{1,0:T(8,128)(2,1)S(1)}, bf16[128,256]{1,0:T(8,128)(2,1)S(1)}, bf16[256,512]{1,0:T(8,128)(2,1)S(1)}, bf16[64,128]{1,0:T(8,128)(2,1)S(1)}) custom-call(bf16[4,3,2,64,64]{4,3,2,1,0:T(8,128)(2,1)S(1)} %copy-done.1), custom_call_target="tpu_custom_call" | custom-call | flops 2000000000 | bytes 1 | tf_op jit(solution)/shard_map/pallas_call | solution.py:314
  2.1 0.0 copy-done
  2.1 1.3 %shard_map.38 = (bf16[13,32,128]{2,1,0:T(8,128)(2,1)S(1)}, bf16[13,32,128]{2,1,0:T(8,128)(2,1)S(1)}, bf16[13,32,128]{2,1,0:T(8,128)(2,1)S(1)}, bf16[13,32,128]{2...) custom-call(bf16[4096,128]{1,0:T(8,128)(2,1)S(1)} %bitcast.10, ...), custom_call_target="tpu_custom_call" | custom-call | flops 1 | bytes 1 | tf_op jit(solution)/shard_map/pallas_call | solution.py:314
  3.4 0.0 copy-start.3
  3.4 3.0 %collective-permute-start = (bf16[13,32,128]{2,1,0:T(8,128)(2,1)S(1)}, bf16[13,32,128]{2,1,0:T(8,128)(2,1)S(1)}, u32[]{:S(2)}, u32[]{:S(2)}) collective-permute-start(bf16[13,32,128]{2,1,0:T(8,128)(2,1)S(1)} %get-tuple-element.45), channel_id=1, source_target_pairs={{0,4},{4,0},{8,12},{12,8},{16,20},{20,16},{24,28},{28,24},{1,5},{5... | collective-permute-start | bytes 319496 | tf_op jit(solution)/shard_map/ppermute | solution.py:327
  6.5 1.5 %collective-permute-start.1 = (bf16[13,32,128]{2,1,0:T(8,128)(2,1)S(1)}, bf16[13,32,128]{2,1,0:T(8,128)(2,1)S(1)}, u32[]{:S(2)}, u32[]{:S(2)}) collective-permute-start(bf16[13,32,128]{2,1,0:T(8,128)(2,1)S(1)} %get-tuple-element.46), channel_id=1, source_target_pairs={{0,12},{4,8},{8,4},{12,0},{16,28},{20,24},{24,20},{28,16},{1,13},{... | collective-permute-start | bytes 319496 | tf_op jit(solution)/shard_map/ppermute | solution.py:327
  8.0 0.1 collective-permute-start.2
  8.0 2.1 %shard_map.40 = (bf16[19,32,128]{2,1,0:T(8,128)(2,1)S(1)}, bf16[19,32,128]{2,1,0:T(8,128)(2,1)S(1)}, bf16[19,32,128]{2,1,0:T(8,128)(2,1)S(1)}, bf16[19,32,128]{2...) custom-call(bf16[2048,256]{1,0:T(8,128)(2,1)S(1)} %get-tuple-element, ...), custom_call_target="tpu_custom_call" | custom-call | flops 1 | bytes 1 | tf_op jit(solution)/shard_map/pallas_call | solution.py:314
  10.2 2.0 %collective-permute-start.9 = (bf16[19,32,128]{2,1,0:T(8,128)(2,1)S(1)}, bf16[19,32,128]{2,1,0:T(8,128)(2,1)S(1)}, u32[]{:S(2)}, u32[]{:S(2)}) collective-permute-start(bf16[19,32,128]{2,1,0:T(8,128)(2,1)S(1)} %get-tuple-element.63), channel_id=1, source_target_pairs={{0,4},{4,0},{8,12},{12,8},{16,20},{20,16},{24,28},{28,24},{1,5},{5... | collective-permute-start | bytes 466952 | tf_op jit(solution)/shard_map/ppermute | solution.py:327
  12.1 1.5 %collective-permute-start.10 = (bf16[19,32,128]{2,1,0:T(8,128)(2,1)S(1)}, bf16[19,32,128]{2,1,0:T(8,128)(2,1)S(1)}, u32[]{:S(2)}, u32[]{:S(2)}) collective-permute-start(bf16[19,32,128]{2,1,0:T(8,128)(2,1)S(1)} %get-tuple-element.64), channel_id=1, source_target_pairs={{0,12},{4,8},{8,4},{12,0},{16,28},{20,24},{24,20},{28,16},{1,13},{... | collective-permute-start | bytes 466952 | tf_op jit(solution)/shard_map/ppermute | solution.py:327
  13.7 0.0 collective-permute-done.refs_1_
  13.7 0.1 collective-permute-start.11
  13.7 0.0 collective-permute-done.1.refs_2_
  13.7 0.0 collective-permute-done.2.refs_3_
  13.7 0.7 %shard_map.39 = (bf16[2,13,16,128]{3,2,1,0:T(8,128)(2,1)S(1)}, bf16[2,13,16,128]{3,2,1,0:T(8,128)(2,1)S(1)}, bf16[2,13,16,128]{3,2,1,0:T(8,128)(2,1)S(1)}, bf16[2,13,16,128]{3,2,1,0:T(8,128)(2,1)S(1)}) custom-call(s32[4]{0:T(128)S(1)} %copy-done.3, bf16[13,32,128]{2,1,0:T(8,128)(2,1)S(1)} %collective-permute-done.refs_1_, ...), custom_call_target="tpu_custom_call" | custom-call | flops 2000000000 | bytes 1 | tf_op jit(solution)/shard_map/pallas_call | solution.py:314
  14.4 2.0 %collective-permute-start.3 = (bf16[2,13,16,128]{3,2,1,0:T(8,128)(2,1)S(1)}, bf16[2,13,16,128]{3,2,1,0:T(8,128)(2,1)S(1)}, u32[]{:S(2)}, u32[]{:S(2)}) collective-permute-start(bf16[2,13,16,128]{3,2,1,0:T(8,128)(2,1)S(1)} %get-tuple-element.49), channel_id=1, source_target_pairs={{0,2},{1,3},{2,0},{3,1},{4,6},{5,7},{6,4},{7,5},{8,10},{9,11},{10,... | collective-permute-start | bytes 319496 | tf_op jit(solution)/shard_map/ppermute | solution.py:344
  16.4 0.0 collective-permute-start.4
  16.4 2.3 %collective-permute-done.9.refs_1_ = bf16[19,32,128]{2,1,0:T(8,128)(2,1)S(1)} collective-permute-done((bf16[19,32,128]{2,1,0:T(8,128)(2,1)S(1)}, bf16[19,32,128]{2,1,0:T(8,128)(2,1)S(1)}, u32[]{:S(2)}, u32[]{:S(2)}) %collective-permute-start.9) | collective-permute-done | bytes 155680 | tf_op jit(solution)/shard_map/ppermute | solution.py:327
  18.6 0.0 collective-permute-start.5
  18.6 0.8 %collective-permute-done.10.refs_2_ = bf16[19,32,128]{2,1,0:T(8,128)(2,1)S(1)} collective-permute-done((bf16[19,32,128]{2,1,0:T(8,128)(2,1)S(1)}, bf16[19,32,128]{2,1,0:T(8,128)(2,1)S(1)}, u32[]{:S(2)}, u32[]{:S(2)}) %collective-permute-start.10) | collective-permute-done | bytes 155680 | tf_op jit(solution)/shard_map/ppermute | solution.py:327
  19.4 0.6 %collective-permute-done.11.refs_3_ = bf16[19,32,128]{2,1,0:T(8,128)(2,1)S(1)} collective-permute-done((bf16[19,32,128]{2,1,0:T(8,128)(2,1)S(1)}, bf16[19,32,128]{2,1,0:T(8,128)(2,1)S(1)}, u32[]{:S(2)}, u32[]{:S(2)}) %collective-permute-start.11) | collective-permute-done | bytes 155680 | tf_op jit(solution)/shard_map/ppermute | solution.py:327
  20.0 0.7 %shard_map.43 = (bf16[2,19,16,128]{3,2,1,0:T(8,128)(2,1)S(1)}, bf16[2,19,16,128]{3,2,1,0:T(8,128)(2,1)S(1)}, bf16[2,19,16,128]{3,2,1,0:T(8,128)(2,1)S(1)}, bf16[2,19,16,128]{3,2,1,0:T(8,128)(2,1)S(1)}) custom-call(s32[4]{0:T(128)S(1)} %copy-done.3, bf16[19,32,128]{2,1,0:T(8,128)(2,1)S(1)} %collective-permute-done.9.refs_1_, ...), custom_call_target="tpu_custom_call" | custom-call | flops 1 | bytes 1 | tf_op jit(solution)/shard_map/pallas_call | solution.py:314
  20.7 1.7 %collective-permute-start.12 = (bf16[2,19,16,128]{3,2,1,0:T(8,128)(2,1)S(1)}, bf16[2,19,16,128]{3,2,1,0:T(8,128)(2,1)S(1)}, u32[]{:S(2)}, u32[]{:S(2)}) collective-permute-start(bf16[2,19,16,128]{3,2,1,0:T(8,128)(2,1)S(1)} %get-tuple-element.67), channel_id=1, source_target_pairs={{0,2},{1,3},{2,0},{3,1},{4,6},{5,7},{6,4},{7,5},{8,10},{9,11},{10,... | collective-permute-start | bytes 466952 | tf_op jit(solution)/shard_map/ppermute | solution.py:344
  22.4 0.0 collective-permute-start.13
  22.4 0.0 collective-permute-done.3.refs_0_
  22.4 0.5 %collective-permute-start.14 = (bf16[2,19,16,128]{3,2,1,0:T(8,128)(2,1)S(1)}, bf16[2,19,16,128]{3,2,1,0:T(8,128)(2,1)S(1)}, u32[]{:S(2)}, u32[]{:S(2)}) collective-permute-start(bf16[2,19,16,128]{3,2,1,0:T(8,128)(2,1)S(1)} %get-tuple-element.69), channel_id=1, source_target_pairs={{0,1},{1,0},{2,3},{3,2},{4,5},{5,4},{6,7},{7,6},{8,9},{9,8},{10,11... | collective-permute-start | bytes 466952 | tf_op jit(solution)/shard_map/ppermute | solution.py:344
  22.9 0.0 collective-permute-done.4.refs_1_
  22.9 0.0 collective-permute-done.5.refs_2_
  22.9 0.5 shard_map.41
  23.5 2.8 %collective-permute-start.6 = (bf16[13,32,128]{2,1,0:T(8,128)(2,1)S(1)}, bf16[13,32,128]{2,1,0:T(8,128)(2,1)S(1)}, u32[]{:S(2)}, u32[]{:S(2)}) collective-permute-start(bf16[13,32,128]{2,1,0:T(8,128)(2,1)S(1)} %get-tuple-element.58), channel_id=1, source_target_pairs={{0,16},{4,20},{8,24},{12,28},{16,0},{20,4},{24,8},{28,12},{1,17},{... | collective-permute-start | bytes 319496 | tf_op jit(solution)/shard_map/ppermute | solution.py:327
  26.2 1.3 %collective-permute-start.7 = (bf16[13,32,128]{2,1,0:T(8,128)(2,1)S(1)}, bf16[13,32,128]{2,1,0:T(8,128)(2,1)S(1)}, u32[]{:S(2)}, u32[]{:S(2)}) collective-permute-start(bf16[13,32,128]{2,1,0:T(8,128)(2,1)S(1)} %get-tuple-element.59), channel_id=1, source_target_pairs={{0,20},{4,16},{8,28},{12,24},{16,4},{20,0},{24,12},{28,8},{1,21},{... | collective-permute-start | bytes 319496 | tf_op jit(solution)/shard_map/ppermute | solution.py:327
  27.5 0.0 collective-permute-done.12.refs_0_
  27.5 0.9 %collective-permute-start.8 = (bf16[13,32,128]{2,1,0:T(8,128)(2,1)S(1)}, bf16[13,32,128]{2,1,0:T(8,128)(2,1)S(1)}, u32[]{:S(2)}, u32[]{:S(2)}) collective-permute-start(bf16[13,32,128]{2,1,0:T(8,128)(2,1)S(1)} %get-tuple-element.60), channel_id=1, source_target_pairs={{0,4},{4,0},{8,12},{12,8},{16,20},{20,16},{24,28},{28,24},{1,5},{5... | collective-permute-start | bytes 319496 | tf_op jit(solution)/shard_map/ppermute | solution.py:327
  28.4 0.3 collective-permute-done.13.refs_1_
  28.7 0.0 collective-permute-done.14.refs_2_
  28.7 0.6 %shard_map.44 = (bf16[19,32,128]{2,1,0:T(8,128)(2,1)S(1)}, bf16[19,32,128]{2,1,0:T(8,128)(2,1)S(1)}, bf16[19,32,128]{2,1,0:T(8,128)(2,1)S(1)}, bf16[19,32,128]{2,1,0:T(8,128)(2,1)S(1)}) custom-call(bf16[2,19,16,128]{3,2,1,0:T(8,128)(2,1)S(1)} %collective-permute-done.12.refs_0_, bf16[2,19,16,128]{3,2,1,0:T(8,128)(2,1)S(1)} %collective-permute-done.13.refs_1_, ...), custom_call_target="tpu_custom_call" | custom-call | flops 1 | bytes 1 | tf_op jit(solution)/shard_map/pallas_call | solution.py:314
  29.4 2.6 %collective-permute-start.15 = (bf16[19,32,128]{2,1,0:T(8,128)(2,1)S(1)}, bf16[19,32,128]{2,1,0:T(8,128)(2,1)S(1)}, u32[]{:S(2)}, u32[]{:S(2)}) collective-permute-start(bf16[19,32,128]{2,1,0:T(8,128)(2,1)S(1)} %get-tuple-element.71), channel_id=1, source_target_pairs={{0,16},{4,20},{8,24},{12,28},{16,0},{20,4},{24,8},{28,12},{1,17},{... | collective-permute-start | bytes 466952 | tf_op jit(solution)/shard_map/ppermute | solution.py:327
  32.0 1.3 %collective-permute-start.16 = (bf16[19,32,128]{2,1,0:T(8,128)(2,1)S(1)}, bf16[19,32,128]{2,1,0:T(8,128)(2,1)S(1)}, u32[]{:S(2)}, u32[]{:S(2)}) collective-permute-start(bf16[19,32,128]{2,1,0:T(8,128)(2,1)S(1)} %get-tuple-element.76), channel_id=1, source_target_pairs={{0,20},{4,16},{8,28},{12,24},{16,4},{20,0},{24,12},{28,8},{1,21},{... | collective-permute-start | bytes 466952 | tf_op jit(solution)/shard_map/ppermute | solution.py:327
  33.3 1.5 %collective-permute-done.6.refs_0_ = bf16[13,32,128]{2,1,0:T(8,128)(2,1)S(1)} collective-permute-done((bf16[13,32,128]{2,1,0:T(8,128)(2,1)S(1)}, bf16[13,32,128]{2,1,0:T(8,128)(2,1)S(1)}, u32[]{:S(2)}, u32[]{:S(2)}) %collective-permute-start.6) | collective-permute-done | bytes 106528 | tf_op jit(solution)/shard_map/ppermute | solution.py:327
  34.8 6.0 %collective-permute-start.17 = (bf16[19,32,128]{2,1,0:T(8,128)(2,1)S(1)}, bf16[19,32,128]{2,1,0:T(8,128)(2,1)S(1)}, u32[]{:S(2)}, u32[]{:S(2)}) collective-permute-start(bf16[19,32,128]{2,1,0:T(8,128)(2,1)S(1)} %get-tuple-element.77), channel_id=1, source_target_pairs={{0,4},{4,0},{8,12},{12,8},{16,20},{20,16},{24,28},{28,24},{1,5},{5... | collective-permute-start | bytes 466952 | tf_op jit(solution)/shard_map/ppermute | solution.py:327
  40.9 4.0 %collective-permute-done.7.refs_1_ = bf16[13,32,128]{2,1,0:T(8,128)(2,1)S(1)} collective-permute-done((bf16[13,32,128]{2,1,0:T(8,128)(2,1)S(1)}, bf16[13,32,128]{2,1,0:T(8,128)(2,1)S(1)}, u32[]{:S(2)}, u32[]{:S(2)}) %collective-permute-start.7) | collective-permute-done | bytes 106528 | tf_op jit(solution)/shard_map/ppermute | solution.py:327
  44.9 0.1 shard_map.42
  44.9 2.2 %collective-permute-done.15.refs_1_ = bf16[19,32,128]{2,1,0:T(8,128)(2,1)S(1)} collective-permute-done((bf16[19,32,128]{2,1,0:T(8,128)(2,1)S(1)}, bf16[19,32,128]{2,1,0:T(8,128)(2,1)S(1)}, u32[]{:S(2)}, u32[]{:S(2)}) %collective-permute-start.15) | collective-permute-done | bytes 155680 | tf_op jit(solution)/shard_map/ppermute | solution.py:327
  47.1 1.4 %shard_map.45 = (bf16[4096,128]{1,0:T(8,128)(2,1)}, f32[2,1056,128]{2,1,0:T(8,128)S(1)}) custom-call(f32[2,1056,128]{2,1,0:T(8,128)S(1)} %get-tuple-element.62.refs_0_, bf16[19,32,128]{2,1,0:T(8,128)(2,1)S(1)} %collective-permute-done.15.refs_1_, bf16[19,32,128]{2,1,0:T(8,128)(2,1)S(1)} %get-tuple-element.72.refs_2_, ...), custom_call_target="tpu_custom_call", output_to_operand_aliasing={{1}: (0, {})} | custom-call | flops 1 | bytes 1 | tf_op jit(solution)/shard_map/pallas_call | solution.py:314
  48.5 2.1 %collective-permute-done.16.refs_2_ = bf16[19,32,128]{2,1,0:T(8,128)(2,1)S(1)} collective-permute-done((bf16[19,32,128]{2,1,0:T(8,128)(2,1)S(1)}, bf16[19,32,128]{2,1,0:T(8,128)(2,1)S(1)}, u32[]{:S(2)}, u32[]{:S(2)}) %collective-permute-start.16) | collective-permute-done | bytes 155680 | tf_op jit(solution)/shard_map/ppermute | solution.py:327
  50.6 0.0 collective-permute-done.17.refs_3_
  50.6 1.4 %shard_map.46 = (bf16[4096,128]{1,0:T(8,128)(2,1)}, f32[2,1056,128]{2,1,0:T(8,128)S(1)}) custom-call(bf16[4096,128]{1,0:T(8,128)(2,1)} %get-tuple-element.74.refs_0_, f32[2,1056,128]{2,1,0:T(8,128)S(1)} %get-tuple-element.75.refs_1_, bf16[19,32,128]{2,1,0:T(8,128)(2,1)S(1)} %collective-permute-done.16.refs_2_, ...), custom_call_target="tpu_custom_call", output_to_operand_aliasing={{0}: (0, {}), {1}: (1, {})} | custom-call | flops 1 | bytes 1 | tf_op jit(solution)/shard_map/pallas_call | solution.py:314
  (6 shorter events, 0.0 us)
Async XLA Ops:
  0.0 2.1 %copy-start = (bf16[2,262144]{1,0:T(2,128)(2,1)S(1)}, bf16[2,262144]{1,0:T(2,128)(2,1)}, u32[]{:S(2)}) copy-start(bf16[2,262144]{1,0:T(2,128)(2,1)} %param.3) | copy-start | bytes 3145732
  0.0 1.1 %copy-start.1 = (bf16[4,3,2,64,64]{4,3,2,1,0:T(8,128)(2,1)S(1)}, bf16[4,3,2,64,64]{4,3,2,1,0:T(8,128)(2,1)}, u32[]{:S(2)}) copy-start(bf16[4,3,2,64,64]{4,3,2,1,0:T(8,128)(2,1)} %refs_5_.1) | copy-start | bytes 589828
  2.1 6.0 %copy-start.2 = (bf16[4,3,2,64,64]{4,3,2,1,0:T(8,128)(2,1)S(1)}, bf16[4,3,2,64,64]{4,3,2,1,0:T(8,128)(2,1)}, u32[]{:S(2)}) copy-start(bf16[4,3,2,64,64]{4,3,2,1,0:T(8,128)(2,1)} %refs_5_.1) | copy-start | bytes 589828
  3.4 10.3 %copy-start.3 = (s32[4]{0:T(128)S(1)}, s32[4]{0:T(128)}, u32[]{:S(2)}) copy-start(s32[4]{0:T(128)} %refs_0_.5) | copy-start | bytes 52
  3.4 10.2 %collective-permute-start = (bf16[13,32,128]{2,1,0:T(8,128)(2,1)S(1)}, bf16[13,32,128]{2,1,0:T(8,128)(2,1)S(1)}, u32[]{:S(2)}, u32[]{:S(2)}) collective-permute-start(bf16[13,32,128]{2,1,0:T(8,128)(2,1)S(1)} %get-tuple-element.45), channel_id=1, source_target_pairs={{0,4},{4,0},{8,12},{12,8},{16,20},{20,16},{24,28},{28,24},{1,5},{5... | collective-permute-start | bytes 319496 | tf_op jit(solution)/shard_map/ppermute | solution.py:327
  6.5 7.3 %collective-permute-start.1 = (bf16[13,32,128]{2,1,0:T(8,128)(2,1)S(1)}, bf16[13,32,128]{2,1,0:T(8,128)(2,1)S(1)}, u32[]{:S(2)}, u32[]{:S(2)}) collective-permute-start(bf16[13,32,128]{2,1,0:T(8,128)(2,1)S(1)} %get-tuple-element.46), channel_id=1, source_target_pairs={{0,12},{4,8},{8,4},{12,0},{16,28},{20,24},{24,20},{28,16},{1,13},{... | collective-permute-start | bytes 319496 | tf_op jit(solution)/shard_map/ppermute | solution.py:327
  8.0 5.8 %collective-permute-start.2 = (bf16[13,32,128]{2,1,0:T(8,128)(2,1)S(1)}, bf16[13,32,128]{2,1,0:T(8,128)(2,1)S(1)}, u32[]{:S(2)}, u32[]{:S(2)}) collective-permute-start(bf16[13,32,128]{2,1,0:T(8,128)(2,1)S(1)} %get-tuple-element.47), channel_id=1, source_target_pairs={{0,8},{4,12},{8,0},{12,4},{16,24},{20,28},{24,16},{28,20},{1,9},{5... | collective-permute-start | bytes 319496 | tf_op jit(solution)/shard_map/ppermute | solution.py:327
  10.2 8.5 %collective-permute-start.9 = (bf16[19,32,128]{2,1,0:T(8,128)(2,1)S(1)}, bf16[19,32,128]{2,1,0:T(8,128)(2,1)S(1)}, u32[]{:S(2)}, u32[]{:S(2)}) collective-permute-start(bf16[19,32,128]{2,1,0:T(8,128)(2,1)S(1)} %get-tuple-element.63), channel_id=1, source_target_pairs={{0,4},{4,0},{8,12},{12,8},{16,20},{20,16},{24,28},{28,24},{1,5},{5... | collective-permute-start | bytes 466952 | tf_op jit(solution)/shard_map/ppermute | solution.py:327
  12.1 7.2 %collective-permute-start.10 = (bf16[19,32,128]{2,1,0:T(8,128)(2,1)S(1)}, bf16[19,32,128]{2,1,0:T(8,128)(2,1)S(1)}, u32[]{:S(2)}, u32[]{:S(2)}) collective-permute-start(bf16[19,32,128]{2,1,0:T(8,128)(2,1)S(1)} %get-tuple-element.64), channel_id=1, source_target_pairs={{0,12},{4,8},{8,4},{12,0},{16,28},{20,24},{24,20},{28,16},{1,13},{... | collective-permute-start | bytes 466952 | tf_op jit(solution)/shard_map/ppermute | solution.py:327
  13.7 6.3 %collective-permute-start.11 = (bf16[19,32,128]{2,1,0:T(8,128)(2,1)S(1)}, bf16[19,32,128]{2,1,0:T(8,128)(2,1)S(1)}, u32[]{:S(2)}, u32[]{:S(2)}) collective-permute-start(bf16[19,32,128]{2,1,0:T(8,128)(2,1)S(1)} %get-tuple-element.65), channel_id=1, source_target_pairs={{0,8},{4,12},{8,0},{12,4},{16,24},{20,28},{24,16},{28,20},{1,9},{5... | collective-permute-start | bytes 466952 | tf_op jit(solution)/shard_map/ppermute | solution.py:327
  14.4 8.0 %collective-permute-start.3 = (bf16[2,13,16,128]{3,2,1,0:T(8,128)(2,1)S(1)}, bf16[2,13,16,128]{3,2,1,0:T(8,128)(2,1)S(1)}, u32[]{:S(2)}, u32[]{:S(2)}) collective-permute-start(bf16[2,13,16,128]{3,2,1,0:T(8,128)(2,1)S(1)} %get-tuple-element.49), channel_id=1, source_target_pairs={{0,2},{1,3},{2,0},{3,1},{4,6},{5,7},{6,4},{7,5},{8,10},{9,11},{10,... | collective-permute-start | bytes 319496 | tf_op jit(solution)/shard_map/ppermute | solution.py:344
  16.4 6.6 %collective-permute-start.4 = (bf16[2,13,16,128]{3,2,1,0:T(8,128)(2,1)S(1)}, bf16[2,13,16,128]{3,2,1,0:T(8,128)(2,1)S(1)}, u32[]{:S(2)}, u32[]{:S(2)}) collective-permute-start(bf16[2,13,16,128]{3,2,1,0:T(8,128)(2,1)S(1)} %get-tuple-element.50), channel_id=1, source_target_pairs={{0,3},{1,2},{2,1},{3,0},{4,7},{5,6},{6,5},{7,4},{8,11},{9,10},{10,... | collective-permute-start | bytes 319496 | tf_op jit(solution)/shard_map/ppermute | solution.py:344
  18.6 4.3 %collective-permute-start.5 = (bf16[2,13,16,128]{3,2,1,0:T(8,128)(2,1)S(1)}, bf16[2,13,16,128]{3,2,1,0:T(8,128)(2,1)S(1)}, u32[]{:S(2)}, u32[]{:S(2)}) collective-permute-start(bf16[2,13,16,128]{3,2,1,0:T(8,128)(2,1)S(1)} %get-tuple-element.51), channel_id=1, source_target_pairs={{0,1},{1,0},{2,3},{3,2},{4,5},{5,4},{6,7},{7,6},{8,9},{9,8},{10,11... | collective-permute-start | bytes 319496 | tf_op jit(solution)/shard_map/ppermute | solution.py:344
  20.7 6.8 %collective-permute-start.12 = (bf16[2,19,16,128]{3,2,1,0:T(8,128)(2,1)S(1)}, bf16[2,19,16,128]{3,2,1,0:T(8,128)(2,1)S(1)}, u32[]{:S(2)}, u32[]{:S(2)}) collective-permute-start(bf16[2,19,16,128]{3,2,1,0:T(8,128)(2,1)S(1)} %get-tuple-element.67), channel_id=1, source_target_pairs={{0,2},{1,3},{2,0},{3,1},{4,6},{5,7},{6,4},{7,5},{8,10},{9,11},{10,... | collective-permute-start | bytes 466952 | tf_op jit(solution)/shard_map/ppermute | solution.py:344
  22.4 6.3 %collective-permute-start.13 = (bf16[2,19,16,128]{3,2,1,0:T(8,128)(2,1)S(1)}, bf16[2,19,16,128]{3,2,1,0:T(8,128)(2,1)S(1)}, u32[]{:S(2)}, u32[]{:S(2)}) collective-permute-start(bf16[2,19,16,128]{3,2,1,0:T(8,128)(2,1)S(1)} %get-tuple-element.68), channel_id=1, source_target_pairs={{0,3},{1,2},{2,1},{3,0},{4,7},{5,6},{6,5},{7,4},{8,11},{9,10},{10,... | collective-permute-start | bytes 466952 | tf_op jit(solution)/shard_map/ppermute | solution.py:344
  22.4 6.3 %collective-permute-start.14 = (bf16[2,19,16,128]{3,2,1,0:T(8,128)(2,1)S(1)}, bf16[2,19,16,128]{3,2,1,0:T(8,128)(2,1)S(1)}, u32[]{:S(2)}, u32[]{:S(2)}) collective-permute-start(bf16[2,19,16,128]{3,2,1,0:T(8,128)(2,1)S(1)} %get-tuple-element.69), channel_id=1, source_target_pairs={{0,1},{1,0},{2,3},{3,2},{4,5},{5,4},{6,7},{7,6},{8,9},{9,8},{10,11... | collective-permute-start | bytes 466952 | tf_op jit(solution)/shard_map/ppermute | solution.py:344
  23.5 11.4 %collective-permute-start.6 = (bf16[13,32,128]{2,1,0:T(8,128)(2,1)S(1)}, bf16[13,32,128]{2,1,0:T(8,128)(2,1)S(1)}, u32[]{:S(2)}, u32[]{:S(2)}) collective-permute-start(bf16[13,32,128]{2,1,0:T(8,128)(2,1)S(1)} %get-tuple-element.58), channel_id=1, source_target_pairs={{0,16},{4,20},{8,24},{12,28},{16,0},{20,4},{24,8},{28,12},{1,17},{... | collective-permute-start | bytes 319496 | tf_op jit(solution)/shard_map/ppermute | solution.py:327
  26.2 18.6 %collective-permute-start.7 = (bf16[13,32,128]{2,1,0:T(8,128)(2,1)S(1)}, bf16[13,32,128]{2,1,0:T(8,128)(2,1)S(1)}, u32[]{:S(2)}, u32[]{:S(2)}) collective-permute-start(bf16[13,32,128]{2,1,0:T(8,128)(2,1)S(1)} %get-tuple-element.59), channel_id=1, source_target_pairs={{0,20},{4,16},{8,28},{12,24},{16,4},{20,0},{24,12},{28,8},{1,21},{... | collective-permute-start | bytes 319496 | tf_op jit(solution)/shard_map/ppermute | solution.py:327
  27.5 17.3 %collective-permute-start.8 = (bf16[13,32,128]{2,1,0:T(8,128)(2,1)S(1)}, bf16[13,32,128]{2,1,0:T(8,128)(2,1)S(1)}, u32[]{:S(2)}, u32[]{:S(2)}) collective-permute-start(bf16[13,32,128]{2,1,0:T(8,128)(2,1)S(1)} %get-tuple-element.60), channel_id=1, source_target_pairs={{0,4},{4,0},{8,12},{12,8},{16,20},{20,16},{24,28},{28,24},{1,5},{5... | collective-permute-start | bytes 319496 | tf_op jit(solution)/shard_map/ppermute | solution.py:327
  29.4 17.7 %collective-permute-start.15 = (bf16[19,32,128]{2,1,0:T(8,128)(2,1)S(1)}, bf16[19,32,128]{2,1,0:T(8,128)(2,1)S(1)}, u32[]{:S(2)}, u32[]{:S(2)}) collective-permute-start(bf16[19,32,128]{2,1,0:T(8,128)(2,1)S(1)} %get-tuple-element.71), channel_id=1, source_target_pairs={{0,16},{4,20},{8,24},{12,28},{16,0},{20,4},{24,8},{28,12},{1,17},{... | collective-permute-start | bytes 466952 | tf_op jit(solution)/shard_map/ppermute | solution.py:327
  32.0 18.6 %collective-permute-start.16 = (bf16[19,32,128]{2,1,0:T(8,128)(2,1)S(1)}, bf16[19,32,128]{2,1,0:T(8,128)(2,1)S(1)}, u32[]{:S(2)}, u32[]{:S(2)}) collective-permute-start(bf16[19,32,128]{2,1,0:T(8,128)(2,1)S(1)} %get-tuple-element.76), channel_id=1, source_target_pairs={{0,20},{4,16},{8,28},{12,24},{16,4},{20,0},{24,12},{28,8},{1,21},{... | collective-permute-start | bytes 466952 | tf_op jit(solution)/shard_map/ppermute | solution.py:327
  34.8 15.8 %collective-permute-start.17 = (bf16[19,32,128]{2,1,0:T(8,128)(2,1)S(1)}, bf16[19,32,128]{2,1,0:T(8,128)(2,1)S(1)}, u32[]{:S(2)}, u32[]{:S(2)}) collective-permute-start(bf16[19,32,128]{2,1,0:T(8,128)(2,1)S(1)} %get-tuple-element.77), channel_id=1, source_target_pairs={{0,4},{4,0},{8,12},{12,8},{16,20},{20,16},{24,28},{28,24},{1,5},{5... | collective-permute-start | bytes 466952 | tf_op jit(solution)/shard_map/ppermute | solution.py:327

commit v10 on v9

--- a/solution.py
+++ b/solution.py
@@ -105,36 +105,39 @@
 
 
 def last_weights(gate, in_bit):
-    k, b = iotas(G, G)
-    t = dot(ones(b == ((k & (HALF - 1)) << 1 | k >> GQ - 1)), gate).astype(BF)
+    k, b = iotas(2 * G, G)
+    t = dot(ones(b == ((k >> 1 & (HALF - 1)) << 1 | k >> GQ)), gate).astype(BF)
     n = columns(4 * G)
     p_in = n >> 5 & 1
     b_in = ((n >> 7 ^ in_bit) << GQ - 1) | n & (HALF - 1)
     ch = n >> 6 & 1
-    rows = []
-    for p in range(2):
-        y = dot(t, placed(2 * G, b_in + (p_in ^ p) * G, (1 - p) * p_in))
-        for b0 in range(2):
-            for c in range(2):
-                rows.append(jnp.where(ch == c, y[b0 * HALF : (b0 + 1) * HALF], 0.0).astype(BF))
-    return jnp.concatenate(rows, axis=0)
-
-
-def turn(parts):
-    lane = lax.broadcasted_iota(jnp.int32, (parts[0].shape[0], 128), 1)
+    real, imag = (dot(t, placed(2 * G, b_in + (p_in ^ p) * G, (1 - p) * p_in)) for p in range(2))
+    y = jnp.where((iotas(2 * G, 4 * G)[0] & 1) == 0, real, imag)
+    rows = [jnp.where(ch == c, y[b0 * G : (b0 + 1) * G], 0.0) for b0 in range(2) for c in range(2)]
+    return jnp.concatenate(rows, axis=0).astype(BF)
+
+
+def turn_four(a):
+    lane = lax.broadcasted_iota(jnp.int32, a[0].shape, 1)
     wide = lane < 64
     narrow = (lane & 32) == 0
+    s, out = [None] * 4, [None] * 4
+    for r in range(2):
+        s[r] = jnp.where(wide, a[r], pltpu.roll(a[r + 2], 64, 1))
+        s[r + 2] = jnp.where(wide, pltpu.roll(a[r], 64, 1), a[r + 2])
+    for r in (0, 2):
+        out[r] = jnp.where(narrow, s[r], pltpu.roll(s[r + 1], 32, 1))
+        out[r + 1] = jnp.where(narrow, pltpu.roll(s[r], 96, 1), s[r + 1])
+    return out
+
+
+def turn(parts):
     out = [[None, None] for _ in range(8)]
     for n in range(2):
         for m in range(2):
-            a = [parts[n * 4 + r][:, m * 128 : (m + 1) * 128] for r in range(4)]
-            s = [None] * 4
-            for r in range(2):
-                s[r] = jnp.where(wide, a[r], pltpu.roll(a[r + 2], 64, 1))
-                s[r + 2] = jnp.where(wide, pltpu.roll(a[r], 64, 1), a[r + 2])
-            for r in (0, 2):
-                out[m * 4 + r][n] = jnp.where(narrow, s[r], pltpu.roll(s[r + 1], 32, 1))
-                out[m * 4 + r + 1][n] = jnp.where(narrow, pltpu.roll(s[r], 96, 1), s[r + 1])
+            four = turn_four([part[:, m * 128 : (m + 1) * 128] for part in parts[n * 4 : n * 4 + 4]])
+            for q in range(4):
+                out[m * 4 + q][n] = four[q]
     return out
 
 
@@ -168,7 +171,7 @@
 STEP = 22
 PITCH = G + 1
 NARROW = HALF + 1
-EARLY = 13
+EARLY = 14
 COST = 2 * 10**9
 
 
@@ -264,7 +267,7 @@
 
 
 def last_kernel(j, *refs):
-    moved, stayed, w_ref, o_ref, wide, spread, made, sems = refs[-8:]
+    moved, stayed, w_ref, o_ref, wide, made, sems = refs[-7:]
     gather_rows(HALF - moved.shape[0], (stayed, moved), wide)
     start = (own_bits()[3] ^ j) * (o_ref.shape[0] // 2)
     copies = []
@@ -273,12 +276,12 @@
         halves = [jnp.concatenate([wide[i, at : at + HALF, :] for at in starts], axis=0) for i in range(2)]
         x = jnp.concatenate(halves, axis=1).astype(BF)
         r = turned_dot(w_ref[...], x).astype(BF)
-        tiles = turn([r[g * HALF : (g + 1) * HALF] for g in range(8)])
-        for q in range(8):
-            for n in range(2):
-                spread[pl.ds((k * 8 + q) * G + n, HALF, stride=2), :] = tiles[q][n].astype(F32)
+        for m in range(2):
+            tiles = turn_four([r[g * G : (g + 1) * G, m * 128 : (m + 1) * 128] for g in range(4)])
+            for q in range(4):
+                at = (k * 8 + m * 4 + q) * G
+                made[at : at + G, :] = tiles[q]
         rows = slice(k * 512, (k + 1) * 512)
-        made[rows, :] = spread[rows, :].astype(BF)
         to = pl.ds(pl.multiple_of(start + k * 512, 512), 512)
         copies.append(pltpu.make_async_copy(made.at[rows], o_ref.at[to], sems.at[k]))
         copies[-1].start()
@@ -293,11 +296,15 @@
     lo = lax.axis_index("lo")
     rows = outs[0].shape[2]
     for o, out in zip(APART, outs):
-        t = regroup[lo ^ o]
+        t = jnp.sum(jnp.where(columns(groups) == lo ^ o, regroup[...], 0))
         j = t >> 1 ^ own
         at = pl.ds(pl.multiple_of((t & 1) * rows, rows), rows)
-        for i in range(2):
-            out[i] = jnp.where(j == 0, blocks[i, 0][:, at, :], blocks[i, 1][:, at, :])
+        for half in range(2):
+
+            @pl.when(j == half)
+            def _():
+                for i in range(2):
+                    out[i] = blocks[i, half][:, at, :]
 
 
 VMEM = pl.BlockSpec(memory_space=pltpu.VMEM)
@@ -339,7 +346,7 @@
     count = blocks[0].shape[-3]
     if groups == 4:
         part = jax.ShapeDtypeStruct((2, count, top, 128), BF)
-        parts = call(functools.partial(pick_kernel, groups), [part] * groups, (regroup, *blocks), [SMEM] + [VMEM] * 4, after=after, flops=flops)
+        parts = call(functools.partial(pick_kernel, groups), [part] * groups, (regroup.reshape(1, groups), *blocks), after=after, flops=flops)
         pairs = [[(d, d ^ o) for d in range(groups)] for o in APART]
         return [lax.ppermute(x, "lo", to) if o else x for o, x, to in zip(APART, parts, pairs)]
     own = lax.axis_index("hi") >> bit & 1
@@ -384,7 +391,7 @@
     wide = jax.ShapeDtypeStruct((2, HALF * NARROW, 128), F32)
     wides = call(gather_kernel, [wide] * 2, early, flops=COST)
     late = by_place(late)
-    scratch = [pltpu.VMEM((whole // 2, 128), F32), pltpu.VMEM((whole // 2, 128), BF), pltpu.SemaphoreType.DMA((HALF // 8,))]
+    scratch = [pltpu.VMEM((whole // 2, 128), BF), pltpu.SemaphoreType.DMA((HALF // 8,))]
     shapes = [jax.ShapeDtypeStruct((whole, 128), BF), wide]
     out = []
     for j in range(2):

time: 52.1 us -> 51.7 us (level)
  waiting for transfers between devices: 13.7 us -> 18.3 us
  starting transfers between devices: 27.2 us -> 22.7 us
    ppermute x12, starting transfers between devices: 23.1 us -> 18.5 us  [swapped(): lax.ppermute(x, 'hi', [(d, d ^ apart) for d in range(lax.axis_size('hi'))])]
    ppermute x12, waiting for transfers between devices: 13.4 us -> 17.9 us  [swapped(): lax.ppermute(x, 'hi', [(d, d ^ apart) for d in range(lax.axis_size('hi'))])]
  transfers between devices with their start and end apart: 18 -> 18, of which waited for: 8 -> 8; matrix products, arithmetic and copies ran while one was open for 0% -> 0% of each run, Pallas kernels for 12% -> 11%
where the time goes in v10:
time: 51.7 us; the launch traced here: 51.6 us
  starting transfers between devices  22.7 us (44%)
  waiting for transfers between devices  18.3 us (35%)
  Pallas kernels  9.45 us (18%)
  local copies, waits for them, and re-layouts  1.1 us (2%)
    ppermute x12, starting transfers between devices, swapped(): lax.ppermute(x, 'hi', [(d, d ^ apart) for d in range(lax.axis_size('hi'))])  18.5 us
    ppermute x12, waiting for transfers between devices, swapped(): lax.ppermute(x, 'hi', [(d, d ^ apart) for d in range(lax.axis_size('hi'))])  17.9 us
    pallas_call x10, Pallas kernels, call(): pl.pallas_call(body, out_shape=outs, in_specs=specs + [ANY] * len(after),...  9.45 us
    ppermute x6, starting transfers between devices, regrouped(): lax.ppermute(x, 'lo', to)  4.18 us
    unnamed x8, local copies, waits for them, and re-layouts  1.1 us
  transfers between devices with their start and end apart: 18, of which 8 were waited for; matrix products, arithmetic and copies ran while one was open for 0% of the time, Pallas kernels for 11%

profile of v10, /device:TPU:0, one launch (start us, length us, event | category | flops | bytes accessed | tf_op | source)
XLA Modules:
  0.0 51.6 jit_solution(1074012970155451231)
XLA Ops:
  0.0 1.1 %copy-done.1 = bf16[4,3,2,64,64]{4,3,2,1,0:T(8,128)(2,1)S(1)} copy-done((bf16[4,3,2,64,64]{4,3,2,1,0:T(8,128)(2,1)S(1)}, bf16[4,3,2,64,64]{4,3,2,1,0:T(8,128)(2,1)}, u32[]{:S(2)}) %copy-start.1) | copy-done | bytes 196632
  1.1 1.0 %shard_map.37 = (bf16[128,256]{1,0:T(8,128)(2,1)S(1)}, bf16[128,256]{1,0:T(8,128)(2,1)S(1)}, bf16[256,512]{1,0:T(8,128)(2,1)S(1)}, bf16[64,128]{1,0:T(8,128)(2,1)S(1)}) custom-call(bf16[4,3,2,64,64]{4,3,2,1,0:T(8,128)(2,1)S(1)} %copy-done.1), custom_call_target="tpu_custom_call" | custom-call | flops 2000000000 | bytes 1 | tf_op jit(solution)/shard_map/pallas_call | solution.py:321
  2.1 0.0 copy-done
  2.1 1.3 %shard_map.38 = (bf16[14,32,128]{2,1,0:T(8,128)(2,1)S(1)}, bf16[14,32,128]{2,1,0:T(8,128)(2,1)S(1)}, bf16[14,32,128]{2,1,0:T(8,128)(2,1)S(1)}, bf16[14,32,128]{2...) custom-call(bf16[4096,128]{1,0:T(8,128)(2,1)S(1)} %bitcast.11, ...), custom_call_target="tpu_custom_call" | custom-call | flops 1 | bytes 1 | tf_op jit(solution)/shard_map/pallas_call | solution.py:321
  3.4 0.0 copy-start.3
  3.4 3.0 %collective-permute-start = (bf16[14,32,128]{2,1,0:T(8,128)(2,1)S(1)}, bf16[14,32,128]{2,1,0:T(8,128)(2,1)S(1)}, u32[]{:S(2)}, u32[]{:S(2)}) collective-permute-start(bf16[14,32,128]{2,1,0:T(8,128)(2,1)S(1)} %get-tuple-element.45), channel_id=1, source_target_pairs={{0,4},{4,0},{8,12},{12,8},{16,20},{20,16},{24,28},{28,24},{1,5},{5... | collective-permute-start | bytes 344072 | tf_op jit(solution)/shard_map/ppermute | solution.py:334
  6.5 1.5 %collective-permute-start.1 = (bf16[14,32,128]{2,1,0:T(8,128)(2,1)S(1)}, bf16[14,32,128]{2,1,0:T(8,128)(2,1)S(1)}, u32[]{:S(2)}, u32[]{:S(2)}) collective-permute-start(bf16[14,32,128]{2,1,0:T(8,128)(2,1)S(1)} %get-tuple-element.46), channel_id=1, source_target_pairs={{0,12},{4,8},{8,4},{12,0},{16,28},{20,24},{24,20},{28,16},{1,13},{... | collective-permute-start | bytes 344072 | tf_op jit(solution)/shard_map/ppermute | solution.py:334
  8.0 0.1 collective-permute-start.2
  8.1 2.1 %shard_map.40 = (bf16[18,32,128]{2,1,0:T(8,128)(2,1)S(1)}, bf16[18,32,128]{2,1,0:T(8,128)(2,1)S(1)}, bf16[18,32,128]{2,1,0:T(8,128)(2,1)S(1)}, bf16[18,32,128]{2...) custom-call(bf16[2048,256]{1,0:T(8,128)(2,1)S(1)} %get-tuple-element, ...), custom_call_target="tpu_custom_call" | custom-call | flops 1 | bytes 1 | tf_op jit(solution)/shard_map/pallas_call | solution.py:321
  10.2 2.0 %collective-permute-start.9 = (bf16[18,32,128]{2,1,0:T(8,128)(2,1)S(1)}, bf16[18,32,128]{2,1,0:T(8,128)(2,1)S(1)}, u32[]{:S(2)}, u32[]{:S(2)}) collective-permute-start(bf16[18,32,128]{2,1,0:T(8,128)(2,1)S(1)} %get-tuple-element.63), channel_id=1, source_target_pairs={{0,4},{4,0},{8,12},{12,8},{16,20},{20,16},{24,28},{28,24},{1,5},{5... | collective-permute-start | bytes 442376 | tf_op jit(solution)/shard_map/ppermute | solution.py:334
  12.1 1.5 %collective-permute-start.10 = (bf16[18,32,128]{2,1,0:T(8,128)(2,1)S(1)}, bf16[18,32,128]{2,1,0:T(8,128)(2,1)S(1)}, u32[]{:S(2)}, u32[]{:S(2)}) collective-permute-start(bf16[18,32,128]{2,1,0:T(8,128)(2,1)S(1)} %get-tuple-element.64), channel_id=1, source_target_pairs={{0,12},{4,8},{8,4},{12,0},{16,28},{20,24},{24,20},{28,16},{1,13},{... | collective-permute-start | bytes 442376 | tf_op jit(solution)/shard_map/ppermute | solution.py:334
  13.7 0.0 collective-permute-done.refs_1_
  13.7 0.1 collective-permute-start.11
  13.7 0.0 collective-permute-done.1.refs_2_
  13.7 0.0 collective-permute-done.2.refs_3_
  13.7 0.6 %shard_map.39 = (bf16[2,14,16,128]{3,2,1,0:T(8,128)(2,1)S(1)}, bf16[2,14,16,128]{3,2,1,0:T(8,128)(2,1)S(1)}, bf16[2,14,16,128]{3,2,1,0:T(8,128)(2,1)S(1)}, bf16[2,14,16,128]{3,2,1,0:T(8,128)(2,1)S(1)}) custom-call(s32[1,4]{1,0:T(1,128)S(1)} %bitcast.12, bf16[14,32,128]{2,1,0:T(8,128)(2,1)S(1)} %collective-permute-done.refs_1_, ...), custom_call_target="tpu_custom_call" | custom-call | flops 2000000000 | bytes 1 | tf_op jit(solution)/shard_map/pallas_call | solution.py:321
  14.3 1.9 %collective-permute-start.3 = (bf16[2,14,16,128]{3,2,1,0:T(8,128)(2,1)S(1)}, bf16[2,14,16,128]{3,2,1,0:T(8,128)(2,1)S(1)}, u32[]{:S(2)}, u32[]{:S(2)}) collective-permute-start(bf16[2,14,16,128]{3,2,1,0:T(8,128)(2,1)S(1)} %get-tuple-element.49), channel_id=1, source_target_pairs={{0,2},{1,3},{2,0},{3,1},{4,6},{5,7},{6,4},{7,5},{8,10},{9,11},{10,... | collective-permute-start | bytes 344072 | tf_op jit(solution)/shard_map/ppermute | solution.py:351
  16.3 0.0 collective-permute-start.4
  16.3 2.0 %collective-permute-done.9.refs_1_ = bf16[18,32,128]{2,1,0:T(8,128)(2,1)S(1)} collective-permute-done((bf16[18,32,128]{2,1,0:T(8,128)(2,1)S(1)}, bf16[18,32,128]{2,1,0:T(8,128)(2,1)S(1)}, u32[]{:S(2)}, u32[]{:S(2)}) %collective-permute-start.9) | collective-permute-done | bytes 147488 | tf_op jit(solution)/shard_map/ppermute | solution.py:334
  18.3 0.0 collective-permute-start.5
  18.3 1.0 %collective-permute-done.10.refs_2_ = bf16[18,32,128]{2,1,0:T(8,128)(2,1)S(1)} collective-permute-done((bf16[18,32,128]{2,1,0:T(8,128)(2,1)S(1)}, bf16[18,32,128]{2,1,0:T(8,128)(2,1)S(1)}, u32[]{:S(2)}, u32[]{:S(2)}) %collective-permute-start.10) | collective-permute-done | bytes 147488 | tf_op jit(solution)/shard_map/ppermute | solution.py:334
  19.3 0.5 collective-permute-done.11.refs_3_
  19.8 0.6 %shard_map.43 = (bf16[2,18,16,128]{3,2,1,0:T(8,128)(2,1)S(1)}, bf16[2,18,16,128]{3,2,1,0:T(8,128)(2,1)S(1)}, bf16[2,18,16,128]{3,2,1,0:T(8,128)(2,1)S(1)}, bf16[2,18,16,128]{3,2,1,0:T(8,128)(2,1)S(1)}) custom-call(s32[1,4]{1,0:T(1,128)S(1)} %bitcast.13, bf16[18,32,128]{2,1,0:T(8,128)(2,1)S(1)} %collective-permute-done.9.refs_1_, ...), custom_call_target="tpu_custom_call" | custom-call | flops 1 | bytes 1 | tf_op jit(solution)/shard_map/pallas_call | solution.py:321
  20.4 1.7 %collective-permute-start.12 = (bf16[2,18,16,128]{3,2,1,0:T(8,128)(2,1)S(1)}, bf16[2,18,16,128]{3,2,1,0:T(8,128)(2,1)S(1)}, u32[]{:S(2)}, u32[]{:S(2)}) collective-permute-start(bf16[2,18,16,128]{3,2,1,0:T(8,128)(2,1)S(1)} %get-tuple-element.67), channel_id=1, source_target_pairs={{0,2},{1,3},{2,0},{3,1},{4,6},{5,7},{6,4},{7,5},{8,10},{9,11},{10,... | collective-permute-start | bytes 442376 | tf_op jit(solution)/shard_map/ppermute | solution.py:351
  22.0 0.0 collective-permute-start.13
  22.0 0.0 collective-permute-done.3.refs_0_
  22.0 0.5 %collective-permute-start.14 = (bf16[2,18,16,128]{3,2,1,0:T(8,128)(2,1)S(1)}, bf16[2,18,16,128]{3,2,1,0:T(8,128)(2,1)S(1)}, u32[]{:S(2)}, u32[]{:S(2)}) collective-permute-start(bf16[2,18,16,128]{3,2,1,0:T(8,128)(2,1)S(1)} %get-tuple-element.69), channel_id=1, source_target_pairs={{0,1},{1,0},{2,3},{3,2},{4,5},{5,4},{6,7},{7,6},{8,9},{9,8},{10,11... | collective-permute-start | bytes 442376 | tf_op jit(solution)/shard_map/ppermute | solution.py:351
  22.6 0.0 collective-permute-done.4.refs_1_
  22.6 0.0 collective-permute-done.5.refs_2_
  22.6 0.5 %shard_map.41 = (bf16[14,32,128]{2,1,0:T(8,128)(2,1)S(1)}, bf16[14,32,128]{2,1,0:T(8,128)(2,1)S(1)}, bf16[14,32,128]{2,1,0:T(8,128)(2,1)S(1)}, bf16[14,32,128]{2,1,0:T(8,128)(2,1)S(1)}) custom-call(bf16[2,14,16,128]{3,2,1,0:T(8,128)(2,1)S(1)} %collective-permute-done.3.refs_0_, bf16[2,14,16,128]{3,2,1,0:T(8,128)(2,1)S(1)} %collective-permute-done.4.refs_1_, ...), custom_call_target="tpu_custom_call" | custom-call | flops 2000000000 | bytes 1 | tf_op jit(solution)/shard_map/pallas_call | solution.py:321
  23.1 2.8 %collective-permute-start.6 = (bf16[14,32,128]{2,1,0:T(8,128)(2,1)S(1)}, bf16[14,32,128]{2,1,0:T(8,128)(2,1)S(1)}, u32[]{:S(2)}, u32[]{:S(2)}) collective-permute-start(bf16[14,32,128]{2,1,0:T(8,128)(2,1)S(1)} %get-tuple-element.58), channel_id=1, source_target_pairs={{0,16},{4,20},{8,24},{12,28},{16,0},{20,4},{24,8},{28,12},{1,17},{... | collective-permute-start | bytes 344072 | tf_op jit(solution)/shard_map/ppermute | solution.py:334
  25.9 1.3 %collective-permute-start.7 = (bf16[14,32,128]{2,1,0:T(8,128)(2,1)S(1)}, bf16[14,32,128]{2,1,0:T(8,128)(2,1)S(1)}, u32[]{:S(2)}, u32[]{:S(2)}) collective-permute-start(bf16[14,32,128]{2,1,0:T(8,128)(2,1)S(1)} %get-tuple-element.59), channel_id=1, source_target_pairs={{0,20},{4,16},{8,28},{12,24},{16,4},{20,0},{24,12},{28,8},{1,21},{... | collective-permute-start | bytes 344072 | tf_op jit(solution)/shard_map/ppermute | solution.py:334
  27.2 0.0 collective-permute-done.12.refs_0_
  27.2 0.7 %collective-permute-start.8 = (bf16[14,32,128]{2,1,0:T(8,128)(2,1)S(1)}, bf16[14,32,128]{2,1,0:T(8,128)(2,1)S(1)}, u32[]{:S(2)}, u32[]{:S(2)}) collective-permute-start(bf16[14,32,128]{2,1,0:T(8,128)(2,1)S(1)} %get-tuple-element.60), channel_id=1, source_target_pairs={{0,4},{4,0},{8,12},{12,8},{16,20},{20,16},{24,28},{28,24},{1,5},{5... | collective-permute-start | bytes 344072 | tf_op jit(solution)/shard_map/ppermute | solution.py:334
  27.9 0.3 collective-permute-done.13.refs_1_
  28.2 0.6 %shard_map.44 = (bf16[18,32,128]{2,1,0:T(8,128)(2,1)S(1)}, bf16[18,32,128]{2,1,0:T(8,128)(2,1)S(1)}, bf16[18,32,128]{2,1,0:T(8,128)(2,1)S(1)}, bf16[18,32,128]{2,1,0:T(8,128)(2,1)S(1)}) custom-call(bf16[2,18,16,128]{3,2,1,0:T(8,128)(2,1)S(1)} %collective-permute-done.12.refs_0_, bf16[2,18,16,128]{3,2,1,0:T(8,128)(2,1)S(1)} %collective-permute-done.13.refs_1_, ...), custom_call_target="tpu_custom_call" | custom-call | flops 1 | bytes 1 | tf_op jit(solution)/shard_map/pallas_call | solution.py:321
  28.8 2.6 %collective-permute-start.15 = (bf16[18,32,128]{2,1,0:T(8,128)(2,1)S(1)}, bf16[18,32,128]{2,1,0:T(8,128)(2,1)S(1)}, u32[]{:S(2)}, u32[]{:S(2)}) collective-permute-start(bf16[18,32,128]{2,1,0:T(8,128)(2,1)S(1)} %get-tuple-element.71), channel_id=1, source_target_pairs={{0,16},{4,20},{8,24},{12,28},{16,0},{20,4},{24,8},{28,12},{1,17},{... | collective-permute-start | bytes 442376 | tf_op jit(solution)/shard_map/ppermute | solution.py:334
  31.5 1.3 %collective-permute-start.16 = (bf16[18,32,128]{2,1,0:T(8,128)(2,1)S(1)}, bf16[18,32,128]{2,1,0:T(8,128)(2,1)S(1)}, u32[]{:S(2)}, u32[]{:S(2)}) collective-permute-start(bf16[18,32,128]{2,1,0:T(8,128)(2,1)S(1)} %get-tuple-element.76), channel_id=1, source_target_pairs={{0,20},{4,16},{8,28},{12,24},{16,4},{20,0},{24,12},{28,8},{1,21},{... | collective-permute-start | bytes 442376 | tf_op jit(solution)/shard_map/ppermute | solution.py:334
  32.8 8.6 %collective-permute-done.6.refs_0_ = bf16[14,32,128]{2,1,0:T(8,128)(2,1)S(1)} collective-permute-done((bf16[14,32,128]{2,1,0:T(8,128)(2,1)S(1)}, bf16[14,32,128]{2,1,0:T(8,128)(2,1)S(1)}, u32[]{:S(2)}, u32[]{:S(2)}) %collective-permute-start.6) | collective-permute-done | bytes 114720 | tf_op jit(solution)/shard_map/ppermute | solution.py:334
  41.3 1.6 %collective-permute-start.17 = (bf16[18,32,128]{2,1,0:T(8,128)(2,1)S(1)}, bf16[18,32,128]{2,1,0:T(8,128)(2,1)S(1)}, u32[]{:S(2)}, u32[]{:S(2)}) collective-permute-start(bf16[18,32,128]{2,1,0:T(8,128)(2,1)S(1)} %get-tuple-element.77), channel_id=1, source_target_pairs={{0,4},{4,0},{8,12},{12,8},{16,20},{20,16},{24,28},{28,24},{1,5},{5... | collective-permute-start | bytes 442376 | tf_op jit(solution)/shard_map/ppermute | solution.py:334
  43.0 1.9 %collective-permute-done.7.refs_1_ = bf16[14,32,128]{2,1,0:T(8,128)(2,1)S(1)} collective-permute-done((bf16[14,32,128]{2,1,0:T(8,128)(2,1)S(1)}, bf16[14,32,128]{2,1,0:T(8,128)(2,1)S(1)}, u32[]{:S(2)}, u32[]{:S(2)}) %collective-permute-start.7) | collective-permute-done | bytes 114720 | tf_op jit(solution)/shard_map/ppermute | solution.py:334
  44.9 0.0 collective-permute-done.8.refs_2_
  44.9 0.1 shard_map.42
  44.9 2.0 %collective-permute-done.15.refs_1_ = bf16[18,32,128]{2,1,0:T(8,128)(2,1)S(1)} collective-permute-done((bf16[18,32,128]{2,1,0:T(8,128)(2,1)S(1)}, bf16[18,32,128]{2,1,0:T(8,128)(2,1)S(1)}, u32[]{:S(2)}, u32[]{:S(2)}) %collective-permute-start.15) | collective-permute-done | bytes 147488 | tf_op jit(solution)/shard_map/ppermute | solution.py:334
  47.0 1.3 %shard_map.45 = (bf16[4096,128]{1,0:T(8,128)(2,1)}, f32[2,1056,128]{2,1,0:T(8,128)S(1)}) custom-call(f32[2,1056,128]{2,1,0:T(8,128)S(1)} %get-tuple-element.62.refs_0_, bf16[18,32,128]{2,1,0:T(8,128)(2,1)S(1)} %collective-permute-done.15.refs_1_, bf16[18,32,128]{2,1,0:T(8,128)(2,1)S(1)} %get-tuple-element.72.refs_2_, ...), custom_call_target="tpu_custom_call", output_to_operand_aliasing={{1}: (0, {})} | custom-call | flops 1 | bytes 1 | tf_op jit(solution)/shard_map/pallas_call | solution.py:321
  48.3 1.9 %collective-permute-done.16.refs_2_ = bf16[18,32,128]{2,1,0:T(8,128)(2,1)S(1)} collective-permute-done((bf16[18,32,128]{2,1,0:T(8,128)(2,1)S(1)}, bf16[18,32,128]{2,1,0:T(8,128)(2,1)S(1)}, u32[]{:S(2)}, u32[]{:S(2)}) %collective-permute-start.16) | collective-permute-done | bytes 147488 | tf_op jit(solution)/shard_map/ppermute | solution.py:334
  50.2 0.0 collective-permute-done.17.refs_3_
  50.2 1.3 %shard_map.46 = (bf16[4096,128]{1,0:T(8,128)(2,1)}, f32[2,1056,128]{2,1,0:T(8,128)S(1)}) custom-call(bf16[4096,128]{1,0:T(8,128)(2,1)} %get-tuple-element.74.refs_0_, f32[2,1056,128]{2,1,0:T(8,128)S(1)} %get-tuple-element.75.refs_1_, bf16[18,32,128]{2,1,0:T(8,128)(2,1)S(1)} %collective-permute-done.16.refs_2_, ...), custom_call_target="tpu_custom_call", output_to_operand_aliasing={{0}: (0, {}), {1}: (1, {})} | custom-call | flops 1 | bytes 1 | tf_op jit(solution)/shard_map/pallas_call | solution.py:321
  (6 shorter events, 0.0 us)
Async XLA Ops:
  0.0 2.1 %copy-start = (bf16[2,262144]{1,0:T(2,128)(2,1)S(1)}, bf16[2,262144]{1,0:T(2,128)(2,1)}, u32[]{:S(2)}) copy-start(bf16[2,262144]{1,0:T(2,128)(2,1)} %param.3) | copy-start | bytes 3145732
  0.0 1.1 %copy-start.1 = (bf16[4,3,2,64,64]{4,3,2,1,0:T(8,128)(2,1)S(1)}, bf16[4,3,2,64,64]{4,3,2,1,0:T(8,128)(2,1)}, u32[]{:S(2)}) copy-start(bf16[4,3,2,64,64]{4,3,2,1,0:T(8,128)(2,1)} %refs_5_.1) | copy-start | bytes 589828
  2.1 6.0 %copy-start.2 = (bf16[4,3,2,64,64]{4,3,2,1,0:T(8,128)(2,1)S(1)}, bf16[4,3,2,64,64]{4,3,2,1,0:T(8,128)(2,1)}, u32[]{:S(2)}) copy-start(bf16[4,3,2,64,64]{4,3,2,1,0:T(8,128)(2,1)} %refs_5_.1) | copy-start | bytes 589828
  3.4 10.3 %copy-start.3 = (s32[4]{0:T(128)S(1)}, s32[4]{0:T(128)}, u32[]{:S(2)}) copy-start(s32[4]{0:T(128)} %param.5) | copy-start | bytes 52
  3.4 10.2 %collective-permute-start = (bf16[14,32,128]{2,1,0:T(8,128)(2,1)S(1)}, bf16[14,32,128]{2,1,0:T(8,128)(2,1)S(1)}, u32[]{:S(2)}, u32[]{:S(2)}) collective-permute-start(bf16[14,32,128]{2,1,0:T(8,128)(2,1)S(1)} %get-tuple-element.45), channel_id=1, source_target_pairs={{0,4},{4,0},{8,12},{12,8},{16,20},{20,16},{24,28},{28,24},{1,5},{5... | collective-permute-start | bytes 344072 | tf_op jit(solution)/shard_map/ppermute | solution.py:334
  6.5 7.3 %collective-permute-start.1 = (bf16[14,32,128]{2,1,0:T(8,128)(2,1)S(1)}, bf16[14,32,128]{2,1,0:T(8,128)(2,1)S(1)}, u32[]{:S(2)}, u32[]{:S(2)}) collective-permute-start(bf16[14,32,128]{2,1,0:T(8,128)(2,1)S(1)} %get-tuple-element.46), channel_id=1, source_target_pairs={{0,12},{4,8},{8,4},{12,0},{16,28},{20,24},{24,20},{28,16},{1,13},{... | collective-permute-start | bytes 344072 | tf_op jit(solution)/shard_map/ppermute | solution.py:334
  8.0 5.7 %collective-permute-start.2 = (bf16[14,32,128]{2,1,0:T(8,128)(2,1)S(1)}, bf16[14,32,128]{2,1,0:T(8,128)(2,1)S(1)}, u32[]{:S(2)}, u32[]{:S(2)}) collective-permute-start(bf16[14,32,128]{2,1,0:T(8,128)(2,1)S(1)} %get-tuple-element.47), channel_id=1, source_target_pairs={{0,8},{4,12},{8,0},{12,4},{16,24},{20,28},{24,16},{28,20},{1,9},{5... | collective-permute-start | bytes 344072 | tf_op jit(solution)/shard_map/ppermute | solution.py:334
  10.2 8.1 %collective-permute-start.9 = (bf16[18,32,128]{2,1,0:T(8,128)(2,1)S(1)}, bf16[18,32,128]{2,1,0:T(8,128)(2,1)S(1)}, u32[]{:S(2)}, u32[]{:S(2)}) collective-permute-start(bf16[18,32,128]{2,1,0:T(8,128)(2,1)S(1)} %get-tuple-element.63), channel_id=1, source_target_pairs={{0,4},{4,0},{8,12},{12,8},{16,20},{20,16},{24,28},{28,24},{1,5},{5... | collective-permute-start | bytes 442376 | tf_op jit(solution)/shard_map/ppermute | solution.py:334
  12.1 7.1 %collective-permute-start.10 = (bf16[18,32,128]{2,1,0:T(8,128)(2,1)S(1)}, bf16[18,32,128]{2,1,0:T(8,128)(2,1)S(1)}, u32[]{:S(2)}, u32[]{:S(2)}) collective-permute-start(bf16[18,32,128]{2,1,0:T(8,128)(2,1)S(1)} %get-tuple-element.64), channel_id=1, source_target_pairs={{0,12},{4,8},{8,4},{12,0},{16,28},{20,24},{24,20},{28,16},{1,13},{... | collective-permute-start | bytes 442376 | tf_op jit(solution)/shard_map/ppermute | solution.py:334
  13.7 6.1 %collective-permute-start.11 = (bf16[18,32,128]{2,1,0:T(8,128)(2,1)S(1)}, bf16[18,32,128]{2,1,0:T(8,128)(2,1)S(1)}, u32[]{:S(2)}, u32[]{:S(2)}) collective-permute-start(bf16[18,32,128]{2,1,0:T(8,128)(2,1)S(1)} %get-tuple-element.65), channel_id=1, source_target_pairs={{0,8},{4,12},{8,0},{12,4},{16,24},{20,28},{24,16},{28,20},{1,9},{5... | collective-permute-start | bytes 442376 | tf_op jit(solution)/shard_map/ppermute | solution.py:334
  14.3 7.7 %collective-permute-start.3 = (bf16[2,14,16,128]{3,2,1,0:T(8,128)(2,1)S(1)}, bf16[2,14,16,128]{3,2,1,0:T(8,128)(2,1)S(1)}, u32[]{:S(2)}, u32[]{:S(2)}) collective-permute-start(bf16[2,14,16,128]{3,2,1,0:T(8,128)(2,1)S(1)} %get-tuple-element.49), channel_id=1, source_target_pairs={{0,2},{1,3},{2,0},{3,1},{4,6},{5,7},{6,4},{7,5},{8,10},{9,11},{10,... | collective-permute-start | bytes 344072 | tf_op jit(solution)/shard_map/ppermute | solution.py:351
  16.3 6.3 %collective-permute-start.4 = (bf16[2,14,16,128]{3,2,1,0:T(8,128)(2,1)S(1)}, bf16[2,14,16,128]{3,2,1,0:T(8,128)(2,1)S(1)}, u32[]{:S(2)}, u32[]{:S(2)}) collective-permute-start(bf16[2,14,16,128]{3,2,1,0:T(8,128)(2,1)S(1)} %get-tuple-element.50), channel_id=1, source_target_pairs={{0,3},{1,2},{2,1},{3,0},{4,7},{5,6},{6,5},{7,4},{8,11},{9,10},{10,... | collective-permute-start | bytes 344072 | tf_op jit(solution)/shard_map/ppermute | solution.py:351
  18.3 4.3 %collective-permute-start.5 = (bf16[2,14,16,128]{3,2,1,0:T(8,128)(2,1)S(1)}, bf16[2,14,16,128]{3,2,1,0:T(8,128)(2,1)S(1)}, u32[]{:S(2)}, u32[]{:S(2)}) collective-permute-start(bf16[2,14,16,128]{3,2,1,0:T(8,128)(2,1)S(1)} %get-tuple-element.51), channel_id=1, source_target_pairs={{0,1},{1,0},{2,3},{3,2},{4,5},{5,4},{6,7},{7,6},{8,9},{9,8},{10,11... | collective-permute-start | bytes 344072 | tf_op jit(solution)/shard_map/ppermute | solution.py:351
  20.4 6.8 %collective-permute-start.12 = (bf16[2,18,16,128]{3,2,1,0:T(8,128)(2,1)S(1)}, bf16[2,18,16,128]{3,2,1,0:T(8,128)(2,1)S(1)}, u32[]{:S(2)}, u32[]{:S(2)}) collective-permute-start(bf16[2,18,16,128]{3,2,1,0:T(8,128)(2,1)S(1)} %get-tuple-element.67), channel_id=1, source_target_pairs={{0,2},{1,3},{2,0},{3,1},{4,6},{5,7},{6,4},{7,5},{8,10},{9,11},{10,... | collective-permute-start | bytes 442376 | tf_op jit(solution)/shard_map/ppermute | solution.py:351
  22.0 6.1 %collective-permute-start.13 = (bf16[2,18,16,128]{3,2,1,0:T(8,128)(2,1)S(1)}, bf16[2,18,16,128]{3,2,1,0:T(8,128)(2,1)S(1)}, u32[]{:S(2)}, u32[]{:S(2)}) collective-permute-start(bf16[2,18,16,128]{3,2,1,0:T(8,128)(2,1)S(1)} %get-tuple-element.68), channel_id=1, source_target_pairs={{0,3},{1,2},{2,1},{3,0},{4,7},{5,6},{6,5},{7,4},{8,11},{9,10},{10,... | collective-permute-start | bytes 442376 | tf_op jit(solution)/shard_map/ppermute | solution.py:351
  22.0 6.1 %collective-permute-start.14 = (bf16[2,18,16,128]{3,2,1,0:T(8,128)(2,1)S(1)}, bf16[2,18,16,128]{3,2,1,0:T(8,128)(2,1)S(1)}, u32[]{:S(2)}, u32[]{:S(2)}) collective-permute-start(bf16[2,18,16,128]{3,2,1,0:T(8,128)(2,1)S(1)} %get-tuple-element.69), channel_id=1, source_target_pairs={{0,1},{1,0},{2,3},{3,2},{4,5},{5,4},{6,7},{7,6},{8,9},{9,8},{10,11... | collective-permute-start | bytes 442376 | tf_op jit(solution)/shard_map/ppermute | solution.py:351
  23.1 18.2 %collective-permute-start.6 = (bf16[14,32,128]{2,1,0:T(8,128)(2,1)S(1)}, bf16[14,32,128]{2,1,0:T(8,128)(2,1)S(1)}, u32[]{:S(2)}, u32[]{:S(2)}) collective-permute-start(bf16[14,32,128]{2,1,0:T(8,128)(2,1)S(1)} %get-tuple-element.58), channel_id=1, source_target_pairs={{0,16},{4,20},{8,24},{12,28},{16,0},{20,4},{24,8},{28,12},{1,17},{... | collective-permute-start | bytes 344072 | tf_op jit(solution)/shard_map/ppermute | solution.py:334
  25.9 18.9 %collective-permute-start.7 = (bf16[14,32,128]{2,1,0:T(8,128)(2,1)S(1)}, bf16[14,32,128]{2,1,0:T(8,128)(2,1)S(1)}, u32[]{:S(2)}, u32[]{:S(2)}) collective-permute-start(bf16[14,32,128]{2,1,0:T(8,128)(2,1)S(1)} %get-tuple-element.59), channel_id=1, source_target_pairs={{0,20},{4,16},{8,28},{12,24},{16,4},{20,0},{24,12},{28,8},{1,21},{... | collective-permute-start | bytes 344072 | tf_op jit(solution)/shard_map/ppermute | solution.py:334
  27.2 17.7 %collective-permute-start.8 = (bf16[14,32,128]{2,1,0:T(8,128)(2,1)S(1)}, bf16[14,32,128]{2,1,0:T(8,128)(2,1)S(1)}, u32[]{:S(2)}, u32[]{:S(2)}) collective-permute-start(bf16[14,32,128]{2,1,0:T(8,128)(2,1)S(1)} %get-tuple-element.60), channel_id=1, source_target_pairs={{0,4},{4,0},{8,12},{12,8},{16,20},{20,16},{24,28},{28,24},{1,5},{5... | collective-permute-start | bytes 344072 | tf_op jit(solution)/shard_map/ppermute | solution.py:334
  28.8 18.1 %collective-permute-start.15 = (bf16[18,32,128]{2,1,0:T(8,128)(2,1)S(1)}, bf16[18,32,128]{2,1,0:T(8,128)(2,1)S(1)}, u32[]{:S(2)}, u32[]{:S(2)}) collective-permute-start(bf16[18,32,128]{2,1,0:T(8,128)(2,1)S(1)} %get-tuple-element.71), channel_id=1, source_target_pairs={{0,16},{4,20},{8,24},{12,28},{16,0},{20,4},{24,8},{28,12},{1,17},{... | collective-permute-start | bytes 442376 | tf_op jit(solution)/shard_map/ppermute | solution.py:334
  31.5 18.8 %collective-permute-start.16 = (bf16[18,32,128]{2,1,0:T(8,128)(2,1)S(1)}, bf16[18,32,128]{2,1,0:T(8,128)(2,1)S(1)}, u32[]{:S(2)}, u32[]{:S(2)}) collective-permute-start(bf16[18,32,128]{2,1,0:T(8,128)(2,1)S(1)} %get-tuple-element.76), channel_id=1, source_target_pairs={{0,20},{4,16},{8,28},{12,24},{16,4},{20,0},{24,12},{28,8},{1,21},{... | collective-permute-start | bytes 442376 | tf_op jit(solution)/shard_map/ppermute | solution.py:334
  41.3 8.9 %collective-permute-start.17 = (bf16[18,32,128]{2,1,0:T(8,128)(2,1)S(1)}, bf16[18,32,128]{2,1,0:T(8,128)(2,1)S(1)}, u32[]{:S(2)}, u32[]{:S(2)}) collective-permute-start(bf16[18,32,128]{2,1,0:T(8,128)(2,1)S(1)} %get-tuple-element.77), channel_id=1, source_target_pairs={{0,4},{4,0},{8,12},{12,8},{16,20},{20,16},{24,28},{28,24},{1,5},{5... | collective-permute-start | bytes 442376 | tf_op jit(solution)/shard_map/ppermute | solution.py:334

commit v11 on v10

--- a/solution.py
+++ b/solution.py
@@ -168,7 +168,6 @@
                 blocks[i, j][at + k] = out[j * HALF : (j + 1) * HALF, i * 128 : (i + 1) * 128]
 
 
-STEP = 22
 PITCH = G + 1
 NARROW = HALF + 1
 EARLY = 14
@@ -179,12 +178,6 @@
     hi_bits = lax.axis_size("hi").bit_length() - 1
     hi = lax.axis_index("hi")
     return [hi >> k % hi_bits & 1 for k in range(4)]
-
-
-def steps(size):
-    parts = -(-size // STEP)
-    ends = [size * k // parts for k in range(parts + 1)]
-    return [(k, end - k) for k, end in zip(ends, ends[1:])]
 
 
 def split_rows(k, x, w, turned):
@@ -242,16 +235,15 @@
     store_blocks(made, rest.shape[0], blocks)
 
 
-def joined(ins, k, n):
+def joined(ins):
     order = [APART.index(o) for o in range(4)] if len(ins) > 1 else [0]
-    halves = [jnp.concatenate([ins[at][i, k : k + n] for at in order], axis=1) for i in range(2)]
+    halves = [jnp.concatenate([ins[at][i] for at in order], axis=1) for i in range(2)]
     return jnp.concatenate(halves, axis=2)
 
 
 def middle_kernel(*refs):
     *ins, w1_ref, g_ref, o0, o1, o2, o3 = refs
-    for k, n in steps(o0.shape[0]):
-        store_blocks(both_gates(joined(ins, k, n), w1_ref[...], g_ref[...]), k, (o0, o1, o2, o3))
+    store_blocks(both_gates(joined(ins), w1_ref[...], g_ref[...]), 0, (o0, o1, o2, o3))
 
 
 def gather_rows(first, pair, wide):
@@ -358,6 +350,10 @@
     return [both.reshape(2, count, G, 128)]
 
 
+def padded(rows):
+    return -(-(rows + PITCH) // 8) * 8
+
+
 def on_device(state, gates, regroup):
     hi_bits = lax.axis_size("hi").bit_length() - 1
     groups = lax.axis_size("lo")
@@ -367,8 +363,8 @@
 
     block = jax.ShapeDtypeStruct((HALF - EARLY, HALF, 128), BF)
     early_block = jax.ShapeDtypeStruct((EARLY, HALF, 128), BF)
-    turned = pltpu.VMEM((2, HALF // 2 * PITCH, 128), F32)
-    spread = pltpu.VMEM((whole, 128), F32)
+    turned = pltpu.VMEM((2, padded(HALF // 2 * PITCH), 128), F32)
+    spread = pltpu.VMEM((padded(whole), 128), F32)
     lanes, rows = (4 * G, 8 * G), (G, 2 * G)
 
     x = state.reshape(2, -1, 128).transpose(1, 0, 2).reshape(whole, 128)
@@ -388,7 +384,7 @@
     early = exchange(early, bits[2], bits[3])
     late = exchange(late, bits[2], bits[3])
 
-    wide = jax.ShapeDtypeStruct((2, HALF * NARROW, 128), F32)
+    wide = jax.ShapeDtypeStruct((2, padded(HALF * NARROW), 128), F32)
     wides = call(gather_kernel, [wide] * 2, early, flops=COST)
     late = by_place(late)
     scratch = [pltpu.VMEM((whole // 2, 128), BF), pltpu.SemaphoreType.DMA((HALF // 8,))]

time: 51.7 us -> 51.7 us (level)
  no operation moved by 1% of the time
where the time goes in v11:
time: 51.7 us; the launch traced here: 51.6 us
  starting transfers between devices  22.6 us (44%)
  waiting for transfers between devices  18.3 us (35%)
  Pallas kernels  9.46 us (18%)
  local copies, waits for them, and re-layouts  1.1 us (2%)
    ppermute x12, starting transfers between devices, swapped(): lax.ppermute(x, 'hi', [(d, d ^ apart) for d in range(lax.axis_size('hi'))])  18.5 us
    ppermute x12, waiting for transfers between devices, swapped(): lax.ppermute(x, 'hi', [(d, d ^ apart) for d in range(lax.axis_size('hi'))])  17.9 us
    pallas_call x10, Pallas kernels, call(): pl.pallas_call(body, out_shape=outs, in_specs=specs + [ANY] * len(after),...  9.46 us
    ppermute x6, starting transfers between devices, regrouped(): lax.ppermute(x, 'lo', to)  4.17 us
    unnamed x8, local copies, waits for them, and re-layouts  1.1 us
  transfers between devices with their start and end apart: 18, of which 8 were waited for; matrix products, arithmetic and copies ran while one was open for 0% of the time, Pallas kernels for 11%

profile of v11, /device:TPU:0, one launch (start us, length us, event | category | flops | bytes accessed | tf_op | source)
XLA Modules:
  0.0 51.6 jit_solution(1124836825179208739)
XLA Ops:
  0.0 1.1 %copy-done.1 = bf16[4,3,2,64,64]{4,3,2,1,0:T(8,128)(2,1)S(1)} copy-done((bf16[4,3,2,64,64]{4,3,2,1,0:T(8,128)(2,1)S(1)}, bf16[4,3,2,64,64]{4,3,2,1,0:T(8,128)(2,1)}, u32[]{:S(2)}) %copy-start.1) | copy-done | bytes 196632
  1.1 1.0 %shard_map.37 = (bf16[128,256]{1,0:T(8,128)(2,1)S(1)}, bf16[128,256]{1,0:T(8,128)(2,1)S(1)}, bf16[256,512]{1,0:T(8,128)(2,1)S(1)}, bf16[64,128]{1,0:T(8,128)(2,1)S(1)}) custom-call(bf16[4,3,2,64,64]{4,3,2,1,0:T(8,128)(2,1)S(1)} %copy-done.1), custom_call_target="tpu_custom_call" | custom-call | flops 2000000000 | bytes 1 | tf_op jit(solution)/shard_map/pallas_call | solution.py:313
  2.1 0.0 copy-done
  2.1 1.4 %shard_map.38 = (bf16[14,32,128]{2,1,0:T(8,128)(2,1)S(1)}, bf16[14,32,128]{2,1,0:T(8,128)(2,1)S(1)}, bf16[14,32,128]{2,1,0:T(8,128)(2,1)S(1)}, bf16[14,32,128]{2...) custom-call(bf16[4096,128]{1,0:T(8,128)(2,1)S(1)} %bitcast.11, ...), custom_call_target="tpu_custom_call" | custom-call | flops 1 | bytes 1 | tf_op jit(solution)/shard_map/pallas_call | solution.py:313
  3.4 0.0 copy-start.3
  3.4 3.0 %collective-permute-start = (bf16[14,32,128]{2,1,0:T(8,128)(2,1)S(1)}, bf16[14,32,128]{2,1,0:T(8,128)(2,1)S(1)}, u32[]{:S(2)}, u32[]{:S(2)}) collective-permute-start(bf16[14,32,128]{2,1,0:T(8,128)(2,1)S(1)} %get-tuple-element.45), channel_id=1, source_target_pairs={{0,4},{4,0},{8,12},{12,8},{16,20},{20,16},{24,28},{28,24},{1,5},{5... | collective-permute-start | bytes 344072 | tf_op jit(solution)/shard_map/ppermute | solution.py:326
  6.5 1.5 %collective-permute-start.1 = (bf16[14,32,128]{2,1,0:T(8,128)(2,1)S(1)}, bf16[14,32,128]{2,1,0:T(8,128)(2,1)S(1)}, u32[]{:S(2)}, u32[]{:S(2)}) collective-permute-start(bf16[14,32,128]{2,1,0:T(8,128)(2,1)S(1)} %get-tuple-element.46), channel_id=1, source_target_pairs={{0,12},{4,8},{8,4},{12,0},{16,28},{20,24},{24,20},{28,16},{1,13},{... | collective-permute-start | bytes 344072 | tf_op jit(solution)/shard_map/ppermute | solution.py:326
  8.0 0.1 collective-permute-start.2
  8.1 2.1 %shard_map.40 = (bf16[18,32,128]{2,1,0:T(8,128)(2,1)S(1)}, bf16[18,32,128]{2,1,0:T(8,128)(2,1)S(1)}, bf16[18,32,128]{2,1,0:T(8,128)(2,1)S(1)}, bf16[18,32,128]{2...) custom-call(bf16[2048,256]{1,0:T(8,128)(2,1)S(1)} %get-tuple-element, ...), custom_call_target="tpu_custom_call" | custom-call | flops 1 | bytes 1 | tf_op jit(solution)/shard_map/pallas_call | solution.py:313
  10.2 2.0 %collective-permute-start.9 = (bf16[18,32,128]{2,1,0:T(8,128)(2,1)S(1)}, bf16[18,32,128]{2,1,0:T(8,128)(2,1)S(1)}, u32[]{:S(2)}, u32[]{:S(2)}) collective-permute-start(bf16[18,32,128]{2,1,0:T(8,128)(2,1)S(1)} %get-tuple-element.63), channel_id=1, source_target_pairs={{0,4},{4,0},{8,12},{12,8},{16,20},{20,16},{24,28},{28,24},{1,5},{5... | collective-permute-start | bytes 442376 | tf_op jit(solution)/shard_map/ppermute | solution.py:326
  12.1 1.5 %collective-permute-start.10 = (bf16[18,32,128]{2,1,0:T(8,128)(2,1)S(1)}, bf16[18,32,128]{2,1,0:T(8,128)(2,1)S(1)}, u32[]{:S(2)}, u32[]{:S(2)}) collective-permute-start(bf16[18,32,128]{2,1,0:T(8,128)(2,1)S(1)} %get-tuple-element.64), channel_id=1, source_target_pairs={{0,12},{4,8},{8,4},{12,0},{16,28},{20,24},{24,20},{28,16},{1,13},{... | collective-permute-start | bytes 442376 | tf_op jit(solution)/shard_map/ppermute | solution.py:326
  13.7 0.0 collective-permute-done.refs_1_
  13.7 0.1 collective-permute-start.11
  13.7 0.0 collective-permute-done.1.refs_2_
  13.7 0.0 collective-permute-done.2.refs_3_
  13.7 0.6 %shard_map.39 = (bf16[2,14,16,128]{3,2,1,0:T(8,128)(2,1)S(1)}, bf16[2,14,16,128]{3,2,1,0:T(8,128)(2,1)S(1)}, bf16[2,14,16,128]{3,2,1,0:T(8,128)(2,1)S(1)}, bf16[2,14,16,128]{3,2,1,0:T(8,128)(2,1)S(1)}) custom-call(s32[1,4]{1,0:T(1,128)S(1)} %bitcast.12, bf16[14,32,128]{2,1,0:T(8,128)(2,1)S(1)} %collective-permute-done.refs_1_, ...), custom_call_target="tpu_custom_call" | custom-call | flops 2000000000 | bytes 1 | tf_op jit(solution)/shard_map/pallas_call | solution.py:313
  14.3 1.9 %collective-permute-start.3 = (bf16[2,14,16,128]{3,2,1,0:T(8,128)(2,1)S(1)}, bf16[2,14,16,128]{3,2,1,0:T(8,128)(2,1)S(1)}, u32[]{:S(2)}, u32[]{:S(2)}) collective-permute-start(bf16[2,14,16,128]{3,2,1,0:T(8,128)(2,1)S(1)} %get-tuple-element.49), channel_id=1, source_target_pairs={{0,2},{1,3},{2,0},{3,1},{4,6},{5,7},{6,4},{7,5},{8,10},{9,11},{10,... | collective-permute-start | bytes 344072 | tf_op jit(solution)/shard_map/ppermute | solution.py:343
  16.3 0.0 collective-permute-start.4
  16.3 2.0 %collective-permute-done.9.refs_1_ = bf16[18,32,128]{2,1,0:T(8,128)(2,1)S(1)} collective-permute-done((bf16[18,32,128]{2,1,0:T(8,128)(2,1)S(1)}, bf16[18,32,128]{2,1,0:T(8,128)(2,1)S(1)}, u32[]{:S(2)}, u32[]{:S(2)}) %collective-permute-start.9) | collective-permute-done | bytes 147488 | tf_op jit(solution)/shard_map/ppermute | solution.py:326
  18.3 0.0 collective-permute-start.5
  18.3 1.0 %collective-permute-done.10.refs_2_ = bf16[18,32,128]{2,1,0:T(8,128)(2,1)S(1)} collective-permute-done((bf16[18,32,128]{2,1,0:T(8,128)(2,1)S(1)}, bf16[18,32,128]{2,1,0:T(8,128)(2,1)S(1)}, u32[]{:S(2)}, u32[]{:S(2)}) %collective-permute-start.10) | collective-permute-done | bytes 147488 | tf_op jit(solution)/shard_map/ppermute | solution.py:326
  19.3 0.5 collective-permute-done.11.refs_3_
  19.8 0.6 %shard_map.43 = (bf16[2,18,16,128]{3,2,1,0:T(8,128)(2,1)S(1)}, bf16[2,18,16,128]{3,2,1,0:T(8,128)(2,1)S(1)}, bf16[2,18,16,128]{3,2,1,0:T(8,128)(2,1)S(1)}, bf16[2,18,16,128]{3,2,1,0:T(8,128)(2,1)S(1)}) custom-call(s32[1,4]{1,0:T(1,128)S(1)} %bitcast.13, bf16[18,32,128]{2,1,0:T(8,128)(2,1)S(1)} %collective-permute-done.9.refs_1_, ...), custom_call_target="tpu_custom_call" | custom-call | flops 1 | bytes 1 | tf_op jit(solution)/shard_map/pallas_call | solution.py:313
  20.4 1.7 %collective-permute-start.12 = (bf16[2,18,16,128]{3,2,1,0:T(8,128)(2,1)S(1)}, bf16[2,18,16,128]{3,2,1,0:T(8,128)(2,1)S(1)}, u32[]{:S(2)}, u32[]{:S(2)}) collective-permute-start(bf16[2,18,16,128]{3,2,1,0:T(8,128)(2,1)S(1)} %get-tuple-element.67), channel_id=1, source_target_pairs={{0,2},{1,3},{2,0},{3,1},{4,6},{5,7},{6,4},{7,5},{8,10},{9,11},{10,... | collective-permute-start | bytes 442376 | tf_op jit(solution)/shard_map/ppermute | solution.py:343
  22.0 0.0 collective-permute-start.13
  22.1 0.0 collective-permute-done.3.refs_0_
  22.1 0.5 %collective-permute-start.14 = (bf16[2,18,16,128]{3,2,1,0:T(8,128)(2,1)S(1)}, bf16[2,18,16,128]{3,2,1,0:T(8,128)(2,1)S(1)}, u32[]{:S(2)}, u32[]{:S(2)}) collective-permute-start(bf16[2,18,16,128]{3,2,1,0:T(8,128)(2,1)S(1)} %get-tuple-element.69), channel_id=1, source_target_pairs={{0,1},{1,0},{2,3},{3,2},{4,5},{5,4},{6,7},{7,6},{8,9},{9,8},{10,11... | collective-permute-start | bytes 442376 | tf_op jit(solution)/shard_map/ppermute | solution.py:343
  22.6 0.0 collective-permute-done.4.refs_1_
  22.6 0.0 collective-permute-done.5.refs_2_
  22.6 0.5 %shard_map.41 = (bf16[14,32,128]{2,1,0:T(8,128)(2,1)S(1)}, bf16[14,32,128]{2,1,0:T(8,128)(2,1)S(1)}, bf16[14,32,128]{2,1,0:T(8,128)(2,1)S(1)}, bf16[14,32,128]{2,1,0:T(8,128)(2,1)S(1)}) custom-call(bf16[2,14,16,128]{3,2,1,0:T(8,128)(2,1)S(1)} %collective-permute-done.3.refs_0_, bf16[2,14,16,128]{3,2,1,0:T(8,128)(2,1)S(1)} %collective-permute-done.4.refs_1_, ...), custom_call_target="tpu_custom_call" | custom-call | flops 2000000000 | bytes 1 | tf_op jit(solution)/shard_map/pallas_call | solution.py:313
  23.1 2.8 %collective-permute-start.6 = (bf16[14,32,128]{2,1,0:T(8,128)(2,1)S(1)}, bf16[14,32,128]{2,1,0:T(8,128)(2,1)S(1)}, u32[]{:S(2)}, u32[]{:S(2)}) collective-permute-start(bf16[14,32,128]{2,1,0:T(8,128)(2,1)S(1)} %get-tuple-element.58), channel_id=1, source_target_pairs={{0,16},{4,20},{8,24},{12,28},{16,0},{20,4},{24,8},{28,12},{1,17},{... | collective-permute-start | bytes 344072 | tf_op jit(solution)/shard_map/ppermute | solution.py:326
  25.9 1.3 %collective-permute-start.7 = (bf16[14,32,128]{2,1,0:T(8,128)(2,1)S(1)}, bf16[14,32,128]{2,1,0:T(8,128)(2,1)S(1)}, u32[]{:S(2)}, u32[]{:S(2)}) collective-permute-start(bf16[14,32,128]{2,1,0:T(8,128)(2,1)S(1)} %get-tuple-element.59), channel_id=1, source_target_pairs={{0,20},{4,16},{8,28},{12,24},{16,4},{20,0},{24,12},{28,8},{1,21},{... | collective-permute-start | bytes 344072 | tf_op jit(solution)/shard_map/ppermute | solution.py:326
  27.2 0.0 collective-permute-done.12.refs_0_
  27.2 0.7 %collective-permute-start.8 = (bf16[14,32,128]{2,1,0:T(8,128)(2,1)S(1)}, bf16[14,32,128]{2,1,0:T(8,128)(2,1)S(1)}, u32[]{:S(2)}, u32[]{:S(2)}) collective-permute-start(bf16[14,32,128]{2,1,0:T(8,128)(2,1)S(1)} %get-tuple-element.60), channel_id=1, source_target_pairs={{0,4},{4,0},{8,12},{12,8},{16,20},{20,16},{24,28},{28,24},{1,5},{5... | collective-permute-start | bytes 344072 | tf_op jit(solution)/shard_map/ppermute | solution.py:326
  27.9 0.3 collective-permute-done.13.refs_1_
  28.2 0.0 collective-permute-done.14.refs_2_
  28.2 0.6 %shard_map.44 = (bf16[18,32,128]{2,1,0:T(8,128)(2,1)S(1)}, bf16[18,32,128]{2,1,0:T(8,128)(2,1)S(1)}, bf16[18,32,128]{2,1,0:T(8,128)(2,1)S(1)}, bf16[18,32,128]{2,1,0:T(8,128)(2,1)S(1)}) custom-call(bf16[2,18,16,128]{3,2,1,0:T(8,128)(2,1)S(1)} %collective-permute-done.12.refs_0_, bf16[2,18,16,128]{3,2,1,0:T(8,128)(2,1)S(1)} %collective-permute-done.13.refs_1_, ...), custom_call_target="tpu_custom_call" | custom-call | flops 1 | bytes 1 | tf_op jit(solution)/shard_map/pallas_call | solution.py:313
  28.8 2.6 %collective-permute-start.15 = (bf16[18,32,128]{2,1,0:T(8,128)(2,1)S(1)}, bf16[18,32,128]{2,1,0:T(8,128)(2,1)S(1)}, u32[]{:S(2)}, u32[]{:S(2)}) collective-permute-start(bf16[18,32,128]{2,1,0:T(8,128)(2,1)S(1)} %get-tuple-element.71), channel_id=1, source_target_pairs={{0,16},{4,20},{8,24},{12,28},{16,0},{20,4},{24,8},{28,12},{1,17},{... | collective-permute-start | bytes 442376 | tf_op jit(solution)/shard_map/ppermute | solution.py:326
  31.5 1.3 %collective-permute-start.16 = (bf16[18,32,128]{2,1,0:T(8,128)(2,1)S(1)}, bf16[18,32,128]{2,1,0:T(8,128)(2,1)S(1)}, u32[]{:S(2)}, u32[]{:S(2)}) collective-permute-start(bf16[18,32,128]{2,1,0:T(8,128)(2,1)S(1)} %get-tuple-element.76), channel_id=1, source_target_pairs={{0,20},{4,16},{8,28},{12,24},{16,4},{20,0},{24,12},{28,8},{1,21},{... | collective-permute-start | bytes 442376 | tf_op jit(solution)/shard_map/ppermute | solution.py:326
  32.8 8.6 %collective-permute-done.6.refs_0_ = bf16[14,32,128]{2,1,0:T(8,128)(2,1)S(1)} collective-permute-done((bf16[14,32,128]{2,1,0:T(8,128)(2,1)S(1)}, bf16[14,32,128]{2,1,0:T(8,128)(2,1)S(1)}, u32[]{:S(2)}, u32[]{:S(2)}) %collective-permute-start.6) | collective-permute-done | bytes 114720 | tf_op jit(solution)/shard_map/ppermute | solution.py:326
  41.3 1.6 %collective-permute-start.17 = (bf16[18,32,128]{2,1,0:T(8,128)(2,1)S(1)}, bf16[18,32,128]{2,1,0:T(8,128)(2,1)S(1)}, u32[]{:S(2)}, u32[]{:S(2)}) collective-permute-start(bf16[18,32,128]{2,1,0:T(8,128)(2,1)S(1)} %get-tuple-element.77), channel_id=1, source_target_pairs={{0,4},{4,0},{8,12},{12,8},{16,20},{20,16},{24,28},{28,24},{1,5},{5... | collective-permute-start | bytes 442376 | tf_op jit(solution)/shard_map/ppermute | solution.py:326
  43.0 1.9 %collective-permute-done.7.refs_1_ = bf16[14,32,128]{2,1,0:T(8,128)(2,1)S(1)} collective-permute-done((bf16[14,32,128]{2,1,0:T(8,128)(2,1)S(1)}, bf16[14,32,128]{2,1,0:T(8,128)(2,1)S(1)}, u32[]{:S(2)}, u32[]{:S(2)}) %collective-permute-start.7) | collective-permute-done | bytes 114720 | tf_op jit(solution)/shard_map/ppermute | solution.py:326
  44.9 0.0 collective-permute-done.8.refs_2_
  44.9 0.1 shard_map.42
  44.9 2.0 %collective-permute-done.15.refs_1_ = bf16[18,32,128]{2,1,0:T(8,128)(2,1)S(1)} collective-permute-done((bf16[18,32,128]{2,1,0:T(8,128)(2,1)S(1)}, bf16[18,32,128]{2,1,0:T(8,128)(2,1)S(1)}, u32[]{:S(2)}, u32[]{:S(2)}) %collective-permute-start.15) | collective-permute-done | bytes 147488 | tf_op jit(solution)/shard_map/ppermute | solution.py:326
  47.0 1.3 %shard_map.45 = (bf16[4096,128]{1,0:T(8,128)(2,1)}, f32[2,1128,128]{2,1,0:T(8,128)S(1)}) custom-call(f32[2,1128,128]{2,1,0:T(8,128)S(1)} %get-tuple-element.62.refs_0_, bf16[18,32,128]{2,1,0:T(8,128)(2,1)S(1)} %collective-permute-done.15.refs_1_, bf16[18,32,128]{2,1,0:T(8,128)(2,1)S(1)} %get-tuple-element.72.refs_2_, ...), custom_call_target="tpu_custom_call", output_to_operand_aliasing={{1}: (0, {})} | custom-call | flops 1 | bytes 1 | tf_op jit(solution)/shard_map/pallas_call | solution.py:313
  48.3 2.0 %collective-permute-done.16.refs_2_ = bf16[18,32,128]{2,1,0:T(8,128)(2,1)S(1)} collective-permute-done((bf16[18,32,128]{2,1,0:T(8,128)(2,1)S(1)}, bf16[18,32,128]{2,1,0:T(8,128)(2,1)S(1)}, u32[]{:S(2)}, u32[]{:S(2)}) %collective-permute-start.16) | collective-permute-done | bytes 147488 | tf_op jit(solution)/shard_map/ppermute | solution.py:326
  50.3 1.3 %shard_map.46 = (bf16[4096,128]{1,0:T(8,128)(2,1)}, f32[2,1128,128]{2,1,0:T(8,128)S(1)}) custom-call(bf16[4096,128]{1,0:T(8,128)(2,1)} %get-tuple-element.74.refs_0_, f32[2,1128,128]{2,1,0:T(8,128)S(1)} %get-tuple-element.75.refs_1_, bf16[18,32,128]{2,1,0:T(8,128)(2,1)S(1)} %collective-permute-done.16.refs_2_, ...), custom_call_target="tpu_custom_call", output_to_operand_aliasing={{0}: (0, {}), {1}: (1, {})} | custom-call | flops 1 | bytes 1 | tf_op jit(solution)/shard_map/pallas_call | solution.py:313
  (6 shorter events, 0.0 us)
Async XLA Ops:
  0.0 2.1 %copy-start = (bf16[2,262144]{1,0:T(2,128)(2,1)S(1)}, bf16[2,262144]{1,0:T(2,128)(2,1)}, u32[]{:S(2)}) copy-start(bf16[2,262144]{1,0:T(2,128)(2,1)} %param.3) | copy-start | bytes 3145732
  0.0 1.1 %copy-start.1 = (bf16[4,3,2,64,64]{4,3,2,1,0:T(8,128)(2,1)S(1)}, bf16[4,3,2,64,64]{4,3,2,1,0:T(8,128)(2,1)}, u32[]{:S(2)}) copy-start(bf16[4,3,2,64,64]{4,3,2,1,0:T(8,128)(2,1)} %refs_5_.1) | copy-start | bytes 589828
  2.1 6.0 %copy-start.2 = (bf16[4,3,2,64,64]{4,3,2,1,0:T(8,128)(2,1)S(1)}, bf16[4,3,2,64,64]{4,3,2,1,0:T(8,128)(2,1)}, u32[]{:S(2)}) copy-start(bf16[4,3,2,64,64]{4,3,2,1,0:T(8,128)(2,1)} %refs_5_.1) | copy-start | bytes 589828
  3.4 10.3 %copy-start.3 = (s32[4]{0:T(128)S(1)}, s32[4]{0:T(128)}, u32[]{:S(2)}) copy-start(s32[4]{0:T(128)} %param.5) | copy-start | bytes 52
  3.4 10.2 %collective-permute-start = (bf16[14,32,128]{2,1,0:T(8,128)(2,1)S(1)}, bf16[14,32,128]{2,1,0:T(8,128)(2,1)S(1)}, u32[]{:S(2)}, u32[]{:S(2)}) collective-permute-start(bf16[14,32,128]{2,1,0:T(8,128)(2,1)S(1)} %get-tuple-element.45), channel_id=1, source_target_pairs={{0,4},{4,0},{8,12},{12,8},{16,20},{20,16},{24,28},{28,24},{1,5},{5... | collective-permute-start | bytes 344072 | tf_op jit(solution)/shard_map/ppermute | solution.py:326
  6.5 7.3 %collective-permute-start.1 = (bf16[14,32,128]{2,1,0:T(8,128)(2,1)S(1)}, bf16[14,32,128]{2,1,0:T(8,128)(2,1)S(1)}, u32[]{:S(2)}, u32[]{:S(2)}) collective-permute-start(bf16[14,32,128]{2,1,0:T(8,128)(2,1)S(1)} %get-tuple-element.46), channel_id=1, source_target_pairs={{0,12},{4,8},{8,4},{12,0},{16,28},{20,24},{24,20},{28,16},{1,13},{... | collective-permute-start | bytes 344072 | tf_op jit(solution)/shard_map/ppermute | solution.py:326
  8.0 5.7 %collective-permute-start.2 = (bf16[14,32,128]{2,1,0:T(8,128)(2,1)S(1)}, bf16[14,32,128]{2,1,0:T(8,128)(2,1)S(1)}, u32[]{:S(2)}, u32[]{:S(2)}) collective-permute-start(bf16[14,32,128]{2,1,0:T(8,128)(2,1)S(1)} %get-tuple-element.47), channel_id=1, source_target_pairs={{0,8},{4,12},{8,0},{12,4},{16,24},{20,28},{24,16},{28,20},{1,9},{5... | collective-permute-start | bytes 344072 | tf_op jit(solution)/shard_map/ppermute | solution.py:326
  10.2 8.1 %collective-permute-start.9 = (bf16[18,32,128]{2,1,0:T(8,128)(2,1)S(1)}, bf16[18,32,128]{2,1,0:T(8,128)(2,1)S(1)}, u32[]{:S(2)}, u32[]{:S(2)}) collective-permute-start(bf16[18,32,128]{2,1,0:T(8,128)(2,1)S(1)} %get-tuple-element.63), channel_id=1, source_target_pairs={{0,4},{4,0},{8,12},{12,8},{16,20},{20,16},{24,28},{28,24},{1,5},{5... | collective-permute-start | bytes 442376 | tf_op jit(solution)/shard_map/ppermute | solution.py:326
  12.1 7.1 %collective-permute-start.10 = (bf16[18,32,128]{2,1,0:T(8,128)(2,1)S(1)}, bf16[18,32,128]{2,1,0:T(8,128)(2,1)S(1)}, u32[]{:S(2)}, u32[]{:S(2)}) collective-permute-start(bf16[18,32,128]{2,1,0:T(8,128)(2,1)S(1)} %get-tuple-element.64), channel_id=1, source_target_pairs={{0,12},{4,8},{8,4},{12,0},{16,28},{20,24},{24,20},{28,16},{1,13},{... | collective-permute-start | bytes 442376 | tf_op jit(solution)/shard_map/ppermute | solution.py:326
  13.7 6.1 %collective-permute-start.11 = (bf16[18,32,128]{2,1,0:T(8,128)(2,1)S(1)}, bf16[18,32,128]{2,1,0:T(8,128)(2,1)S(1)}, u32[]{:S(2)}, u32[]{:S(2)}) collective-permute-start(bf16[18,32,128]{2,1,0:T(8,128)(2,1)S(1)} %get-tuple-element.65), channel_id=1, source_target_pairs={{0,8},{4,12},{8,0},{12,4},{16,24},{20,28},{24,16},{28,20},{1,9},{5... | collective-permute-start | bytes 442376 | tf_op jit(solution)/shard_map/ppermute | solution.py:326
  14.3 7.7 %collective-permute-start.3 = (bf16[2,14,16,128]{3,2,1,0:T(8,128)(2,1)S(1)}, bf16[2,14,16,128]{3,2,1,0:T(8,128)(2,1)S(1)}, u32[]{:S(2)}, u32[]{:S(2)}) collective-permute-start(bf16[2,14,16,128]{3,2,1,0:T(8,128)(2,1)S(1)} %get-tuple-element.49), channel_id=1, source_target_pairs={{0,2},{1,3},{2,0},{3,1},{4,6},{5,7},{6,4},{7,5},{8,10},{9,11},{10,... | collective-permute-start | bytes 344072 | tf_op jit(solution)/shard_map/ppermute | solution.py:343
  16.3 6.3 %collective-permute-start.4 = (bf16[2,14,16,128]{3,2,1,0:T(8,128)(2,1)S(1)}, bf16[2,14,16,128]{3,2,1,0:T(8,128)(2,1)S(1)}, u32[]{:S(2)}, u32[]{:S(2)}) collective-permute-start(bf16[2,14,16,128]{3,2,1,0:T(8,128)(2,1)S(1)} %get-tuple-element.50), channel_id=1, source_target_pairs={{0,3},{1,2},{2,1},{3,0},{4,7},{5,6},{6,5},{7,4},{8,11},{9,10},{10,... | collective-permute-start | bytes 344072 | tf_op jit(solution)/shard_map/ppermute | solution.py:343
  18.3 4.3 %collective-permute-start.5 = (bf16[2,14,16,128]{3,2,1,0:T(8,128)(2,1)S(1)}, bf16[2,14,16,128]{3,2,1,0:T(8,128)(2,1)S(1)}, u32[]{:S(2)}, u32[]{:S(2)}) collective-permute-start(bf16[2,14,16,128]{3,2,1,0:T(8,128)(2,1)S(1)} %get-tuple-element.51), channel_id=1, source_target_pairs={{0,1},{1,0},{2,3},{3,2},{4,5},{5,4},{6,7},{7,6},{8,9},{9,8},{10,11... | collective-permute-start | bytes 344072 | tf_op jit(solution)/shard_map/ppermute | solution.py:343
  20.4 6.8 %collective-permute-start.12 = (bf16[2,18,16,128]{3,2,1,0:T(8,128)(2,1)S(1)}, bf16[2,18,16,128]{3,2,1,0:T(8,128)(2,1)S(1)}, u32[]{:S(2)}, u32[]{:S(2)}) collective-permute-start(bf16[2,18,16,128]{3,2,1,0:T(8,128)(2,1)S(1)} %get-tuple-element.67), channel_id=1, source_target_pairs={{0,2},{1,3},{2,0},{3,1},{4,6},{5,7},{6,4},{7,5},{8,10},{9,11},{10,... | collective-permute-start | bytes 442376 | tf_op jit(solution)/shard_map/ppermute | solution.py:343
  22.0 6.1 %collective-permute-start.13 = (bf16[2,18,16,128]{3,2,1,0:T(8,128)(2,1)S(1)}, bf16[2,18,16,128]{3,2,1,0:T(8,128)(2,1)S(1)}, u32[]{:S(2)}, u32[]{:S(2)}) collective-permute-start(bf16[2,18,16,128]{3,2,1,0:T(8,128)(2,1)S(1)} %get-tuple-element.68), channel_id=1, source_target_pairs={{0,3},{1,2},{2,1},{3,0},{4,7},{5,6},{6,5},{7,4},{8,11},{9,10},{10,... | collective-permute-start | bytes 442376 | tf_op jit(solution)/shard_map/ppermute | solution.py:343
  22.1 6.1 %collective-permute-start.14 = (bf16[2,18,16,128]{3,2,1,0:T(8,128)(2,1)S(1)}, bf16[2,18,16,128]{3,2,1,0:T(8,128)(2,1)S(1)}, u32[]{:S(2)}, u32[]{:S(2)}) collective-permute-start(bf16[2,18,16,128]{3,2,1,0:T(8,128)(2,1)S(1)} %get-tuple-element.69), channel_id=1, source_target_pairs={{0,1},{1,0},{2,3},{3,2},{4,5},{5,4},{6,7},{7,6},{8,9},{9,8},{10,11... | collective-permute-start | bytes 442376 | tf_op jit(solution)/shard_map/ppermute | solution.py:343
  23.1 18.2 %collective-permute-start.6 = (bf16[14,32,128]{2,1,0:T(8,128)(2,1)S(1)}, bf16[14,32,128]{2,1,0:T(8,128)(2,1)S(1)}, u32[]{:S(2)}, u32[]{:S(2)}) collective-permute-start(bf16[14,32,128]{2,1,0:T(8,128)(2,1)S(1)} %get-tuple-element.58), channel_id=1, source_target_pairs={{0,16},{4,20},{8,24},{12,28},{16,0},{20,4},{24,8},{28,12},{1,17},{... | collective-permute-start | bytes 344072 | tf_op jit(solution)/shard_map/ppermute | solution.py:326
  25.9 19.0 %collective-permute-start.7 = (bf16[14,32,128]{2,1,0:T(8,128)(2,1)S(1)}, bf16[14,32,128]{2,1,0:T(8,128)(2,1)S(1)}, u32[]{:S(2)}, u32[]{:S(2)}) collective-permute-start(bf16[14,32,128]{2,1,0:T(8,128)(2,1)S(1)} %get-tuple-element.59), channel_id=1, source_target_pairs={{0,20},{4,16},{8,28},{12,24},{16,4},{20,0},{24,12},{28,8},{1,21},{... | collective-permute-start | bytes 344072 | tf_op jit(solution)/shard_map/ppermute | solution.py:326
  27.2 17.7 %collective-permute-start.8 = (bf16[14,32,128]{2,1,0:T(8,128)(2,1)S(1)}, bf16[14,32,128]{2,1,0:T(8,128)(2,1)S(1)}, u32[]{:S(2)}, u32[]{:S(2)}) collective-permute-start(bf16[14,32,128]{2,1,0:T(8,128)(2,1)S(1)} %get-tuple-element.60), channel_id=1, source_target_pairs={{0,4},{4,0},{8,12},{12,8},{16,20},{20,16},{24,28},{28,24},{1,5},{5... | collective-permute-start | bytes 344072 | tf_op jit(solution)/shard_map/ppermute | solution.py:326
  28.8 18.1 %collective-permute-start.15 = (bf16[18,32,128]{2,1,0:T(8,128)(2,1)S(1)}, bf16[18,32,128]{2,1,0:T(8,128)(2,1)S(1)}, u32[]{:S(2)}, u32[]{:S(2)}) collective-permute-start(bf16[18,32,128]{2,1,0:T(8,128)(2,1)S(1)} %get-tuple-element.71), channel_id=1, source_target_pairs={{0,16},{4,20},{8,24},{12,28},{16,0},{20,4},{24,8},{28,12},{1,17},{... | collective-permute-start | bytes 442376 | tf_op jit(solution)/shard_map/ppermute | solution.py:326
  31.5 18.8 %collective-permute-start.16 = (bf16[18,32,128]{2,1,0:T(8,128)(2,1)S(1)}, bf16[18,32,128]{2,1,0:T(8,128)(2,1)S(1)}, u32[]{:S(2)}, u32[]{:S(2)}) collective-permute-start(bf16[18,32,128]{2,1,0:T(8,128)(2,1)S(1)} %get-tuple-element.76), channel_id=1, source_target_pairs={{0,20},{4,16},{8,28},{12,24},{16,4},{20,0},{24,12},{28,8},{1,21},{... | collective-permute-start | bytes 442376 | tf_op jit(solution)/shard_map/ppermute | solution.py:326
  41.3 8.9 %collective-permute-start.17 = (bf16[18,32,128]{2,1,0:T(8,128)(2,1)S(1)}, bf16[18,32,128]{2,1,0:T(8,128)(2,1)S(1)}, u32[]{:S(2)}, u32[]{:S(2)}) collective-permute-start(bf16[18,32,128]{2,1,0:T(8,128)(2,1)S(1)} %get-tuple-element.77), channel_id=1, source_target_pairs={{0,4},{4,0},{8,12},{12,8},{16,20},{20,16},{24,28},{28,24},{1,5},{5... | collective-permute-start | bytes 442376 | tf_op jit(solution)/shard_map/ppermute | solution.py:326

commit v12 on v11

--- a/solution.py
+++ b/solution.py
@@ -153,7 +153,7 @@
 
 
 PLACES = ((1, 0), (1, 1), (0, 1), (0, 0))
-APART = (2, 3, 1, 0)
+APART = (3, 2, 1, 0)
 
 
 def by_place(blocks):

time: 51.7 us -> 51.8 us (level)
  starting transfers between devices: 22.6 us -> 23.4 us
  waiting for transfers between devices: 18.3 us -> 17.6 us
    ppermute x12, waiting for transfers between devices: 17.9 us -> 16 us  [swapped(): lax.ppermute(x, 'hi', [(d, d ^ apart) for d in range(lax.axis_size('hi'))])]
    ppermute x6, waiting for transfers between devices: 0.33 us -> 1.58 us  [regrouped(): lax.ppermute(x, 'lo', to)]
    ppermute x12, starting transfers between devices: 18.5 us -> 19.4 us  [swapped(): lax.ppermute(x, 'hi', [(d, d ^ apart) for d in range(lax.axis_size('hi'))])]
where the time goes in v12:
time: 51.8 us; the launch traced here: 51.6 us
  starting transfers between devices  23.4 us (45%)
  waiting for transfers between devices  17.6 us (34%)
  Pallas kernels  9.46 us (18%)
  local copies, waits for them, and re-layouts  1.1 us (2%)
    ppermute x12, starting transfers between devices, swapped(): lax.ppermute(x, 'hi', [(d, d ^ apart) for d in range(lax.axis_size('hi'))])  19.4 us
    ppermute x12, waiting for transfers between devices, swapped(): lax.ppermute(x, 'hi', [(d, d ^ apart) for d in range(lax.axis_size('hi'))])  16 us
    pallas_call x10, Pallas kernels, call(): pl.pallas_call(body, out_shape=outs, in_specs=specs + [ANY] * len(after),...  9.46 us
    ppermute x6, starting transfers between devices, regrouped(): lax.ppermute(x, 'lo', to)  3.94 us
    ppermute x6, waiting for transfers between devices, regrouped(): lax.ppermute(x, 'lo', to)  1.58 us
    unnamed x8, local copies, waits for them, and re-layouts  1.1 us
  transfers between devices with their start and end apart: 18, of which 8 were waited for; matrix products, arithmetic and copies ran while one was open for 0% of the time, Pallas kernels for 11%

profile of v12, /device:TPU:0, one launch (start us, length us, event | category | flops | bytes accessed | tf_op | source)
XLA Modules:
  0.0 51.6 jit_solution(16983933562316791911)
XLA Ops:
  0.0 1.1 %copy-done.1 = bf16[4,3,2,64,64]{4,3,2,1,0:T(8,128)(2,1)S(1)} copy-done((bf16[4,3,2,64,64]{4,3,2,1,0:T(8,128)(2,1)S(1)}, bf16[4,3,2,64,64]{4,3,2,1,0:T(8,128)(2,1)}, u32[]{:S(2)}) %copy-start.1) | copy-done | bytes 196632
  1.1 1.0 %shard_map.37 = (bf16[128,256]{1,0:T(8,128)(2,1)S(1)}, bf16[128,256]{1,0:T(8,128)(2,1)S(1)}, bf16[256,512]{1,0:T(8,128)(2,1)S(1)}, bf16[64,128]{1,0:T(8,128)(2,1)S(1)}) custom-call(bf16[4,3,2,64,64]{4,3,2,1,0:T(8,128)(2,1)S(1)} %copy-done.1), custom_call_target="tpu_custom_call" | custom-call | flops 2000000000 | bytes 1 | tf_op jit(solution)/shard_map/pallas_call | solution.py:313
  2.1 0.0 copy-done
  2.1 1.4 %shard_map.38 = (bf16[14,32,128]{2,1,0:T(8,128)(2,1)S(1)}, bf16[14,32,128]{2,1,0:T(8,128)(2,1)S(1)}, bf16[14,32,128]{2,1,0:T(8,128)(2,1)S(1)}, bf16[14,32,128]{2...) custom-call(bf16[4096,128]{1,0:T(8,128)(2,1)S(1)} %bitcast.11, ...), custom_call_target="tpu_custom_call" | custom-call | flops 1 | bytes 1 | tf_op jit(solution)/shard_map/pallas_call | solution.py:313
  3.4 0.0 copy-start.3
  3.4 3.0 %collective-permute-start = (bf16[14,32,128]{2,1,0:T(8,128)(2,1)S(1)}, bf16[14,32,128]{2,1,0:T(8,128)(2,1)S(1)}, u32[]{:S(2)}, u32[]{:S(2)}) collective-permute-start(bf16[14,32,128]{2,1,0:T(8,128)(2,1)S(1)} %get-tuple-element.45), channel_id=1, source_target_pairs={{0,4},{4,0},{8,12},{12,8},{16,20},{20,16},{24,28},{28,24},{1,5},{5... | collective-permute-start | bytes 344072 | tf_op jit(solution)/shard_map/ppermute | solution.py:326
  6.5 1.5 %collective-permute-start.1 = (bf16[14,32,128]{2,1,0:T(8,128)(2,1)S(1)}, bf16[14,32,128]{2,1,0:T(8,128)(2,1)S(1)}, u32[]{:S(2)}, u32[]{:S(2)}) collective-permute-start(bf16[14,32,128]{2,1,0:T(8,128)(2,1)S(1)} %get-tuple-element.46), channel_id=1, source_target_pairs={{0,12},{4,8},{8,4},{12,0},{16,28},{20,24},{24,20},{28,16},{1,13},{... | collective-permute-start | bytes 344072 | tf_op jit(solution)/shard_map/ppermute | solution.py:326
  8.0 0.1 collective-permute-start.2
  8.1 2.1 %shard_map.40 = (bf16[18,32,128]{2,1,0:T(8,128)(2,1)S(1)}, bf16[18,32,128]{2,1,0:T(8,128)(2,1)S(1)}, bf16[18,32,128]{2,1,0:T(8,128)(2,1)S(1)}, bf16[18,32,128]{2...) custom-call(bf16[2048,256]{1,0:T(8,128)(2,1)S(1)} %get-tuple-element, ...), custom_call_target="tpu_custom_call" | custom-call | flops 1 | bytes 1 | tf_op jit(solution)/shard_map/pallas_call | solution.py:313
  10.2 2.0 %collective-permute-start.9 = (bf16[18,32,128]{2,1,0:T(8,128)(2,1)S(1)}, bf16[18,32,128]{2,1,0:T(8,128)(2,1)S(1)}, u32[]{:S(2)}, u32[]{:S(2)}) collective-permute-start(bf16[18,32,128]{2,1,0:T(8,128)(2,1)S(1)} %get-tuple-element.63), channel_id=1, source_target_pairs={{0,4},{4,0},{8,12},{12,8},{16,20},{20,16},{24,28},{28,24},{1,5},{5... | collective-permute-start | bytes 442376 | tf_op jit(solution)/shard_map/ppermute | solution.py:326
  12.1 1.5 %collective-permute-start.10 = (bf16[18,32,128]{2,1,0:T(8,128)(2,1)S(1)}, bf16[18,32,128]{2,1,0:T(8,128)(2,1)S(1)}, u32[]{:S(2)}, u32[]{:S(2)}) collective-permute-start(bf16[18,32,128]{2,1,0:T(8,128)(2,1)S(1)} %get-tuple-element.64), channel_id=1, source_target_pairs={{0,12},{4,8},{8,4},{12,0},{16,28},{20,24},{24,20},{28,16},{1,13},{... | collective-permute-start | bytes 442376 | tf_op jit(solution)/shard_map/ppermute | solution.py:326
  13.7 0.0 collective-permute-done.refs_1_
  13.7 0.1 collective-permute-start.11
  13.7 0.0 collective-permute-done.1.refs_2_
  13.7 0.0 collective-permute-done.2.refs_3_
  13.7 0.6 %shard_map.39 = (bf16[2,14,16,128]{3,2,1,0:T(8,128)(2,1)S(1)}, bf16[2,14,16,128]{3,2,1,0:T(8,128)(2,1)S(1)}, bf16[2,14,16,128]{3,2,1,0:T(8,128)(2,1)S(1)}, bf16[2,14,16,128]{3,2,1,0:T(8,128)(2,1)S(1)}) custom-call(s32[1,4]{1,0:T(1,128)S(1)} %bitcast.12, bf16[14,32,128]{2,1,0:T(8,128)(2,1)S(1)} %collective-permute-done.refs_1_, ...), custom_call_target="tpu_custom_call" | custom-call | flops 2000000000 | bytes 1 | tf_op jit(solution)/shard_map/pallas_call | solution.py:313
  14.3 0.1 collective-permute-start.3
  14.4 1.9 %collective-permute-start.4 = (bf16[2,14,16,128]{3,2,1,0:T(8,128)(2,1)S(1)}, bf16[2,14,16,128]{3,2,1,0:T(8,128)(2,1)S(1)}, u32[]{:S(2)}, u32[]{:S(2)}) collective-permute-start(bf16[2,14,16,128]{3,2,1,0:T(8,128)(2,1)S(1)} %get-tuple-element.50), channel_id=1, source_target_pairs={{0,2},{1,3},{2,0},{3,1},{4,6},{5,7},{6,4},{7,5},{8,10},{9,11},{10,... | collective-permute-start | bytes 344072 | tf_op jit(solution)/shard_map/ppermute | solution.py:343
  16.3 2.0 %collective-permute-done.9.refs_1_ = bf16[18,32,128]{2,1,0:T(8,128)(2,1)S(1)} collective-permute-done((bf16[18,32,128]{2,1,0:T(8,128)(2,1)S(1)}, bf16[18,32,128]{2,1,0:T(8,128)(2,1)S(1)}, u32[]{:S(2)}, u32[]{:S(2)}) %collective-permute-start.9) | collective-permute-done | bytes 147488 | tf_op jit(solution)/shard_map/ppermute | solution.py:326
  18.3 0.0 collective-permute-start.5
  18.3 1.0 %collective-permute-done.10.refs_2_ = bf16[18,32,128]{2,1,0:T(8,128)(2,1)S(1)} collective-permute-done((bf16[18,32,128]{2,1,0:T(8,128)(2,1)S(1)}, bf16[18,32,128]{2,1,0:T(8,128)(2,1)S(1)}, u32[]{:S(2)}, u32[]{:S(2)}) %collective-permute-start.10) | collective-permute-done | bytes 147488 | tf_op jit(solution)/shard_map/ppermute | solution.py:326
  19.3 0.5 collective-permute-done.11.refs_3_
  19.8 0.6 %shard_map.43 = (bf16[2,18,16,128]{3,2,1,0:T(8,128)(2,1)S(1)}, bf16[2,18,16,128]{3,2,1,0:T(8,128)(2,1)S(1)}, bf16[2,18,16,128]{3,2,1,0:T(8,128)(2,1)S(1)}, bf16[2,18,16,128]{3,2,1,0:T(8,128)(2,1)S(1)}) custom-call(s32[1,4]{1,0:T(1,128)S(1)} %bitcast.13, bf16[18,32,128]{2,1,0:T(8,128)(2,1)S(1)} %collective-permute-done.9.refs_1_, ...), custom_call_target="tpu_custom_call" | custom-call | flops 1 | bytes 1 | tf_op jit(solution)/shard_map/pallas_call | solution.py:313
  20.4 0.3 collective-permute-start.12
  20.7 1.5 %collective-permute-start.13 = (bf16[2,18,16,128]{3,2,1,0:T(8,128)(2,1)S(1)}, bf16[2,18,16,128]{3,2,1,0:T(8,128)(2,1)S(1)}, u32[]{:S(2)}, u32[]{:S(2)}) collective-permute-start(bf16[2,18,16,128]{3,2,1,0:T(8,128)(2,1)S(1)} %get-tuple-element.68), channel_id=1, source_target_pairs={{0,2},{1,3},{2,0},{3,1},{4,6},{5,7},{6,4},{7,5},{8,10},{9,11},{10,... | collective-permute-start | bytes 442376 | tf_op jit(solution)/shard_map/ppermute | solution.py:343
  22.1 0.2 collective-permute-start.14
  22.3 0.0 collective-permute-done.4.refs_1_
  22.3 0.0 collective-permute-done.5.refs_2_
  22.3 0.5 %shard_map.41 = (bf16[14,32,128]{2,1,0:T(8,128)(2,1)S(1)}, bf16[14,32,128]{2,1,0:T(8,128)(2,1)S(1)}, bf16[14,32,128]{2,1,0:T(8,128)(2,1)S(1)}, bf16[14,32,128]{2,1,0:T(8,128)(2,1)S(1)}) custom-call(bf16[2,14,16,128]{3,2,1,0:T(8,128)(2,1)S(1)} %collective-permute-done.3.refs_0_, bf16[2,14,16,128]{3,2,1,0:T(8,128)(2,1)S(1)} %collective-permute-done.4.refs_1_, ...), custom_call_target="tpu_custom_call" | custom-call | flops 2000000000 | bytes 1 | tf_op jit(solution)/shard_map/pallas_call | solution.py:313
  22.8 3.0 %collective-permute-start.6 = (bf16[14,32,128]{2,1,0:T(8,128)(2,1)S(1)}, bf16[14,32,128]{2,1,0:T(8,128)(2,1)S(1)}, u32[]{:S(2)}, u32[]{:S(2)}) collective-permute-start(bf16[14,32,128]{2,1,0:T(8,128)(2,1)S(1)} %get-tuple-element.58), channel_id=1, source_target_pairs={{0,16},{4,20},{8,24},{12,28},{16,0},{20,4},{24,8},{28,12},{1,17},{... | collective-permute-start | bytes 344072 | tf_op jit(solution)/shard_map/ppermute | solution.py:326
  25.9 1.3 %collective-permute-start.7 = (bf16[14,32,128]{2,1,0:T(8,128)(2,1)S(1)}, bf16[14,32,128]{2,1,0:T(8,128)(2,1)S(1)}, u32[]{:S(2)}, u32[]{:S(2)}) collective-permute-start(bf16[14,32,128]{2,1,0:T(8,128)(2,1)S(1)} %get-tuple-element.59), channel_id=1, source_target_pairs={{0,20},{4,16},{8,28},{12,24},{16,4},{20,0},{24,12},{28,8},{1,21},{... | collective-permute-start | bytes 344072 | tf_op jit(solution)/shard_map/ppermute | solution.py:326
  27.2 0.0 collective-permute-done.12.refs_0_
  27.2 1.0 %collective-permute-start.8 = (bf16[14,32,128]{2,1,0:T(8,128)(2,1)S(1)}, bf16[14,32,128]{2,1,0:T(8,128)(2,1)S(1)}, u32[]{:S(2)}, u32[]{:S(2)}) collective-permute-start(bf16[14,32,128]{2,1,0:T(8,128)(2,1)S(1)} %get-tuple-element.60), channel_id=1, source_target_pairs={{0,4},{4,0},{8,12},{12,8},{16,20},{20,16},{24,28},{28,24},{1,5},{5... | collective-permute-start | bytes 344072 | tf_op jit(solution)/shard_map/ppermute | solution.py:326
  28.2 1.6 %collective-permute-done.13.refs_1_ = bf16[2,18,16,128]{3,2,1,0:T(8,128)(2,1)S(1)} collective-permute-done((bf16[2,18,16,128]{3,2,1,0:T(8,128)(2,1)S(1)}, bf16[2,18,16,128]{3,2,1,0:T(8,128)(2,1)S(1)}, u32[]{:S(2)}, u32[]{:S(2)}) %collective-permute-start.13) | collective-permute-done | bytes 147488 | tf_op jit(solution)/shard_map/ppermute | solution.py:343
  29.7 0.0 collective-permute-done.14.refs_2_
  29.7 0.6 %shard_map.44 = (bf16[18,32,128]{2,1,0:T(8,128)(2,1)S(1)}, bf16[18,32,128]{2,1,0:T(8,128)(2,1)S(1)}, bf16[18,32,128]{2,1,0:T(8,128)(2,1)S(1)}, bf16[18,32,128]{2,1,0:T(8,128)(2,1)S(1)}) custom-call(bf16[2,18,16,128]{3,2,1,0:T(8,128)(2,1)S(1)} %collective-permute-done.12.refs_0_, bf16[2,18,16,128]{3,2,1,0:T(8,128)(2,1)S(1)} %collective-permute-done.13.refs_1_, ...), custom_call_target="tpu_custom_call" | custom-call | flops 1 | bytes 1 | tf_op jit(solution)/shard_map/pallas_call | solution.py:313
  30.4 2.8 %collective-permute-start.15 = (bf16[18,32,128]{2,1,0:T(8,128)(2,1)S(1)}, bf16[18,32,128]{2,1,0:T(8,128)(2,1)S(1)}, u32[]{:S(2)}, u32[]{:S(2)}) collective-permute-start(bf16[18,32,128]{2,1,0:T(8,128)(2,1)S(1)} %get-tuple-element.71), channel_id=1, source_target_pairs={{0,16},{4,20},{8,24},{12,28},{16,0},{20,4},{24,8},{28,12},{1,17},{... | collective-permute-start | bytes 442376 | tf_op jit(solution)/shard_map/ppermute | solution.py:326
  33.1 1.3 %collective-permute-start.16 = (bf16[18,32,128]{2,1,0:T(8,128)(2,1)S(1)}, bf16[18,32,128]{2,1,0:T(8,128)(2,1)S(1)}, u32[]{:S(2)}, u32[]{:S(2)}) collective-permute-start(bf16[18,32,128]{2,1,0:T(8,128)(2,1)S(1)} %get-tuple-element.76), channel_id=1, source_target_pairs={{0,20},{4,16},{8,28},{12,24},{16,4},{20,0},{24,12},{28,8},{1,21},{... | collective-permute-start | bytes 442376 | tf_op jit(solution)/shard_map/ppermute | solution.py:326
  34.4 0.3 collective-permute-done.6.refs_0_
  34.7 1.9 %collective-permute-start.17 = (bf16[18,32,128]{2,1,0:T(8,128)(2,1)S(1)}, bf16[18,32,128]{2,1,0:T(8,128)(2,1)S(1)}, u32[]{:S(2)}, u32[]{:S(2)}) collective-permute-start(bf16[18,32,128]{2,1,0:T(8,128)(2,1)S(1)} %get-tuple-element.77), channel_id=1, source_target_pairs={{0,4},{4,0},{8,12},{12,8},{16,20},{20,16},{24,28},{28,24},{1,5},{5... | collective-permute-start | bytes 442376 | tf_op jit(solution)/shard_map/ppermute | solution.py:326
  36.6 8.2 %collective-permute-done.7.refs_1_ = bf16[14,32,128]{2,1,0:T(8,128)(2,1)S(1)} collective-permute-done((bf16[14,32,128]{2,1,0:T(8,128)(2,1)S(1)}, bf16[14,32,128]{2,1,0:T(8,128)(2,1)S(1)}, u32[]{:S(2)}, u32[]{:S(2)}) %collective-permute-start.7) | collective-permute-done | bytes 114720 | tf_op jit(solution)/shard_map/ppermute | solution.py:326
  44.8 0.0 collective-permute-done.8.refs_2_
  44.8 0.1 shard_map.42
  44.9 1.8 %collective-permute-done.15.refs_1_ = bf16[18,32,128]{2,1,0:T(8,128)(2,1)S(1)} collective-permute-done((bf16[18,32,128]{2,1,0:T(8,128)(2,1)S(1)}, bf16[18,32,128]{2,1,0:T(8,128)(2,1)S(1)}, u32[]{:S(2)}, u32[]{:S(2)}) %collective-permute-start.15) | collective-permute-done | bytes 147488 | tf_op jit(solution)/shard_map/ppermute | solution.py:326
  46.7 1.3 %shard_map.45 = (bf16[4096,128]{1,0:T(8,128)(2,1)}, f32[2,1128,128]{2,1,0:T(8,128)S(1)}) custom-call(f32[2,1128,128]{2,1,0:T(8,128)S(1)} %get-tuple-element.62.refs_0_, bf16[18,32,128]{2,1,0:T(8,128)(2,1)S(1)} %collective-permute-done.15.refs_1_, bf16[18,32,128]{2,1,0:T(8,128)(2,1)S(1)} %get-tuple-element.72.refs_2_, ...), custom_call_target="tpu_custom_call", output_to_operand_aliasing={{1}: (0, {})} | custom-call | flops 1 | bytes 1 | tf_op jit(solution)/shard_map/pallas_call | solution.py:313
  48.0 2.3 %collective-permute-done.16.refs_2_ = bf16[18,32,128]{2,1,0:T(8,128)(2,1)S(1)} collective-permute-done((bf16[18,32,128]{2,1,0:T(8,128)(2,1)S(1)}, bf16[18,32,128]{2,1,0:T(8,128)(2,1)S(1)}, u32[]{:S(2)}, u32[]{:S(2)}) %collective-permute-start.16) | collective-permute-done | bytes 147488 | tf_op jit(solution)/shard_map/ppermute | solution.py:326
  50.3 0.0 collective-permute-done.17.refs_3_
  50.3 1.3 %shard_map.46 = (bf16[4096,128]{1,0:T(8,128)(2,1)}, f32[2,1128,128]{2,1,0:T(8,128)S(1)}) custom-call(bf16[4096,128]{1,0:T(8,128)(2,1)} %get-tuple-element.74.refs_0_, f32[2,1128,128]{2,1,0:T(8,128)S(1)} %get-tuple-element.75.refs_1_, bf16[18,32,128]{2,1,0:T(8,128)(2,1)S(1)} %collective-permute-done.16.refs_2_, ...), custom_call_target="tpu_custom_call", output_to_operand_aliasing={{0}: (0, {}), {1}: (1, {})} | custom-call | flops 1 | bytes 1 | tf_op jit(solution)/shard_map/pallas_call | solution.py:313
  (6 shorter events, 0.0 us)
Async XLA Ops:
  0.0 2.1 %copy-start = (bf16[2,262144]{1,0:T(2,128)(2,1)S(1)}, bf16[2,262144]{1,0:T(2,128)(2,1)}, u32[]{:S(2)}) copy-start(bf16[2,262144]{1,0:T(2,128)(2,1)} %param.3) | copy-start | bytes 3145732
  0.0 1.1 %copy-start.1 = (bf16[4,3,2,64,64]{4,3,2,1,0:T(8,128)(2,1)S(1)}, bf16[4,3,2,64,64]{4,3,2,1,0:T(8,128)(2,1)}, u32[]{:S(2)}) copy-start(bf16[4,3,2,64,64]{4,3,2,1,0:T(8,128)(2,1)} %refs_5_.1) | copy-start | bytes 589828
  2.1 6.0 %copy-start.2 = (bf16[4,3,2,64,64]{4,3,2,1,0:T(8,128)(2,1)S(1)}, bf16[4,3,2,64,64]{4,3,2,1,0:T(8,128)(2,1)}, u32[]{:S(2)}) copy-start(bf16[4,3,2,64,64]{4,3,2,1,0:T(8,128)(2,1)} %refs_5_.1) | copy-start | bytes 589828
  3.4 10.3 %copy-start.3 = (s32[4]{0:T(128)S(1)}, s32[4]{0:T(128)}, u32[]{:S(2)}) copy-start(s32[4]{0:T(128)} %param.5) | copy-start | bytes 52
  3.4 10.2 %collective-permute-start = (bf16[14,32,128]{2,1,0:T(8,128)(2,1)S(1)}, bf16[14,32,128]{2,1,0:T(8,128)(2,1)S(1)}, u32[]{:S(2)}, u32[]{:S(2)}) collective-permute-start(bf16[14,32,128]{2,1,0:T(8,128)(2,1)S(1)} %get-tuple-element.45), channel_id=1, source_target_pairs={{0,4},{4,0},{8,12},{12,8},{16,20},{20,16},{24,28},{28,24},{1,5},{5... | collective-permute-start | bytes 344072 | tf_op jit(solution)/shard_map/ppermute | solution.py:326
  6.5 7.3 %collective-permute-start.1 = (bf16[14,32,128]{2,1,0:T(8,128)(2,1)S(1)}, bf16[14,32,128]{2,1,0:T(8,128)(2,1)S(1)}, u32[]{:S(2)}, u32[]{:S(2)}) collective-permute-start(bf16[14,32,128]{2,1,0:T(8,128)(2,1)S(1)} %get-tuple-element.46), channel_id=1, source_target_pairs={{0,12},{4,8},{8,4},{12,0},{16,28},{20,24},{24,20},{28,16},{1,13},{... | collective-permute-start | bytes 344072 | tf_op jit(solution)/shard_map/ppermute | solution.py:326
  8.0 5.7 %collective-permute-start.2 = (bf16[14,32,128]{2,1,0:T(8,128)(2,1)S(1)}, bf16[14,32,128]{2,1,0:T(8,128)(2,1)S(1)}, u32[]{:S(2)}, u32[]{:S(2)}) collective-permute-start(bf16[14,32,128]{2,1,0:T(8,128)(2,1)S(1)} %get-tuple-element.47), channel_id=1, source_target_pairs={{0,8},{4,12},{8,0},{12,4},{16,24},{20,28},{24,16},{28,20},{1,9},{5... | collective-permute-start | bytes 344072 | tf_op jit(solution)/shard_map/ppermute | solution.py:326
  10.2 8.1 %collective-permute-start.9 = (bf16[18,32,128]{2,1,0:T(8,128)(2,1)S(1)}, bf16[18,32,128]{2,1,0:T(8,128)(2,1)S(1)}, u32[]{:S(2)}, u32[]{:S(2)}) collective-permute-start(bf16[18,32,128]{2,1,0:T(8,128)(2,1)S(1)} %get-tuple-element.63), channel_id=1, source_target_pairs={{0,4},{4,0},{8,12},{12,8},{16,20},{20,16},{24,28},{28,24},{1,5},{5... | collective-permute-start | bytes 442376 | tf_op jit(solution)/shard_map/ppermute | solution.py:326
  12.1 7.1 %collective-permute-start.10 = (bf16[18,32,128]{2,1,0:T(8,128)(2,1)S(1)}, bf16[18,32,128]{2,1,0:T(8,128)(2,1)S(1)}, u32[]{:S(2)}, u32[]{:S(2)}) collective-permute-start(bf16[18,32,128]{2,1,0:T(8,128)(2,1)S(1)} %get-tuple-element.64), channel_id=1, source_target_pairs={{0,12},{4,8},{8,4},{12,0},{16,28},{20,24},{24,20},{28,16},{1,13},{... | collective-permute-start | bytes 442376 | tf_op jit(solution)/shard_map/ppermute | solution.py:326
  13.7 6.1 %collective-permute-start.11 = (bf16[18,32,128]{2,1,0:T(8,128)(2,1)S(1)}, bf16[18,32,128]{2,1,0:T(8,128)(2,1)S(1)}, u32[]{:S(2)}, u32[]{:S(2)}) collective-permute-start(bf16[18,32,128]{2,1,0:T(8,128)(2,1)S(1)} %get-tuple-element.65), channel_id=1, source_target_pairs={{0,8},{4,12},{8,0},{12,4},{16,24},{20,28},{24,16},{28,20},{1,9},{5... | collective-permute-start | bytes 442376 | tf_op jit(solution)/shard_map/ppermute | solution.py:326
  14.3 7.8 %collective-permute-start.3 = (bf16[2,14,16,128]{3,2,1,0:T(8,128)(2,1)S(1)}, bf16[2,14,16,128]{3,2,1,0:T(8,128)(2,1)S(1)}, u32[]{:S(2)}, u32[]{:S(2)}) collective-permute-start(bf16[2,14,16,128]{3,2,1,0:T(8,128)(2,1)S(1)} %get-tuple-element.49), channel_id=1, source_target_pairs={{0,3},{1,2},{2,1},{3,0},{4,7},{5,6},{6,5},{7,4},{8,11},{9,10},{10,... | collective-permute-start | bytes 344072 | tf_op jit(solution)/shard_map/ppermute | solution.py:343
  14.4 7.9 %collective-permute-start.4 = (bf16[2,14,16,128]{3,2,1,0:T(8,128)(2,1)S(1)}, bf16[2,14,16,128]{3,2,1,0:T(8,128)(2,1)S(1)}, u32[]{:S(2)}, u32[]{:S(2)}) collective-permute-start(bf16[2,14,16,128]{3,2,1,0:T(8,128)(2,1)S(1)} %get-tuple-element.50), channel_id=1, source_target_pairs={{0,2},{1,3},{2,0},{3,1},{4,6},{5,7},{6,4},{7,5},{8,10},{9,11},{10,... | collective-permute-start | bytes 344072 | tf_op jit(solution)/shard_map/ppermute | solution.py:343
  18.3 4.0 %collective-permute-start.5 = (bf16[2,14,16,128]{3,2,1,0:T(8,128)(2,1)S(1)}, bf16[2,14,16,128]{3,2,1,0:T(8,128)(2,1)S(1)}, u32[]{:S(2)}, u32[]{:S(2)}) collective-permute-start(bf16[2,14,16,128]{3,2,1,0:T(8,128)(2,1)S(1)} %get-tuple-element.51), channel_id=1, source_target_pairs={{0,1},{1,0},{2,3},{3,2},{4,5},{5,4},{6,7},{7,6},{8,9},{9,8},{10,11... | collective-permute-start | bytes 344072 | tf_op jit(solution)/shard_map/ppermute | solution.py:343
  20.4 6.8 %collective-permute-start.12 = (bf16[2,18,16,128]{3,2,1,0:T(8,128)(2,1)S(1)}, bf16[2,18,16,128]{3,2,1,0:T(8,128)(2,1)S(1)}, u32[]{:S(2)}, u32[]{:S(2)}) collective-permute-start(bf16[2,18,16,128]{3,2,1,0:T(8,128)(2,1)S(1)} %get-tuple-element.67), channel_id=1, source_target_pairs={{0,3},{1,2},{2,1},{3,0},{4,7},{5,6},{6,5},{7,4},{8,11},{9,10},{10,... | collective-permute-start | bytes 442376 | tf_op jit(solution)/shard_map/ppermute | solution.py:343
  20.7 9.1 %collective-permute-start.13 = (bf16[2,18,16,128]{3,2,1,0:T(8,128)(2,1)S(1)}, bf16[2,18,16,128]{3,2,1,0:T(8,128)(2,1)S(1)}, u32[]{:S(2)}, u32[]{:S(2)}) collective-permute-start(bf16[2,18,16,128]{3,2,1,0:T(8,128)(2,1)S(1)} %get-tuple-element.68), channel_id=1, source_target_pairs={{0,2},{1,3},{2,0},{3,1},{4,6},{5,7},{6,4},{7,5},{8,10},{9,11},{10,... | collective-permute-start | bytes 442376 | tf_op jit(solution)/shard_map/ppermute | solution.py:343
  22.1 7.6 %collective-permute-start.14 = (bf16[2,18,16,128]{3,2,1,0:T(8,128)(2,1)S(1)}, bf16[2,18,16,128]{3,2,1,0:T(8,128)(2,1)S(1)}, u32[]{:S(2)}, u32[]{:S(2)}) collective-permute-start(bf16[2,18,16,128]{3,2,1,0:T(8,128)(2,1)S(1)} %get-tuple-element.69), channel_id=1, source_target_pairs={{0,1},{1,0},{2,3},{3,2},{4,5},{5,4},{6,7},{7,6},{8,9},{9,8},{10,11... | collective-permute-start | bytes 442376 | tf_op jit(solution)/shard_map/ppermute | solution.py:343
  22.8 11.9 %collective-permute-start.6 = (bf16[14,32,128]{2,1,0:T(8,128)(2,1)S(1)}, bf16[14,32,128]{2,1,0:T(8,128)(2,1)S(1)}, u32[]{:S(2)}, u32[]{:S(2)}) collective-permute-start(bf16[14,32,128]{2,1,0:T(8,128)(2,1)S(1)} %get-tuple-element.58), channel_id=1, source_target_pairs={{0,16},{4,20},{8,24},{12,28},{16,0},{20,4},{24,8},{28,12},{1,17},{... | collective-permute-start | bytes 344072 | tf_op jit(solution)/shard_map/ppermute | solution.py:326
  25.9 19.0 %collective-permute-start.7 = (bf16[14,32,128]{2,1,0:T(8,128)(2,1)S(1)}, bf16[14,32,128]{2,1,0:T(8,128)(2,1)S(1)}, u32[]{:S(2)}, u32[]{:S(2)}) collective-permute-start(bf16[14,32,128]{2,1,0:T(8,128)(2,1)S(1)} %get-tuple-element.59), channel_id=1, source_target_pairs={{0,20},{4,16},{8,28},{12,24},{16,4},{20,0},{24,12},{28,8},{1,21},{... | collective-permute-start | bytes 344072 | tf_op jit(solution)/shard_map/ppermute | solution.py:326
  27.2 17.7 %collective-permute-start.8 = (bf16[14,32,128]{2,1,0:T(8,128)(2,1)S(1)}, bf16[14,32,128]{2,1,0:T(8,128)(2,1)S(1)}, u32[]{:S(2)}, u32[]{:S(2)}) collective-permute-start(bf16[14,32,128]{2,1,0:T(8,128)(2,1)S(1)} %get-tuple-element.60), channel_id=1, source_target_pairs={{0,4},{4,0},{8,12},{12,8},{16,20},{20,16},{24,28},{28,24},{1,5},{5... | collective-permute-start | bytes 344072 | tf_op jit(solution)/shard_map/ppermute | solution.py:326
  30.4 16.3 %collective-permute-start.15 = (bf16[18,32,128]{2,1,0:T(8,128)(2,1)S(1)}, bf16[18,32,128]{2,1,0:T(8,128)(2,1)S(1)}, u32[]{:S(2)}, u32[]{:S(2)}) collective-permute-start(bf16[18,32,128]{2,1,0:T(8,128)(2,1)S(1)} %get-tuple-element.71), channel_id=1, source_target_pairs={{0,16},{4,20},{8,24},{12,28},{16,0},{20,4},{24,8},{28,12},{1,17},{... | collective-permute-start | bytes 442376 | tf_op jit(solution)/shard_map/ppermute | solution.py:326
  33.1 17.1 %collective-permute-start.16 = (bf16[18,32,128]{2,1,0:T(8,128)(2,1)S(1)}, bf16[18,32,128]{2,1,0:T(8,128)(2,1)S(1)}, u32[]{:S(2)}, u32[]{:S(2)}) collective-permute-start(bf16[18,32,128]{2,1,0:T(8,128)(2,1)S(1)} %get-tuple-element.76), channel_id=1, source_target_pairs={{0,20},{4,16},{8,28},{12,24},{16,4},{20,0},{24,12},{28,8},{1,21},{... | collective-permute-start | bytes 442376 | tf_op jit(solution)/shard_map/ppermute | solution.py:326
  34.7 15.6 %collective-permute-start.17 = (bf16[18,32,128]{2,1,0:T(8,128)(2,1)S(1)}, bf16[18,32,128]{2,1,0:T(8,128)(2,1)S(1)}, u32[]{:S(2)}, u32[]{:S(2)}) collective-permute-start(bf16[18,32,128]{2,1,0:T(8,128)(2,1)S(1)} %get-tuple-element.77), channel_id=1, source_target_pairs={{0,4},{4,0},{8,12},{12,8},{16,20},{20,16},{24,28},{28,24},{1,5},{5... | collective-permute-start | bytes 442376 | tf_op jit(solution)/shard_map/ppermute | solution.py:326

commit v13 on v11

--- a/solution.py
+++ b/solution.py
@@ -170,7 +170,7 @@
 
 PITCH = G + 1
 NARROW = HALF + 1
-EARLY = 14
+EARLY = 15
 COST = 2 * 10**9
 
 

time: 51.7 us -> 51.8 us (level)
  transfers between devices with their start and end apart: 18 -> 18, of which waited for: 8 -> 9; matrix products, arithmetic and copies ran while one was open for 0% -> 0% of each run, Pallas kernels for 11% -> 11%
where the time goes in v13:
time: 51.8 us; the launch traced here: 51.6 us
  starting transfers between devices  22.2 us (43%)
  waiting for transfers between devices  18.8 us (36%)
  Pallas kernels  9.48 us (18%)
  local copies, waits for them, and re-layouts  1.1 us (2%)
    ppermute x12, waiting for transfers between devices, swapped(): lax.ppermute(x, 'hi', [(d, d ^ apart) for d in range(lax.axis_size('hi'))])  18.4 us
    ppermute x12, starting transfers between devices, swapped(): lax.ppermute(x, 'hi', [(d, d ^ apart) for d in range(lax.axis_size('hi'))])  18.3 us
    pallas_call x10, Pallas kernels, call(): pl.pallas_call(body, out_shape=outs, in_specs=specs + [ANY] * len(after),...  9.48 us
    ppermute x6, starting transfers between devices, regrouped(): lax.ppermute(x, 'lo', to)  3.9 us
    unnamed x8, local copies, waits for them, and re-layouts  1.1 us
  transfers between devices with their start and end apart: 18, of which 9 were waited for; matrix products, arithmetic and copies ran while one was open for 0% of the time, Pallas kernels for 11%

profile of v13, /device:TPU:0, one launch (start us, length us, event | category | flops | bytes accessed | tf_op | source)
XLA Modules:
  0.0 51.6 jit_solution(9179210859330287581)
XLA Ops:
  0.0 1.1 %copy-done.1 = bf16[4,3,2,64,64]{4,3,2,1,0:T(8,128)(2,1)S(1)} copy-done((bf16[4,3,2,64,64]{4,3,2,1,0:T(8,128)(2,1)S(1)}, bf16[4,3,2,64,64]{4,3,2,1,0:T(8,128)(2,1)}, u32[]{:S(2)}) %copy-start.1) | copy-done | bytes 196632
  1.1 1.0 %shard_map.37 = (bf16[128,256]{1,0:T(8,128)(2,1)S(1)}, bf16[128,256]{1,0:T(8,128)(2,1)S(1)}, bf16[256,512]{1,0:T(8,128)(2,1)S(1)}, bf16[64,128]{1,0:T(8,128)(2,1)S(1)}) custom-call(bf16[4,3,2,64,64]{4,3,2,1,0:T(8,128)(2,1)S(1)} %copy-done.1), custom_call_target="tpu_custom_call" | custom-call | flops 2000000000 | bytes 1 | tf_op jit(solution)/shard_map/pallas_call | solution.py:313
  2.1 0.0 copy-done
  2.1 1.4 %shard_map.38 = (bf16[15,32,128]{2,1,0:T(8,128)(2,1)S(1)}, bf16[15,32,128]{2,1,0:T(8,128)(2,1)S(1)}, bf16[15,32,128]{2,1,0:T(8,128)(2,1)S(1)}, bf16[15,32,128]{2...) custom-call(bf16[4096,128]{1,0:T(8,128)(2,1)S(1)} %bitcast.11, ...), custom_call_target="tpu_custom_call" | custom-call | flops 1 | bytes 1 | tf_op jit(solution)/shard_map/pallas_call | solution.py:313
  3.4 0.0 copy-start.3
  3.5 3.0 %collective-permute-start = (bf16[15,32,128]{2,1,0:T(8,128)(2,1)S(1)}, bf16[15,32,128]{2,1,0:T(8,128)(2,1)S(1)}, u32[]{:S(2)}, u32[]{:S(2)}) collective-permute-start(bf16[15,32,128]{2,1,0:T(8,128)(2,1)S(1)} %get-tuple-element.45), channel_id=1, source_target_pairs={{0,4},{4,0},{8,12},{12,8},{16,20},{20,16},{24,28},{28,24},{1,5},{5... | collective-permute-start | bytes 368648 | tf_op jit(solution)/shard_map/ppermute | solution.py:326
  6.5 1.5 %collective-permute-start.1 = (bf16[15,32,128]{2,1,0:T(8,128)(2,1)S(1)}, bf16[15,32,128]{2,1,0:T(8,128)(2,1)S(1)}, u32[]{:S(2)}, u32[]{:S(2)}) collective-permute-start(bf16[15,32,128]{2,1,0:T(8,128)(2,1)S(1)} %get-tuple-element.46), channel_id=1, source_target_pairs={{0,12},{4,8},{8,4},{12,0},{16,28},{20,24},{24,20},{28,16},{1,13},{... | collective-permute-start | bytes 368648 | tf_op jit(solution)/shard_map/ppermute | solution.py:326
  8.0 0.1 collective-permute-start.2
  8.1 2.1 %shard_map.40 = (bf16[17,32,128]{2,1,0:T(8,128)(2,1)S(1)}, bf16[17,32,128]{2,1,0:T(8,128)(2,1)S(1)}, bf16[17,32,128]{2,1,0:T(8,128)(2,1)S(1)}, bf16[17,32,128]{2...) custom-call(bf16[2048,256]{1,0:T(8,128)(2,1)S(1)} %get-tuple-element, ...), custom_call_target="tpu_custom_call" | custom-call | flops 1 | bytes 1 | tf_op jit(solution)/shard_map/pallas_call | solution.py:313
  10.2 2.0 %collective-permute-start.9 = (bf16[17,32,128]{2,1,0:T(8,128)(2,1)S(1)}, bf16[17,32,128]{2,1,0:T(8,128)(2,1)S(1)}, u32[]{:S(2)}, u32[]{:S(2)}) collective-permute-start(bf16[17,32,128]{2,1,0:T(8,128)(2,1)S(1)} %get-tuple-element.63), channel_id=1, source_target_pairs={{0,4},{4,0},{8,12},{12,8},{16,20},{20,16},{24,28},{28,24},{1,5},{5... | collective-permute-start | bytes 417800 | tf_op jit(solution)/shard_map/ppermute | solution.py:326
  12.2 1.5 %collective-permute-start.10 = (bf16[17,32,128]{2,1,0:T(8,128)(2,1)S(1)}, bf16[17,32,128]{2,1,0:T(8,128)(2,1)S(1)}, u32[]{:S(2)}, u32[]{:S(2)}) collective-permute-start(bf16[17,32,128]{2,1,0:T(8,128)(2,1)S(1)} %get-tuple-element.64), channel_id=1, source_target_pairs={{0,12},{4,8},{8,4},{12,0},{16,28},{20,24},{24,20},{28,16},{1,13},{... | collective-permute-start | bytes 417800 | tf_op jit(solution)/shard_map/ppermute | solution.py:326
  13.7 0.0 collective-permute-done.refs_1_
  13.7 0.1 collective-permute-start.11
  13.7 0.0 collective-permute-done.1.refs_2_
  13.7 0.4 collective-permute-done.2.refs_3_
  14.2 0.6 %shard_map.39 = (bf16[2,15,16,128]{3,2,1,0:T(8,128)(2,1)S(1)}, bf16[2,15,16,128]{3,2,1,0:T(8,128)(2,1)S(1)}, bf16[2,15,16,128]{3,2,1,0:T(8,128)(2,1)S(1)}, bf16[2,15,16,128]{3,2,1,0:T(8,128)(2,1)S(1)}) custom-call(s32[1,4]{1,0:T(1,128)S(1)} %bitcast.12, bf16[15,32,128]{2,1,0:T(8,128)(2,1)S(1)} %collective-permute-done.refs_1_, ...), custom_call_target="tpu_custom_call" | custom-call | flops 2000000000 | bytes 1 | tf_op jit(solution)/shard_map/pallas_call | solution.py:313
  14.8 1.7 %collective-permute-start.3 = (bf16[2,15,16,128]{3,2,1,0:T(8,128)(2,1)S(1)}, bf16[2,15,16,128]{3,2,1,0:T(8,128)(2,1)S(1)}, u32[]{:S(2)}, u32[]{:S(2)}) collective-permute-start(bf16[2,15,16,128]{3,2,1,0:T(8,128)(2,1)S(1)} %get-tuple-element.49), channel_id=1, source_target_pairs={{0,2},{1,3},{2,0},{3,1},{4,6},{5,7},{6,4},{7,5},{8,10},{9,11},{10,... | collective-permute-start | bytes 368648 | tf_op jit(solution)/shard_map/ppermute | solution.py:343
  16.5 0.0 collective-permute-start.4
  16.5 1.6 %collective-permute-done.9.refs_1_ = bf16[17,32,128]{2,1,0:T(8,128)(2,1)S(1)} collective-permute-done((bf16[17,32,128]{2,1,0:T(8,128)(2,1)S(1)}, bf16[17,32,128]{2,1,0:T(8,128)(2,1)S(1)}, u32[]{:S(2)}, u32[]{:S(2)}) %collective-permute-start.9) | collective-permute-done | bytes 139296 | tf_op jit(solution)/shard_map/ppermute | solution.py:326
  18.0 0.0 collective-permute-start.5
  18.0 1.4 %collective-permute-done.10.refs_2_ = bf16[17,32,128]{2,1,0:T(8,128)(2,1)S(1)} collective-permute-done((bf16[17,32,128]{2,1,0:T(8,128)(2,1)S(1)}, bf16[17,32,128]{2,1,0:T(8,128)(2,1)S(1)}, u32[]{:S(2)}, u32[]{:S(2)}) %collective-permute-start.10) | collective-permute-done | bytes 139296 | tf_op jit(solution)/shard_map/ppermute | solution.py:326
  19.4 0.4 collective-permute-done.11.refs_3_
  19.8 0.6 %shard_map.43 = (bf16[2,17,16,128]{3,2,1,0:T(8,128)(2,1)S(1)}, bf16[2,17,16,128]{3,2,1,0:T(8,128)(2,1)S(1)}, bf16[2,17,16,128]{3,2,1,0:T(8,128)(2,1)S(1)}, bf16[2,17,16,128]{3,2,1,0:T(8,128)(2,1)S(1)}) custom-call(s32[1,4]{1,0:T(1,128)S(1)} %bitcast.13, bf16[17,32,128]{2,1,0:T(8,128)(2,1)S(1)} %collective-permute-done.9.refs_1_, ...), custom_call_target="tpu_custom_call" | custom-call | flops 1 | bytes 1 | tf_op jit(solution)/shard_map/pallas_call | solution.py:313
  20.4 1.7 %collective-permute-start.12 = (bf16[2,17,16,128]{3,2,1,0:T(8,128)(2,1)S(1)}, bf16[2,17,16,128]{3,2,1,0:T(8,128)(2,1)S(1)}, u32[]{:S(2)}, u32[]{:S(2)}) collective-permute-start(bf16[2,17,16,128]{3,2,1,0:T(8,128)(2,1)S(1)} %get-tuple-element.67), channel_id=1, source_target_pairs={{0,2},{1,3},{2,0},{3,1},{4,6},{5,7},{6,4},{7,5},{8,10},{9,11},{10,... | collective-permute-start | bytes 417800 | tf_op jit(solution)/shard_map/ppermute | solution.py:343
  22.0 0.0 collective-permute-start.13
  22.0 0.0 collective-permute-done.3.refs_0_
  22.0 0.5 %collective-permute-start.14 = (bf16[2,17,16,128]{3,2,1,0:T(8,128)(2,1)S(1)}, bf16[2,17,16,128]{3,2,1,0:T(8,128)(2,1)S(1)}, u32[]{:S(2)}, u32[]{:S(2)}) collective-permute-start(bf16[2,17,16,128]{3,2,1,0:T(8,128)(2,1)S(1)} %get-tuple-element.69), channel_id=1, source_target_pairs={{0,1},{1,0},{2,3},{3,2},{4,5},{5,4},{6,7},{7,6},{8,9},{9,8},{10,11... | collective-permute-start | bytes 417800 | tf_op jit(solution)/shard_map/ppermute | solution.py:343
  22.6 0.0 collective-permute-done.4.refs_1_
  22.6 0.0 collective-permute-done.5.refs_2_
  22.6 0.6 %shard_map.41 = (bf16[15,32,128]{2,1,0:T(8,128)(2,1)S(1)}, bf16[15,32,128]{2,1,0:T(8,128)(2,1)S(1)}, bf16[15,32,128]{2,1,0:T(8,128)(2,1)S(1)}, bf16[15,32,128]{2,1,0:T(8,128)(2,1)S(1)}) custom-call(bf16[2,15,16,128]{3,2,1,0:T(8,128)(2,1)S(1)} %collective-permute-done.3.refs_0_, bf16[2,15,16,128]{3,2,1,0:T(8,128)(2,1)S(1)} %collective-permute-done.4.refs_1_, ...), custom_call_target="tpu_custom_call" | custom-call | flops 2000000000 | bytes 1 | tf_op jit(solution)/shard_map/pallas_call | solution.py:313
  23.2 2.8 %collective-permute-start.6 = (bf16[15,32,128]{2,1,0:T(8,128)(2,1)S(1)}, bf16[15,32,128]{2,1,0:T(8,128)(2,1)S(1)}, u32[]{:S(2)}, u32[]{:S(2)}) collective-permute-start(bf16[15,32,128]{2,1,0:T(8,128)(2,1)S(1)} %get-tuple-element.58), channel_id=1, source_target_pairs={{0,16},{4,20},{8,24},{12,28},{16,0},{20,4},{24,8},{28,12},{1,17},{... | collective-permute-start | bytes 368648 | tf_op jit(solution)/shard_map/ppermute | solution.py:326
  25.9 1.3 %collective-permute-start.7 = (bf16[15,32,128]{2,1,0:T(8,128)(2,1)S(1)}, bf16[15,32,128]{2,1,0:T(8,128)(2,1)S(1)}, u32[]{:S(2)}, u32[]{:S(2)}) collective-permute-start(bf16[15,32,128]{2,1,0:T(8,128)(2,1)S(1)} %get-tuple-element.59), channel_id=1, source_target_pairs={{0,20},{4,16},{8,28},{12,24},{16,4},{20,0},{24,12},{28,8},{1,21},{... | collective-permute-start | bytes 368648 | tf_op jit(solution)/shard_map/ppermute | solution.py:326
  27.2 0.0 collective-permute-done.12.refs_0_
  27.2 0.5 collective-permute-start.8
  27.7 0.3 collective-permute-done.13.refs_1_
  28.0 0.0 collective-permute-done.14.refs_2_
  28.0 0.6 %shard_map.44 = (bf16[17,32,128]{2,1,0:T(8,128)(2,1)S(1)}, bf16[17,32,128]{2,1,0:T(8,128)(2,1)S(1)}, bf16[17,32,128]{2,1,0:T(8,128)(2,1)S(1)}, bf16[17,32,128]{2,1,0:T(8,128)(2,1)S(1)}) custom-call(bf16[2,17,16,128]{3,2,1,0:T(8,128)(2,1)S(1)} %collective-permute-done.12.refs_0_, bf16[2,17,16,128]{3,2,1,0:T(8,128)(2,1)S(1)} %collective-permute-done.13.refs_1_, ...), custom_call_target="tpu_custom_call" | custom-call | flops 1 | bytes 1 | tf_op jit(solution)/shard_map/pallas_call | solution.py:313
  28.6 2.6 %collective-permute-start.15 = (bf16[17,32,128]{2,1,0:T(8,128)(2,1)S(1)}, bf16[17,32,128]{2,1,0:T(8,128)(2,1)S(1)}, u32[]{:S(2)}, u32[]{:S(2)}) collective-permute-start(bf16[17,32,128]{2,1,0:T(8,128)(2,1)S(1)} %get-tuple-element.71), channel_id=1, source_target_pairs={{0,16},{4,20},{8,24},{12,28},{16,0},{20,4},{24,8},{28,12},{1,17},{... | collective-permute-start | bytes 417800 | tf_op jit(solution)/shard_map/ppermute | solution.py:326
  31.3 1.3 %collective-permute-start.16 = (bf16[17,32,128]{2,1,0:T(8,128)(2,1)S(1)}, bf16[17,32,128]{2,1,0:T(8,128)(2,1)S(1)}, u32[]{:S(2)}, u32[]{:S(2)}) collective-permute-start(bf16[17,32,128]{2,1,0:T(8,128)(2,1)S(1)} %get-tuple-element.76), channel_id=1, source_target_pairs={{0,20},{4,16},{8,28},{12,24},{16,4},{20,0},{24,12},{28,8},{1,21},{... | collective-permute-start | bytes 417800 | tf_op jit(solution)/shard_map/ppermute | solution.py:326
  32.6 9.0 %collective-permute-done.6.refs_0_ = bf16[15,32,128]{2,1,0:T(8,128)(2,1)S(1)} collective-permute-done((bf16[15,32,128]{2,1,0:T(8,128)(2,1)S(1)}, bf16[15,32,128]{2,1,0:T(8,128)(2,1)S(1)}, u32[]{:S(2)}, u32[]{:S(2)}) %collective-permute-start.6) | collective-permute-done | bytes 122912 | tf_op jit(solution)/shard_map/ppermute | solution.py:326
  41.5 1.6 %collective-permute-start.17 = (bf16[17,32,128]{2,1,0:T(8,128)(2,1)S(1)}, bf16[17,32,128]{2,1,0:T(8,128)(2,1)S(1)}, u32[]{:S(2)}, u32[]{:S(2)}) collective-permute-start(bf16[17,32,128]{2,1,0:T(8,128)(2,1)S(1)} %get-tuple-element.77), channel_id=1, source_target_pairs={{0,4},{4,0},{8,12},{12,8},{16,20},{20,16},{24,28},{28,24},{1,5},{5... | collective-permute-start | bytes 417800 | tf_op jit(solution)/shard_map/ppermute | solution.py:326
  43.2 2.1 %collective-permute-done.7.refs_1_ = bf16[15,32,128]{2,1,0:T(8,128)(2,1)S(1)} collective-permute-done((bf16[15,32,128]{2,1,0:T(8,128)(2,1)S(1)}, bf16[15,32,128]{2,1,0:T(8,128)(2,1)S(1)}, u32[]{:S(2)}, u32[]{:S(2)}) %collective-permute-start.7) | collective-permute-done | bytes 122912 | tf_op jit(solution)/shard_map/ppermute | solution.py:326
  45.2 0.0 collective-permute-done.8.refs_2_
  45.2 0.1 shard_map.42
  45.3 1.8 %collective-permute-done.15.refs_1_ = bf16[17,32,128]{2,1,0:T(8,128)(2,1)S(1)} collective-permute-done((bf16[17,32,128]{2,1,0:T(8,128)(2,1)S(1)}, bf16[17,32,128]{2,1,0:T(8,128)(2,1)S(1)}, u32[]{:S(2)}, u32[]{:S(2)}) %collective-permute-start.15) | collective-permute-done | bytes 139296 | tf_op jit(solution)/shard_map/ppermute | solution.py:326
  47.2 1.3 %shard_map.45 = (bf16[4096,128]{1,0:T(8,128)(2,1)}, f32[2,1128,128]{2,1,0:T(8,128)S(1)}) custom-call(f32[2,1128,128]{2,1,0:T(8,128)S(1)} %get-tuple-element.62.refs_0_, bf16[17,32,128]{2,1,0:T(8,128)(2,1)S(1)} %collective-permute-done.15.refs_1_, bf16[17,32,128]{2,1,0:T(8,128)(2,1)S(1)} %get-tuple-element.72.refs_2_, ...), custom_call_target="tpu_custom_call", output_to_operand_aliasing={{1}: (0, {})} | custom-call | flops 1 | bytes 1 | tf_op jit(solution)/shard_map/pallas_call | solution.py:313
  48.5 1.8 %collective-permute-done.16.refs_2_ = bf16[17,32,128]{2,1,0:T(8,128)(2,1)S(1)} collective-permute-done((bf16[17,32,128]{2,1,0:T(8,128)(2,1)S(1)}, bf16[17,32,128]{2,1,0:T(8,128)(2,1)S(1)}, u32[]{:S(2)}, u32[]{:S(2)}) %collective-permute-start.16) | collective-permute-done | bytes 139296 | tf_op jit(solution)/shard_map/ppermute | solution.py:326
  50.3 1.3 %shard_map.46 = (bf16[4096,128]{1,0:T(8,128)(2,1)}, f32[2,1128,128]{2,1,0:T(8,128)S(1)}) custom-call(bf16[4096,128]{1,0:T(8,128)(2,1)} %get-tuple-element.74.refs_0_, f32[2,1128,128]{2,1,0:T(8,128)S(1)} %get-tuple-element.75.refs_1_, bf16[17,32,128]{2,1,0:T(8,128)(2,1)S(1)} %collective-permute-done.16.refs_2_, ...), custom_call_target="tpu_custom_call", output_to_operand_aliasing={{0}: (0, {}), {1}: (1, {})} | custom-call | flops 1 | bytes 1 | tf_op jit(solution)/shard_map/pallas_call | solution.py:313
  (6 shorter events, 0.0 us)
Async XLA Ops:
  0.0 2.1 %copy-start = (bf16[2,262144]{1,0:T(2,128)(2,1)S(1)}, bf16[2,262144]{1,0:T(2,128)(2,1)}, u32[]{:S(2)}) copy-start(bf16[2,262144]{1,0:T(2,128)(2,1)} %param.3) | copy-start | bytes 3145732
  0.0 1.1 %copy-start.1 = (bf16[4,3,2,64,64]{4,3,2,1,0:T(8,128)(2,1)S(1)}, bf16[4,3,2,64,64]{4,3,2,1,0:T(8,128)(2,1)}, u32[]{:S(2)}) copy-start(bf16[4,3,2,64,64]{4,3,2,1,0:T(8,128)(2,1)} %refs_5_.1) | copy-start | bytes 589828
  2.1 6.0 %copy-start.2 = (bf16[4,3,2,64,64]{4,3,2,1,0:T(8,128)(2,1)S(1)}, bf16[4,3,2,64,64]{4,3,2,1,0:T(8,128)(2,1)}, u32[]{:S(2)}) copy-start(bf16[4,3,2,64,64]{4,3,2,1,0:T(8,128)(2,1)} %refs_5_.1) | copy-start | bytes 589828
  3.4 10.7 %copy-start.3 = (s32[4]{0:T(128)S(1)}, s32[4]{0:T(128)}, u32[]{:S(2)}) copy-start(s32[4]{0:T(128)} %param.5) | copy-start | bytes 52
  3.5 10.2 %collective-permute-start = (bf16[15,32,128]{2,1,0:T(8,128)(2,1)S(1)}, bf16[15,32,128]{2,1,0:T(8,128)(2,1)S(1)}, u32[]{:S(2)}, u32[]{:S(2)}) collective-permute-start(bf16[15,32,128]{2,1,0:T(8,128)(2,1)S(1)} %get-tuple-element.45), channel_id=1, source_target_pairs={{0,4},{4,0},{8,12},{12,8},{16,20},{20,16},{24,28},{28,24},{1,5},{5... | collective-permute-start | bytes 368648 | tf_op jit(solution)/shard_map/ppermute | solution.py:326
  6.5 7.3 %collective-permute-start.1 = (bf16[15,32,128]{2,1,0:T(8,128)(2,1)S(1)}, bf16[15,32,128]{2,1,0:T(8,128)(2,1)S(1)}, u32[]{:S(2)}, u32[]{:S(2)}) collective-permute-start(bf16[15,32,128]{2,1,0:T(8,128)(2,1)S(1)} %get-tuple-element.46), channel_id=1, source_target_pairs={{0,12},{4,8},{8,4},{12,0},{16,28},{20,24},{24,20},{28,16},{1,13},{... | collective-permute-start | bytes 368648 | tf_op jit(solution)/shard_map/ppermute | solution.py:326
  8.0 6.2 %collective-permute-start.2 = (bf16[15,32,128]{2,1,0:T(8,128)(2,1)S(1)}, bf16[15,32,128]{2,1,0:T(8,128)(2,1)S(1)}, u32[]{:S(2)}, u32[]{:S(2)}) collective-permute-start(bf16[15,32,128]{2,1,0:T(8,128)(2,1)S(1)} %get-tuple-element.47), channel_id=1, source_target_pairs={{0,8},{4,12},{8,0},{12,4},{16,24},{20,28},{24,16},{28,20},{1,9},{5... | collective-permute-start | bytes 368648 | tf_op jit(solution)/shard_map/ppermute | solution.py:326
  10.2 7.8 %collective-permute-start.9 = (bf16[17,32,128]{2,1,0:T(8,128)(2,1)S(1)}, bf16[17,32,128]{2,1,0:T(8,128)(2,1)S(1)}, u32[]{:S(2)}, u32[]{:S(2)}) collective-permute-start(bf16[17,32,128]{2,1,0:T(8,128)(2,1)S(1)} %get-tuple-element.63), channel_id=1, source_target_pairs={{0,4},{4,0},{8,12},{12,8},{16,20},{20,16},{24,28},{28,24},{1,5},{5... | collective-permute-start | bytes 417800 | tf_op jit(solution)/shard_map/ppermute | solution.py:326
  12.2 7.2 %collective-permute-start.10 = (bf16[17,32,128]{2,1,0:T(8,128)(2,1)S(1)}, bf16[17,32,128]{2,1,0:T(8,128)(2,1)S(1)}, u32[]{:S(2)}, u32[]{:S(2)}) collective-permute-start(bf16[17,32,128]{2,1,0:T(8,128)(2,1)S(1)} %get-tuple-element.64), channel_id=1, source_target_pairs={{0,12},{4,8},{8,4},{12,0},{16,28},{20,24},{24,20},{28,16},{1,13},{... | collective-permute-start | bytes 417800 | tf_op jit(solution)/shard_map/ppermute | solution.py:326
  13.7 6.1 %collective-permute-start.11 = (bf16[17,32,128]{2,1,0:T(8,128)(2,1)S(1)}, bf16[17,32,128]{2,1,0:T(8,128)(2,1)S(1)}, u32[]{:S(2)}, u32[]{:S(2)}) collective-permute-start(bf16[17,32,128]{2,1,0:T(8,128)(2,1)S(1)} %get-tuple-element.65), channel_id=1, source_target_pairs={{0,8},{4,12},{8,0},{12,4},{16,24},{20,28},{24,16},{28,20},{1,9},{5... | collective-permute-start | bytes 417800 | tf_op jit(solution)/shard_map/ppermute | solution.py:326
  14.8 7.3 %collective-permute-start.3 = (bf16[2,15,16,128]{3,2,1,0:T(8,128)(2,1)S(1)}, bf16[2,15,16,128]{3,2,1,0:T(8,128)(2,1)S(1)}, u32[]{:S(2)}, u32[]{:S(2)}) collective-permute-start(bf16[2,15,16,128]{3,2,1,0:T(8,128)(2,1)S(1)} %get-tuple-element.49), channel_id=1, source_target_pairs={{0,2},{1,3},{2,0},{3,1},{4,6},{5,7},{6,4},{7,5},{8,10},{9,11},{10,... | collective-permute-start | bytes 368648 | tf_op jit(solution)/shard_map/ppermute | solution.py:343
  16.5 6.1 %collective-permute-start.4 = (bf16[2,15,16,128]{3,2,1,0:T(8,128)(2,1)S(1)}, bf16[2,15,16,128]{3,2,1,0:T(8,128)(2,1)S(1)}, u32[]{:S(2)}, u32[]{:S(2)}) collective-permute-start(bf16[2,15,16,128]{3,2,1,0:T(8,128)(2,1)S(1)} %get-tuple-element.50), channel_id=1, source_target_pairs={{0,3},{1,2},{2,1},{3,0},{4,7},{5,6},{6,5},{7,4},{8,11},{9,10},{10,... | collective-permute-start | bytes 368648 | tf_op jit(solution)/shard_map/ppermute | solution.py:343
  18.0 4.6 %collective-permute-start.5 = (bf16[2,15,16,128]{3,2,1,0:T(8,128)(2,1)S(1)}, bf16[2,15,16,128]{3,2,1,0:T(8,128)(2,1)S(1)}, u32[]{:S(2)}, u32[]{:S(2)}) collective-permute-start(bf16[2,15,16,128]{3,2,1,0:T(8,128)(2,1)S(1)} %get-tuple-element.51), channel_id=1, source_target_pairs={{0,1},{1,0},{2,3},{3,2},{4,5},{5,4},{6,7},{7,6},{8,9},{9,8},{10,11... | collective-permute-start | bytes 368648 | tf_op jit(solution)/shard_map/ppermute | solution.py:343
  20.4 6.8 %collective-permute-start.12 = (bf16[2,17,16,128]{3,2,1,0:T(8,128)(2,1)S(1)}, bf16[2,17,16,128]{3,2,1,0:T(8,128)(2,1)S(1)}, u32[]{:S(2)}, u32[]{:S(2)}) collective-permute-start(bf16[2,17,16,128]{3,2,1,0:T(8,128)(2,1)S(1)} %get-tuple-element.67), channel_id=1, source_target_pairs={{0,2},{1,3},{2,0},{3,1},{4,6},{5,7},{6,4},{7,5},{8,10},{9,11},{10,... | collective-permute-start | bytes 417800 | tf_op jit(solution)/shard_map/ppermute | solution.py:343
  22.0 6.0 %collective-permute-start.13 = (bf16[2,17,16,128]{3,2,1,0:T(8,128)(2,1)S(1)}, bf16[2,17,16,128]{3,2,1,0:T(8,128)(2,1)S(1)}, u32[]{:S(2)}, u32[]{:S(2)}) collective-permute-start(bf16[2,17,16,128]{3,2,1,0:T(8,128)(2,1)S(1)} %get-tuple-element.68), channel_id=1, source_target_pairs={{0,3},{1,2},{2,1},{3,0},{4,7},{5,6},{6,5},{7,4},{8,11},{9,10},{10,... | collective-permute-start | bytes 417800 | tf_op jit(solution)/shard_map/ppermute | solution.py:343
  22.0 6.0 %collective-permute-start.14 = (bf16[2,17,16,128]{3,2,1,0:T(8,128)(2,1)S(1)}, bf16[2,17,16,128]{3,2,1,0:T(8,128)(2,1)S(1)}, u32[]{:S(2)}, u32[]{:S(2)}) collective-permute-start(bf16[2,17,16,128]{3,2,1,0:T(8,128)(2,1)S(1)} %get-tuple-element.69), channel_id=1, source_target_pairs={{0,1},{1,0},{2,3},{3,2},{4,5},{5,4},{6,7},{7,6},{8,9},{9,8},{10,11... | collective-permute-start | bytes 417800 | tf_op jit(solution)/shard_map/ppermute | solution.py:343
  23.2 18.4 %collective-permute-start.6 = (bf16[15,32,128]{2,1,0:T(8,128)(2,1)S(1)}, bf16[15,32,128]{2,1,0:T(8,128)(2,1)S(1)}, u32[]{:S(2)}, u32[]{:S(2)}) collective-permute-start(bf16[15,32,128]{2,1,0:T(8,128)(2,1)S(1)} %get-tuple-element.58), channel_id=1, source_target_pairs={{0,16},{4,20},{8,24},{12,28},{16,0},{20,4},{24,8},{28,12},{1,17},{... | collective-permute-start | bytes 368648 | tf_op jit(solution)/shard_map/ppermute | solution.py:326
  25.9 19.3 %collective-permute-start.7 = (bf16[15,32,128]{2,1,0:T(8,128)(2,1)S(1)}, bf16[15,32,128]{2,1,0:T(8,128)(2,1)S(1)}, u32[]{:S(2)}, u32[]{:S(2)}) collective-permute-start(bf16[15,32,128]{2,1,0:T(8,128)(2,1)S(1)} %get-tuple-element.59), channel_id=1, source_target_pairs={{0,20},{4,16},{8,28},{12,24},{16,4},{20,0},{24,12},{28,8},{1,21},{... | collective-permute-start | bytes 368648 | tf_op jit(solution)/shard_map/ppermute | solution.py:326
  27.2 18.0 %collective-permute-start.8 = (bf16[15,32,128]{2,1,0:T(8,128)(2,1)S(1)}, bf16[15,32,128]{2,1,0:T(8,128)(2,1)S(1)}, u32[]{:S(2)}, u32[]{:S(2)}) collective-permute-start(bf16[15,32,128]{2,1,0:T(8,128)(2,1)S(1)} %get-tuple-element.60), channel_id=1, source_target_pairs={{0,4},{4,0},{8,12},{12,8},{16,20},{20,16},{24,28},{28,24},{1,5},{5... | collective-permute-start | bytes 368648 | tf_op jit(solution)/shard_map/ppermute | solution.py:326
  28.6 18.5 %collective-permute-start.15 = (bf16[17,32,128]{2,1,0:T(8,128)(2,1)S(1)}, bf16[17,32,128]{2,1,0:T(8,128)(2,1)S(1)}, u32[]{:S(2)}, u32[]{:S(2)}) collective-permute-start(bf16[17,32,128]{2,1,0:T(8,128)(2,1)S(1)} %get-tuple-element.71), channel_id=1, source_target_pairs={{0,16},{4,20},{8,24},{12,28},{16,0},{20,4},{24,8},{28,12},{1,17},{... | collective-permute-start | bytes 417800 | tf_op jit(solution)/shard_map/ppermute | solution.py:326
  31.3 19.0 %collective-permute-start.16 = (bf16[17,32,128]{2,1,0:T(8,128)(2,1)S(1)}, bf16[17,32,128]{2,1,0:T(8,128)(2,1)S(1)}, u32[]{:S(2)}, u32[]{:S(2)}) collective-permute-start(bf16[17,32,128]{2,1,0:T(8,128)(2,1)S(1)} %get-tuple-element.76), channel_id=1, source_target_pairs={{0,20},{4,16},{8,28},{12,24},{16,4},{20,0},{24,12},{28,8},{1,21},{... | collective-permute-start | bytes 417800 | tf_op jit(solution)/shard_map/ppermute | solution.py:326
  41.5 8.7 %collective-permute-start.17 = (bf16[17,32,128]{2,1,0:T(8,128)(2,1)S(1)}, bf16[17,32,128]{2,1,0:T(8,128)(2,1)S(1)}, u32[]{:S(2)}, u32[]{:S(2)}) collective-permute-start(bf16[17,32,128]{2,1,0:T(8,128)(2,1)S(1)} %get-tuple-element.77), channel_id=1, source_target_pairs={{0,4},{4,0},{8,12},{12,8},{16,20},{20,16},{24,28},{28,24},{1,5},{5... | collective-permute-start | bytes 417800 | tf_op jit(solution)/shard_map/ppermute | solution.py:326
